TPU v7x, 128 devices: a whole 4x4x4 slice. The times are simulated.
128 devices in a mesh: dp: 8 (over x_lo, y), tensor: 16 (over z, x_hi, core).
Axes of the slice: x: 4 (x_hi: 2, x_lo: 2; x = x_hi * 2 + x_lo), y: 4, z: 4, core: 2. Of those that a mesh axis runs over, the one named last changes fastest.
Arguments:
- hidden: bfloat16 [2, 64, 8192], P(None, 'dp'), may hold values from -6 to 6
- norm_gain: bfloat16 [8192], replicated, may hold values from 0.099609375 to 1.8984375
- qkv_bias: bfloat16 [5120], P('tensor'), may hold values from -16 to 16
- key_cache: bfloat16 [64, 4096, 512], P('dp', 'tensor'), may hold values from -18 to 18
- value_cache: bfloat16 [64, 4096, 512], P('dp', 'tensor'), may hold values from -6 to 6
- lengths: int32 [64], P('dp'), may hold values from 2 to 4094, as said below
- fresh_qkv: bfloat16 [8192, 5120], P(('dp', 'tensor')), may hold values from -0.0625 to 0.0625
- fresh_out: bfloat16 [8192, 4096], P(('dp', 'tensor')), may hold values from -0.1875 to 0.1875
Outputs:
- attn_output: bfloat16 [2, 64, 8192], P(None, 'dp', 'tensor')
- grouped_qkv: bfloat16 [8192, 5120], P(None, 'tensor')
- grouped_out: bfloat16 [8192, 4096], P(None, 'tensor')
Inputs may be any that keep to these rules, and one draw needn't show every extreme that they name: `lengths`: each request has at least 2 cached positions; in every block of 8 requests one has 4094 and one has 2.
All inputs are finite; a program needn't handle non-finite values.
Results may differ from a plain program's by a relative error of at most 0.027.
Values may be sent and summed in bfloat16 or wider, within the bound.
No kernel may reach another device: no remote copies, remote signals or barrier semaphores. Data moves between devices by JAX's collectives and lax.ppermute only.
A program may use at most 128 MiB of HBM per device.

v0:
```python
import math

import jax
import jax.numpy as jnp
from jax import lax
from jax.sharding import PartitionSpec as P

HD = 128
QH = 32
KVH = 4


THETA = 1000000.0
EPS = 1e-06
FLOOR = -1e30


def merged(value, axis, combine):
    everything = jax.tree.map(
        lambda part, kind: lax.all_gather(part.astype(kind), axis),
        value,
        (jnp.bfloat16, jnp.bfloat16, jnp.bfloat16),
    )

    def take(k):
        return jax.tree.map(lambda part, own: part[k].astype(own.dtype), everything, value)

    return lax.fori_loop(
        1, lax.axis_size(axis), lambda k, so_far: combine(so_far, take(k)), take(0)
    )


def rotate(values, position):
    full_width = values.shape[-1]
    half_width = full_width // 2
    inverse = THETA ** (-jnp.arange(half_width, dtype=jnp.float32) * 2.0 / full_width)
    angles = position[..., None] * inverse
    cosine = jnp.cos(angles)
    sine_part = jnp.sin(angles)
    cosine = jnp.concatenate([cosine, cosine], -1)
    sine_part = jnp.concatenate([sine_part, sine_part], -1)
    turned = jnp.concatenate([-values[..., half_width:], values[..., :half_width]], -1)
    return values * cosine + turned * sine_part


def join_pair(former, latter):
    best_score = jnp.maximum(former[0], latter[0])
    former_scale = jnp.exp(former[0] - best_score)
    latter_scale = jnp.exp(latter[0] - best_score)
    totals = former[1] * former_scale + latter[1] * latter_scale
    partial_value = former[2] * former_scale[..., None] + latter[2] * latter_scale[..., None]
    return (best_score, totals, partial_value)


def regroup(natural, groups):
    row_count = natural.shape[0]
    query_part = natural[:, : QH * HD].reshape(row_count, groups, -1)
    key_part = natural[:, QH * HD : QH * HD + KVH * HD].reshape(row_count, groups, -1)
    value_part = natural[:, QH * HD + KVH * HD :].reshape(row_count, groups, -1)
    return jnp.concatenate([query_part, key_part, value_part], 2).reshape(row_count, -1)


def on_device(hidden, norm_gain, qkv_bias, key_cache, value_cache, lengths, fresh_qkv, fresh_out):
    groups = lax.axis_size("tensor")
    member = lax.axis_index("tensor")
    local_qkv = regroup(fresh_qkv, groups)
    replicas = lax.axis_size("dp")
    rows_qkv, rows_out = (
        lax.all_gather(local_qkv, "dp", axis=0, tiled=True),
        lax.all_gather(fresh_out, "dp", axis=0, tiled=True),
    )
    moved_qkv, moved_out = (
        lax.all_to_all(rows_qkv, "tensor", split_axis=1, concat_axis=0, tiled=True),
        lax.all_to_all(rows_out, "tensor", split_axis=1, concat_axis=0, tiled=True),
    )
    grouped_qkv = (
        moved_qkv.reshape(groups, replicas, -1, moved_qkv.shape[1])
        .transpose(1, 0, 2, 3)
        .reshape(-1, moved_qkv.shape[1])
    )
    grouped_out = (
        moved_out.reshape(groups, replicas, -1, moved_out.shape[1])
        .transpose(1, 0, 2, 3)
        .reshape(-1, moved_out.shape[1])
    )
    step_count, row_count, feature_width = hidden.shape
    group_width = grouped_qkv.shape[1]
    query_width = QH * HD // groups
    kv_width = KVH * HD // groups
    own_heads = QH // groups
    per_kv = QH // KVH
    score_scale = 1.0 / math.sqrt(HD)
    states = hidden.astype(jnp.float32)
    normed = (
        states
        * lax.rsqrt(jnp.mean(states * states, -1, keepdims=True) + EPS)
        * norm_gain.astype(jnp.float32)
    )
    normed = normed.astype(jnp.bfloat16).reshape(step_count * row_count, feature_width)
    projected = jnp.dot(normed, grouped_qkv, preferred_element_type=jnp.float32) + qkv_bias.astype(
        jnp.float32
    )
    projected = projected.astype(jnp.bfloat16)
    gathered = lax.all_gather(projected, "tensor", axis=1, tiled=True)
    grouped = gathered.reshape(step_count, row_count, groups, group_width)
    queries = grouped[..., :query_width].reshape(step_count, row_count, QH, HD)
    new_keys = grouped[..., query_width : query_width + kv_width].reshape(
        step_count, row_count, KVH, HD
    )
    new_values = grouped[..., query_width + kv_width :].reshape(step_count, row_count, KVH, HD)
    position = (lengths[None, :] + jnp.arange(step_count, dtype=jnp.int32)[:, None]).astype(
        jnp.float32
    )[:, :, None]
    queries = rotate(queries.astype(jnp.float32), position).astype(jnp.bfloat16)
    new_keys = rotate(new_keys.astype(jnp.float32), position).astype(jnp.bfloat16)
    cache_span = key_cache.shape[1]
    offset = member * cache_span
    valid_rows = (offset + jnp.arange(cache_span, dtype=jnp.int32))[None, :] < lengths[:, None]
    valid_mask = valid_rows[None, :, None, None, :]
    cache_keys = key_cache.reshape(row_count, cache_span, KVH, HD)
    cache_values = value_cache.reshape(row_count, cache_span, KVH, HD)
    grouped_queries = queries.reshape(step_count, row_count, KVH, per_kv, HD)
    scores = (
        jnp.einsum(
            "srkgd,rpkd->srkgp", grouped_queries, cache_keys, preferred_element_type=jnp.float32
        )
        * score_scale
    )
    scores = jnp.where(valid_mask, scores, FLOOR)
    highest = jnp.max(scores, -1)
    weights = jnp.where(valid_mask, jnp.exp(scores - highest[..., None]), 0.0)
    totals = jnp.sum(weights, -1)
    partial_value = jnp.einsum(
        "srkgp,rpkd->srkgd",
        weights.astype(jnp.bfloat16),
        cache_values,
        preferred_element_type=jnp.float32,
    )
    highest = highest.reshape(step_count, row_count, QH)
    totals = totals.reshape(step_count, row_count, QH)
    partial_value = partial_value.reshape(step_count, row_count, QH, HD)
    head_start = member * own_heads
    highest, totals, partial_value = merged((highest, totals, partial_value), "tensor", join_pair)
    highest = lax.dynamic_slice_in_dim(highest, head_start, own_heads, 2)
    totals = lax.dynamic_slice_in_dim(totals, head_start, own_heads, 2)
    partial_value = lax.dynamic_slice_in_dim(partial_value, head_start, own_heads, 2)
    own_queries = lax.dynamic_slice_in_dim(queries, head_start, own_heads, 2)
    kv_index = head_start // per_kv
    own_keys = lax.dynamic_slice_in_dim(new_keys, kv_index, 1, 2)[:, :, 0]
    own_values = lax.dynamic_slice_in_dim(new_values, kv_index, 1, 2)[:, :, 0]
    fresh_scores = (
        jnp.einsum("srhd,trd->srht", own_queries, own_keys, preferred_element_type=jnp.float32)
        * score_scale
    )
    causal = (jnp.arange(step_count)[None, :] <= jnp.arange(step_count)[:, None])[:, None, None, :]
    fresh_scores = jnp.where(causal, fresh_scores, FLOOR)
    best_score = jnp.maximum(highest, jnp.max(fresh_scores, -1))
    rescale = jnp.exp(highest - best_score)
    fresh_weights = jnp.where(causal, jnp.exp(fresh_scores - best_score[..., None]), 0.0)
    totals = totals * rescale + jnp.sum(fresh_weights, -1)
    mixture = partial_value * rescale[..., None] + jnp.einsum(
        "srht,trd->srhd",
        fresh_weights.astype(jnp.bfloat16),
        own_values,
        preferred_element_type=jnp.float32,
    )
    attended = (
        (mixture / totals[..., None])
        .astype(jnp.bfloat16)
        .reshape(step_count * row_count, own_heads * HD)
    )
    term_sums = jnp.dot(attended, grouped_out.T, preferred_element_type=jnp.float32).reshape(
        step_count, row_count, feature_width
    )
    attn_output = lax.psum_scatter(
        term_sums.astype(jnp.bfloat16), "tensor", scatter_dimension=2, tiled=True
    )
    return (attn_output, grouped_qkv, grouped_out)


def solution(mesh):
    return jax.shard_map(
        on_device,
        mesh=mesh,
        in_specs=(
            P(None, "dp", None),
            P(),
            P("tensor"),
            P("dp", "tensor", None),
            P("dp", "tensor", None),
            P("dp"),
            P(("dp", "tensor"), None),
            P(("dp", "tensor"), None),
        ),
        out_specs=(P(None, "dp", "tensor"), P(None, "tensor"), P(None, "tensor")),
        check_vma=False,
    )
```

profile of v0, /device:TPU:1, one launch (start us, length us, event | category | flops | bytes accessed | tf_op | source)
XLA Modules:
  0.0 408.1 jit_solution(17517418591911707181)
XLA Ops:
  7.2 0.9 fusion.64
  9.2 1.5 reshape.219
  10.8 0.7 all-gather.9.cloned.1.call-update
  11.5 65.0 %all-gather.5.cloned.1.call-done = bf16[512,5120]{1,0:T(8,128)(2,1)} async-done(((bf16[64,5120]{1,0:T(8,128)(2,1)}), bf16[512,5120]{1,0:T(8,128)(2,1)}) %all-gather.5.cloned.1.call-update) | async-done | bytes 5242896 | tf_op jit(solution)/shard_map/all_gather | solution.py:69
  76.5 7.9 %copy.151 = bf16[512,5120]{0,1:T(8,128)(2,1)} copy(bf16[512,5120]{1,0:T(8,128)(2,1)} %all-gather.5.cloned.1.call-done) | data formatting | bytes 10485760 | tf_op jit(solution)/shard_map/all_gather | solution.py:69
  84.4 7.4 %all-to-all-start = ((bf16[512,16,320]{0,2,1:T(8,128)(2,1)}), bf16[512,16,320]{0,2,1:T(8,128)(2,1)}, u32[]{:S(2)}, u32[]{:S(2)}) async-start(bf16[512,16,320]{0,2,1:T(8,128)(2,1)} %bitcast.119), calls=%async_computation | async-start | bytes 10485760 | tf_op jit(solution)/shard_map/all_to_all | solution.py:73
  92.4 72.9 %all-gather.9.cloned.1.call-done = bf16[512,4096]{1,0:T(8,128)(2,1)} async-done(((bf16[64,4096]{1,0:T(8,128)(2,1)}), bf16[512,4096]{1,0:T(8,128)(2,1)}) %all-gather.9.cloned.1.call-update) | async-done | bytes 4194320 | tf_op jit(solution)/shard_map/all_gather | solution.py:70
  165.3 6.4 %copy.178 = bf16[512,4096]{0,1:T(8,128)(2,1)} copy(bf16[512,4096]{1,0:T(8,128)(2,1)} %all-gather.9.cloned.1.call-done) | data formatting | bytes 8388608 | tf_op jit(solution)/shard_map/all_gather | solution.py:70
  171.7 15.6 %all-to-all-done = bf16[512,16,320]{0,2,1:T(8,128)(2,1)} async-done(((bf16[512,16,320]{0,2,1:T(8,128)(2,1)}), bf16[512,16,320]{0,2,1:T(8,128)(2,1)}, u32[]{:S(2)}, u32[]{:S(2)}) %all-to-all-start) | async-done | bytes 5242912 | tf_op jit(solution)/shard_map/all_to_all | solution.py:73
  187.3 5.0 %all-to-all-start.1 = ((bf16[512,16,256]{0,2,1:T(8,128)(2,1)}), bf16[512,16,256]{0,2,1:T(8,128)(2,1)}, u32[]{:S(2)}, u32[]{:S(2)}) async-start(bf16[512,16,256]{0,2,1:T(8,128)(2,1)} %bitcast.122), calls=%async_computation.1 | async-start | bytes 8388608 | tf_op jit(solution)/shard_map/all_to_all | solution.py:74
  192.5 2.6 reshape.223
  195.1 4.0 reshape.224
  199.1 8.1 %copy.152 = bf16[16,512,320]{2,1,0:T(8,128)(2,1)} copy(bf16[16,512,320]{1,2,0:T(8,128)(2,1)} %bitcast.8) | data formatting | bytes 10485760 | tf_op jit(solution)/shard_map/all_to_all | solution.py:73
  207.2 3.6 copy.153
  210.8 1.0 fusion.26
  211.8 1.7 copy-done
  213.5 44.4 %all-gather = bf16[16,320,16]{1,2,0:T(8,128)(2,1)S(1)} all-gather(bf16[1,320,16]{1,2,0:T(8,128)(2,1)S(1)} %fusion.26), channel_id=1, replica_groups=mesh['dp'=8,'tensor'=16] {'tensor'}, dimensions={0}, use_global_device_ids=true | all-gather | bytes 174080 | tf_op jit(solution)/shard_map/all_gather | solution.py:104
  258.5 0.9 copy_bitcast_fusion.3
  259.4 0.8 fusion.68
  260.2 0.8 copy-done.1
  261.0 0.5 fusion.19
  261.5 0.7 copy.259
  262.3 6.4 %copy.179 = bf16[16,512,256]{2,1,0:T(8,128)(2,1)} copy(bf16[16,512,256]{1,2,0:T(8,128)(2,1)} %bitcast.36) | data formatting | bytes 8388608 | tf_op jit(solution)/shard_map/all_to_all | solution.py:74
  268.7 4.9 %copy.180 = bf16[8,16,64,256]{3,2,1,0:T(8,128)(2,1)} copy(bf16[8,16,64,256]{3,2,0,1:T(8,128)(2,1)} %bitcast.123) | data formatting | bytes 8388608 | tf_op jit(solution)/shard_map/transpose | solution.py:83
  273.6 0.3 fusion.31
  274.5 0.3 fusion.51
  275.2 21.2 %all_gather.24 = bf16[16,2,8,32]{3,2,1,0:T(8,128)(2,1)S(1)} all-gather(bf16[1,2,8,32]{3,2,1,0:T(8,128)(2,1)S(1)} %convert_element_type.176), channel_id=1, replica_groups=mesh['dp'=8,'tensor'=16] {'tensor'}, dimensions={0}, use_global_device_ids=true | all-gather | bytes 17408 | tf_op jit(solution)/shard_map/all_gather | solution.py:20
  296.4 20.7 %all_gather.23 = bf16[16,2,8,32]{3,2,1,0:T(8,128)(2,1)S(1)} all-gather(bf16[1,2,8,32]{3,2,1,0:T(8,128)(2,1)S(1)} %convert_element_type.172), channel_id=1, replica_groups=mesh['dp'=8,'tensor'=16] {'tensor'}, dimensions={0}, use_global_device_ids=true | all-gather | bytes 17408 | tf_op jit(solution)/shard_map/all_gather | solution.py:20
  317.2 0.9 fusion.42
  318.1 18.4 %while.19 = (s32[]{:T(128)}, f32[2,8,32]{2,1,0:T(8,128)S(1)}, f32[2,8,32]{2,1,0:T(8,128)S(1)}, f32[2,8,32,128]{3,2,1,0:T(8,128)S(1)}, bf16[16,2,8,32]{3,2,1,0:T(...) while((s32[]{:T(128)}, f32[2,8,32]{2,1,0:T(8,128)S(1)}, ...), condition=%wide.region_4.5_spmd, body=%wide.region_3.4_spmd.sunk | while | flops 266245 | bytes 673943 | solution.py:28
  318.2 1.2 fusion.78
  319.4 1.2 fusion.78
  320.6 1.2 fusion.78
  321.9 1.2 fusion.78
  323.1 1.2 fusion.78
  324.3 1.2 fusion.78
  325.6 1.2 fusion.78
  326.8 1.2 fusion.78
  328.0 1.2 fusion.78
  329.2 1.2 fusion.78
  330.5 1.2 fusion.78
  331.7 1.2 fusion.78
  332.9 1.2 fusion.78
  334.1 1.2 fusion.78
  335.4 1.2 fusion.78
  337.3 4.1 %convolution_convert_fusion = bf16[2,8,8192]{2,1,0:T(8,128)(2,1)} fusion(bf16[8192,256,1]{1,0,2:T(8,128)(2,1)} %bitcast.120, bf16[2,8,256]{2,0,1:T(2,128)(2,1)S(1)} %dot_general.25), kind=kOutput, calls=%fused_computation.8 | convolution fusion | flops 67239936 | bytes 4464640 | tf_op jit(solution)/shard_map/dot_general | solution.py:172
  341.5 8.2 %copy.182 = bf16[8192,320]{0,1:T(8,128)(2,1)} copy(bf16[8192,320]{1,0:T(8,128)(2,1)} %bitcast.117) | data formatting | bytes 10485760
  349.6 51.9 %reduce-scatter.2.cloned.1.call-done = bf16[2,8,512]{2,1,0:T(8,128)(2,1)} async-done(((bf16[2,8,8192]{2,1,0:T(8,128)(2,1)}), bf16[2,8,512]{2,1,0:T(8,128)(2,1)}) %reduce-scatter.2.cloned.1.call-update) | async-done | bytes 16400 | tf_op jit(solution)/shard_map/reduce_scatter | solution.py:175
  (94 shorter events, 4.5 us)
Async XLA Ops:
  7.2 1.8 slice-start
  7.2 69.3 %all-gather.5.cloned.1.call-start = ((), (), s32[]{:S(2)}) async-start(), calls=%async_computation.3 | async-start | bytes 5898240 | tf_op jit(solution)/shard_map/all_gather | solution.py:69
  10.7 154.6 %all-gather.9.cloned.1.call-start = ((), (), s32[]{:S(2)}) async-start(), calls=%async_computation.5 | async-start | bytes 4718592 | tf_op jit(solution)/shard_map/all_gather | solution.py:70
  84.4 7.4 %copy-start.2 = (bf16[2,8,8192]{2,1,0:T(8,128)(2,1)S(1)}, bf16[2,8,8192]{2,1,0:T(8,128)(2,1)}, u32[]{:S(2)}) copy-start(bf16[2,8,8192]{2,1,0:T(8,128)(2,1)} %param.10) | copy-start | bytes 786436
  84.4 7.6 %copy-start.6 = (s32[8]{0:T(128)S(1)}, s32[8]{0:T(128)}, u32[]{:S(2)}) copy-start(s32[8]{0:T(128)} %param.15) | copy-start | bytes 100
  84.4 102.9 %all-to-all-start = ((bf16[512,16,320]{0,2,1:T(8,128)(2,1)}), bf16[512,16,320]{0,2,1:T(8,128)(2,1)}, u32[]{:S(2)}, u32[]{:S(2)}) async-start(bf16[512,16,320]{0,2,1:T(8,128)(2,1)} %bitcast.119), calls=%async_computation | async-start | bytes 10485760 | tf_op jit(solution)/shard_map/all_to_all | solution.py:73
  187.3 5.1 %copy-start.5 = (bf16[8192]{0:T(1024)(128)(2,1)S(1)}, bf16[8192]{0:T(1024)(128)(2,1)}, u32[]{:S(2)}) copy-start(bf16[8192]{0:T(1024)(128)(2,1)} %param.11) | copy-start | bytes 49156
  187.3 5.2 %copy-start.7 = (bf16[320]{0:T(512)(128)(2,1)S(1)}, bf16[320]{0:T(512)(128)(2,1)}, u32[]{:S(2)}) copy-start(bf16[320]{0:T(512)(128)(2,1)} %param.12) | copy-start | bytes 1924
  187.3 74.9 %all-to-all-start.1 = ((bf16[512,16,256]{0,2,1:T(8,128)(2,1)}), bf16[512,16,256]{0,2,1:T(8,128)(2,1)}, u32[]{:S(2)}, u32[]{:S(2)}) async-start(bf16[512,16,256]{0,2,1:T(8,128)(2,1)} %bitcast.122), calls=%async_computation.1 | async-start | bytes 8388608 | tf_op jit(solution)/shard_map/all_to_all | solution.py:74
  192.3 124.9 %all-gather.7.cloned.1.call-start = ((), (), s32[]{:S(2)}) async-start(), calls=%async_computation.4 | async-start | bytes 2228224 | tf_op jit(solution)/shard_map/all_gather | solution.py:20
  210.8 2.7 copy-start
  259.4 1.6 copy-start.1
  262.2 139.4 %reduce-scatter.2.cloned.1.call-start = ((), (), s32[]{:S(2)}) async-start(), calls=%async_computation.6 | async-start | bytes 278528 | tf_op jit(solution)/shard_map/reduce_scatter | solution.py:175
  268.7 5.8 %copy-start.3 = (f32[2,8,32,64]{3,2,0,1:T(8,128)S(1)}, f32[2,8,32,64]{3,2,0,1:T(8,128)}, u32[]{:S(2)}) copy-start(f32[2,8,32,64]{3,2,0,1:T(8,128)} %get-tuple-element.226) | copy-start | bytes 393220
  268.7 5.8 %copy-start.4 = (f32[2,8,32,64]{3,2,0,1:T(8,128)S(1)}, f32[2,8,32,64]{3,2,0,1:T(8,128)}, u32[]{:S(2)}) copy-start(f32[2,8,32,64]{3,2,0,1:T(8,128)} %get-tuple-element.237) | copy-start | bytes 393220
Sparse Core Ops, SparseCore 0:
  10.8 65.6 all-gather.4
  78.1 87.0 all-gather.8
  262.3 44.6 all-gather.6
  341.6 59.9 reduce-scatter.1
where the time goes:
time: 411 us; the launch traced here: 408 us
  waiting for transfers between devices  206 us (50%)
  blocking collectives  86.3 us (21%)
  local copies, waits for them, and re-layouts  60.1 us (15%)
  other arithmetic  21.4 us (5%)
  between operations  14.2 us (3%)
  starting transfers between devices  12.5 us (3%)
  matrix products  6.79 us (2%)
    all_gather x1, waiting for transfers between devices, on_device(): lax.all_gather(fresh_out, 'dp', axis=0, tiled=True)  72.9 us
    all_gather x1, waiting for transfers between devices, on_device(): lax.all_gather(local_qkv, 'dp', axis=0, tiled=True)  65 us
    reduce_scatter x1, waiting for transfers between devices, on_device(): lax.psum_scatter(term_sums.astype(jnp.bfloat16), 'tensor', scatter_dimens...  51.9 us
    all_gather x1, blocking collectives, on_device(): gathered = lax.all_gather(projected, 'tensor', axis=1, tiled=True)  44.4 us
    all_gather x2, blocking collectives, merged(): lax.all_gather(part.astype(kind), axis)  41.9 us
    add x15, other arithmetic, join_pair(): former[2] * former_scale[..., None] + latter[2] * latter_scale[..., None]  17.6 us
    all_to_all x1, waiting for transfers between devices, on_device(): lax.all_to_all(rows_qkv, 'tensor', split_axis=1, concat_axis=0, tiled=True)  15.6 us
    unnamed x24, local copies, waits for them, and re-layouts  11.4 us
  transfers between devices with their start and end apart: 6, of which 4 were waited for; matrix products, arithmetic and copies ran while one was open for 14% of the time, Pallas kernels for 0%

commit v1 on v0

v1 whole, which is shorter than its diff:
```python
import math

import jax
import jax.numpy as jnp
from jax import lax
from jax.sharding import PartitionSpec as P

HD = 128
QH = 32
KVH = 4
THETA = 1000000.0
EPS = 1e-06
FLOOR = -1e30


def rotate(values, position):
    full_width = values.shape[-1]
    half_width = full_width // 2
    inverse = THETA ** (-jnp.arange(half_width, dtype=jnp.float32) * 2.0 / full_width)
    angles = position[..., None] * inverse
    cosine = jnp.cos(angles)
    sine_part = jnp.sin(angles)
    cosine = jnp.concatenate([cosine, cosine], -1)
    sine_part = jnp.concatenate([sine_part, sine_part], -1)
    turned = jnp.concatenate([-values[..., half_width:], values[..., :half_width]], -1)
    return values * cosine + turned * sine_part


def column_groups(natural, groups):
    row_count = natural.shape[0]
    query_part = natural[:, : QH * HD].reshape(row_count, groups, -1)
    key_part = natural[:, QH * HD : QH * HD + KVH * HD].reshape(row_count, groups, -1)
    value_part = natural[:, QH * HD + KVH * HD :].reshape(row_count, groups, -1)
    return jnp.concatenate([query_part, key_part, value_part], 2).transpose(1, 0, 2)


def exchange(blocks, axis):
    return lax.all_to_all(blocks, axis, split_axis=0, concat_axis=0, tiled=True)


def two_halves(value):
    upper = lax.reduce_precision(value, 8, 7)
    return upper, lax.reduce_precision(value - upper, 8, 7)


def on_device(hidden, norm_gain, qkv_bias, key_cache, value_cache, lengths, fresh_qkv, fresh_out):
    groups = lax.axis_size("tensor")
    member = lax.axis_index("tensor")
    replicas = lax.axis_size("dp")
    step_count, row_count, feature_width = hidden.shape
    slots = step_count * row_count
    share = feature_width // replicas
    query_width = QH * HD // groups
    kv_width = KVH * HD // groups
    own_heads = QH // groups
    per_kv = QH // KVH
    score_scale = 1.0 / math.sqrt(HD)

    own_qkv = exchange(column_groups(fresh_qkv, groups), "tensor").reshape(share, -1)
    own_out = exchange(
        fresh_out.reshape(fresh_out.shape[0], groups, -1).transpose(1, 0, 2), "tensor"
    ).reshape(share, -1)

    states = hidden.astype(jnp.float32)
    normed = (
        states
        * lax.rsqrt(jnp.mean(states * states, -1, keepdims=True) + EPS)
        * norm_gain.astype(jnp.float32)
    )
    normed = normed.astype(jnp.bfloat16).reshape(slots, replicas, share).transpose(1, 0, 2)
    all_normed = exchange(normed, "dp").reshape(replicas * slots, share)

    grouped_out = lax.all_gather(own_out, "dp", axis=0, tiled=True)
    grouped_qkv = lax.all_gather(own_qkv.T, "dp", axis=1, tiled=True).T

    terms = jnp.dot(all_normed, own_qkv, preferred_element_type=jnp.float32)
    terms = exchange(terms.reshape(replicas, slots, -1), "dp")
    projected = (jnp.sum(terms, 0) + qkv_bias.astype(jnp.float32)).astype(jnp.bfloat16)
    gathered = exchange(jnp.broadcast_to(projected[None], (groups,) + projected.shape), "tensor")

    grouped = gathered.reshape(groups, step_count, row_count, -1).transpose(1, 2, 0, 3)
    queries = grouped[..., :query_width].reshape(step_count, row_count, QH, HD)
    new_keys = grouped[..., query_width : query_width + kv_width].reshape(
        step_count, row_count, KVH, HD
    )
    new_values = grouped[..., query_width + kv_width :].reshape(step_count, row_count, KVH, HD)
    position = (lengths[None, :] + jnp.arange(step_count, dtype=jnp.int32)[:, None]).astype(
        jnp.float32
    )[:, :, None]
    queries = rotate(queries.astype(jnp.float32), position).astype(jnp.bfloat16)
    new_keys = rotate(new_keys.astype(jnp.float32), position).astype(jnp.bfloat16)

    cache_span = key_cache.shape[1]
    offset = member * cache_span
    valid_rows = (offset + jnp.arange(cache_span, dtype=jnp.int32))[None, :] < lengths[:, None]
    valid_mask = valid_rows[None, :, None, None, :]
    cache_keys = key_cache.reshape(row_count, cache_span, KVH, HD)
    cache_values = value_cache.reshape(row_count, cache_span, KVH, HD)
    grouped_queries = queries.reshape(step_count, row_count, KVH, per_kv, HD)
    scores = (
        jnp.einsum(
            "srkgd,rpkd->srkgp", grouped_queries, cache_keys, preferred_element_type=jnp.float32
        )
        * score_scale
    )
    scores = jnp.where(valid_mask, scores, FLOOR)
    highest_upper, highest_lower = two_halves(jnp.max(scores, -1))
    highest = highest_upper + highest_lower
    weights = jnp.where(valid_mask, jnp.exp(scores - highest[..., None]), 0.0)
    totals_upper, totals_lower = two_halves(jnp.sum(weights, -1))
    partial_value = jnp.einsum(
        "srkgp,rpkd->srkgd",
        weights.astype(jnp.bfloat16),
        cache_values,
        preferred_element_type=jnp.float32,
    )

    def by_head(part):
        return part.reshape(slots, groups, own_heads, -1).transpose(1, 0, 2, 3)

    facts = jnp.concatenate(
        [
            by_head(part).reshape(groups, 1, slots * own_heads)
            for part in (highest_upper, highest_lower, totals_upper, totals_lower)
        ],
        2,
    )
    message = jnp.concatenate(
        [
            by_head(partial_value).astype(jnp.bfloat16).reshape(groups, slots * own_heads, HD),
            facts.astype(jnp.bfloat16),
        ],
        1,
    )
    message = exchange(message, "tensor")
    parts = message[:, : slots * own_heads].astype(jnp.float32)
    facts = message[:, slots * own_heads].astype(jnp.float32).reshape(groups, 4, slots * own_heads)
    highest = facts[:, 0] + facts[:, 1]
    totals = facts[:, 2] + facts[:, 3]

    head_start = member * own_heads
    own_queries = lax.dynamic_slice_in_dim(queries, head_start, own_heads, 2)
    kv_index = head_start // per_kv
    own_keys = lax.dynamic_slice_in_dim(new_keys, kv_index, 1, 2)[:, :, 0]
    own_values = lax.dynamic_slice_in_dim(new_values, kv_index, 1, 2)[:, :, 0]
    fresh_scores = (
        jnp.einsum("srhd,trd->srht", own_queries, own_keys, preferred_element_type=jnp.float32)
        * score_scale
    )
    causal = (jnp.arange(step_count)[None, :] <= jnp.arange(step_count)[:, None])[:, None, None, :]
    fresh_scores = jnp.where(causal, fresh_scores, FLOOR).reshape(slots * own_heads, step_count)
    best_score = jnp.maximum(jnp.max(highest, 0), jnp.max(fresh_scores, -1))
    rescale = jnp.exp(highest - best_score)
    fresh_weights = jnp.exp(fresh_scores - best_score[:, None])
    totals = jnp.sum(totals * rescale, 0) + jnp.sum(fresh_weights, -1)
    mixture = jnp.sum(parts * rescale[..., None], 0) + jnp.einsum(
        "srht,trd->srhd",
        fresh_weights.astype(jnp.bfloat16).reshape(step_count, row_count, own_heads, step_count),
        own_values,
        preferred_element_type=jnp.float32,
    ).reshape(slots * own_heads, HD)
    attended = (mixture / totals[:, None]).astype(jnp.bfloat16).reshape(slots, own_heads * HD)

    term_sums = jnp.dot(attended, grouped_out.T, preferred_element_type=jnp.float32)
    term_sums = term_sums.astype(jnp.bfloat16).reshape(slots, groups, -1).transpose(1, 0, 2)
    attn_output = jnp.sum(exchange(term_sums, "tensor").astype(jnp.float32), 0)
    attn_output = attn_output.astype(jnp.bfloat16).reshape(step_count, row_count, -1)
    return (attn_output, grouped_qkv, grouped_out)


def solution(mesh):
    return jax.shard_map(
        on_device,
        mesh=mesh,
        in_specs=(
            P(None, "dp", None),
            P(),
            P("tensor"),
            P("dp", "tensor", None),
            P("dp", "tensor", None),
            P("dp"),
            P(("dp", "tensor"), None),
            P(("dp", "tensor"), None),
        ),
        out_specs=(P(None, "dp", "tensor"), P(None, "tensor"), P(None, "tensor")),
        check_vma=False,
    )
```

time: 411 us -> 190 us (0.46)
  waiting for transfers between devices: 206 us -> 54.2 us
  local copies, waits for them, and re-layouts: 60.1 us -> 25.7 us
  blocking collectives: 86.3 us -> 62.3 us
  other arithmetic: 21.4 us -> 5.24 us
  starting transfers between devices: 12.5 us -> 18.4 us
    all_gather x3 -> x2, waiting for transfers between devices: 138 us -> 24.4 us  [the longest x1 24.4 us: on_device(): grouped_qkv = lax.all_gather(own_qkv.T, 'dp', axis=1, tiled=True).T]
    all_gather x3 -> x0, blocking collectives: 86.3 us -> none  [the longest x1 44.4 us: on_device(): gathered = lax.all_gather(projected, 'tensor', axis=1, tiled=True)]
    all_to_all x0 -> x3, blocking collectives: none -> 62.3 us  [exchange(): return lax.all_to_all(blocks, axis, split_axis=0, concat_axis=0, tiled=True)]
    reduce_scatter x1 -> x0, waiting for transfers between devices: 51.9 us -> none  [on_device(): lax.psum_scatter(term_sums.astype(jnp.bfloat16), 'tensor', scatter_dimens...]
    add x31 -> x2, other arithmetic: 18 us -> 0.02 us  [the longest x1 0.01 us: on_device(): highest = highest_upper + highest_lower]
    all_to_all x2 -> x0, local copies, waits for them, and re-layouts: 14.5 us -> none  [the longest x1 8.15 us: on_device(): lax.all_to_all(rows_qkv, 'tensor', split_axis=1, concat_axis=0, tiled=True)]
    all_gather x3 -> x0, local copies, waits for them, and re-layouts: 14.4 us -> none  [the longest x1 7.92 us: on_device(): lax.all_gather(local_qkv, 'dp', axis=0, tiled=True)]
    all_to_all x2 -> x4, waiting for transfers between devices: 15.6 us -> 29.8 us  [exchange(): return lax.all_to_all(blocks, axis, split_axis=0, concat_axis=0, tiled=True)]
  transfers between devices with their start and end apart: 6 -> 6, of which waited for: 4 -> 5; matrix products, arithmetic and copies ran while one was open for 14% -> 14% of each run, Pallas kernels for 0% -> 0%
where the time goes in v1:
time: 190 us; the launch traced here: 189 us
  blocking collectives  62.3 us (33%)
  waiting for transfers between devices  54.2 us (29%)
  local copies, waits for them, and re-layouts  25.7 us (14%)
  starting transfers between devices  18.4 us (10%)
  between operations  14.6 us (8%)
  matrix products  8.52 us (4%)
  other arithmetic  5.24 us (3%)
    all_to_all x3, blocking collectives, exchange(): return lax.all_to_all(blocks, axis, split_axis=0, concat_axis=0, tiled=True)  62.3 us
    all_to_all x4, waiting for transfers between devices, exchange(): return lax.all_to_all(blocks, axis, split_axis=0, concat_axis=0, tiled=True)  29.8 us
    all_gather x1, waiting for transfers between devices, on_device(): grouped_qkv = lax.all_gather(own_qkv.T, 'dp', axis=1, tiled=True).T  24.4 us
    all_to_all x4, starting transfers between devices, exchange(): return lax.all_to_all(blocks, axis, split_axis=0, concat_axis=0, tiled=True)  18.4 us
    unnamed x29, local copies, waits for them, and re-layouts  13.1 us
    reshape x1, local copies, waits for them, and re-layouts, on_device(): cache_values = value_cache.reshape(row_count, cache_span, KVH, HD)  3.96 us
  transfers between devices with their start and end apart: 6, of which 5 were waited for; matrix products, arithmetic and copies ran while one was open for 14% of the time, Pallas kernels for 0%

profile of v1, /device:TPU:1, one launch (start us, length us, event | category | flops | bytes accessed | tf_op | source)
XLA Modules:
  0.0 189.0 jit_solution(14271373833033149019)
XLA Ops:
  7.2 1.1 copy.270
  8.4 20.6 %all_to_all.35 = bf16[16,64,256]{2,1,0:T(8,128)(2,1)} all-to-all(bf16[16,64,256]{2,1,0:T(8,128)(2,1)S(1)} %bitcast.137), channel_id=1, replica_groups=mesh['dp'=8,'tensor'=16] {'tensor'}, dimensions={0} | all-to-all | bytes 1048576 | tf_op jit(solution)/shard_map/all_to_all | solution.py:38
  29.1 0.1 copy.215
  29.2 0.2 copy.156
  29.4 0.1 copy.216
  29.5 0.2 copy.157
  29.8 0.2 maximum_bitcast_fusion
  30.0 26.4 %all_to_all.36 = bf16[16,64,320]{2,1,0:T(8,128)(2,1)} all-to-all(bf16[16,64,320]{2,1,0:T(8,128)(2,1)S(1)} %maximum_bitcast_fusion), channel_id=1, replica_groups=mesh['dp'=8,'tensor'=16] {'tensor'}, dimensions={0} | all-to-all | bytes 1310720 | tf_op jit(solution)/shard_map/all_to_all | solution.py:38
  56.5 0.2 fusion.21
  56.7 0.1 fusion.23
  56.8 0.2 copy.222
  57.0 0.9 copy.273
  57.8 5.0 %all-to-all-start = ((bf16[8,16,1024]{2,1,0:T(8,128)(2,1)}), bf16[8,16,1024]{2,1,0:T(8,128)(2,1)S(1)}, u32[]{:S(2)}, u32[]{:S(2)}) async-start(bf16[8,16,1024]{2,1,0:T(8,128)(2,1)} %bitcast.128), calls=%async_computation | async-start | bytes 524288 | tf_op jit(solution)/shard_map/all_to_all | solution.py:38
  62.9 0.2 multiply_cosine_fusion
  63.1 11.0 %all-to-all-done = bf16[8,16,1024]{2,1,0:T(8,128)(2,1)S(1)} async-done(((bf16[8,16,1024]{2,1,0:T(8,128)(2,1)}), bf16[8,16,1024]{2,1,0:T(8,128)(2,1)S(1)}, u32[]{:S(2)}, u32[]{:S(2)}) %all-to-all-start) | async-done | bytes 262176 | tf_op jit(solution)/shard_map/all_to_all | solution.py:38
  74.1 1.0 fusion.68
  75.1 3.4 %all-to-all-start.2 = ((f32[8,16,320]{2,1,0:T(8,128)}), f32[8,16,320]{2,1,0:T(8,128)S(1)}, u32[]{:S(2)}, u32[]{:S(2)}) async-start(f32[8,16,320]{2,1,0:T(8,128)} %fusion.68), calls=%async_computation.2 | async-start | bytes 393216 | tf_op jit(solution)/shard_map/all_to_all | solution.py:38
  78.5 0.7 broadcast_compare_fusion
  79.1 9.2 %all-to-all-done.2 = f32[8,16,320]{2,1,0:T(8,128)S(1)} async-done(((f32[8,16,320]{2,1,0:T(8,128)}), f32[8,16,320]{2,1,0:T(8,128)S(1)}, u32[]{:S(2)}, u32[]{:S(2)}) %all-to-all-start.2) | async-done | bytes 163872 | tf_op jit(solution)/shard_map/all_to_all | solution.py:38
  88.3 0.7 broadcast_in_dim.36
  89.0 3.7 %all-to-all-start.3 = ((bf16[16,16,320]{2,1,0:T(8,128)(2,1)}), bf16[16,16,320]{2,1,0:T(8,128)(2,1)S(1)}, u32[]{:S(2)}, u32[]{:S(2)}) async-start(bf16[16,16,320]{2,1,0:T(8,128)(2,1)} %broadcast_in_dim.36), calls=%async_computation.3 | async-start | bytes 393216 | tf_op jit(solution)/shard_map/all_to_all | solution.py:38
  92.9 2.6 %reshape.397 = bf16[8,256,4,128]{3,2,1,0:T(4,128)(2,1)S(1)} reshape(bf16[8,256,512]{2,1,0:T(8,128)(2,1)} %param.11) | data formatting | bytes 4194304 | tf_op jit(solution)/shard_map/reshape | solution.py:97
  95.5 4.0 %reshape.398 = bf16[8,256,4,128]{3,2,1,0:T(4,128)(2,1)} reshape(bf16[8,256,512]{2,1,0:T(8,128)(2,1)} %param.12) | data formatting | bytes 4194304 | tf_op jit(solution)/shard_map/reshape | solution.py:98
  99.4 0.5 iota_compare_fusion
  100.0 1.0 all-to-all-done.3
  101.0 0.2 copy.161
  101.1 0.2 copy.159
  101.6 0.8 slice_negate_fusion
  102.4 1.5 fusion.66
  104.0 1.0 fusion.24
  105.1 0.1 reduce_sum.77
  105.6 2.1 %fusion.16 = bf16[2,8,4,8,128]{4,3,0,2,1:T(8,128)(2,1)S(1)} fusion(bf16[8,256,4,128,1]{3,2,1,0,4:T(4,128)(2,1)} %bitcast.134, f32[2,8,4,8,256]{4,3,0,2,1:T(8,128)S(1)} %get-tuple-element.37, f32[2,8,4,8]{3,0,2,1:T(2,128)S(1)} %copy.169, pred[8,256]{1,0:T(8,128)(4,1)} %broadcast_compare_fusion), kind=kOutput, calls=%fused_computation.9 | convolution fusion | flops 34013184 | bytes 2756608 | tf_op jit(solution)/shard_map/srkgp,rpkd->srkgd/dot_general | solution.py:111
  107.8 0.1 reduce_max.34
  108.3 0.1 maximum_maximum_fusion
  108.4 0.7 copy.183
  109.1 6.3 %all-to-all-start.4 = ((bf16[16,33,128]{2,1,0:T(8,128)(2,1)}), bf16[16,33,128]{2,1,0:T(8,128)(2,1)S(1)}, u32[]{:S(2)}, u32[]{:S(2)}) async-start(bf16[16,33,128]{2,1,0:T(8,128)(2,1)} %copy.183), calls=%async_computation.4 | async-start | bytes 327680 | tf_op jit(solution)/shard_map/all_to_all | solution.py:38
  115.5 0.1 fusion.56
  115.6 0.4 fusion.67
  116.0 0.1 reshape.400
  116.2 8.6 %all-to-all-done.4 = bf16[16,33,128]{2,1,0:T(8,128)(2,1)S(1)} async-done(((bf16[16,33,128]{2,1,0:T(8,128)(2,1)}), bf16[16,33,128]{2,1,0:T(8,128)(2,1)S(1)}, u32[]{:S(2)}, u32[]{:S(2)}) %all-to-all-start.4) | async-done | bytes 135200 | tf_op jit(solution)/shard_map/all_to_all | solution.py:38
  125.1 0.1 multiply_reduce_fusion
  125.5 0.2 convolution_bitcast_fusion
  125.7 3.4 %convolution_convert_fusion = bf16[16,8192]{1,0:T(8,128)(2,1)S(1)} fusion(bf16[8192,256]{1,0:T(8,128)(2,1)} %all-gather.3.cloned.1.call-done, f32[2,8,2,128]{3,2,1,0:T(2,128)S(1)} %bitcast.153, f32[16,256]{1,0:T(8,128)S(1)} %reduce_sum.79, f32[2,8,2,128]{3,2,0,1:T(2,128)S(1)} %convolution_bitcast_fusion), kind=kOutput, calls=%fused_computation | convolution fusion | flops 67252224 | bytes 4505600 | tf_op jit(solution)/shard_map/dot_general | solution.py:164
  129.2 15.3 %all_to_all.37 = bf16[16,16,512]{2,1,0:T(8,128)(2,1)S(1)} all-to-all(bf16[16,16,512]{2,1,0:T(8,128)(2,1)S(1)} %bitcast.143), channel_id=1, replica_groups=mesh['dp'=8,'tensor'=16] {'tensor'}, dimensions={0} | all-to-all | bytes 524288 | tf_op jit(solution)/shard_map/all_to_all | solution.py:38
  144.5 0.6 reduce_sum.84
  145.2 24.4 %all-gather.5.cloned.1.call-done = bf16[320,8192]{0,1:T(8,128)(2,1)} async-done(((bf16[320,1024]{0,1:T(8,128)(2,1)}), bf16[320,8192]{0,1:T(8,128)(2,1)}) %all-gather.5.cloned.1.call-update) | async-done | bytes 5242896 | tf_op jit(solution)/shard_map/all_gather | solution.py:74
  169.5 8.2 %copy.200 = bf16[8192,320]{0,1:T(8,128)(2,1)} copy(bf16[8192,320]{1,0:T(8,128)(2,1)} %bitcast.132) | data formatting | bytes 10485760
  177.7 4.5 %copy.275 = bf16[8192,256]{1,0:T(8,128)(2,1)} copy(bf16[8192,256]{1,0:T(8,128)(2,1)} %all-gather.3.cloned.1.call-done) | data formatting | bytes 8388608
  (85 shorter events, 2.5 us)
Async XLA Ops:
  7.2 21.9 %copy-start.1 = (bf16[64,5120]{1,0:T(8,128)(2,1)S(1)}, bf16[64,5120]{1,0:T(8,128)(2,1)}, u32[]{:S(2)}) copy-start(bf16[64,5120]{1,0:T(8,128)(2,1)} %param.14) | copy-start | bytes 1966084
  7.2 118.5 %all-gather.3.cloned.1.call-start = ((), (), s32[]{:S(2)}) async-start(), calls=%async_computation.7 | async-start | bytes 4718592 | tf_op jit(solution)/shard_map/all_gather | solution.py:73
  8.4 21.4 %slice-start = ((bf16[64,5120]{1,0:T(8,128)(2,1)}), bf16[64,4096]{1,0:T(8,128)(2,1)S(1)}, s32[]{:S(2)}) async-start(bf16[64,5120]{1,0:T(8,128)(2,1)} %param.14), calls=%async_computation.9 | async-start | bytes 1048576 | tf_op jit(solution)/shard_map/slice | solution.py:31
  29.0 140.5 %all-gather.5.cloned.1.call-start = ((), (), s32[]{:S(2)}) async-start(), calls=%async_computation.8 | async-start | bytes 7077888 | tf_op jit(solution)/shard_map/all_gather | solution.py:74
  29.8 26.7 %copy-start.8 = (bf16[8192]{0:T(1024)(128)(2,1)S(1)}, bf16[8192]{0:T(1024)(128)(2,1)}, u32[]{:S(2)}) copy-start(bf16[8192]{0:T(1024)(128)(2,1)} %param.9) | copy-start | bytes 49156
  29.8 26.7 %copy-start.2 = (bf16[2,8,8192]{2,1,0:T(8,128)(2,1)S(1)}, bf16[2,8,8192]{2,1,0:T(8,128)(2,1)}, u32[]{:S(2)}) copy-start(bf16[2,8,8192]{2,1,0:T(8,128)(2,1)} %param.8) | copy-start | bytes 786436
  30.0 32.8 %copy-start.9 = (s32[8]{0:T(128)S(1)}, s32[8]{0:T(128)}, u32[]{:S(2)}) copy-start(s32[8]{0:T(128)} %param.13) | copy-start | bytes 100
  30.0 32.9 %copy-start.10 = (bf16[320]{0:T(512)(128)(2,1)S(1)}, bf16[320]{0:T(512)(128)(2,1)}, u32[]{:S(2)}) copy-start(bf16[320]{0:T(512)(128)(2,1)} %param.10) | copy-start | bytes 1924
  56.4 17.6 %copy-start = (bf16[16,64,320]{2,1,0:T(8,128)(2,1)S(1)}, bf16[16,64,320]{2,1,0:T(8,128)(2,1)}, u32[]{:S(2)}) copy-start(bf16[16,64,320]{2,1,0:T(8,128)(2,1)} %all_to_all.36) | copy-start | bytes 1966084
  57.8 16.3 %all-to-all-start = ((bf16[8,16,1024]{2,1,0:T(8,128)(2,1)}), bf16[8,16,1024]{2,1,0:T(8,128)(2,1)S(1)}, u32[]{:S(2)}, u32[]{:S(2)}) async-start(bf16[8,16,1024]{2,1,0:T(8,128)(2,1)} %bitcast.128), calls=%async_computation | async-start | bytes 524288 | tf_op jit(solution)/shard_map/all_to_all | solution.py:38
  75.1 13.2 %all-to-all-start.2 = ((f32[8,16,320]{2,1,0:T(8,128)}), f32[8,16,320]{2,1,0:T(8,128)S(1)}, u32[]{:S(2)}, u32[]{:S(2)}) async-start(f32[8,16,320]{2,1,0:T(8,128)} %fusion.68), calls=%async_computation.2 | async-start | bytes 393216 | tf_op jit(solution)/shard_map/all_to_all | solution.py:38
  89.0 11.9 %all-to-all-start.3 = ((bf16[16,16,320]{2,1,0:T(8,128)(2,1)}), bf16[16,16,320]{2,1,0:T(8,128)(2,1)S(1)}, u32[]{:S(2)}, u32[]{:S(2)}) async-start(bf16[16,16,320]{2,1,0:T(8,128)(2,1)} %broadcast_in_dim.36), calls=%async_computation.3 | async-start | bytes 393216 | tf_op jit(solution)/shard_map/all_to_all | solution.py:38
  92.8 2.6 %copy-start.4 = (f32[2,8,128]{2,0,1:T(2,128)}, f32[2,8,128]{2,0,1:T(2,128)S(1)}, u32[]{:S(2)}) copy-start(f32[2,8,128]{2,0,1:T(2,128)S(1)} %get-tuple-element.40) | copy-start | bytes 24580
  92.8 2.6 %copy-start.6 = (f32[2,8,128]{2,0,1:T(2,128)}, f32[2,8,128]{2,0,1:T(2,128)S(1)}, u32[]{:S(2)}) copy-start(f32[2,8,128]{2,0,1:T(2,128)S(1)} %get-tuple-element.41) | copy-start | bytes 24580
  105.6 10.0 %copy-start.3 = (f32[2,8,32,64]{3,2,0,1:T(8,128)S(1)}, f32[2,8,32,64]{3,2,0,1:T(8,128)}, u32[]{:S(2)}) copy-start(f32[2,8,32,64]{3,2,0,1:T(8,128)} %get-tuple-element.22) | copy-start | bytes 393220
  105.6 10.0 %copy-start.5 = (f32[2,8,128]{2,0,1:T(2,128)S(1)}, f32[2,8,128]{2,0,1:T(2,128)}, u32[]{:S(2)}) copy-start(f32[2,8,128]{2,0,1:T(2,128)} %copy-done.4) | copy-start | bytes 24580
  105.6 10.0 %copy-start.7 = (f32[2,8,128]{2,0,1:T(2,128)S(1)}, f32[2,8,128]{2,0,1:T(2,128)}, u32[]{:S(2)}) copy-start(f32[2,8,128]{2,0,1:T(2,128)} %copy-done.6) | copy-start | bytes 24580
  105.6 10.0 %copy-start.11 = (pred[2,2]{1,0:T(4,128)(4,1)S(1)}, pred[2,2]{1,0:T(4,128)(4,1)}, u32[]{:S(2)}) copy-start(pred[2,2]{1,0:T(4,128)(4,1)} %iota_compare_fusion) | copy-start | bytes 16
  109.1 15.8 %all-to-all-start.4 = ((bf16[16,33,128]{2,1,0:T(8,128)(2,1)}), bf16[16,33,128]{2,1,0:T(8,128)(2,1)S(1)}, u32[]{:S(2)}, u32[]{:S(2)}) async-start(bf16[16,33,128]{2,1,0:T(8,128)(2,1)} %copy.183), calls=%async_computation.4 | async-start | bytes 327680 | tf_op jit(solution)/shard_map/all_to_all | solution.py:38
Sparse Core Ops, SparseCore 0:
  29.1 62.5 all-gather.2
  93.4 76.1 all-gather.4

commit v2 on v1

v2 whole, which is shorter than its diff:
```python
import math

import jax
import jax.numpy as jnp
from jax import lax
from jax.experimental import pallas as pl
from jax.experimental.pallas import tpu as pltpu
from jax.sharding import PartitionSpec as P

HD = 128
QH = 32
KVH = 4
THETA = 1000000.0
EPS = 1e-06
FLOOR = -1e30


def pack_kernel(groups, spot_ref, states_ref, gain_ref, qkv_ref, out_ref, packed_ref, own_ref, send_ref):
    query_width = QH * HD // groups
    kv_width = KVH * HD // groups
    rows = qkv_ref.shape[0]
    for g in range(groups):
        keys_at = QH * HD + g * kv_width
        values_at = QH * HD + KVH * HD + g * kv_width
        packed_ref[g, :, :query_width] = qkv_ref[:, g * query_width : (g + 1) * query_width]
        packed_ref[g, :, query_width : query_width + HD] = jnp.concatenate(
            [
                qkv_ref[:, keys_at : keys_at + kv_width],
                qkv_ref[:, values_at : values_at + kv_width],
                jnp.zeros((rows, HD - 2 * kv_width), qkv_ref.dtype),
            ],
            1,
        )
        packed_ref[g, :, query_width + HD :] = out_ref[:, g * query_width : (g + 1) * query_width]
    states = states_ref[...].astype(jnp.float32)
    normed = (
        states
        * lax.rsqrt(jnp.mean(states * states, -1, keepdims=True) + EPS)
        * gain_ref[...].astype(jnp.float32)
    ).astype(jnp.bfloat16)
    column, y_at = spot_ref[0], spot_ref[1]
    count, _, share = own_ref.shape
    for y in range(count):
        first = normed[:, y * share : (y + 1) * share]
        second = normed[:, (count + y) * share : (count + y + 1) * share]
        slot = (y - y_at) & 3
        own_ref[slot] = jnp.where(column == 0, first, second)
        send_ref[slot] = jnp.where(column == 0, second, first)


def terms_kernel(group_width, order_ref, own, got, low, high, far, packed_ref, terms_ref, out_ref):
    weights = packed_ref[:, :group_width]
    states = jnp.concatenate(
        [own[0], got[0], low[0], low[1], high[0], high[1], far[0], far[1]], 0
    )
    terms = jnp.dot(states, weights, preferred_element_type=jnp.float32)
    slots = own.shape[1]
    for i in range(terms.shape[0] // slots):
        terms_ref[order_ref[i]] = terms[i * slots : (i + 1) * slots]
    out_ref[...] = packed_ref[:, group_width + 64 :]


def hold_kernel(*refs):
    pass


def hold(*values):
    anywhere = pl.BlockSpec(memory_space=pl.ANY)
    return pl.pallas_call(
        hold_kernel,
        out_shape=tuple(jax.ShapeDtypeStruct(v.shape, v.dtype) for v in values),
        in_specs=[anywhere] * len(values),
        out_specs=(anywhere,) * len(values),
        input_output_aliases={i: i for i in range(len(values))},
        name="hold",
    )(*values)


def sum_kernel(groups, terms_ref, bias_ref, *refs):
    projected_ref = refs[4]
    total = jnp.sum(terms_ref[...], 0) + bias_ref[...].astype(jnp.float32)
    total = total.astype(projected_ref.dtype)
    for g in range(groups):
        projected_ref[g] = total


def turn_kernel(packed_ref, turned_ref):
    width = turned_ref.shape[0]
    turned_ref[...] = packed_ref[:, : width + 64].T[:width]


def place_kernel(axis, count, *refs):
    starts_ref, parts, whole_ref, sems = refs[0], refs[1 : 1 + count], refs[-2], refs[-1]
    pieces = sems.shape[1]
    copies = []
    for i, part in enumerate(parts):
        rows, columns = part.shape
        step = rows // pieces
        at = pl.multiple_of(starts_ref[i] * 512, 512)
        for j in range(pieces):
            if axis == 0:
                target = whole_ref.at[pl.ds(at + j * step, step), :]
            else:
                target = whole_ref.at[pl.ds(j * step, step), pl.ds(at, columns)]
            source = part.at[pl.ds(j * step, step), :]
            copies.append(pltpu.make_async_copy(source, target, sems.at[i, j]))
    for copy in copies:
        copy.start()
    for copy in copies:
        copy.wait()


def place(whole, parts, starts, axis, shape):
    count = len(parts)
    continued = whole is not None
    vmem = pl.BlockSpec(memory_space=pltpu.VMEM)
    anywhere = pl.BlockSpec(memory_space=pl.ANY)
    return pl.pallas_call(
        lambda *refs: place_kernel(axis, count, *refs),
        out_shape=jax.ShapeDtypeStruct(shape, parts[0].dtype),
        in_specs=[pl.BlockSpec(memory_space=pltpu.SMEM)]
        + [vmem] * count
        + ([anywhere] if continued else []),
        out_specs=anywhere,
        scratch_shapes=[pltpu.SemaphoreType.DMA((count, 4))],
        input_output_aliases={1 + count: 0} if continued else {},
        name="place",
    )(jnp.stack(starts).astype(jnp.int32), *parts, *((whole,) if continued else ()))


def attend_kernel(scale, facts_ref, cosine_ref, sine_ref, new_ref, key_ref, value_ref, message_ref, query_s, message_s):
    groups, slots, _ = new_ref.shape
    rows, span, _ = key_ref.shape
    per_row = query_s.shape[0] // rows
    cosine, sine = cosine_ref[...], sine_ref[...]

    def turned(values):
        values = values.astype(jnp.float32)
        return values * cosine + pltpu.roll(values, HD // 2, 1) * sine

    for t in range(groups):
        for j in range(2):
            query = turned(new_ref[t, :, j * HD : (j + 1) * HD])
            for s in range(2):
                query_s[pl.ds(t * 4 + j * 2 + s, rows, stride=per_row), :] = query[
                    s * rows : (s + 1) * rows
                ]
    start, width = 2 * HD, KVH * HD // groups
    new_keys = jnp.concatenate([new_ref[t, :, start : start + width] for t in range(groups)], 1)
    new_keys = jnp.concatenate(
        [turned(new_keys[:, k * HD : (k + 1) * HD]) for k in range(KVH)], 1
    ).astype(jnp.bfloat16)
    new_values = jnp.concatenate(
        [new_ref[t, :, start + width : start + 2 * width] for t in range(groups)], 1
    )

    member = facts_ref[rows]
    kv_of = lax.broadcasted_iota(jnp.int32, (per_row, 1), 0) // (per_row // KVH)
    position = lax.broadcasted_iota(jnp.int32, (per_row, span), 1) + member * span
    slot = lax.broadcasted_iota(jnp.int32, (per_row, slots), 1)
    step = lax.broadcasted_iota(jnp.int32, (per_row, slots), 0) % 2
    lane = lax.broadcasted_iota(jnp.int32, (per_row, HD), 1)
    for r in range(rows):
        query = query_s[r * per_row : (r + 1) * per_row, :].astype(jnp.bfloat16)
        query = jnp.concatenate(
            [jnp.where(kv_of == k, query, jnp.zeros_like(query)) for k in range(KVH)], 1
        )

        def product(keys):
            return (
                lax.dot_general(
                    query, keys, (((1,), (1,)), ((), ())), preferred_element_type=jnp.float32
                )
                * scale
            )

        valid = position < facts_ref[r]
        scores = jnp.where(valid, product(key_ref[r]), FLOOR)
        fresh = (slot % rows == r) & (slot // rows <= step) & (member == 0)
        fresh_scores = jnp.where(fresh, product(new_keys), FLOOR)
        highest = jnp.maximum(
            jnp.max(scores, 1, keepdims=True), jnp.max(fresh_scores, 1, keepdims=True)
        )
        upper = highest.astype(jnp.bfloat16).astype(jnp.float32)
        lower = (highest - upper).astype(jnp.bfloat16).astype(jnp.float32)
        highest = upper + lower
        weights = jnp.where(valid, jnp.exp(scores - highest), 0.0)
        fresh_weights = jnp.where(fresh, jnp.exp(fresh_scores - highest), 0.0)
        total = jnp.sum(weights, 1, keepdims=True) + jnp.sum(fresh_weights, 1, keepdims=True)
        mixed = jnp.dot(
            weights.astype(jnp.bfloat16), value_ref[r], preferred_element_type=jnp.float32
        ) + jnp.dot(
            fresh_weights.astype(jnp.bfloat16), new_values, preferred_element_type=jnp.float32
        )
        own = jnp.zeros((per_row, HD), jnp.float32)
        for k in range(KVH):
            own = jnp.where(kv_of == k, mixed[:, k * HD : (k + 1) * HD], own)
        total_upper = total.astype(jnp.bfloat16).astype(jnp.float32)
        total_lower = total - total_upper
        facts = jnp.where(
            lane < 64,
            jnp.where(lane < 32, upper, lower),
            jnp.where(lane < 96, total_upper, total_lower),
        )
        for t in range(groups):
            message_s[t, pl.ds(r, 4, stride=rows), :] = own[t * 4 : (t + 1) * 4]
            message_s[t, pl.ds(4 * rows + r, 4, stride=rows), :] = facts[t * 4 : (t + 1) * 4]
    message_ref[...] = message_s[...].astype(message_ref.dtype)


def merge_kernel(message_ref, attended_ref):
    message = message_ref[...].astype(jnp.float32)
    half = message.shape[1] // 2
    facts = message[:, half:]
    highest = facts[:, :, 0:1] + facts[:, :, 32:33]
    totals = facts[:, :, 64:65] + facts[:, :, 96:97]
    rescale = jnp.exp(highest - jnp.max(highest, 0, keepdims=True))
    total = jnp.sum(totals * rescale, 0)
    mixture = jnp.sum(message[:, :half] * rescale, 0)
    attended = (mixture / total).astype(attended_ref.dtype)
    attended_ref[...] = jnp.concatenate([attended[: half // 2], attended[half // 2 :]], 1)


def project_kernel(attended_ref, weight_ref, terms_ref):
    terms = lax.dot_general(
        attended_ref[...],
        weight_ref[...],
        (((1,), (1,)), ((), ())),
        preferred_element_type=jnp.float32,
    )
    terms_ref[0] = terms.astype(terms_ref.dtype)


def exchange(blocks, axis):
    return lax.all_to_all(blocks, axis, split_axis=0, concat_axis=0, tiled=True)


def on_device(hidden, norm_gain, qkv_bias, key_cache, value_cache, lengths, fresh_qkv, fresh_out):
    groups = lax.axis_size("tensor")
    member = lax.axis_index("tensor")
    replicas = lax.axis_size("dp")
    step_count, row_count, feature_width = hidden.shape
    slots = step_count * row_count
    share = feature_width // replicas
    query_width = QH * HD // groups
    kv_width = KVH * HD // groups
    own_heads = QH // groups
    score_scale = 1.0 / math.sqrt(HD)

    replica = lax.axis_index("dp")
    column, y_at = replica // 4, replica % 4
    vmem = pl.BlockSpec(memory_space=pltpu.VMEM)
    smem = pl.BlockSpec(memory_space=pltpu.SMEM)
    anywhere = pl.BlockSpec(memory_space=pl.ANY)
    across = [(i, i ^ 4) for i in range(replicas)]
    ahead = [(i, (i & 4) | ((i + 1) & 3)) for i in range(replicas)]
    behind = [(i, (i & 4) | ((i + 3) & 3)) for i in range(replicas)]
    beyond = [(i, (i & 4) | ((i + 2) & 3)) for i in range(replicas)]

    def send(value, pairs):
        return lax.ppermute(value, "dp", pairs)

    width = 2 * query_width + HD
    group_width = query_width + 2 * kv_width
    packed, own_states, other_states = pl.pallas_call(
        lambda *refs: pack_kernel(groups, *refs),
        out_shape=(
            jax.ShapeDtypeStruct((groups, fresh_qkv.shape[0], width), fresh_qkv.dtype),
            jax.ShapeDtypeStruct((replicas // 2, slots, share), jnp.bfloat16),
            jax.ShapeDtypeStruct((replicas // 2, slots, share), jnp.bfloat16),
        ),
        in_specs=[smem] + [vmem] * 4,
        name="pack",
    )(
        jnp.stack([column, y_at]).astype(jnp.int32),
        hidden.reshape(slots, feature_width),
        norm_gain.reshape(1, feature_width),
        fresh_qkv,
        fresh_out,
    )
    packed = exchange(packed, "tensor").reshape(share, width)

    cross_states = send(other_states, across)
    low_states, far_states, high_states = (
        send(jnp.stack([own_states[k], cross_states[k]]), pairs)
        for k, pairs in ((1, ahead), (2, beyond), (3, behind))
    )
    order = jnp.stack(
        [(column ^ c) * 4 + ((y_at + y) & 3) for y in (0, -1, 1, 2) for c in (0, 1)]
    ).astype(jnp.int32)

    terms, own_out = pl.pallas_call(
        lambda *refs: terms_kernel(group_width, *refs),
        out_shape=(
            jax.ShapeDtypeStruct((replicas, slots, group_width), jnp.float32),
            jax.ShapeDtypeStruct((share, query_width), packed.dtype),
        ),
        in_specs=[smem] + [vmem] * 6,
        name="terms",
    )(order, own_states, cross_states, low_states, high_states, far_states, packed)
    terms = exchange(terms, "dp")
    out_across = send(own_out, across)
    out_low, out_high = send(own_out, ahead), send(own_out, behind)
    own_qkv = pl.pallas_call(
        turn_kernel,
        out_shape=jax.ShapeDtypeStruct((group_width, share), packed.dtype),
        name="turn",
    )(packed)
    moved = (out_across, out_low, out_high, own_qkv)
    projected, out_across, out_low, out_high, own_qkv = pl.pallas_call(
        lambda terms_ref, bias_ref, *refs: sum_kernel(groups, terms_ref, bias_ref, *refs),
        out_shape=(
            jax.ShapeDtypeStruct((groups, slots, group_width), jnp.bfloat16),
            *(jax.ShapeDtypeStruct(v.shape, v.dtype) for v in moved),
        ),
        in_specs=[vmem] * 2 + [anywhere] * 4,
        out_specs=(vmem,) + (anywhere,) * 4,
        input_output_aliases={2 + i: 1 + i for i in range(4)},
        name="sum",
    )(terms, qkv_bias.reshape(1, group_width), *moved)
    gathered = exchange(projected, "tensor")

    out_cross_low, out_cross_high = send(out_across, ahead), send(out_across, behind)
    qkv_low, qkv_high = send(own_qkv, ahead), send(own_qkv, behind)
    qkv_across = send(own_qkv, across)

    def index_of(column_at, y):
        return (column_at * 4 + ((y_at + y) & 3)) * (share // 512)

    other = 1 - column
    out_shape, qkv_shape = (feature_width, query_width), (group_width, feature_width)

    half_width = HD // 2
    inverse = THETA ** (-jnp.arange(half_width, dtype=jnp.float32) * 2.0 / HD)
    position = (lengths[None, :] + jnp.arange(step_count, dtype=jnp.int32)[:, None]).astype(
        jnp.float32
    )
    angles = position.reshape(slots, 1) * inverse
    cosine, sine = jnp.cos(angles), jnp.sin(angles)
    cosine = jnp.concatenate([cosine, cosine], 1)
    sine = jnp.concatenate([-sine, sine], 1)

    grouped_out = place(
        None, [own_out, out_across], [index_of(column, 0), index_of(other, 0)], 0, out_shape
    )
    grouped_out = place(
        grouped_out, [out_low, out_high], [index_of(column, -1), index_of(column, 1)], 0, out_shape
    )

    facts = jnp.concatenate([lengths, jnp.full((1,), member, jnp.int32)])
    message = pl.pallas_call(
        lambda *refs: attend_kernel(score_scale, *refs),
        out_shape=jax.ShapeDtypeStruct((groups, 2 * slots * own_heads, HD), jnp.bfloat16),
        in_specs=[smem] + [vmem] * 5,
        scratch_shapes=[
            pltpu.VMEM((slots * QH, HD), jnp.float32),
            pltpu.VMEM((groups, 2 * slots * own_heads, HD), jnp.float32),
        ],
        name="attend",
    )(facts, cosine, sine, gathered, key_cache, value_cache)
    message, out_cross_low, out_cross_high, qkv_low, qkv_high, qkv_across, grouped_out = hold(
        message, out_cross_low, out_cross_high, qkv_low, qkv_high, qkv_across, grouped_out
    )
    message = exchange(message, "tensor")
    out_far, out_cross_far = send(out_low, ahead), send(out_cross_high, behind)
    qkv_cross_high = send(qkv_high, across)
    grouped_out = place(
        grouped_out,
        [out_cross_low, out_cross_high],
        [index_of(other, -1), index_of(other, 1)],
        0,
        out_shape,
    )
    grouped_qkv = place(
        None, [own_qkv, qkv_across], [index_of(column, 0), index_of(other, 0)], 1, qkv_shape
    )
    attended = pl.pallas_call(
        merge_kernel,
        out_shape=jax.ShapeDtypeStruct((slots, own_heads * HD), jnp.bfloat16),
        name="merge",
    )(message)
    attended, out_far, out_cross_far, qkv_cross_high, qkv_low, grouped_out, grouped_qkv = hold(
        attended, out_far, out_cross_far, qkv_cross_high, qkv_low, grouped_out, grouped_qkv
    )
    grouped_out = place(
        grouped_out,
        [out_far, out_cross_far],
        [index_of(column, 2), index_of(other, 2)],
        0,
        out_shape,
    )
    qkv_far, qkv_cross_far = send(qkv_low, ahead), send(qkv_cross_high, behind)
    qkv_cross_low = send(qkv_low, across)
    grouped_qkv = place(
        grouped_qkv,
        [qkv_low, qkv_high, qkv_cross_high],
        [index_of(column, -1), index_of(column, 1), index_of(other, 1)],
        1,
        qkv_shape,
    )
    grouped_qkv = place(
        grouped_qkv,
        [qkv_far, qkv_cross_low, qkv_cross_far],
        [index_of(column, 2), index_of(other, -1), index_of(other, 2)],
        1,
        qkv_shape,
    ).T

    span = feature_width // groups
    term_sums = pl.pallas_call(
        project_kernel,
        grid=(groups,),
        out_shape=jax.ShapeDtypeStruct((groups, slots, span), jnp.bfloat16),
        in_specs=[
            pl.BlockSpec((slots, own_heads * HD), lambda i: (0, 0)),
            pl.BlockSpec((span, own_heads * HD), lambda i: (i, 0)),
        ],
        out_specs=pl.BlockSpec((1, slots, span), lambda i: (i, 0, 0)),
        name="project",
    )(attended, grouped_out)
    attn_output = jnp.sum(exchange(term_sums, "tensor").astype(jnp.float32), 0)
    attn_output = attn_output.astype(jnp.bfloat16).reshape(step_count, row_count, -1)
    return (attn_output, grouped_qkv, grouped_out)


def solution(mesh):
    return jax.shard_map(
        on_device,
        mesh=mesh,
        in_specs=(
            P(None, "dp", None),
            P(),
            P("tensor"),
            P("dp", "tensor", None),
            P("dp", "tensor", None),
            P("dp"),
            P(("dp", "tensor"), None),
            P(("dp", "tensor"), None),
        ),
        out_specs=(P(None, "dp", "tensor"), P(None, "tensor"), P(None, "tensor")),
        check_vma=False,
    )
```

time: 190 us -> 162 us (0.85)
  blocking collectives: 62.3 us -> 0 us
  Pallas kernels: 0 us -> 45.3 us
  starting transfers between devices: 18.4 us -> 56 us
  waiting for transfers between devices: 54.2 us -> 39.3 us
  between operations: 14.6 us -> 0.95 us
  local copies, waits for them, and re-layouts: 25.7 us -> 12.9 us
  matrix products: 8.52 us -> 0 us
    all_to_all x3 -> x0, blocking collectives: 62.3 us -> none  [exchange(): return lax.all_to_all(blocks, axis, split_axis=0, concat_axis=0, tiled=True)]
    pallas_call x0 -> x16, Pallas kernels: none -> 45.3 us  [the longest x7 17.1 us: place(): pl.pallas_call(lambda *refs: place_kernel(axis, count, *refs), out_shape=...]
    all_gather x2 -> x0, waiting for transfers between devices: 24.4 us -> none  [the longest x1 24.4 us: on_device(): grouped_qkv = lax.all_gather(own_qkv.T, 'dp', axis=1, tiled=True).T]
    ppermute x0 -> x18, starting transfers between devices: none -> 19.9 us  [send(): return lax.ppermute(value, 'dp', pairs)]
    ppermute x0 -> x18, waiting for transfers between devices: none -> 19.7 us  [send(): return lax.ppermute(value, 'dp', pairs)]
    all_to_all x4 -> x5, starting transfers between devices: 18.4 us -> 36.1 us  [exchange(): return lax.all_to_all(blocks, axis, split_axis=0, concat_axis=0, tiled=True)]
    all_to_all x4 -> x5, waiting for transfers between devices: 29.8 us -> 19.6 us  [exchange(): return lax.all_to_all(blocks, axis, split_axis=0, concat_axis=0, tiled=True)]
    dot_general x6 -> x0, matrix products: 8.52 us -> none  [the longest x1 3.42 us: on_device(): jnp.dot(attended, grouped_out.T, preferred_element_type=jnp.float32)]
  transfers between devices with their start and end apart: 6 -> 23, of which waited for: 5 -> 6; matrix products, arithmetic and copies ran while one was open for 14% -> 5% of each run, Pallas kernels for 0% -> 22%
where the time goes in v2:
time: 162 us; the launch traced here: 161 us
  starting transfers between devices  56 us (35%)
  Pallas kernels  45.3 us (28%)
  waiting for transfers between devices  39.3 us (24%)
  local copies, waits for them, and re-layouts  12.9 us (8%)
  other arithmetic  6.32 us (4%)
    all_to_all x5, starting transfers between devices, exchange(): return lax.all_to_all(blocks, axis, split_axis=0, concat_axis=0, tiled=True)  36.1 us
    ppermute x18, starting transfers between devices, send(): return lax.ppermute(value, 'dp', pairs)  19.9 us
    ppermute x18, waiting for transfers between devices, send(): return lax.ppermute(value, 'dp', pairs)  19.7 us
    all_to_all x5, waiting for transfers between devices, exchange(): return lax.all_to_all(blocks, axis, split_axis=0, concat_axis=0, tiled=True)  19.6 us
    pallas_call x7, Pallas kernels, place(): pl.pallas_call(lambda *refs: place_kernel(axis, count, *refs), out_shape=...  17.1 us
    pallas_call x1, Pallas kernels, on_device(): pl.pallas_call(project_kernel, grid=(groups,), out_shape=jax.ShapeDtypeSt...  10.5 us
    unnamed x50, local copies, waits for them, and re-layouts  9.46 us
    pallas_call x1, Pallas kernels, on_device(): pl.pallas_call(lambda *refs: attend_kernel(score_scale, *refs), out_shape...  6.3 us
  transfers between devices with their start and end apart: 23, of which 6 were waited for; matrix products, arithmetic and copies ran while one was open for 5% of the time, Pallas kernels for 22%

profile of v2, /device:TPU:1, one launch (start us, length us, event | category | flops | bytes accessed | tf_op | source)
XLA Modules:
  0.0 160.8 jit_solution(5524546508602969883)
XLA Ops:
  0.7 1.4 reshape.46.refs_2_
  2.0 0.7 pad_add_fusion.1.refs_0_
  2.7 2.8 %pack.1 = (bf16[16,64,640]{2,1,0:T(8,128)(2,1)}, bf16[4,16,1024]{2,1,0:T(8,128)(2,1)}, bf16[4,16,1024]{2,1,0:T(8,128)(2,1)}) custom-call(s32[2]{0:T(128)} %pad_add_fusion.1.refs_0_, bf16[16,8192]{1,0:T(8,128)(2,1)} %bitcast.26, bf16[1,8192]{1,0:T(2,128)(2,1)} %reshape.46.refs_2_, bf16[64,5120]{1,0:T(8,128)(2,1)} %refs_3_.1, bf16[64,4096]{1,0:T(8,128)(2,1)} %refs_4_.2), custom_call_target="tpu_custom_call" | custom-call | tf_op jit(solution)/shard_map/pack/pallas_call | solution.py:265
  5.5 9.3 %all-to-all-start = ((bf16[16,64,640]{2,1,0:T(8,128)(2,1)}), bf16[16,64,640]{2,1,0:T(8,128)(2,1)S(1)}, u32[]{:S(2)}, u32[]{:S(2)}) async-start(bf16[16,64,640]{2,1,0:T(8,128)(2,1)} %get-tuple-element.29), calls=%async_computation | async-start | bytes 2621440 | tf_op jit(solution)/shard_map/all_to_all | solution.py:235
  15.1 0.8 fusion.1
  15.9 17.3 %collective-permute-done.refs_2_ = bf16[4,16,1024]{2,1,0:T(8,128)(2,1)S(1)} collective-permute-done((bf16[4,16,1024]{2,1,0:T(8,128)(2,1)}, bf16[4,16,1024]{2,1,0:T(8,128)(2,1)S(1)}, u32[]{:S(2)}, u32[]{:S(2)}) %collective-permute-start) | collective-permute-done | bytes 131104 | tf_op jit(solution)/shard_map/ppermute | solution.py:261
  33.3 1.4 collective-permute-start.1
  34.7 1.5 collective-permute-start.2
  36.2 1.7 %collective-permute-start.3 = (bf16[2,16,1024]{2,1,0:T(8,128)(2,1)S(1)}, bf16[2,16,1024]{2,1,0:T(8,128)(2,1)S(1)}, u32[]{:S(2)}, u32[]{:S(2)}) collective-permute-start(bf16[2,16,1024]{2,1,0:T(8,128)(2,1)S(1)} %pad_maximum_fusion.2), channel_id=1, source_target_pairs={{0,32},{16,48},{32,0},{48,16},{64,96},{80,112},{96,64},{112,80},{1... | collective-permute-start | bytes 196616 | tf_op jit(solution)/shard_map/ppermute | solution.py:261
  38.5 2.4 %collective-permute-done.3.refs_5_ = bf16[2,16,1024]{2,1,0:T(8,128)(2,1)S(1)} collective-permute-done((bf16[2,16,1024]{2,1,0:T(8,128)(2,1)S(1)}, bf16[2,16,1024]{2,1,0:T(8,128)(2,1)S(1)}, u32[]{:S(2)}, u32[]{:S(2)}) %collective-permute-start.3) | collective-permute-done | bytes 65568 | tf_op jit(solution)/shard_map/ppermute | solution.py:261
  42.0 2.7 %terms.1 = (f32[8,16,320]{2,1,0:T(8,128)}, bf16[1024,256]{1,0:T(8,128)(2,1)}) custom-call(s32[8]{0:T(128)} %stack.104.refs_0_, bf16[4,16,1024]{2,1,0:T(8,128)(2,1)} %get-tuple-element.27.refs_1_, bf16[4,16,1024]{2,1,0:T(8,128)(2,1)} %copy-done.19, bf16[2,16,1024]{2,1,0:T(8,128)(2,1)} %copy-done.20, bf16[2,16,1024]{2,1,0:T(8,128)(2,1)} %copy-done.21, ...), custom_call_target="tpu_custom_call" | custom-call | tf_op jit(solution)/shard_map/terms/pallas_call | solution.py:292
  44.6 1.5 collective-permute-start.6
  46.2 2.1 %collective-permute-start.4 = (bf16[1024,256]{1,0:T(8,128)(2,1)}, bf16[1024,256]{1,0:T(8,128)(2,1)S(1)}, u32[]{:S(2)}, u32[]{:S(2)}) collective-permute-start(bf16[1024,256]{1,0:T(8,128)(2,1)} %get-tuple-element.31.refs_1_), channel_id=1, source_target_pairs={{0,64},{16,80},{32,96},{48,112},{64,0},{80,16},{96,32},{112,48},{1... | collective-permute-start | bytes 1572872 | tf_op jit(solution)/shard_map/ppermute | solution.py:261
  48.3 4.0 %all-to-all-start.1 = ((f32[8,16,320]{2,1,0:T(8,128)}), f32[8,16,320]{2,1,0:T(8,128)S(1)}, u32[]{:S(2)}, u32[]{:S(2)}) async-start(f32[8,16,320]{2,1,0:T(8,128)} %get-tuple-element.30), calls=%async_computation.1 | async-start | bytes 393216 | tf_op jit(solution)/shard_map/all_to_all | solution.py:235
  52.9 2.4 %turn.1.refs_3_ = bf16[320,1024]{1,0:T(8,128)(2,1)} custom-call(bf16[1024,640]{1,0:T(8,128)(2,1)} %bitcast.25), custom_call_target="tpu_custom_call" | custom-call | tf_op jit(solution)/shard_map/turn/pallas_call | solution.py:304
  55.3 6.5 %all-to-all-done.1.terms_ref = f32[8,16,320]{2,1,0:T(8,128)S(1)} async-done(((f32[8,16,320]{2,1,0:T(8,128)}), f32[8,16,320]{2,1,0:T(8,128)S(1)}, u32[]{:S(2)}, u32[]{:S(2)}) %all-to-all-start.1) | async-done | bytes 163872 | tf_op jit(solution)/shard_map/all_to_all | solution.py:235
  62.8 0.8 copy-done.12
  63.7 1.6 %sum.1 = (bf16[16,16,320]{2,1,0:T(8,128)(2,1)}, bf16[1024,256]{1,0:T(8,128)(2,1)}, bf16[1024,256]{1,0:T(8,128)(2,1)}, bf16[1024,256]{1,0:T(8,128)(2,1)}, bf16[320,1024]{1,0:T(8,128)(2,1)}) custom-call(f32[8,16,320]{2,1,0:T(8,128)} %copy-done.15, ...), custom_call_target="tpu_custom_call", output_to_operand_aliasing={{1}: (2, {}), {2}: (3, {}), {3}: (4, {}), {4}: (5, {})} | custom-call | tf_op jit(solution)/shard_map/sum/pallas_call | solution.py:310
  65.3 1.0 collective-permute-start.11
  66.3 1.1 collective-permute-start.10
  68.4 2.3 %collective-permute-start.8 = (bf16[1024,256]{1,0:T(8,128)(2,1)}, bf16[1024,256]{1,0:T(8,128)(2,1)S(1)}, u32[]{:S(2)}, u32[]{:S(2)}) collective-permute-start(bf16[1024,256]{1,0:T(8,128)(2,1)} %get-tuple-element.33.refs_2_), channel_id=1, source_target_pairs={{0,48},{16,0},{32,16},{48,32},{64,112},{80,64},{96,80},{112,96},{1... | collective-permute-start | bytes 1572872 | tf_op jit(solution)/shard_map/ppermute | solution.py:261
  71.4 10.6 %all-to-all-start.2 = ((bf16[16,16,320]{2,1,0:T(8,128)(2,1)}), bf16[16,16,320]{2,1,0:T(8,128)(2,1)S(1)}, u32[]{:S(2)}, u32[]{:S(2)}) async-start(bf16[16,16,320]{2,1,0:T(8,128)(2,1)} %get-tuple-element.32), calls=%async_computation.2 | async-start | bytes 393216 | tf_op jit(solution)/shard_map/all_to_all | solution.py:235
  82.6 0.7 pad_maximum_fusion.3
  83.3 2.2 %place.7.refs_3_ = bf16[8192,256]{1,0:T(8,128)(2,1)} custom-call(s32[2]{0:T(128)} %pad_add_fusion.3.refs_0_, bf16[1024,256]{1,0:T(8,128)(2,1)} %get-tuple-element.31.refs_1_, bf16[1024,256]{1,0:T(8,128)(2,1)} %get-tuple-element.33.refs_2_), custom_call_target="tpu_custom_call" | custom-call | tf_op jit(solution)/shard_map/place/pallas_call | solution.py:118
  85.5 2.2 %place.8.refs_6_ = bf16[8192,256]{1,0:T(8,128)(2,1)} custom-call(s32[2]{0:T(128)} %pad_add_fusion.2.refs_0_, bf16[1024,256]{1,0:T(8,128)(2,1)} %get-tuple-element.35.refs_1_, bf16[1024,256]{1,0:T(8,128)(2,1)} %get-tuple-element.36.refs_2_, bf16[8192,256]{1,0:T(8,128)(2,1)} %place.7.refs_3_), custom_call_target="tpu_custom_call", output_to_operand_aliasing={{}: (3, {})} | custom-call | tf_op jit(solution)/shard_map/place/pallas_call | solution.py:118
  87.8 2.4 %all-to-all-done.2.refs_3_ = bf16[16,16,320]{2,1,0:T(8,128)(2,1)S(1)} async-done(((bf16[16,16,320]{2,1,0:T(8,128)(2,1)}), bf16[16,16,320]{2,1,0:T(8,128)(2,1)S(1)}, u32[]{:S(2)}, u32[]{:S(2)}) %all-to-all-start.2) | async-done | bytes 163872 | tf_op jit(solution)/shard_map/all_to_all | solution.py:235
  90.2 0.7 copy-done.14
  90.9 6.3 %attend.1.refs_0_ = bf16[16,64,128]{2,1,0:T(8,128)(2,1)} custom-call(s32[9]{0:T(128)} %pad_add_fusion.refs_0_, f32[16,128]{1,0:T(8,128)} %get-tuple-element.60.refs_1_, f32[16,128]{1,0:T(8,128)} %get-tuple-element.61.refs_2_, bf16[16,16,320]{2,1,0:T(8,128)(2,1)} %copy-done.14, bf16[8,256,512]{2,1,0:T(8,128)(2,1)} %refs_4_.3, bf16[8,256,512]{2,1,0:T(8,128)(2,1)} %refs_5_.1), custom_call_target="tpu_custom_call" | custom-call | tf_op jit(solution)/shard_map/attend/pallas_call | solution.py:351
  97.2 0.7 copy-done.5
  98.6 0.8 copy-done.1
  100.3 2.7 %collective-permute-start.13 = (bf16[1024,256]{1,0:T(8,128)(2,1)}, bf16[1024,256]{1,0:T(8,128)(2,1)S(1)}, u32[]{:S(2)}, u32[]{:S(2)}) collective-permute-start(bf16[1024,256]{1,0:T(8,128)(2,1)} %get-tuple-element.38.refs_2_), channel_id=1, source_target_pairs={{0,48},{16,0},{32,16},{48,32},{64,112},{80,64},{96,80},{112,96},{1... | collective-permute-start | bytes 1572872 | tf_op jit(solution)/shard_map/ppermute | solution.py:261
  103.0 6.7 %all-to-all-start.3 = ((bf16[16,64,128]{2,1,0:T(8,128)(2,1)}), bf16[16,64,128]{2,1,0:T(8,128)(2,1)S(1)}, u32[]{:S(2)}, u32[]{:S(2)}) async-start(bf16[16,64,128]{2,1,0:T(8,128)(2,1)} %get-tuple-element.37), calls=%async_computation.3 | async-start | bytes 524288 | tf_op jit(solution)/shard_map/all_to_all | solution.py:235
  110.3 2.4 %place.10.refs_6_ = bf16[320,8192]{1,0:T(8,128)(2,1)} custom-call(s32[2]{0:T(128)} %pad_add_fusion.3.refs_0_, bf16[320,1024]{1,0:T(8,128)(2,1)} %get-tuple-element.34.refs_1_, bf16[320,1024]{1,0:T(8,128)(2,1)} %get-tuple-element.43.refs_2_), custom_call_target="tpu_custom_call" | custom-call | tf_op jit(solution)/shard_map/place/pallas_call | solution.py:118
  112.7 2.2 %place.9.refs_5_ = bf16[8192,256]{1,0:T(8,128)(2,1)} custom-call(s32[2]{0:T(128)} %pad_add_fusion.4.refs_0_, bf16[1024,256]{1,0:T(8,128)(2,1)} %get-tuple-element.41.refs_1_, bf16[1024,256]{1,0:T(8,128)(2,1)} %get-tuple-element.38.refs_2_, bf16[8192,256]{1,0:T(8,128)(2,1)} %get-tuple-element.42.refs_3_), custom_call_target="tpu_custom_call", output_to_operand_aliasing={{}: (3, {})} | custom-call | tf_op jit(solution)/shard_map/place/pallas_call | solution.py:118
  114.9 6.1 %all-to-all-done.3.message_ref = bf16[16,64,128]{2,1,0:T(8,128)(2,1)S(1)} async-done(((bf16[16,64,128]{2,1,0:T(8,128)(2,1)}), bf16[16,64,128]{2,1,0:T(8,128)(2,1)S(1)}, u32[]{:S(2)}, u32[]{:S(2)}) %all-to-all-start.3) | async-done | bytes 262176 | tf_op jit(solution)/shard_map/all_to_all | solution.py:235
  121.0 0.7 copy-done.13
  121.7 1.9 %merge.1.refs_0_ = bf16[16,256]{1,0:T(8,128)(2,1)} custom-call(bf16[16,64,128]{2,1,0:T(8,128)(2,1)} %copy-done.13), custom_call_target="tpu_custom_call" | custom-call | tf_op jit(solution)/shard_map/merge/pallas_call | solution.py:377
  123.6 0.8 copy-done.10
  124.8 3.0 %collective-permute-start.17 = (bf16[320,1024]{1,0:T(8,128)(2,1)}, bf16[320,1024]{1,0:T(8,128)(2,1)S(1)}, u32[]{:S(2)}, u32[]{:S(2)}) collective-permute-start(bf16[320,1024]{1,0:T(8,128)(2,1)} %get-tuple-element.49.refs_3_), channel_id=1, source_target_pairs={{0,48},{16,0},{32,16},{48,32},{64,112},{80,64},{96,80},{112,96},{1... | collective-permute-start | bytes 1966088 | tf_op jit(solution)/shard_map/ppermute | solution.py:261
  128.3 2.2 %place.11.weight_ref = bf16[8192,256]{1,0:T(8,128)(2,1)} custom-call(s32[2]{0:T(128)} %pad_add_fusion.5.refs_0_, bf16[1024,256]{1,0:T(8,128)(2,1)} %get-tuple-element.45.refs_1_, bf16[1024,256]{1,0:T(8,128)(2,1)} %get-tuple-element.46.refs_2_, bf16[8192,256]{1,0:T(8,128)(2,1)} %get-tuple-element.47.refs_3_), custom_call_target="tpu_custom_call", output_to_operand_aliasing={{}: (3, {})} | custom-call | tf_op jit(solution)/shard_map/place/pallas_call | solution.py:118
  130.6 10.5 %project.1 = bf16[16,16,512]{2,1,0:T(8,128)(2,1)} custom-call(bf16[16,256]{1,0:T(8,128)(2,1)} %get-tuple-element.44.attended_ref, bf16[8192,256]{1,0:T(8,128)(2,1)} %place.11.weight_ref), custom_call_target="tpu_custom_call" | custom-call | tf_op jit(solution)/shard_map/project/pallas_call | solution.py:410
  141.1 5.6 %all-to-all-start.4 = ((bf16[16,16,512]{2,1,0:T(8,128)(2,1)}), bf16[16,16,512]{2,1,0:T(8,128)(2,1)S(1)}, u32[]{:S(2)}, u32[]{:S(2)}) async-start(bf16[16,16,512]{2,1,0:T(8,128)(2,1)} %project.1), calls=%async_computation.4 | async-start | bytes 524288 | tf_op jit(solution)/shard_map/all_to_all | solution.py:235
  147.9 2.9 %place.12.refs_4_ = bf16[320,8192]{1,0:T(8,128)(2,1)} custom-call(s32[3]{0:T(128)} %pad_add_fusion.7.refs_0_, bf16[320,1024]{1,0:T(8,128)(2,1)} %get-tuple-element.48.refs_1_, bf16[320,1024]{1,0:T(8,128)(2,1)} %get-tuple-element.39.refs_2_, bf16[320,1024]{1,0:T(8,128)(2,1)} %get-tuple-element.49.refs_3_, ...), custom_call_target="tpu_custom_call", output_to_operand_aliasing={{}: (4, {})} | custom-call | tf_op jit(solution)/shard_map/place/pallas_call | solution.py:118
  150.7 4.6 %all-to-all-done.4 = bf16[16,16,512]{2,1,0:T(8,128)(2,1)S(1)} async-done(((bf16[16,16,512]{2,1,0:T(8,128)(2,1)}), bf16[16,16,512]{2,1,0:T(8,128)(2,1)S(1)}, u32[]{:S(2)}, u32[]{:S(2)}) %all-to-all-start.4) | async-done | bytes 262176 | tf_op jit(solution)/shard_map/all_to_all | solution.py:235
  155.3 0.6 reduce_sum.12
  156.0 0.8 copy-done.16
  157.1 0.8 copy-done.18
  157.9 2.9 %place.13 = bf16[320,8192]{1,0:T(8,128)(2,1)} custom-call(s32[3]{0:T(128)} %pad_add_fusion.6.refs_0_, bf16[320,1024]{1,0:T(8,128)(2,1)} %copy-done.18, bf16[320,1024]{1,0:T(8,128)(2,1)} %copy-done.17, bf16[320,1024]{1,0:T(8,128)(2,1)} %copy-done.16, bf16[320,8192]{1,0:T(8,128)(2,1)} %place.12.refs_4_), custom_call_target="tpu_custom_call", output_to_operand_aliasing={{}: (4, {})} | custom-call | tf_op jit(solution)/shard_map/place/pallas_call | solution.py:118
  (86 shorter events, 10.6 us)
Async XLA Ops:
  0.6 51.6 %copy-start.24 = (s32[8]{0:T(128)S(1)}, s32[8]{0:T(128)}, u32[]{:S(2)}) copy-start(s32[8]{0:T(128)} %param.13) | copy-start | bytes 100
  0.6 51.7 %copy-start.23 = (bf16[320]{0:T(512)(128)(2,1)S(1)}, bf16[320]{0:T(512)(128)(2,1)}, u32[]{:S(2)}) copy-start(bf16[320]{0:T(512)(128)(2,1)} %param.10) | copy-start | bytes 1924
  5.5 35.4 %all-to-all-start = ((bf16[16,64,640]{2,1,0:T(8,128)(2,1)}), bf16[16,64,640]{2,1,0:T(8,128)(2,1)S(1)}, u32[]{:S(2)}, u32[]{:S(2)}) async-start(bf16[16,64,640]{2,1,0:T(8,128)(2,1)} %get-tuple-element.29), calls=%async_computation | async-start | bytes 2621440 | tf_op jit(solution)/shard_map/all_to_all | solution.py:235
  14.8 18.4 %collective-permute-start = (bf16[4,16,1024]{2,1,0:T(8,128)(2,1)}, bf16[4,16,1024]{2,1,0:T(8,128)(2,1)S(1)}, u32[]{:S(2)}, u32[]{:S(2)}) collective-permute-start(bf16[4,16,1024]{2,1,0:T(8,128)(2,1)} %get-tuple-element.28), channel_id=1, source_target_pairs={{0,64},{16,80},{32,96},{48,112},{64,0},{80,16},{96,32},{112,48},{1... | collective-permute-start | bytes 393224 | tf_op jit(solution)/shard_map/ppermute | solution.py:261
  33.3 7.6 %copy-start.19 = (bf16[4,16,1024]{2,1,0:T(8,128)(2,1)}, bf16[4,16,1024]{2,1,0:T(8,128)(2,1)S(1)}, u32[]{:S(2)}) copy-start(bf16[4,16,1024]{2,1,0:T(8,128)(2,1)S(1)} %collective-permute-done.refs_2_) | copy-start | bytes 393220
  33.3 5.2 %collective-permute-start.1 = (bf16[2,16,1024]{2,1,0:T(8,128)(2,1)S(1)}, bf16[2,16,1024]{2,1,0:T(8,128)(2,1)S(1)}, u32[]{:S(2)}, u32[]{:S(2)}) collective-permute-start(bf16[2,16,1024]{2,1,0:T(8,128)(2,1)S(1)} %pad_maximum_fusion), channel_id=1, source_target_pairs={{0,16},{16,32},{32,48},{48,0},{64,80},{80,96},{96,112},{112,64},{1... | collective-permute-start | bytes 196616 | tf_op jit(solution)/shard_map/ppermute | solution.py:261
  34.7 3.9 %collective-permute-start.2 = (bf16[2,16,1024]{2,1,0:T(8,128)(2,1)S(1)}, bf16[2,16,1024]{2,1,0:T(8,128)(2,1)S(1)}, u32[]{:S(2)}, u32[]{:S(2)}) collective-permute-start(bf16[2,16,1024]{2,1,0:T(8,128)(2,1)S(1)} %pad_maximum_fusion.1), channel_id=1, source_target_pairs={{0,48},{16,0},{32,16},{48,32},{64,112},{80,64},{96,80},{112,96},{1... | collective-permute-start | bytes 196616 | tf_op jit(solution)/shard_map/ppermute | solution.py:261
  36.2 4.7 %collective-permute-start.3 = (bf16[2,16,1024]{2,1,0:T(8,128)(2,1)S(1)}, bf16[2,16,1024]{2,1,0:T(8,128)(2,1)S(1)}, u32[]{:S(2)}, u32[]{:S(2)}) collective-permute-start(bf16[2,16,1024]{2,1,0:T(8,128)(2,1)S(1)} %pad_maximum_fusion.2), channel_id=1, source_target_pairs={{0,32},{16,48},{32,0},{48,16},{64,96},{80,112},{96,64},{112,80},{1... | collective-permute-start | bytes 196616 | tf_op jit(solution)/shard_map/ppermute | solution.py:261
  38.5 2.4 %copy-start.20 = (bf16[2,16,1024]{2,1,0:T(8,128)(2,1)}, bf16[2,16,1024]{2,1,0:T(8,128)(2,1)S(1)}, u32[]{:S(2)}) copy-start(bf16[2,16,1024]{2,1,0:T(8,128)(2,1)S(1)} %collective-permute-done.1.refs_3_) | copy-start | bytes 196612
  38.5 2.4 %copy-start.21 = (bf16[2,16,1024]{2,1,0:T(8,128)(2,1)}, bf16[2,16,1024]{2,1,0:T(8,128)(2,1)S(1)}, u32[]{:S(2)}) copy-start(bf16[2,16,1024]{2,1,0:T(8,128)(2,1)S(1)} %collective-permute-done.2.refs_4_) | copy-start | bytes 196612
  40.9 0.6 copy-start.22
  40.9 1.1 copy-start
  44.6 17.2 %collective-permute-start.6 = (bf16[1024,256]{1,0:T(8,128)(2,1)}, bf16[1024,256]{1,0:T(8,128)(2,1)S(1)}, u32[]{:S(2)}, u32[]{:S(2)}) collective-permute-start(bf16[1024,256]{1,0:T(8,128)(2,1)} %get-tuple-element.31.refs_1_), channel_id=1, source_target_pairs={{0,48},{16,0},{32,16},{48,32},{64,112},{80,64},{96,80},{112,96},{1... | collective-permute-start | bytes 1572872 | tf_op jit(solution)/shard_map/ppermute | solution.py:261
  46.2 15.6 %collective-permute-start.5 = (bf16[1024,256]{1,0:T(8,128)(2,1)}, bf16[1024,256]{1,0:T(8,128)(2,1)S(1)}, u32[]{:S(2)}, u32[]{:S(2)}) collective-permute-start(bf16[1024,256]{1,0:T(8,128)(2,1)} %get-tuple-element.31.refs_1_), channel_id=1, source_target_pairs={{0,16},{16,32},{32,48},{48,0},{64,80},{80,96},{96,112},{112,64},{1... | collective-permute-start | bytes 1572872 | tf_op jit(solution)/shard_map/ppermute | solution.py:261
  46.2 15.6 %collective-permute-start.4 = (bf16[1024,256]{1,0:T(8,128)(2,1)}, bf16[1024,256]{1,0:T(8,128)(2,1)S(1)}, u32[]{:S(2)}, u32[]{:S(2)}) collective-permute-start(bf16[1024,256]{1,0:T(8,128)(2,1)} %get-tuple-element.31.refs_1_), channel_id=1, source_target_pairs={{0,64},{16,80},{32,96},{48,112},{64,0},{80,16},{96,32},{112,48},{1... | collective-permute-start | bytes 1572872 | tf_op jit(solution)/shard_map/ppermute | solution.py:261
  48.3 13.5 %all-to-all-start.1 = ((f32[8,16,320]{2,1,0:T(8,128)}), f32[8,16,320]{2,1,0:T(8,128)S(1)}, u32[]{:S(2)}, u32[]{:S(2)}) async-start(f32[8,16,320]{2,1,0:T(8,128)} %get-tuple-element.30), calls=%async_computation.1 | async-start | bytes 393216 | tf_op jit(solution)/shard_map/all_to_all | solution.py:235
  61.8 0.7 copy-start.15
  61.8 0.9 copy-start.7
  61.8 1.0 copy-start.8
  62.8 0.8 copy-start.12
  65.3 31.9 %collective-permute-start.11 = (bf16[320,1024]{1,0:T(8,128)(2,1)}, bf16[320,1024]{1,0:T(8,128)(2,1)S(1)}, u32[]{:S(2)}, u32[]{:S(2)}) collective-permute-start(bf16[320,1024]{1,0:T(8,128)(2,1)} %get-tuple-element.34.refs_1_), channel_id=1, source_target_pairs={{0,64},{16,80},{32,96},{48,112},{64,0},{80,16},{96,32},{112,48},{1... | collective-permute-start | bytes 1966088 | tf_op jit(solution)/shard_map/ppermute | solution.py:261
  66.3 30.9 %collective-permute-start.10 = (bf16[320,1024]{1,0:T(8,128)(2,1)}, bf16[320,1024]{1,0:T(8,128)(2,1)S(1)}, u32[]{:S(2)}, u32[]{:S(2)}) collective-permute-start(bf16[320,1024]{1,0:T(8,128)(2,1)} %get-tuple-element.34.refs_1_), channel_id=1, source_target_pairs={{0,48},{16,0},{32,16},{48,32},{64,112},{80,64},{96,80},{112,96},{1... | collective-permute-start | bytes 1966088 | tf_op jit(solution)/shard_map/ppermute | solution.py:261
  67.4 29.8 %collective-permute-start.9 = (bf16[320,1024]{1,0:T(8,128)(2,1)}, bf16[320,1024]{1,0:T(8,128)(2,1)S(1)}, u32[]{:S(2)}, u32[]{:S(2)}) collective-permute-start(bf16[320,1024]{1,0:T(8,128)(2,1)} %get-tuple-element.34.refs_1_), channel_id=1, source_target_pairs={{0,16},{16,32},{32,48},{48,0},{64,80},{80,96},{96,112},{112,64},{1... | collective-permute-start | bytes 1966088 | tf_op jit(solution)/shard_map/ppermute | solution.py:261
  68.4 28.8 %collective-permute-start.8 = (bf16[1024,256]{1,0:T(8,128)(2,1)}, bf16[1024,256]{1,0:T(8,128)(2,1)S(1)}, u32[]{:S(2)}, u32[]{:S(2)}) collective-permute-start(bf16[1024,256]{1,0:T(8,128)(2,1)} %get-tuple-element.33.refs_2_), channel_id=1, source_target_pairs={{0,48},{16,0},{32,16},{48,32},{64,112},{80,64},{96,80},{112,96},{1... | collective-permute-start | bytes 1572872 | tf_op jit(solution)/shard_map/ppermute | solution.py:261
  70.7 26.5 %collective-permute-start.7 = (bf16[1024,256]{1,0:T(8,128)(2,1)}, bf16[1024,256]{1,0:T(8,128)(2,1)S(1)}, u32[]{:S(2)}, u32[]{:S(2)}) collective-permute-start(bf16[1024,256]{1,0:T(8,128)(2,1)} %get-tuple-element.33.refs_2_), channel_id=1, source_target_pairs={{0,16},{16,32},{32,48},{48,0},{64,80},{80,96},{96,112},{112,64},{1... | collective-permute-start | bytes 1572872 | tf_op jit(solution)/shard_map/ppermute | solution.py:261
  71.4 18.8 %all-to-all-start.2 = ((bf16[16,16,320]{2,1,0:T(8,128)(2,1)}), bf16[16,16,320]{2,1,0:T(8,128)(2,1)S(1)}, u32[]{:S(2)}, u32[]{:S(2)}) async-start(bf16[16,16,320]{2,1,0:T(8,128)(2,1)} %get-tuple-element.32), calls=%async_computation.2 | async-start | bytes 393216 | tf_op jit(solution)/shard_map/all_to_all | solution.py:235
  90.2 0.7 copy-start.14
  97.2 2.9 %copy-start.9 = (bf16[1024,256]{1,0:T(8,128)(2,1)S(1)}, bf16[1024,256]{1,0:T(8,128)(2,1)}, u32[]{:S(2)}) copy-start(bf16[1024,256]{1,0:T(8,128)(2,1)} %get-tuple-element.35.refs_1_) | copy-start | bytes 1572868
  97.2 0.8 copy-start.5
  97.2 0.9 copy-start.6
  97.2 1.1 copy-start.4
  97.2 1.3 copy-start.2
  98.6 0.8 copy-start.1
  99.4 24.2 %collective-permute-start.14 = (bf16[320,1024]{1,0:T(8,128)(2,1)}, bf16[320,1024]{1,0:T(8,128)(2,1)S(1)}, u32[]{:S(2)}, u32[]{:S(2)}) collective-permute-start(bf16[320,1024]{1,0:T(8,128)(2,1)} %get-tuple-element.39.refs_2_), channel_id=1, source_target_pairs={{0,64},{16,80},{32,96},{48,112},{64,0},{80,16},{96,32},{112,48},{1... | collective-permute-start | bytes 1966088 | tf_op jit(solution)/shard_map/ppermute | solution.py:261
  100.0 23.6 %collective-permute-start.12 = (bf16[1024,256]{1,0:T(8,128)(2,1)S(1)}, bf16[1024,256]{1,0:T(8,128)(2,1)S(1)}, u32[]{:S(2)}, u32[]{:S(2)}) collective-permute-start(bf16[1024,256]{1,0:T(8,128)(2,1)S(1)} %copy-done.9), channel_id=1, source_target_pairs={{0,16},{16,32},{32,48},{48,0},{64,80},{80,96},{96,112},{112,64},{1... | collective-permute-start | bytes 1572872 | tf_op jit(solution)/shard_map/ppermute | solution.py:261
  100.3 23.3 %collective-permute-start.13 = (bf16[1024,256]{1,0:T(8,128)(2,1)}, bf16[1024,256]{1,0:T(8,128)(2,1)S(1)}, u32[]{:S(2)}, u32[]{:S(2)}) collective-permute-start(bf16[1024,256]{1,0:T(8,128)(2,1)} %get-tuple-element.38.refs_2_), channel_id=1, source_target_pairs={{0,48},{16,0},{32,16},{48,32},{64,112},{80,64},{96,80},{112,96},{1... | collective-permute-start | bytes 1572872 | tf_op jit(solution)/shard_map/ppermute | solution.py:261
  103.0 18.0 %all-to-all-start.3 = ((bf16[16,64,128]{2,1,0:T(8,128)(2,1)}), bf16[16,64,128]{2,1,0:T(8,128)(2,1)S(1)}, u32[]{:S(2)}, u32[]{:S(2)}) async-start(bf16[16,64,128]{2,1,0:T(8,128)(2,1)} %get-tuple-element.37), calls=%async_computation.3 | async-start | bytes 524288 | tf_op jit(solution)/shard_map/all_to_all | solution.py:235
  121.0 0.7 copy-start.13
  123.6 0.8 copy-start.10
  123.6 1.0 copy-start.11
  123.6 1.1 copy-start.3
  124.8 31.2 %collective-permute-start.17 = (bf16[320,1024]{1,0:T(8,128)(2,1)}, bf16[320,1024]{1,0:T(8,128)(2,1)S(1)}, u32[]{:S(2)}, u32[]{:S(2)}) collective-permute-start(bf16[320,1024]{1,0:T(8,128)(2,1)} %get-tuple-element.49.refs_3_), channel_id=1, source_target_pairs={{0,48},{16,0},{32,16},{48,32},{64,112},{80,64},{96,80},{112,96},{1... | collective-permute-start | bytes 1966088 | tf_op jit(solution)/shard_map/ppermute | solution.py:261
  127.7 28.3 %collective-permute-start.16 = (bf16[320,1024]{1,0:T(8,128)(2,1)}, bf16[320,1024]{1,0:T(8,128)(2,1)S(1)}, u32[]{:S(2)}, u32[]{:S(2)}) collective-permute-start(bf16[320,1024]{1,0:T(8,128)(2,1)} %get-tuple-element.48.refs_1_), channel_id=1, source_target_pairs={{0,64},{16,80},{32,96},{48,112},{64,0},{80,16},{96,32},{112,48},{1... | collective-permute-start | bytes 1966088 | tf_op jit(solution)/shard_map/ppermute | solution.py:261
  127.7 28.3 %collective-permute-start.15 = (bf16[320,1024]{1,0:T(8,128)(2,1)}, bf16[320,1024]{1,0:T(8,128)(2,1)S(1)}, u32[]{:S(2)}, u32[]{:S(2)}) collective-permute-start(bf16[320,1024]{1,0:T(8,128)(2,1)} %get-tuple-element.48.refs_1_), channel_id=1, source_target_pairs={{0,16},{16,32},{32,48},{48,0},{64,80},{80,96},{96,112},{112,64},{1... | collective-permute-start | bytes 1966088 | tf_op jit(solution)/shard_map/ppermute | solution.py:261
  141.1 14.3 %all-to-all-start.4 = ((bf16[16,16,512]{2,1,0:T(8,128)(2,1)}), bf16[16,16,512]{2,1,0:T(8,128)(2,1)S(1)}, u32[]{:S(2)}, u32[]{:S(2)}) async-start(bf16[16,16,512]{2,1,0:T(8,128)(2,1)} %project.1), calls=%async_computation.4 | async-start | bytes 524288 | tf_op jit(solution)/shard_map/all_to_all | solution.py:235
  156.0 0.8 copy-start.16
  156.0 1.1 copy-start.17
  157.1 0.8 copy-start.18

commit v3 on v2

--- a/solution.py
+++ b/solution.py
@@ -15,7 +15,7 @@
 FLOOR = -1e30
 
 
-def pack_kernel(groups, spot_ref, states_ref, gain_ref, qkv_ref, out_ref, packed_ref, own_ref, send_ref):
+def pack_kernel(groups, after_ref, qkv_ref, out_ref, packed_ref):
     query_width = QH * HD // groups
     kv_width = KVH * HD // groups
     rows = qkv_ref.shape[0]
@@ -32,13 +32,17 @@
             1,
         )
         packed_ref[g, :, query_width + HD :] = out_ref[:, g * query_width : (g + 1) * query_width]
-    states = states_ref[...].astype(jnp.float32)
+
+
+def norm_kernel(states_ref, gain_ref, own_ref, send_ref):
+    states = jnp.concatenate([states_ref[0], states_ref[1]], 0).astype(jnp.float32)
     normed = (
         states
         * lax.rsqrt(jnp.mean(states * states, -1, keepdims=True) + EPS)
         * gain_ref[...].astype(jnp.float32)
     ).astype(jnp.bfloat16)
-    column, y_at = spot_ref[0], spot_ref[1]
+    replica = lax.axis_index("dp")
+    column, y_at = replica // 4, replica % 4
     count, _, share = own_ref.shape
     for y in range(count):
         first = normed[:, y * share : (y + 1) * share]
@@ -48,15 +52,18 @@
         send_ref[slot] = jnp.where(column == 0, second, first)
 
 
-def terms_kernel(group_width, order_ref, own, got, low, high, far, packed_ref, terms_ref, out_ref):
+def terms_kernel(group_width, own, got, low, high, far, packed_ref, terms_ref, out_ref):
     weights = packed_ref[:, :group_width]
     states = jnp.concatenate(
         [own[0], got[0], low[0], low[1], high[0], high[1], far[0], far[1]], 0
     )
     terms = jnp.dot(states, weights, preferred_element_type=jnp.float32)
     slots = own.shape[1]
-    for i in range(terms.shape[0] // slots):
-        terms_ref[order_ref[i]] = terms[i * slots : (i + 1) * slots]
+    replica = lax.axis_index("dp")
+    order = [(c, y) for y in (0, -1, 1, 2) for c in (0, 1)]
+    for i, (c, y) in enumerate(order):
+        source = ((replica // 4) ^ c) * 4 + ((replica + y) & 3)
+        terms_ref[source] = terms[i * slots : (i + 1) * slots]
     out_ref[...] = packed_ref[:, group_width + 64 :]
 
 
@@ -89,46 +96,39 @@
     turned_ref[...] = packed_ref[:, : width + 64].T[:width]
 
 
-def place_kernel(axis, count, *refs):
-    starts_ref, parts, whole_ref, sems = refs[0], refs[1 : 1 + count], refs[-2], refs[-1]
-    pieces = sems.shape[1]
+def place_kernel(axis, where, *refs):
+    parts, whole_ref, sems = refs[: len(where)], refs[-2], refs[-1]
+    replica = lax.axis_index("dp")
     copies = []
-    for i, part in enumerate(parts):
-        rows, columns = part.shape
-        step = rows // pieces
-        at = pl.multiple_of(starts_ref[i] * 512, 512)
-        for j in range(pieces):
-            if axis == 0:
-                target = whole_ref.at[pl.ds(at + j * step, step), :]
-            else:
-                target = whole_ref.at[pl.ds(j * step, step), pl.ds(at, columns)]
-            source = part.at[pl.ds(j * step, step), :]
-            copies.append(pltpu.make_async_copy(source, target, sems.at[i, j]))
+    for i, (part, (c, y)) in enumerate(zip(parts, where)):
+        size = part.shape[axis]
+        source = ((replica // 4) ^ c) * 4 + ((replica + y) & 3)
+        at = pl.ds(pl.multiple_of(source * size, size), size)
+        target = whole_ref.at[at, :] if axis == 0 else whole_ref.at[:, at]
+        copies.append(pltpu.make_async_copy(part, target, sems.at[i]))
     for copy in copies:
         copy.start()
     for copy in copies:
         copy.wait()
 
 
-def place(whole, parts, starts, axis, shape):
+def place(whole, parts, where, axis, shape):
     count = len(parts)
     continued = whole is not None
     vmem = pl.BlockSpec(memory_space=pltpu.VMEM)
     anywhere = pl.BlockSpec(memory_space=pl.ANY)
     return pl.pallas_call(
-        lambda *refs: place_kernel(axis, count, *refs),
+        lambda *refs: place_kernel(axis, where, *refs),
         out_shape=jax.ShapeDtypeStruct(shape, parts[0].dtype),
-        in_specs=[pl.BlockSpec(memory_space=pltpu.SMEM)]
-        + [vmem] * count
-        + ([anywhere] if continued else []),
+        in_specs=[vmem] * count + ([anywhere] if continued else []),
         out_specs=anywhere,
-        scratch_shapes=[pltpu.SemaphoreType.DMA((count, 4))],
-        input_output_aliases={1 + count: 0} if continued else {},
+        scratch_shapes=[pltpu.SemaphoreType.DMA((count,))],
+        input_output_aliases={count: 0} if continued else {},
         name="place",
-    )(jnp.stack(starts).astype(jnp.int32), *parts, *((whole,) if continued else ()))
-
-
-def attend_kernel(scale, facts_ref, cosine_ref, sine_ref, new_ref, key_ref, value_ref, message_ref, query_s, message_s):
+    )(*parts, *((whole,) if continued else ()))
+
+
+def attend_kernel(scale, lengths_ref, cosine_ref, sine_ref, new_ref, key_ref, value_ref, message_ref, query_s, message_s):
     groups, slots, _ = new_ref.shape
     rows, span, _ = key_ref.shape
     per_row = query_s.shape[0] // rows
@@ -154,7 +154,7 @@
         [new_ref[t, :, start + width : start + 2 * width] for t in range(groups)], 1
     )
 
-    member = facts_ref[rows]
+    member = lax.axis_index("tensor")
     kv_of = lax.broadcasted_iota(jnp.int32, (per_row, 1), 0) // (per_row // KVH)
     position = lax.broadcasted_iota(jnp.int32, (per_row, span), 1) + member * span
     slot = lax.broadcasted_iota(jnp.int32, (per_row, slots), 1)
@@ -174,7 +174,7 @@
                 * scale
             )
 
-        valid = position < facts_ref[r]
+        valid = position < lengths_ref[r]
         scores = jnp.where(valid, product(key_ref[r]), FLOOR)
         fresh = (slot % rows == r) & (slot // rows <= step) & (member == 0)
         fresh_scores = jnp.where(fresh, product(new_keys), FLOOR)
@@ -221,14 +221,8 @@
     attended_ref[...] = jnp.concatenate([attended[: half // 2], attended[half // 2 :]], 1)
 
 
-def project_kernel(attended_ref, weight_ref, terms_ref):
-    terms = lax.dot_general(
-        attended_ref[...],
-        weight_ref[...],
-        (((1,), (1,)), ((), ())),
-        preferred_element_type=jnp.float32,
-    )
-    terms_ref[0] = terms.astype(terms_ref.dtype)
+def total_kernel(terms_ref, after_ref, output_ref):
+    output_ref[...] = jnp.sum(terms_ref[...].astype(jnp.float32), 0).astype(output_ref.dtype)
 
 
 def exchange(blocks, axis):
@@ -237,7 +231,6 @@
 
 def on_device(hidden, norm_gain, qkv_bias, key_cache, value_cache, lengths, fresh_qkv, fresh_out):
     groups = lax.axis_size("tensor")
-    member = lax.axis_index("tensor")
     replicas = lax.axis_size("dp")
     step_count, row_count, feature_width = hidden.shape
     slots = step_count * row_count
@@ -247,8 +240,6 @@
     own_heads = QH // groups
     score_scale = 1.0 / math.sqrt(HD)
 
-    replica = lax.axis_index("dp")
-    column, y_at = replica // 4, replica % 4
     vmem = pl.BlockSpec(memory_space=pltpu.VMEM)
     smem = pl.BlockSpec(memory_space=pltpu.SMEM)
     anywhere = pl.BlockSpec(memory_space=pl.ANY)
@@ -262,42 +253,33 @@
 
     width = 2 * query_width + HD
     group_width = query_width + 2 * kv_width
-    packed, own_states, other_states = pl.pallas_call(
+    own_states, other_states = pl.pallas_call(
+        norm_kernel,
+        out_shape=(jax.ShapeDtypeStruct((replicas // 2, slots, share), jnp.bfloat16),) * 2,
+        name="norm",
+    )(hidden, norm_gain.reshape(1, feature_width))
+    cross_states = send(other_states, across)
+    packed = pl.pallas_call(
         lambda *refs: pack_kernel(groups, *refs),
-        out_shape=(
-            jax.ShapeDtypeStruct((groups, fresh_qkv.shape[0], width), fresh_qkv.dtype),
-            jax.ShapeDtypeStruct((replicas // 2, slots, share), jnp.bfloat16),
-            jax.ShapeDtypeStruct((replicas // 2, slots, share), jnp.bfloat16),
-        ),
-        in_specs=[smem] + [vmem] * 4,
+        out_shape=jax.ShapeDtypeStruct((groups, fresh_qkv.shape[0], width), fresh_qkv.dtype),
+        in_specs=[anywhere] + [vmem] * 2,
         name="pack",
-    )(
-        jnp.stack([column, y_at]).astype(jnp.int32),
-        hidden.reshape(slots, feature_width),
-        norm_gain.reshape(1, feature_width),
-        fresh_qkv,
-        fresh_out,
-    )
+    )(own_states, fresh_qkv, fresh_out)
+    packed, cross_states = hold(packed, cross_states)
     packed = exchange(packed, "tensor").reshape(share, width)
 
-    cross_states = send(other_states, across)
     low_states, far_states, high_states = (
         send(jnp.stack([own_states[k], cross_states[k]]), pairs)
         for k, pairs in ((1, ahead), (2, beyond), (3, behind))
     )
-    order = jnp.stack(
-        [(column ^ c) * 4 + ((y_at + y) & 3) for y in (0, -1, 1, 2) for c in (0, 1)]
-    ).astype(jnp.int32)
-
     terms, own_out = pl.pallas_call(
         lambda *refs: terms_kernel(group_width, *refs),
         out_shape=(
             jax.ShapeDtypeStruct((replicas, slots, group_width), jnp.float32),
             jax.ShapeDtypeStruct((share, query_width), packed.dtype),
         ),
-        in_specs=[smem] + [vmem] * 6,
         name="terms",
-    )(order, own_states, cross_states, low_states, high_states, far_states, packed)
+    )(own_states, cross_states, low_states, high_states, far_states, packed)
     terms = exchange(terms, "dp")
     out_across = send(own_out, across)
     out_low, out_high = send(own_out, ahead), send(own_out, behind)
@@ -324,10 +306,6 @@
     qkv_low, qkv_high = send(own_qkv, ahead), send(own_qkv, behind)
     qkv_across = send(own_qkv, across)
 
-    def index_of(column_at, y):
-        return (column_at * 4 + ((y_at + y) & 3)) * (share // 512)
-
-    other = 1 - column
     out_shape, qkv_shape = (feature_width, query_width), (group_width, feature_width)
 
     half_width = HD // 2
@@ -341,13 +319,12 @@
     sine = jnp.concatenate([-sine, sine], 1)
 
     grouped_out = place(
-        None, [own_out, out_across], [index_of(column, 0), index_of(other, 0)], 0, out_shape
+        None, [own_out, out_across], [(0, 0), (1, 0)], 0, out_shape
     )
     grouped_out = place(
-        grouped_out, [out_low, out_high], [index_of(column, -1), index_of(column, 1)], 0, out_shape
-    )
-
-    facts = jnp.concatenate([lengths, jnp.full((1,), member, jnp.int32)])
+        grouped_out, [out_low, out_high], [(0, -1), (0, 1)], 0, out_shape
+    )
+
     message = pl.pallas_call(
         lambda *refs: attend_kernel(score_scale, *refs),
         out_shape=jax.ShapeDtypeStruct((groups, 2 * slots * own_heads, HD), jnp.bfloat16),
@@ -357,7 +334,7 @@
             pltpu.VMEM((groups, 2 * slots * own_heads, HD), jnp.float32),
         ],
         name="attend",
-    )(facts, cosine, sine, gathered, key_cache, value_cache)
+    )(lengths, cosine, sine, gathered, key_cache, value_cache)
     message, out_cross_low, out_cross_high, qkv_low, qkv_high, qkv_across, grouped_out = hold(
         message, out_cross_low, out_cross_high, qkv_low, qkv_high, qkv_across, grouped_out
     )
@@ -367,12 +344,12 @@
     grouped_out = place(
         grouped_out,
         [out_cross_low, out_cross_high],
-        [index_of(other, -1), index_of(other, 1)],
+        [(1, -1), (1, 1)],
         0,
         out_shape,
     )
     grouped_qkv = place(
-        None, [own_qkv, qkv_across], [index_of(column, 0), index_of(other, 0)], 1, qkv_shape
+        None, [own_qkv, qkv_across], [(0, 0), (1, 0)], 1, qkv_shape
     )
     attended = pl.pallas_call(
         merge_kernel,
@@ -385,7 +362,7 @@
     grouped_out = place(
         grouped_out,
         [out_far, out_cross_far],
-        [index_of(column, 2), index_of(other, 2)],
+        [(0, 2), (1, 2)],
         0,
         out_shape,
     )
@@ -394,33 +371,29 @@
     grouped_qkv = place(
         grouped_qkv,
         [qkv_low, qkv_high, qkv_cross_high],
-        [index_of(column, -1), index_of(column, 1), index_of(other, 1)],
+        [(0, -1), (0, 1), (1, 1)],
         1,
         qkv_shape,
     )
     grouped_qkv = place(
         grouped_qkv,
         [qkv_far, qkv_cross_low, qkv_cross_far],
-        [index_of(column, 2), index_of(other, -1), index_of(other, 2)],
+        [(0, 2), (1, -1), (1, 2)],
         1,
         qkv_shape,
-    ).T
-
-    span = feature_width // groups
-    term_sums = pl.pallas_call(
-        project_kernel,
-        grid=(groups,),
-        out_shape=jax.ShapeDtypeStruct((groups, slots, span), jnp.bfloat16),
-        in_specs=[
-            pl.BlockSpec((slots, own_heads * HD), lambda i: (0, 0)),
-            pl.BlockSpec((span, own_heads * HD), lambda i: (i, 0)),
-        ],
-        out_specs=pl.BlockSpec((1, slots, span), lambda i: (i, 0, 0)),
-        name="project",
-    )(attended, grouped_out)
-    attn_output = jnp.sum(exchange(term_sums, "tensor").astype(jnp.float32), 0)
-    attn_output = attn_output.astype(jnp.bfloat16).reshape(step_count, row_count, -1)
-    return (attn_output, grouped_qkv, grouped_out)
+    )
+
+    term_sums = jnp.dot(attended, grouped_out.T, preferred_element_type=jnp.float32)
+    term_sums = term_sums.astype(jnp.bfloat16).reshape(slots, groups, -1).transpose(1, 0, 2)
+    term_sums = exchange(term_sums, "tensor")
+    attn_output = pl.pallas_call(
+        total_kernel,
+        out_shape=jax.ShapeDtypeStruct((slots, feature_width // groups), jnp.bfloat16),
+        in_specs=[vmem, anywhere],
+        name="total",
+    )(term_sums, grouped_qkv)
+    attn_output = attn_output.reshape(step_count, row_count, -1)
+    return (attn_output, grouped_qkv.T, grouped_out)
 
 
 def solution(mesh):

time: 162 us -> 149 us (0.920)
  Pallas kernels: 45.3 us -> 37.5 us
  other arithmetic: 6.32 us -> 0.83 us
  matrix products: 0 us -> 3.38 us
  starting transfers between devices: 56 us -> 53 us
    ppermute x18, waiting for transfers between devices: 19.7 us -> 5.16 us  [send(): return lax.ppermute(value, 'dp', pairs)]
    all_to_all x5, waiting for transfers between devices: 19.6 us -> 32.8 us  [exchange(): return lax.all_to_all(blocks, axis, split_axis=0, concat_axis=0, tiled=True)]
    pallas_call x9 -> x10, Pallas kernels: 30.4 us -> 22.6 us  [the longest x7 16.6 us: place(): pl.pallas_call(lambda *refs: place_kernel(axis, where, *refs), out_shape=...]
    another operation x7 -> x0, other arithmetic: 4.24 us -> none  [the longest x6 3.58 us: place(): jnp.stack(starts).astype(jnp.int32)]
    dot_general x0 -> x1, matrix products: none -> 3.38 us  [on_device(): jnp.dot(attended, grouped_out.T, preferred_element_type=jnp.float32)]
    all_to_all x5, starting transfers between devices: 36.1 us -> 34.2 us  [exchange(): return lax.all_to_all(blocks, axis, split_axis=0, concat_axis=0, tiled=True)]
    unnamed x50 -> x56, local copies, waits for them, and re-layouts: 9.46 us -> 9.89 us
  transfers between devices with their start and end apart: 23 -> 23, of which waited for: 6 -> 10; matrix products, arithmetic and copies ran while one was open for 5% -> 4% of each run, Pallas kernels for 22% -> 20%
where the time goes in v3:
time: 149 us; the launch traced here: 147 us
  starting transfers between devices  53 us (36%)
  waiting for transfers between devices  37.9 us (25%)
  Pallas kernels  37.5 us (25%)
  local copies, waits for them, and re-layouts  13.5 us (9%)
  matrix products  3.38 us (2%)
    all_to_all x5, starting transfers between devices, exchange(): return lax.all_to_all(blocks, axis, split_axis=0, concat_axis=0, tiled=True)  34.2 us
    all_to_all x5, waiting for transfers between devices, exchange(): return lax.all_to_all(blocks, axis, split_axis=0, concat_axis=0, tiled=True)  32.8 us
    ppermute x18, starting transfers between devices, send(): return lax.ppermute(value, 'dp', pairs)  18.8 us
    pallas_call x7, Pallas kernels, place(): pl.pallas_call(lambda *refs: place_kernel(axis, where, *refs), out_shape=...  16.6 us
    unnamed x56, local copies, waits for them, and re-layouts  9.89 us
    pallas_call x1, Pallas kernels, on_device(): pl.pallas_call(lambda *refs: attend_kernel(score_scale, *refs), out_shape...  6.3 us
    ppermute x18, waiting for transfers between devices, send(): return lax.ppermute(value, 'dp', pairs)  5.16 us
    dot_general x1, matrix products, on_device(): jnp.dot(attended, grouped_out.T, preferred_element_type=jnp.float32)  3.38 us
  transfers between devices with their start and end apart: 23, of which 10 were waited for; matrix products, arithmetic and copies ran while one was open for 4% of the time, Pallas kernels for 20%

profile of v3, /device:TPU:1, one launch (start us, length us, event | category | flops | bytes accessed | tf_op | source)
XLA Modules:
  0.0 147.0 jit_solution(12455279848259455093)
XLA Ops:
  0.6 1.4 reshape.45.gain_ref
  2.0 1.9 %norm.1 = (bf16[4,16,1024]{2,1,0:T(8,128)(2,1)}, bf16[4,16,1024]{2,1,0:T(8,128)(2,1)}) custom-call(bf16[2,8,8192]{2,1,0:T(8,128)(2,1)} %states_ref.1, bf16[1,8192]{1,0:T(2,128)(2,1)} %reshape.45.gain_ref), custom_call_target="tpu_custom_call" | custom-call | tf_op jit(solution)/shard_map/norm/pallas_call | solution.py:256
  3.9 2.0 %collective-permute-start = (bf16[4,16,1024]{2,1,0:T(8,128)(2,1)}, bf16[4,16,1024]{2,1,0:T(8,128)(2,1)S(1)}, u32[]{:S(2)}, u32[]{:S(2)}) collective-permute-start(bf16[4,16,1024]{2,1,0:T(8,128)(2,1)} %get-tuple-element.29), channel_id=1, source_target_pairs={{0,64},{16,80},{32,96},{48,112},{64,0},{80,16},{96,32},{112,48},{1... | collective-permute-start | bytes 393224 | tf_op jit(solution)/shard_map/ppermute | solution.py:252
  5.9 2.5 %pack.1.refs_0_ = bf16[16,64,640]{2,1,0:T(8,128)(2,1)} custom-call(bf16[4,16,1024]{2,1,0:T(8,128)(2,1)} %get-tuple-element.28.refs_0_, bf16[64,5120]{1,0:T(8,128)(2,1)} %refs_1_.1, bf16[64,4096]{1,0:T(8,128)(2,1)} %refs_2_.1), custom_call_target="tpu_custom_call" | custom-call | tf_op jit(solution)/shard_map/pack/pallas_call | solution.py:262
  9.5 9.8 %all-to-all-start = ((bf16[16,64,640]{2,1,0:T(8,128)(2,1)}), bf16[16,64,640]{2,1,0:T(8,128)(2,1)S(1)}, u32[]{:S(2)}, u32[]{:S(2)}) async-start(bf16[16,64,640]{2,1,0:T(8,128)(2,1)} %get-tuple-element.31), calls=%async_computation | async-start | bytes 2621440 | tf_op jit(solution)/shard_map/all_to_all | solution.py:229
  19.3 0.8 fusion.2
  20.1 1.4 collective-permute-start.1
  21.5 1.5 %collective-permute-start.2 = (bf16[2,16,1024]{2,1,0:T(8,128)(2,1)S(1)}, bf16[2,16,1024]{2,1,0:T(8,128)(2,1)S(1)}, u32[]{:S(2)}, u32[]{:S(2)}) collective-permute-start(bf16[2,16,1024]{2,1,0:T(8,128)(2,1)S(1)} %pad_maximum_fusion.1), channel_id=1, source_target_pairs={{0,48},{16,0},{32,16},{48,32},{64,112},{80,64},{96,80},{112,96},{1... | collective-permute-start | bytes 196616 | tf_op jit(solution)/shard_map/ppermute | solution.py:252
  23.0 1.7 %collective-permute-start.3 = (bf16[2,16,1024]{2,1,0:T(8,128)(2,1)S(1)}, bf16[2,16,1024]{2,1,0:T(8,128)(2,1)S(1)}, u32[]{:S(2)}, u32[]{:S(2)}) collective-permute-start(bf16[2,16,1024]{2,1,0:T(8,128)(2,1)S(1)} %pad_maximum_fusion.2), channel_id=1, source_target_pairs={{0,32},{16,48},{32,0},{48,16},{64,96},{80,112},{96,64},{112,80},{1... | collective-permute-start | bytes 196616 | tf_op jit(solution)/shard_map/ppermute | solution.py:252
  25.1 2.9 %collective-permute-done.3.refs_4_ = bf16[2,16,1024]{2,1,0:T(8,128)(2,1)S(1)} collective-permute-done((bf16[2,16,1024]{2,1,0:T(8,128)(2,1)S(1)}, bf16[2,16,1024]{2,1,0:T(8,128)(2,1)S(1)}, u32[]{:S(2)}, u32[]{:S(2)}) %collective-permute-start.3) | collective-permute-done | bytes 65568 | tf_op jit(solution)/shard_map/ppermute | solution.py:252
  28.0 11.3 %all-to-all-done = bf16[16,64,640]{2,1,0:T(8,128)(2,1)S(1)} async-done(((bf16[16,64,640]{2,1,0:T(8,128)(2,1)}), bf16[16,64,640]{2,1,0:T(8,128)(2,1)S(1)}, u32[]{:S(2)}, u32[]{:S(2)}) %all-to-all-start) | async-done | bytes 1310752 | tf_op jit(solution)/shard_map/all_to_all | solution.py:229
  39.3 1.0 copy-done
  40.4 2.7 %terms.1 = (f32[8,16,320]{2,1,0:T(8,128)}, bf16[1024,256]{1,0:T(8,128)(2,1)}) custom-call(bf16[4,16,1024]{2,1,0:T(8,128)(2,1)} %get-tuple-element.28.refs_0_, bf16[4,16,1024]{2,1,0:T(8,128)(2,1)} %get-tuple-element.30.refs_1_, bf16[2,16,1024]{2,1,0:T(8,128)(2,1)} %copy-done.23, bf16[2,16,1024]{2,1,0:T(8,128)(2,1)} %copy-done.24, ...), custom_call_target="tpu_custom_call" | custom-call | tf_op jit(solution)/shard_map/terms/pallas_call | solution.py:275
  43.0 2.7 %collective-permute-start.6 = (bf16[1024,256]{1,0:T(8,128)(2,1)}, bf16[1024,256]{1,0:T(8,128)(2,1)S(1)}, u32[]{:S(2)}, u32[]{:S(2)}) collective-permute-start(bf16[1024,256]{1,0:T(8,128)(2,1)} %get-tuple-element.33.refs_0_), channel_id=1, source_target_pairs={{0,48},{16,0},{32,16},{48,32},{64,112},{80,64},{96,80},{112,96},{1... | collective-permute-start | bytes 1572872 | tf_op jit(solution)/shard_map/ppermute | solution.py:252
  46.1 4.8 %all-to-all-start.1 = ((f32[8,16,320]{2,1,0:T(8,128)}), f32[8,16,320]{2,1,0:T(8,128)S(1)}, u32[]{:S(2)}, u32[]{:S(2)}) async-start(f32[8,16,320]{2,1,0:T(8,128)} %get-tuple-element.32), calls=%async_computation.1 | async-start | bytes 393216 | tf_op jit(solution)/shard_map/all_to_all | solution.py:229
  51.5 2.4 %turn.1.refs_3_ = bf16[320,1024]{1,0:T(8,128)(2,1)} custom-call(bf16[1024,640]{1,0:T(8,128)(2,1)} %bitcast.14), custom_call_target="tpu_custom_call" | custom-call | tf_op jit(solution)/shard_map/turn/pallas_call | solution.py:286
  53.9 7.7 %all-to-all-done.1.terms_ref = f32[8,16,320]{2,1,0:T(8,128)S(1)} async-done(((f32[8,16,320]{2,1,0:T(8,128)}), f32[8,16,320]{2,1,0:T(8,128)S(1)}, u32[]{:S(2)}, u32[]{:S(2)}) %all-to-all-start.1) | async-done | bytes 163872 | tf_op jit(solution)/shard_map/all_to_all | solution.py:229
  62.6 0.8 copy-done.12
  63.4 1.6 %sum.1 = (bf16[16,16,320]{2,1,0:T(8,128)(2,1)}, bf16[1024,256]{1,0:T(8,128)(2,1)}, bf16[1024,256]{1,0:T(8,128)(2,1)}, bf16[1024,256]{1,0:T(8,128)(2,1)}, bf16[320,1024]{1,0:T(8,128)(2,1)}) custom-call(f32[8,16,320]{2,1,0:T(8,128)} %copy-done.18, ...), custom_call_target="tpu_custom_call", output_to_operand_aliasing={{1}: (2, {}), {2}: (3, {}), {3}: (4, {}), {4}: (5, {})} | custom-call | tf_op jit(solution)/shard_map/sum/pallas_call | solution.py:292
  65.1 1.1 collective-permute-start.8
  66.8 2.3 %collective-permute-start.10 = (bf16[320,1024]{1,0:T(8,128)(2,1)}, bf16[320,1024]{1,0:T(8,128)(2,1)S(1)}, u32[]{:S(2)}, u32[]{:S(2)}) collective-permute-start(bf16[320,1024]{1,0:T(8,128)(2,1)} %get-tuple-element.36.refs_0_), channel_id=1, source_target_pairs={{0,48},{16,0},{32,16},{48,32},{64,112},{80,64},{96,80},{112,96},{1... | collective-permute-start | bytes 1966088 | tf_op jit(solution)/shard_map/ppermute | solution.py:252
  69.3 7.1 %all-to-all-start.2 = ((bf16[16,16,320]{2,1,0:T(8,128)(2,1)}), bf16[16,16,320]{2,1,0:T(8,128)(2,1)S(1)}, u32[]{:S(2)}, u32[]{:S(2)}) async-start(bf16[16,16,320]{2,1,0:T(8,128)(2,1)} %get-tuple-element.34), calls=%async_computation.2 | async-start | bytes 393216 | tf_op jit(solution)/shard_map/all_to_all | solution.py:229
  77.1 2.2 %place.7.refs_2_ = bf16[8192,256]{1,0:T(8,128)(2,1)} custom-call(bf16[1024,256]{1,0:T(8,128)(2,1)} %get-tuple-element.33.refs_0_, bf16[1024,256]{1,0:T(8,128)(2,1)} %get-tuple-element.35.refs_1_), custom_call_target="tpu_custom_call" | custom-call | tf_op jit(solution)/shard_map/place/pallas_call | solution.py:120
  79.3 2.2 %place.8.refs_6_ = bf16[8192,256]{1,0:T(8,128)(2,1)} custom-call(bf16[1024,256]{1,0:T(8,128)(2,1)} %get-tuple-element.37.refs_0_, bf16[1024,256]{1,0:T(8,128)(2,1)} %get-tuple-element.38.refs_1_, bf16[8192,256]{1,0:T(8,128)(2,1)} %place.7.refs_2_), custom_call_target="tpu_custom_call", output_to_operand_aliasing={{}: (2, {})} | custom-call | tf_op jit(solution)/shard_map/place/pallas_call | solution.py:120
  81.5 5.3 %all-to-all-done.2.refs_3_ = bf16[16,16,320]{2,1,0:T(8,128)(2,1)S(1)} async-done(((bf16[16,16,320]{2,1,0:T(8,128)(2,1)}), bf16[16,16,320]{2,1,0:T(8,128)(2,1)S(1)}, u32[]{:S(2)}, u32[]{:S(2)}) %all-to-all-start.2) | async-done | bytes 163872 | tf_op jit(solution)/shard_map/all_to_all | solution.py:229
  87.5 6.3 %attend.1.refs_0_ = bf16[16,64,128]{2,1,0:T(8,128)(2,1)} custom-call(s32[8]{0:T(128)} %refs_0_.1, f32[16,128]{1,0:T(8,128)} %get-tuple-element.62.refs_1_, f32[16,128]{1,0:T(8,128)} %get-tuple-element.63.refs_2_, bf16[16,16,320]{2,1,0:T(8,128)(2,1)} %copy-done.17, bf16[8,256,512]{2,1,0:T(8,128)(2,1)} %refs_4_.1, bf16[8,256,512]{2,1,0:T(8,128)(2,1)} %refs_5_.1), custom_call_target="tpu_custom_call" | custom-call | tf_op jit(solution)/shard_map/attend/pallas_call | solution.py:328
  93.8 0.7 copy-done.5
  95.2 0.9 copy-done.1
  96.1 2.7 %collective-permute-start.13 = (bf16[1024,256]{1,0:T(8,128)(2,1)}, bf16[1024,256]{1,0:T(8,128)(2,1)S(1)}, u32[]{:S(2)}, u32[]{:S(2)}) collective-permute-start(bf16[1024,256]{1,0:T(8,128)(2,1)} %get-tuple-element.40.refs_1_), channel_id=1, source_target_pairs={{0,48},{16,0},{32,16},{48,32},{64,112},{80,64},{96,80},{112,96},{1... | collective-permute-start | bytes 1572872 | tf_op jit(solution)/shard_map/ppermute | solution.py:252
  98.7 6.8 %all-to-all-start.3 = ((bf16[16,64,128]{2,1,0:T(8,128)(2,1)}), bf16[16,64,128]{2,1,0:T(8,128)(2,1)S(1)}, u32[]{:S(2)}, u32[]{:S(2)}) async-start(bf16[16,64,128]{2,1,0:T(8,128)(2,1)} %get-tuple-element.39), calls=%async_computation.3 | async-start | bytes 524288 | tf_op jit(solution)/shard_map/all_to_all | solution.py:229
  105.5 2.4 %place.10.refs_6_ = bf16[320,8192]{1,0:T(8,128)(2,1)} custom-call(bf16[320,1024]{1,0:T(8,128)(2,1)} %get-tuple-element.36.refs_0_, bf16[320,1024]{1,0:T(8,128)(2,1)} %get-tuple-element.45.refs_1_), custom_call_target="tpu_custom_call" | custom-call | tf_op jit(solution)/shard_map/place/pallas_call | solution.py:120
  107.9 2.2 %place.9.refs_5_ = bf16[8192,256]{1,0:T(8,128)(2,1)} custom-call(bf16[1024,256]{1,0:T(8,128)(2,1)} %get-tuple-element.43.refs_0_, bf16[1024,256]{1,0:T(8,128)(2,1)} %get-tuple-element.40.refs_1_, bf16[8192,256]{1,0:T(8,128)(2,1)} %get-tuple-element.44.refs_2_), custom_call_target="tpu_custom_call", output_to_operand_aliasing={{}: (2, {})} | custom-call | tf_op jit(solution)/shard_map/place/pallas_call | solution.py:120
  110.1 7.7 %all-to-all-done.3.message_ref = bf16[16,64,128]{2,1,0:T(8,128)(2,1)S(1)} async-done(((bf16[16,64,128]{2,1,0:T(8,128)(2,1)}), bf16[16,64,128]{2,1,0:T(8,128)(2,1)S(1)}, u32[]{:S(2)}, u32[]{:S(2)}) %all-to-all-start.3) | async-done | bytes 262176 | tf_op jit(solution)/shard_map/all_to_all | solution.py:229
  117.8 0.7 copy-done.13
  118.5 1.9 %merge.1.refs_0_ = bf16[16,256]{1,0:T(8,128)(2,1)} custom-call(bf16[16,64,128]{2,1,0:T(8,128)(2,1)} %copy-done.13), custom_call_target="tpu_custom_call" | custom-call | tf_op jit(solution)/shard_map/merge/pallas_call | solution.py:354
  120.4 0.8 copy-done.7
  121.6 2.3 %collective-permute-start.17 = (bf16[320,1024]{1,0:T(8,128)(2,1)}, bf16[320,1024]{1,0:T(8,128)(2,1)S(1)}, u32[]{:S(2)}, u32[]{:S(2)}) collective-permute-start(bf16[320,1024]{1,0:T(8,128)(2,1)} %get-tuple-element.51.refs_2_), channel_id=1, source_target_pairs={{0,48},{16,0},{32,16},{48,32},{64,112},{80,64},{96,80},{112,96},{1... | collective-permute-start | bytes 1966088 | tf_op jit(solution)/shard_map/ppermute | solution.py:252
  123.9 2.2 %place.11 = bf16[8192,256]{1,0:T(8,128)(2,1)} custom-call(bf16[1024,256]{1,0:T(8,128)(2,1)} %get-tuple-element.47.refs_0_, bf16[1024,256]{1,0:T(8,128)(2,1)} %get-tuple-element.48.refs_1_, bf16[8192,256]{1,0:T(8,128)(2,1)} %get-tuple-element.49.refs_2_), custom_call_target="tpu_custom_call", output_to_operand_aliasing={{}: (2, {})} | custom-call | tf_op jit(solution)/shard_map/place/pallas_call | solution.py:120
  126.1 3.4 %convolution_convert_fusion = bf16[16,8192]{1,0:T(8,128)(2,1)S(1)} fusion(bf16[16,256]{1,0:T(8,128)(2,1)S(1)} %copy-done.22, bf16[8192,256]{1,0:T(8,128)(2,1)} %place.11), kind=kOutput, calls=%fused_computation | convolution fusion | flops 67239936 | bytes 4464640 | tf_op jit(solution)/shard_map/dot_general | solution.py:386
  129.5 0.8 copy.39
  130.2 5.7 %all-to-all-start.4 = ((bf16[16,16,512]{2,1,0:T(8,128)(2,1)}), bf16[16,16,512]{2,1,0:T(8,128)(2,1)S(1)}, u32[]{:S(2)}, u32[]{:S(2)}) async-start(bf16[16,16,512]{2,1,0:T(8,128)(2,1)} %bitcast.11), calls=%async_computation.4 | async-start | bytes 524288 | tf_op jit(solution)/shard_map/all_to_all | solution.py:229
  135.9 2.8 %place.12.refs_3_ = bf16[320,8192]{1,0:T(8,128)(2,1)} custom-call(bf16[320,1024]{1,0:T(8,128)(2,1)} %get-tuple-element.50.refs_0_, bf16[320,1024]{1,0:T(8,128)(2,1)} %get-tuple-element.41.refs_1_, bf16[320,1024]{1,0:T(8,128)(2,1)} %get-tuple-element.51.refs_2_, bf16[320,8192]{1,0:T(8,128)(2,1)} %get-tuple-element.52.refs_3_), custom_call_target="tpu_custom_call", output_to_operand_aliasing={{}: (3, {})} | custom-call | tf_op jit(solution)/shard_map/place/pallas_call | solution.py:120
  139.0 1.2 collective-permute-done.15.refs_0_
  140.2 0.9 copy-done.21
  141.1 2.8 %place.13.after_ref = bf16[320,8192]{1,0:T(8,128)(2,1)} custom-call(bf16[320,1024]{1,0:T(8,128)(2,1)} %copy-done.21, bf16[320,1024]{1,0:T(8,128)(2,1)} %copy-done.20, bf16[320,1024]{1,0:T(8,128)(2,1)} %copy-done.19, bf16[320,8192]{1,0:T(8,128)(2,1)} %place.12.refs_3_), custom_call_target="tpu_custom_call", output_to_operand_aliasing={{}: (3, {})} | custom-call | tf_op jit(solution)/shard_map/place/pallas_call | solution.py:120
  143.8 0.8 all-to-all-done.4.terms_ref
  144.7 0.7 copy-done.14
  145.4 1.6 %total.1 = bf16[16,512]{1,0:T(8,128)(2,1)} custom-call(bf16[16,16,512]{2,1,0:T(8,128)(2,1)} %copy-done.14, bf16[320,8192]{1,0:T(8,128)(2,1)} %place.13.after_ref), custom_call_target="tpu_custom_call" | custom-call | tf_op jit(solution)/shard_map/total/pallas_call | solution.py:389
  (86 shorter events, 7.0 us)
Async XLA Ops:
  3.9 15.4 %copy-start.15 = (bf16[4,16,1024]{2,1,0:T(8,128)(2,1)S(1)}, bf16[4,16,1024]{2,1,0:T(8,128)(2,1)}, u32[]{:S(2)}) copy-start(bf16[4,16,1024]{2,1,0:T(8,128)(2,1)} %get-tuple-element.28.refs_0_) | copy-start | bytes 393220
  3.9 5.0 %collective-permute-start = (bf16[4,16,1024]{2,1,0:T(8,128)(2,1)}, bf16[4,16,1024]{2,1,0:T(8,128)(2,1)S(1)}, u32[]{:S(2)}, u32[]{:S(2)}) collective-permute-start(bf16[4,16,1024]{2,1,0:T(8,128)(2,1)} %get-tuple-element.29), channel_id=1, source_target_pairs={{0,64},{16,80},{32,96},{48,112},{64,0},{80,16},{96,32},{112,48},{1... | collective-permute-start | bytes 393224 | tf_op jit(solution)/shard_map/ppermute | solution.py:252
  5.9 45.0 %copy-start.26 = (bf16[320]{0:T(512)(128)(2,1)S(1)}, bf16[320]{0:T(512)(128)(2,1)}, u32[]{:S(2)}) copy-start(bf16[320]{0:T(512)(128)(2,1)} %param.10) | copy-start | bytes 1924
  9.5 29.8 %all-to-all-start = ((bf16[16,64,640]{2,1,0:T(8,128)(2,1)}), bf16[16,64,640]{2,1,0:T(8,128)(2,1)S(1)}, u32[]{:S(2)}, u32[]{:S(2)}) async-start(bf16[16,64,640]{2,1,0:T(8,128)(2,1)} %get-tuple-element.31), calls=%async_computation | async-start | bytes 2621440 | tf_op jit(solution)/shard_map/all_to_all | solution.py:229
  19.3 49.9 %copy-start.27 = (s32[8]{0:T(128)S(1)}, s32[8]{0:T(128)}, u32[]{:S(2)}) copy-start(s32[8]{0:T(128)} %refs_0_.1) | copy-start | bytes 100
  20.1 5.0 %collective-permute-start.1 = (bf16[2,16,1024]{2,1,0:T(8,128)(2,1)S(1)}, bf16[2,16,1024]{2,1,0:T(8,128)(2,1)S(1)}, u32[]{:S(2)}, u32[]{:S(2)}) collective-permute-start(bf16[2,16,1024]{2,1,0:T(8,128)(2,1)S(1)} %pad_maximum_fusion), channel_id=1, source_target_pairs={{0,16},{16,32},{32,48},{48,0},{64,80},{80,96},{96,112},{112,64},{1... | collective-permute-start | bytes 196616 | tf_op jit(solution)/shard_map/ppermute | solution.py:252
  21.5 3.6 %collective-permute-start.2 = (bf16[2,16,1024]{2,1,0:T(8,128)(2,1)S(1)}, bf16[2,16,1024]{2,1,0:T(8,128)(2,1)S(1)}, u32[]{:S(2)}, u32[]{:S(2)}) collective-permute-start(bf16[2,16,1024]{2,1,0:T(8,128)(2,1)S(1)} %pad_maximum_fusion.1), channel_id=1, source_target_pairs={{0,48},{16,0},{32,16},{48,32},{64,112},{80,64},{96,80},{112,96},{1... | collective-permute-start | bytes 196616 | tf_op jit(solution)/shard_map/ppermute | solution.py:252
  23.0 5.0 %collective-permute-start.3 = (bf16[2,16,1024]{2,1,0:T(8,128)(2,1)S(1)}, bf16[2,16,1024]{2,1,0:T(8,128)(2,1)S(1)}, u32[]{:S(2)}, u32[]{:S(2)}) collective-permute-start(bf16[2,16,1024]{2,1,0:T(8,128)(2,1)S(1)} %pad_maximum_fusion.2), channel_id=1, source_target_pairs={{0,32},{16,48},{32,0},{48,16},{64,96},{80,112},{96,64},{112,80},{1... | collective-permute-start | bytes 196616 | tf_op jit(solution)/shard_map/ppermute | solution.py:252
  25.1 14.2 %copy-start.23 = (bf16[2,16,1024]{2,1,0:T(8,128)(2,1)}, bf16[2,16,1024]{2,1,0:T(8,128)(2,1)S(1)}, u32[]{:S(2)}) copy-start(bf16[2,16,1024]{2,1,0:T(8,128)(2,1)S(1)} %collective-permute-done.1.refs_2_) | copy-start | bytes 196612
  25.1 14.2 %copy-start.24 = (bf16[2,16,1024]{2,1,0:T(8,128)(2,1)}, bf16[2,16,1024]{2,1,0:T(8,128)(2,1)S(1)}, u32[]{:S(2)}) copy-start(bf16[2,16,1024]{2,1,0:T(8,128)(2,1)S(1)} %collective-permute-done.2.refs_3_) | copy-start | bytes 196612
  28.0 11.3 %copy-start.25 = (bf16[2,16,1024]{2,1,0:T(8,128)(2,1)}, bf16[2,16,1024]{2,1,0:T(8,128)(2,1)S(1)}, u32[]{:S(2)}) copy-start(bf16[2,16,1024]{2,1,0:T(8,128)(2,1)S(1)} %collective-permute-done.3.refs_4_) | copy-start | bytes 196612
  39.3 1.1 copy-start
  43.0 18.6 %collective-permute-start.6 = (bf16[1024,256]{1,0:T(8,128)(2,1)}, bf16[1024,256]{1,0:T(8,128)(2,1)S(1)}, u32[]{:S(2)}, u32[]{:S(2)}) collective-permute-start(bf16[1024,256]{1,0:T(8,128)(2,1)} %get-tuple-element.33.refs_0_), channel_id=1, source_target_pairs={{0,48},{16,0},{32,16},{48,32},{64,112},{80,64},{96,80},{112,96},{1... | collective-permute-start | bytes 1572872 | tf_op jit(solution)/shard_map/ppermute | solution.py:252
  45.8 15.8 %collective-permute-start.5 = (bf16[1024,256]{1,0:T(8,128)(2,1)}, bf16[1024,256]{1,0:T(8,128)(2,1)S(1)}, u32[]{:S(2)}, u32[]{:S(2)}) collective-permute-start(bf16[1024,256]{1,0:T(8,128)(2,1)} %get-tuple-element.33.refs_0_), channel_id=1, source_target_pairs={{0,16},{16,32},{32,48},{48,0},{64,80},{80,96},{96,112},{112,64},{1... | collective-permute-start | bytes 1572872 | tf_op jit(solution)/shard_map/ppermute | solution.py:252
  45.8 15.8 %collective-permute-start.4 = (bf16[1024,256]{1,0:T(8,128)(2,1)}, bf16[1024,256]{1,0:T(8,128)(2,1)S(1)}, u32[]{:S(2)}, u32[]{:S(2)}) collective-permute-start(bf16[1024,256]{1,0:T(8,128)(2,1)} %get-tuple-element.33.refs_0_), channel_id=1, source_target_pairs={{0,64},{16,80},{32,96},{48,112},{64,0},{80,16},{96,32},{112,48},{1... | collective-permute-start | bytes 1572872 | tf_op jit(solution)/shard_map/ppermute | solution.py:252
  46.1 15.5 %all-to-all-start.1 = ((f32[8,16,320]{2,1,0:T(8,128)}), f32[8,16,320]{2,1,0:T(8,128)S(1)}, u32[]{:S(2)}, u32[]{:S(2)}) async-start(f32[8,16,320]{2,1,0:T(8,128)} %get-tuple-element.32), calls=%async_computation.1 | async-start | bytes 393216 | tf_op jit(solution)/shard_map/all_to_all | solution.py:229
  61.6 0.9 copy-start.9
  61.6 1.0 copy-start.10
  62.6 0.8 copy-start.12
  65.1 28.7 %collective-permute-start.8 = (bf16[1024,256]{1,0:T(8,128)(2,1)}, bf16[1024,256]{1,0:T(8,128)(2,1)S(1)}, u32[]{:S(2)}, u32[]{:S(2)}) collective-permute-start(bf16[1024,256]{1,0:T(8,128)(2,1)} %get-tuple-element.35.refs_1_), channel_id=1, source_target_pairs={{0,48},{16,0},{32,16},{48,32},{64,112},{80,64},{96,80},{112,96},{1... | collective-permute-start | bytes 1572872 | tf_op jit(solution)/shard_map/ppermute | solution.py:252
  66.2 27.6 %collective-permute-start.7 = (bf16[1024,256]{1,0:T(8,128)(2,1)}, bf16[1024,256]{1,0:T(8,128)(2,1)S(1)}, u32[]{:S(2)}, u32[]{:S(2)}) collective-permute-start(bf16[1024,256]{1,0:T(8,128)(2,1)} %get-tuple-element.35.refs_1_), channel_id=1, source_target_pairs={{0,16},{16,32},{32,48},{48,0},{64,80},{80,96},{96,112},{112,64},{1... | collective-permute-start | bytes 1572872 | tf_op jit(solution)/shard_map/ppermute | solution.py:252
  66.5 27.3 %collective-permute-start.11 = (bf16[320,1024]{1,0:T(8,128)(2,1)}, bf16[320,1024]{1,0:T(8,128)(2,1)S(1)}, u32[]{:S(2)}, u32[]{:S(2)}) collective-permute-start(bf16[320,1024]{1,0:T(8,128)(2,1)} %get-tuple-element.36.refs_0_), channel_id=1, source_target_pairs={{0,64},{16,80},{32,96},{48,112},{64,0},{80,16},{96,32},{112,48},{1... | collective-permute-start | bytes 1966088 | tf_op jit(solution)/shard_map/ppermute | solution.py:252
  66.8 27.0 %collective-permute-start.10 = (bf16[320,1024]{1,0:T(8,128)(2,1)}, bf16[320,1024]{1,0:T(8,128)(2,1)S(1)}, u32[]{:S(2)}, u32[]{:S(2)}) collective-permute-start(bf16[320,1024]{1,0:T(8,128)(2,1)} %get-tuple-element.36.refs_0_), channel_id=1, source_target_pairs={{0,48},{16,0},{32,16},{48,32},{64,112},{80,64},{96,80},{112,96},{1... | collective-permute-start | bytes 1966088 | tf_op jit(solution)/shard_map/ppermute | solution.py:252
  69.2 24.7 %collective-permute-start.9 = (bf16[320,1024]{1,0:T(8,128)(2,1)}, bf16[320,1024]{1,0:T(8,128)(2,1)S(1)}, u32[]{:S(2)}, u32[]{:S(2)}) collective-permute-start(bf16[320,1024]{1,0:T(8,128)(2,1)} %get-tuple-element.36.refs_0_), channel_id=1, source_target_pairs={{0,16},{16,32},{32,48},{48,0},{64,80},{80,96},{96,112},{112,64},{1... | collective-permute-start | bytes 1966088 | tf_op jit(solution)/shard_map/ppermute | solution.py:252
  69.3 17.5 %all-to-all-start.2 = ((bf16[16,16,320]{2,1,0:T(8,128)(2,1)}), bf16[16,16,320]{2,1,0:T(8,128)(2,1)S(1)}, u32[]{:S(2)}, u32[]{:S(2)}) async-start(bf16[16,16,320]{2,1,0:T(8,128)(2,1)} %get-tuple-element.34), calls=%async_computation.2 | async-start | bytes 393216 | tf_op jit(solution)/shard_map/all_to_all | solution.py:229
  93.8 2.3 %copy-start.11 = (bf16[1024,256]{1,0:T(8,128)(2,1)S(1)}, bf16[1024,256]{1,0:T(8,128)(2,1)}, u32[]{:S(2)}) copy-start(bf16[1024,256]{1,0:T(8,128)(2,1)} %get-tuple-element.37.refs_0_) | copy-start | bytes 1572868
  93.8 0.8 copy-start.5
  93.8 1.0 copy-start.6
  93.8 1.1 copy-start.4
  93.8 1.4 copy-start.2
  95.2 0.9 copy-start.1
  96.0 24.3 %collective-permute-start.14 = (bf16[320,1024]{1,0:T(8,128)(2,1)}, bf16[320,1024]{1,0:T(8,128)(2,1)S(1)}, u32[]{:S(2)}, u32[]{:S(2)}) collective-permute-start(bf16[320,1024]{1,0:T(8,128)(2,1)} %get-tuple-element.41.refs_1_), channel_id=1, source_target_pairs={{0,64},{16,80},{32,96},{48,112},{64,0},{80,16},{96,32},{112,48},{1... | collective-permute-start | bytes 1966088 | tf_op jit(solution)/shard_map/ppermute | solution.py:252
  96.1 24.3 %collective-permute-start.12 = (bf16[1024,256]{1,0:T(8,128)(2,1)S(1)}, bf16[1024,256]{1,0:T(8,128)(2,1)S(1)}, u32[]{:S(2)}, u32[]{:S(2)}) collective-permute-start(bf16[1024,256]{1,0:T(8,128)(2,1)S(1)} %copy-done.11), channel_id=1, source_target_pairs={{0,16},{16,32},{32,48},{48,0},{64,80},{80,96},{96,112},{112,64},{1... | collective-permute-start | bytes 1572872 | tf_op jit(solution)/shard_map/ppermute | solution.py:252
  96.1 24.3 %collective-permute-start.13 = (bf16[1024,256]{1,0:T(8,128)(2,1)}, bf16[1024,256]{1,0:T(8,128)(2,1)S(1)}, u32[]{:S(2)}, u32[]{:S(2)}) collective-permute-start(bf16[1024,256]{1,0:T(8,128)(2,1)} %get-tuple-element.40.refs_1_), channel_id=1, source_target_pairs={{0,48},{16,0},{32,16},{48,32},{64,112},{80,64},{96,80},{112,96},{1... | collective-permute-start | bytes 1572872 | tf_op jit(solution)/shard_map/ppermute | solution.py:252
  98.7 19.0 %all-to-all-start.3 = ((bf16[16,64,128]{2,1,0:T(8,128)(2,1)}), bf16[16,64,128]{2,1,0:T(8,128)(2,1)S(1)}, u32[]{:S(2)}, u32[]{:S(2)}) async-start(bf16[16,64,128]{2,1,0:T(8,128)(2,1)} %get-tuple-element.39), calls=%async_computation.3 | async-start | bytes 524288 | tf_op jit(solution)/shard_map/all_to_all | solution.py:229
  117.8 0.7 copy-start.13
  120.4 0.8 copy-start.7
  120.4 1.0 copy-start.8
  120.4 1.2 copy-start.3
  121.6 17.2 %collective-permute-start.17 = (bf16[320,1024]{1,0:T(8,128)(2,1)}, bf16[320,1024]{1,0:T(8,128)(2,1)S(1)}, u32[]{:S(2)}, u32[]{:S(2)}) collective-permute-start(bf16[320,1024]{1,0:T(8,128)(2,1)} %get-tuple-element.51.refs_2_), channel_id=1, source_target_pairs={{0,48},{16,0},{32,16},{48,32},{64,112},{80,64},{96,80},{112,96},{1... | collective-permute-start | bytes 1966088 | tf_op jit(solution)/shard_map/ppermute | solution.py:252
  123.9 15.1 %collective-permute-start.16 = (bf16[320,1024]{1,0:T(8,128)(2,1)}, bf16[320,1024]{1,0:T(8,128)(2,1)S(1)}, u32[]{:S(2)}, u32[]{:S(2)}) collective-permute-start(bf16[320,1024]{1,0:T(8,128)(2,1)} %get-tuple-element.50.refs_0_), channel_id=1, source_target_pairs={{0,64},{16,80},{32,96},{48,112},{64,0},{80,16},{96,32},{112,48},{1... | collective-permute-start | bytes 1966088 | tf_op jit(solution)/shard_map/ppermute | solution.py:252
  123.9 16.3 %collective-permute-start.15 = (bf16[320,1024]{1,0:T(8,128)(2,1)}, bf16[320,1024]{1,0:T(8,128)(2,1)S(1)}, u32[]{:S(2)}, u32[]{:S(2)}) collective-permute-start(bf16[320,1024]{1,0:T(8,128)(2,1)} %get-tuple-element.50.refs_0_), channel_id=1, source_target_pairs={{0,16},{16,32},{32,48},{48,0},{64,80},{80,96},{96,112},{112,64},{1... | collective-permute-start | bytes 1966088 | tf_op jit(solution)/shard_map/ppermute | solution.py:252
  123.9 2.2 %copy-start.22 = (bf16[16,256]{1,0:T(8,128)(2,1)S(1)}, bf16[16,256]{1,0:T(8,128)(2,1)}, u32[]{:S(2)}) copy-start(bf16[16,256]{1,0:T(8,128)(2,1)} %get-tuple-element.46) | copy-start | bytes 24580
  130.2 14.4 %all-to-all-start.4 = ((bf16[16,16,512]{2,1,0:T(8,128)(2,1)}), bf16[16,16,512]{2,1,0:T(8,128)(2,1)S(1)}, u32[]{:S(2)}, u32[]{:S(2)}) async-start(bf16[16,16,512]{2,1,0:T(8,128)(2,1)} %bitcast.11), calls=%async_computation.4 | async-start | bytes 524288 | tf_op jit(solution)/shard_map/all_to_all | solution.py:229
  138.7 1.5 copy-start.19
  139.0 1.2 copy-start.20
  140.2 0.9 copy-start.21
  144.7 0.7 copy-start.14
  (3 other events, 2.0 us)

commit v4 on v3

--- a/solution.py
+++ b/solution.py
@@ -19,19 +19,39 @@
     query_width = QH * HD // groups
     kv_width = KVH * HD // groups
     rows = qkv_ref.shape[0]
+    quarter = rows // 4
     for g in range(groups):
         keys_at = QH * HD + g * kv_width
         values_at = QH * HD + KVH * HD + g * kv_width
-        packed_ref[g, :, :query_width] = qkv_ref[:, g * query_width : (g + 1) * query_width]
-        packed_ref[g, :, query_width : query_width + HD] = jnp.concatenate(
+        at = slice(g * query_width, (g + 1) * query_width)
+        packed_ref[g, :rows, :] = qkv_ref[:, at]
+        packed_ref[g, rows : 2 * rows, :] = out_ref[:, at]
+        pair = jnp.concatenate(
             [
                 qkv_ref[:, keys_at : keys_at + kv_width],
                 qkv_ref[:, values_at : values_at + kv_width],
-                jnp.zeros((rows, HD - 2 * kv_width), qkv_ref.dtype),
             ],
             1,
         )
-        packed_ref[g, :, query_width + HD :] = out_ref[:, g * query_width : (g + 1) * query_width]
+        packed_ref[g, 2 * rows :, :] = jnp.concatenate(
+            [pair[i * quarter : (i + 1) * quarter] for i in range(4)], 1
+        )
+
+
+def unpacked(packed_ref):
+    groups, rows, query_width = packed_ref.shape
+    rows = rows * 4 // 9
+    pair_width = query_width // 4
+    queries = jnp.concatenate([packed_ref[t, :rows, :] for t in range(groups)], 0)
+    pairs = jnp.concatenate(
+        [
+            packed_ref[t, 2 * rows :, i * pair_width : (i + 1) * pair_width]
+            for t in range(groups)
+            for i in range(4)
+        ],
+        0,
+    )
+    return queries, pairs
 
 
 def norm_kernel(states_ref, gain_ref, own_ref, send_ref):
@@ -39,7 +59,7 @@
     normed = (
         states
         * lax.rsqrt(jnp.mean(states * states, -1, keepdims=True) + EPS)
-        * gain_ref[...].astype(jnp.float32)
+        * gain_ref[...].reshape(1, -1).astype(jnp.float32)
     ).astype(jnp.bfloat16)
     replica = lax.axis_index("dp")
     column, y_at = replica // 4, replica % 4
@@ -52,19 +72,27 @@
         send_ref[slot] = jnp.where(column == 0, second, first)
 
 
-def terms_kernel(group_width, own, got, low, high, far, packed_ref, terms_ref, out_ref):
-    weights = packed_ref[:, :group_width]
+def terms_kernel(own, got, low, high, far, packed_ref, terms_ref, out_ref):
     states = jnp.concatenate(
         [own[0], got[0], low[0], low[1], high[0], high[1], far[0], far[1]], 0
     )
-    terms = jnp.dot(states, weights, preferred_element_type=jnp.float32)
+    terms = jnp.concatenate(
+        [
+            jnp.dot(states, weights, preferred_element_type=jnp.float32)
+            for weights in unpacked(packed_ref)
+        ],
+        1,
+    ).astype(terms_ref.dtype)
     slots = own.shape[1]
     replica = lax.axis_index("dp")
     order = [(c, y) for y in (0, -1, 1, 2) for c in (0, 1)]
     for i, (c, y) in enumerate(order):
         source = ((replica // 4) ^ c) * 4 + ((replica + y) & 3)
         terms_ref[source] = terms[i * slots : (i + 1) * slots]
-    out_ref[...] = packed_ref[:, group_width + 64 :]
+    groups, rows, _ = packed_ref.shape
+    rows = rows * 4 // 9
+    for t in range(groups):
+        out_ref[t * rows : (t + 1) * rows] = packed_ref[t, rows : 2 * rows, :]
 
 
 def hold_kernel(*refs):
@@ -79,26 +107,29 @@
         in_specs=[anywhere] * len(values),
         out_specs=(anywhere,) * len(values),
         input_output_aliases={i: i for i in range(len(values))},
+        compiler_params=pltpu.CompilerParams(vmem_limit_bytes=1 << 20),
         name="hold",
     )(*values)
 
 
-def sum_kernel(groups, terms_ref, bias_ref, *refs):
-    projected_ref = refs[4]
-    total = jnp.sum(terms_ref[...], 0) + bias_ref[...].astype(jnp.float32)
+def sum_kernel(groups, terms_ref, bias_ref, projected_ref):
+    total = jnp.sum(terms_ref[...].astype(jnp.float32), 0) + bias_ref[...].astype(jnp.float32)
     total = total.astype(projected_ref.dtype)
     for g in range(groups):
         projected_ref[g] = total
 
 
 def turn_kernel(packed_ref, turned_ref):
-    width = turned_ref.shape[0]
-    turned_ref[...] = packed_ref[:, : width + 64].T[:width]
+    queries, pairs = unpacked(packed_ref)
+    width = queries.shape[1]
+    turned_ref[:width] = queries.T
+    turned_ref[width:] = pairs.T
 
 
 def place_kernel(axis, where, *refs):
-    parts, whole_ref, sems = refs[: len(where)], refs[-2], refs[-1]
+    parts = refs[: len(where)]
     replica = lax.axis_index("dp")
+    whole_ref, sems = refs[-2:]
     copies = []
     for i, (part, (c, y)) in enumerate(zip(parts, where)):
         size = part.shape[axis]
@@ -124,6 +155,7 @@
         out_specs=anywhere,
         scratch_shapes=[pltpu.SemaphoreType.DMA((count,))],
         input_output_aliases={count: 0} if continued else {},
+        compiler_params=pltpu.CompilerParams(vmem_limit_bytes=4 << 20),
         name="place",
     )(*parts, *((whole,) if continued else ()))
 
@@ -197,23 +229,29 @@
             own = jnp.where(kv_of == k, mixed[:, k * HD : (k + 1) * HD], own)
         total_upper = total.astype(jnp.bfloat16).astype(jnp.float32)
         total_lower = total - total_upper
+        part = lane // 16 % 4
         facts = jnp.where(
-            lane < 64,
-            jnp.where(lane < 32, upper, lower),
-            jnp.where(lane < 96, total_upper, total_lower),
-        )
+            part < 2,
+            jnp.where(part == 0, upper, lower),
+            jnp.where(part == 2, total_upper, total_lower),
+        )
+        facts = jnp.where(lane < 64, facts, pltpu.roll(facts, per_row - 2, 0))
         for t in range(groups):
             message_s[t, pl.ds(r, 4, stride=rows), :] = own[t * 4 : (t + 1) * 4]
-            message_s[t, pl.ds(4 * rows + r, 4, stride=rows), :] = facts[t * 4 : (t + 1) * 4]
+            message_s[t, pl.ds(4 * rows + r, 2, stride=rows), :] = facts[t * 4 : t * 4 + 2]
     message_ref[...] = message_s[...].astype(message_ref.dtype)
 
 
 def merge_kernel(message_ref, attended_ref):
     message = message_ref[...].astype(jnp.float32)
-    half = message.shape[1] // 2
+    half = message.shape[1] * 2 // 3
     facts = message[:, half:]
-    highest = facts[:, :, 0:1] + facts[:, :, 32:33]
-    totals = facts[:, :, 64:65] + facts[:, :, 96:97]
+
+    def fact(i):
+        at = (16 * i, 64 + 16 * i)
+        return jnp.concatenate([facts[:, :, lane : lane + 1] for lane in at], 1)
+
+    highest, totals = fact(0) + fact(1), fact(2) + fact(3)
     rescale = jnp.exp(highest - jnp.max(highest, 0, keepdims=True))
     total = jnp.sum(totals * rescale, 0)
     mixture = jnp.sum(message[:, :half] * rescale, 0)
@@ -251,33 +289,35 @@
     def send(value, pairs):
         return lax.ppermute(value, "dp", pairs)
 
-    width = 2 * query_width + HD
     group_width = query_width + 2 * kv_width
     own_states, other_states = pl.pallas_call(
         norm_kernel,
         out_shape=(jax.ShapeDtypeStruct((replicas // 2, slots, share), jnp.bfloat16),) * 2,
+        compiler_params=pltpu.CompilerParams(vmem_limit_bytes=6 << 20),
         name="norm",
-    )(hidden, norm_gain.reshape(1, feature_width))
+    )(hidden, norm_gain)
     cross_states = send(other_states, across)
     packed = pl.pallas_call(
         lambda *refs: pack_kernel(groups, *refs),
-        out_shape=jax.ShapeDtypeStruct((groups, fresh_qkv.shape[0], width), fresh_qkv.dtype),
+        out_shape=jax.ShapeDtypeStruct((groups, fresh_qkv.shape[0] * 9 // 4, query_width), fresh_qkv.dtype),
         in_specs=[anywhere] + [vmem] * 2,
+        compiler_params=pltpu.CompilerParams(vmem_limit_bytes=6 << 20),
         name="pack",
     )(own_states, fresh_qkv, fresh_out)
     packed, cross_states = hold(packed, cross_states)
-    packed = exchange(packed, "tensor").reshape(share, width)
+    packed = exchange(packed, "tensor")
 
     low_states, far_states, high_states = (
         send(jnp.stack([own_states[k], cross_states[k]]), pairs)
         for k, pairs in ((1, ahead), (2, beyond), (3, behind))
     )
     terms, own_out = pl.pallas_call(
-        lambda *refs: terms_kernel(group_width, *refs),
+        terms_kernel,
         out_shape=(
-            jax.ShapeDtypeStruct((replicas, slots, group_width), jnp.float32),
+            jax.ShapeDtypeStruct((replicas, slots, group_width), jnp.bfloat16),
             jax.ShapeDtypeStruct((share, query_width), packed.dtype),
         ),
+        compiler_params=pltpu.CompilerParams(vmem_limit_bytes=8 << 20),
         name="terms",
     )(own_states, cross_states, low_states, high_states, far_states, packed)
     terms = exchange(terms, "dp")
@@ -286,20 +326,22 @@
     own_qkv = pl.pallas_call(
         turn_kernel,
         out_shape=jax.ShapeDtypeStruct((group_width, share), packed.dtype),
+        compiler_params=pltpu.CompilerParams(vmem_limit_bytes=4 << 20),
         name="turn",
     )(packed)
-    moved = (out_across, out_low, out_high, own_qkv)
-    projected, out_across, out_low, out_high, own_qkv = pl.pallas_call(
-        lambda terms_ref, bias_ref, *refs: sum_kernel(groups, terms_ref, bias_ref, *refs),
+    moved = (out_across, own_qkv)
+    projected, out_across, own_qkv = pl.pallas_call(
+        lambda terms_ref, bias_ref, *refs: sum_kernel(groups, terms_ref, bias_ref, refs[4]),
         out_shape=(
             jax.ShapeDtypeStruct((groups, slots, group_width), jnp.bfloat16),
             *(jax.ShapeDtypeStruct(v.shape, v.dtype) for v in moved),
         ),
         in_specs=[vmem] * 2 + [anywhere] * 4,
-        out_specs=(vmem,) + (anywhere,) * 4,
-        input_output_aliases={2 + i: 1 + i for i in range(4)},
+        out_specs=(vmem,) + (anywhere,) * 2,
+        input_output_aliases={2: 1, 3: 2},
+        compiler_params=pltpu.CompilerParams(vmem_limit_bytes=3 << 20),
         name="sum",
-    )(terms, qkv_bias.reshape(1, group_width), *moved)
+    )(terms, qkv_bias.reshape(1, group_width), *moved, out_low, out_high)
     gathered = exchange(projected, "tensor")
 
     out_cross_low, out_cross_high = send(out_across, ahead), send(out_across, behind)
@@ -327,12 +369,13 @@
 
     message = pl.pallas_call(
         lambda *refs: attend_kernel(score_scale, *refs),
-        out_shape=jax.ShapeDtypeStruct((groups, 2 * slots * own_heads, HD), jnp.bfloat16),
+        out_shape=jax.ShapeDtypeStruct((groups, 3 * slots, HD), jnp.bfloat16),
         in_specs=[smem] + [vmem] * 5,
         scratch_shapes=[
             pltpu.VMEM((slots * QH, HD), jnp.float32),
-            pltpu.VMEM((groups, 2 * slots * own_heads, HD), jnp.float32),
+            pltpu.VMEM((groups, 3 * slots, HD), jnp.float32),
         ],
+        compiler_params=pltpu.CompilerParams(vmem_limit_bytes=14 << 20),
         name="attend",
     )(lengths, cosine, sine, gathered, key_cache, value_cache)
     message, out_cross_low, out_cross_high, qkv_low, qkv_high, qkv_across, grouped_out = hold(
@@ -354,6 +397,7 @@
     attended = pl.pallas_call(
         merge_kernel,
         out_shape=jax.ShapeDtypeStruct((slots, own_heads * HD), jnp.bfloat16),
+        compiler_params=pltpu.CompilerParams(vmem_limit_bytes=3 << 20),
         name="merge",
     )(message)
     attended, out_far, out_cross_far, qkv_cross_high, qkv_low, grouped_out, grouped_qkv = hold(
@@ -390,6 +434,7 @@
         total_kernel,
         out_shape=jax.ShapeDtypeStruct((slots, feature_width // groups), jnp.bfloat16),
         in_specs=[vmem, anywhere],
+        compiler_params=pltpu.CompilerParams(vmem_limit_bytes=56 << 20),
         name="total",
     )(term_sums, grouped_qkv)
     attn_output = attn_output.reshape(step_count, row_count, -1)

time: 149 us -> 133 us (0.89)
  Pallas kernels: 37.5 us -> 23.2 us
  waiting for transfers between devices: 37.9 us -> 40.3 us
  local copies, waits for them, and re-layouts: 13.5 us -> 11.5 us
    pallas_call x7, Pallas kernels: 16.6 us -> 13.2 us  [place(): pl.pallas_call(lambda *refs: place_kernel(axis, where, *refs), out_shape=...]
    pallas_call x1, Pallas kernels: 2.41 us -> 0.3 us  [on_device(): pl.pallas_call(turn_kernel, out_shape=jax.ShapeDtypeStruct((group_width,...]
    pallas_call x1, Pallas kernels: 6.3 us -> 4.49 us  [on_device(): pl.pallas_call(lambda *refs: attend_kernel(score_scale, *refs), out_shape...]
    pallas_call x1, Pallas kernels: 2.67 us -> 0.98 us  [on_device(): pl.pallas_call(terms_kernel, out_shape=(jax.ShapeDtypeStruct((replicas, s...]
    pallas_call x1, Pallas kernels: 1.89 us -> 0.24 us  [on_device(): pl.pallas_call(norm_kernel, out_shape=(jax.ShapeDtypeStruct((replicas //...]
    pallas_call x1, Pallas kernels: 1.88 us -> 0.36 us  [on_device(): pl.pallas_call(merge_kernel, out_shape=jax.ShapeDtypeStruct((slots, own_h...]
    unnamed x56 -> x30, local copies, waits for them, and re-layouts: 9.89 us -> 10.6 us
  transfers between devices with their start and end apart: 23 -> 23, of which waited for: 10 -> 10; matrix products, arithmetic and copies ran while one was open for 4% -> 3% of each run, Pallas kernels for 20% -> 15%
where the time goes in v4:
time: 133 us; the launch traced here: 132 us
  starting transfers between devices  52.3 us (39%)
  waiting for transfers between devices  40.3 us (30%)
  Pallas kernels  23.2 us (17%)
  local copies, waits for them, and re-layouts  11.5 us (9%)
  matrix products  3.38 us (3%)
    all_to_all x5, waiting for transfers between devices, exchange(): return lax.all_to_all(blocks, axis, split_axis=0, concat_axis=0, tiled=True)  33.8 us
    all_to_all x5, starting transfers between devices, exchange(): return lax.all_to_all(blocks, axis, split_axis=0, concat_axis=0, tiled=True)  33.6 us
    ppermute x18, starting transfers between devices, send(): return lax.ppermute(value, 'dp', pairs)  18.6 us
    pallas_call x7, Pallas kernels, place(): pl.pallas_call(lambda *refs: place_kernel(axis, where, *refs), out_shape=...  13.2 us
    unnamed x30, local copies, waits for them, and re-layouts  10.6 us
    ppermute x18, waiting for transfers between devices, send(): return lax.ppermute(value, 'dp', pairs)  6.45 us
    pallas_call x1, Pallas kernels, on_device(): pl.pallas_call(lambda *refs: attend_kernel(score_scale, *refs), out_shape...  4.49 us
    dot_general x1, matrix products, on_device(): jnp.dot(attended, grouped_out.T, preferred_element_type=jnp.float32)  3.38 us
  transfers between devices with their start and end apart: 23, of which 10 were waited for; matrix products, arithmetic and copies ran while one was open for 3% of the time, Pallas kernels for 15%

profile of v4, /device:TPU:1, one launch (start us, length us, event | category | flops | bytes accessed | tf_op | source)
XLA Modules:
  0.0 131.8 jit_solution(4513674167529929922)
XLA Ops:
  0.6 0.9 copy-done.10
  1.6 0.7 copy-done.11
  2.5 2.1 %collective-permute-start = (bf16[4,16,1024]{2,1,0:T(8,128)(2,1)S(1)}, bf16[4,16,1024]{2,1,0:T(8,128)(2,1)S(1)}, u32[]{:S(2)}, u32[]{:S(2)}) collective-permute-start(bf16[4,16,1024]{2,1,0:T(8,128)(2,1)S(1)} %get-tuple-element.27), channel_id=1, source_target_pairs={{0,64},{16,80},{32,96},{48,112},{64,0},{80,16},{96,32},{112,48},{1... | collective-permute-start | bytes 393224 | tf_op jit(solution)/shard_map/ppermute | solution.py:290
  4.7 1.1 copy-done.6
  5.8 1.0 copy-done.7
  6.8 1.3 pack.1.refs_0_
  8.1 9.2 %all-to-all-start = ((bf16[16,144,256]{2,1,0:T(8,128)(2,1)}), bf16[16,144,256]{2,1,0:T(8,128)(2,1)S(1)}, u32[]{:S(2)}, u32[]{:S(2)}) async-start(bf16[16,144,256]{2,1,0:T(8,128)(2,1)} %get-tuple-element.29), calls=%async_computation | async-start | bytes 2359296 | tf_op jit(solution)/shard_map/all_to_all | solution.py:267
  17.3 1.4 %collective-permute-start.1 = (bf16[2,16,1024]{2,1,0:T(8,128)(2,1)S(1)}, bf16[2,16,1024]{2,1,0:T(8,128)(2,1)S(1)}, u32[]{:S(2)}, u32[]{:S(2)}) collective-permute-start(bf16[2,16,1024]{2,1,0:T(8,128)(2,1)S(1)} %pad_maximum_fusion), channel_id=1, source_target_pairs={{0,16},{16,32},{32,48},{48,0},{64,80},{80,96},{96,112},{112,64},{1... | collective-permute-start | bytes 196616 | tf_op jit(solution)/shard_map/ppermute | solution.py:290
  18.7 1.5 %collective-permute-start.2 = (bf16[2,16,1024]{2,1,0:T(8,128)(2,1)S(1)}, bf16[2,16,1024]{2,1,0:T(8,128)(2,1)S(1)}, u32[]{:S(2)}, u32[]{:S(2)}) collective-permute-start(bf16[2,16,1024]{2,1,0:T(8,128)(2,1)S(1)} %pad_maximum_fusion.1), channel_id=1, source_target_pairs={{0,48},{16,0},{32,16},{48,32},{64,112},{80,64},{96,80},{112,96},{1... | collective-permute-start | bytes 196616 | tf_op jit(solution)/shard_map/ppermute | solution.py:290
  20.2 1.7 %collective-permute-start.3 = (bf16[2,16,1024]{2,1,0:T(8,128)(2,1)S(1)}, bf16[2,16,1024]{2,1,0:T(8,128)(2,1)S(1)}, u32[]{:S(2)}, u32[]{:S(2)}) collective-permute-start(bf16[2,16,1024]{2,1,0:T(8,128)(2,1)S(1)} %pad_maximum_fusion.2), channel_id=1, source_target_pairs={{0,32},{16,48},{32,0},{48,16},{64,96},{80,112},{96,64},{112,80},{1... | collective-permute-start | bytes 196616 | tf_op jit(solution)/shard_map/ppermute | solution.py:290
  22.0 0.4 collective-permute-done.1.low
  22.4 2.9 %collective-permute-done.3.far = bf16[2,16,1024]{2,1,0:T(8,128)(2,1)S(1)} collective-permute-done((bf16[2,16,1024]{2,1,0:T(8,128)(2,1)S(1)}, bf16[2,16,1024]{2,1,0:T(8,128)(2,1)S(1)}, u32[]{:S(2)}, u32[]{:S(2)}) %collective-permute-start.3) | collective-permute-done | bytes 65568 | tf_op jit(solution)/shard_map/ppermute | solution.py:290
  25.2 10.7 %all-to-all-done.packed_ref = bf16[16,144,256]{2,1,0:T(8,128)(2,1)S(1)} async-done(((bf16[16,144,256]{2,1,0:T(8,128)(2,1)}), bf16[16,144,256]{2,1,0:T(8,128)(2,1)S(1)}, u32[]{:S(2)}, u32[]{:S(2)}) %all-to-all-start) | async-done | bytes 1179680 | tf_op jit(solution)/shard_map/all_to_all | solution.py:267
  35.9 1.0 terms.1
  36.9 2.7 %collective-permute-start.6 = (bf16[1024,256]{1,0:T(8,128)(2,1)S(1)}, bf16[1024,256]{1,0:T(8,128)(2,1)S(1)}, u32[]{:S(2)}, u32[]{:S(2)}) collective-permute-start(bf16[1024,256]{1,0:T(8,128)(2,1)S(1)} %get-tuple-element.31.refs_0_), channel_id=1, source_target_pairs={{0,48},{16,0},{32,16},{48,32},{64,112},{80,64},{96,80},{112,96},{1... | collective-permute-start | bytes 1572872 | tf_op jit(solution)/shard_map/ppermute | solution.py:290
  40.0 4.8 %all-to-all-start.1 = ((bf16[8,16,320]{2,1,0:T(8,128)(2,1)}), bf16[8,16,320]{2,1,0:T(8,128)(2,1)S(1)}, u32[]{:S(2)}, u32[]{:S(2)}) async-start(bf16[8,16,320]{2,1,0:T(8,128)(2,1)} %get-tuple-element.30), calls=%async_computation.1 | async-start | bytes 196608 | tf_op jit(solution)/shard_map/all_to_all | solution.py:267
  45.1 9.4 %all-to-all-done.1.terms_ref = bf16[8,16,320]{2,1,0:T(8,128)(2,1)S(1)} async-done(((bf16[8,16,320]{2,1,0:T(8,128)(2,1)}), bf16[8,16,320]{2,1,0:T(8,128)(2,1)S(1)}, u32[]{:S(2)}, u32[]{:S(2)}) %all-to-all-start.1) | async-done | bytes 81952 | tf_op jit(solution)/shard_map/all_to_all | solution.py:267
  54.5 0.8 sum.1
  55.3 0.9 collective-permute-start.8
  56.2 0.5 collective-permute-start.7
  57.1 2.2 %collective-permute-start.10 = (bf16[320,1024]{1,0:T(8,128)(2,1)S(1)}, bf16[320,1024]{1,0:T(8,128)(2,1)S(1)}, u32[]{:S(2)}, u32[]{:S(2)}) collective-permute-start(bf16[320,1024]{1,0:T(8,128)(2,1)S(1)} %get-tuple-element.34.refs_0_), channel_id=1, source_target_pairs={{0,48},{16,0},{32,16},{48,32},{64,112},{80,64},{96,80},{112,96},{1... | collective-permute-start | bytes 1966088 | tf_op jit(solution)/shard_map/ppermute | solution.py:290
  59.3 7.1 %all-to-all-start.2 = ((bf16[16,16,320]{2,1,0:T(8,128)(2,1)}), bf16[16,16,320]{2,1,0:T(8,128)(2,1)S(1)}, u32[]{:S(2)}, u32[]{:S(2)}) async-start(bf16[16,16,320]{2,1,0:T(8,128)(2,1)} %get-tuple-element.32), calls=%async_computation.2 | async-start | bytes 393216 | tf_op jit(solution)/shard_map/all_to_all | solution.py:267
  66.6 1.0 copy-done.9
  67.7 2.0 %place.7.refs_2_ = bf16[8192,256]{1,0:T(8,128)(2,1)} custom-call(bf16[1024,256]{1,0:T(8,128)(2,1)S(1)} %copy-done.9, bf16[1024,256]{1,0:T(8,128)(2,1)} %get-tuple-element.33.refs_1_), custom_call_target="tpu_custom_call" | custom-call | tf_op jit(solution)/shard_map/place/pallas_call | solution.py:151
  69.7 2.0 %place.8.refs_6_ = bf16[8192,256]{1,0:T(8,128)(2,1)} custom-call(bf16[1024,256]{1,0:T(8,128)(2,1)} %collective-permute-done.5.refs_2_.refs_0_, bf16[1024,256]{1,0:T(8,128)(2,1)S(1)} %copy-done.3, bf16[8192,256]{1,0:T(8,128)(2,1)} %place.7.refs_2_), custom_call_target="tpu_custom_call", output_to_operand_aliasing={{}: (2, {})} | custom-call | tf_op jit(solution)/shard_map/place/pallas_call | solution.py:151
  71.7 5.0 %all-to-all-done.2.refs_3_ = bf16[16,16,320]{2,1,0:T(8,128)(2,1)S(1)} async-done(((bf16[16,16,320]{2,1,0:T(8,128)(2,1)}), bf16[16,16,320]{2,1,0:T(8,128)(2,1)S(1)}, u32[]{:S(2)}, u32[]{:S(2)}) %all-to-all-start.2) | async-done | bytes 163872 | tf_op jit(solution)/shard_map/all_to_all | solution.py:267
  76.8 1.6 %copy-done.4 = bf16[8,256,512]{2,1,0:T(8,128)(2,1)S(1)} copy-done((bf16[8,256,512]{2,1,0:T(8,128)(2,1)S(1)}, bf16[8,256,512]{2,1,0:T(8,128)(2,1)}, u32[]{:S(2)}) %copy-start.4) | copy-done | bytes 2097176
  78.4 1.6 %copy-done.5 = bf16[8,256,512]{2,1,0:T(8,128)(2,1)S(1)} copy-done((bf16[8,256,512]{2,1,0:T(8,128)(2,1)S(1)}, bf16[8,256,512]{2,1,0:T(8,128)(2,1)}, u32[]{:S(2)}) %copy-start.5) | copy-done | bytes 2097176
  80.0 4.5 %attend.1.refs_0_ = bf16[16,48,128]{2,1,0:T(8,128)(2,1)} custom-call(s32[8]{0:T(128)S(1)} %copy-done.12, f32[16,128]{1,0:T(8,128)S(1)} %get-tuple-element.58.refs_1_, f32[16,128]{1,0:T(8,128)S(1)} %get-tuple-element.59.refs_2_, bf16[16,16,320]{2,1,0:T(8,128)(2,1)S(1)} %all-to-all-done.2.refs_3_, bf16[8,256,512]{2,1,0:T(8,128)(2,1)S(1)} %copy-done.4, ...), custom_call_target="tpu_custom_call" | custom-call | tf_op jit(solution)/shard_map/attend/pallas_call | solution.py:370
  84.5 0.8 copy-done
  85.4 2.6 %collective-permute-start.13 = (bf16[1024,256]{1,0:T(8,128)(2,1)S(1)}, bf16[1024,256]{1,0:T(8,128)(2,1)}, u32[]{:S(2)}, u32[]{:S(2)}) collective-permute-start(bf16[1024,256]{1,0:T(8,128)(2,1)S(1)} %get-tuple-element.36.refs_1_), channel_id=1, source_target_pairs={{0,48},{16,0},{32,16},{48,32},{64,112},{80,64},{96,80},{112,96},{1... | collective-permute-start | bytes 1572872 | tf_op jit(solution)/shard_map/ppermute | solution.py:290
  88.0 7.0 %all-to-all-start.3 = ((bf16[16,48,128]{2,1,0:T(8,128)(2,1)}), bf16[16,48,128]{2,1,0:T(8,128)(2,1)S(1)}, u32[]{:S(2)}, u32[]{:S(2)}) async-start(bf16[16,48,128]{2,1,0:T(8,128)(2,1)} %get-tuple-element.35), calls=%async_computation.3 | async-start | bytes 393216 | tf_op jit(solution)/shard_map/all_to_all | solution.py:267
  95.0 1.1 copy-done.1
  96.1 1.1 place.10.refs_6_
  97.2 2.0 %place.9.refs_5_ = bf16[8192,256]{1,0:T(8,128)(2,1)} custom-call(bf16[1024,256]{1,0:T(8,128)(2,1)} %get-tuple-element.39.refs_0_, bf16[1024,256]{1,0:T(8,128)(2,1)S(1)} %get-tuple-element.36.refs_1_, bf16[8192,256]{1,0:T(8,128)(2,1)} %get-tuple-element.40.refs_2_), custom_call_target="tpu_custom_call", output_to_operand_aliasing={{}: (2, {})} | custom-call | tf_op jit(solution)/shard_map/place/pallas_call | solution.py:151
  99.2 7.1 %all-to-all-done.3.message_ref = bf16[16,48,128]{2,1,0:T(8,128)(2,1)S(1)} async-done(((bf16[16,48,128]{2,1,0:T(8,128)(2,1)}), bf16[16,48,128]{2,1,0:T(8,128)(2,1)S(1)}, u32[]{:S(2)}, u32[]{:S(2)}) %all-to-all-start.3) | async-done | bytes 196640 | tf_op jit(solution)/shard_map/all_to_all | solution.py:267
  106.7 2.2 %collective-permute-start.17 = (bf16[320,1024]{1,0:T(8,128)(2,1)S(1)}, bf16[320,1024]{1,0:T(8,128)(2,1)S(1)}, u32[]{:S(2)}, u32[]{:S(2)}) collective-permute-start(bf16[320,1024]{1,0:T(8,128)(2,1)S(1)} %get-tuple-element.47.refs_2_), channel_id=1, source_target_pairs={{0,48},{16,0},{32,16},{48,32},{64,112},{80,64},{96,80},{112,96},{1... | collective-permute-start | bytes 1966088 | tf_op jit(solution)/shard_map/ppermute | solution.py:290
  108.9 2.2 %place.11 = bf16[8192,256]{1,0:T(8,128)(2,1)} custom-call(bf16[1024,256]{1,0:T(8,128)(2,1)} %get-tuple-element.43.refs_0_, bf16[1024,256]{1,0:T(8,128)(2,1)} %get-tuple-element.44.refs_1_, bf16[8192,256]{1,0:T(8,128)(2,1)} %get-tuple-element.45.refs_2_), custom_call_target="tpu_custom_call", output_to_operand_aliasing={{}: (2, {})} | custom-call | tf_op jit(solution)/shard_map/place/pallas_call | solution.py:151
  111.1 3.4 %convolution_convert_fusion = bf16[16,8192]{1,0:T(8,128)(2,1)S(1)} fusion(bf16[16,256]{1,0:T(8,128)(2,1)S(1)} %get-tuple-element.42, bf16[8192,256]{1,0:T(8,128)(2,1)} %place.11), kind=kOutput, calls=%fused_computation | convolution fusion | flops 67239936 | bytes 4464640 | tf_op jit(solution)/shard_map/dot_general | solution.py:430
  114.5 0.8 copy.37
  115.2 5.6 %all-to-all-start.4 = ((bf16[16,16,512]{2,1,0:T(8,128)(2,1)}), bf16[16,16,512]{2,1,0:T(8,128)(2,1)S(1)}, u32[]{:S(2)}, u32[]{:S(2)}) async-start(bf16[16,16,512]{2,1,0:T(8,128)(2,1)} %bitcast.10), calls=%async_computation.4 | async-start | bytes 524288 | tf_op jit(solution)/shard_map/all_to_all | solution.py:267
  120.8 1.3 place.12.refs_3_
  122.2 1.9 %collective-permute-done.16.refs_1_ = bf16[320,1024]{1,0:T(8,128)(2,1)} collective-permute-done((bf16[320,1024]{1,0:T(8,128)(2,1)S(1)}, bf16[320,1024]{1,0:T(8,128)(2,1)}, u32[]{:S(2)}, u32[]{:S(2)}) %collective-permute-start.16) | collective-permute-done | bytes 655392 | tf_op jit(solution)/shard_map/ppermute | solution.py:290
  124.0 1.2 collective-permute-done.15.refs_0_
  125.2 2.6 %place.13.after_ref = bf16[320,8192]{1,0:T(8,128)(2,1)} custom-call(bf16[320,1024]{1,0:T(8,128)(2,1)} %collective-permute-done.15.refs_0_, bf16[320,1024]{1,0:T(8,128)(2,1)} %collective-permute-done.16.refs_1_, bf16[320,1024]{1,0:T(8,128)(2,1)S(1)} %collective-permute-done.17.refs_2_, bf16[320,8192]{1,0:T(8,128)(2,1)} %place.12.refs_3_), custom_call_target="tpu_custom_call", output_to_operand_aliasing={{}: (3, {})} | custom-call | tf_op jit(solution)/shard_map/place/pallas_call | solution.py:151
  127.8 1.6 %all-to-all-done.4.terms_ref = bf16[16,16,512]{2,1,0:T(8,128)(2,1)S(1)} async-done(((bf16[16,16,512]{2,1,0:T(8,128)(2,1)}), bf16[16,16,512]{2,1,0:T(8,128)(2,1)S(1)}, u32[]{:S(2)}, u32[]{:S(2)}) %all-to-all-start.4) | async-done | bytes 262176 | tf_op jit(solution)/shard_map/all_to_all | solution.py:267
  129.5 0.7 copy-done.13
  130.2 1.6 %total.1 = bf16[16,512]{1,0:T(8,128)(2,1)} custom-call(bf16[16,16,512]{2,1,0:T(8,128)(2,1)} %copy-done.13, bf16[320,8192]{1,0:T(8,128)(2,1)} %place.13.after_ref), custom_call_target="tpu_custom_call" | custom-call | tf_op jit(solution)/shard_map/total/pallas_call | solution.py:433
  (59 shorter events, 2.1 us)
Async XLA Ops:
  0.6 1.0 copy-start.10
  1.6 0.7 copy-start.11
  2.5 5.5 %collective-permute-start = (bf16[4,16,1024]{2,1,0:T(8,128)(2,1)S(1)}, bf16[4,16,1024]{2,1,0:T(8,128)(2,1)S(1)}, u32[]{:S(2)}, u32[]{:S(2)}) collective-permute-start(bf16[4,16,1024]{2,1,0:T(8,128)(2,1)S(1)} %get-tuple-element.27), channel_id=1, source_target_pairs={{0,64},{16,80},{32,96},{48,112},{64,0},{80,16},{96,32},{112,48},{1... | collective-permute-start | bytes 393224 | tf_op jit(solution)/shard_map/ppermute | solution.py:290
  4.7 1.1 copy-start.6
  5.8 1.0 copy-start.7
  6.8 38.0 %copy-start.14 = (bf16[320]{0:T(512)(128)(2,1)S(1)}, bf16[320]{0:T(512)(128)(2,1)}, u32[]{:S(2)}) copy-start(bf16[320]{0:T(512)(128)(2,1)} %param.10) | copy-start | bytes 1924
  8.1 51.1 %copy-start.12 = (s32[8]{0:T(128)S(1)}, s32[8]{0:T(128)}, u32[]{:S(2)}) copy-start(s32[8]{0:T(128)} %refs_0_.1) | copy-start | bytes 100
  8.1 27.8 %all-to-all-start = ((bf16[16,144,256]{2,1,0:T(8,128)(2,1)}), bf16[16,144,256]{2,1,0:T(8,128)(2,1)S(1)}, u32[]{:S(2)}, u32[]{:S(2)}) async-start(bf16[16,144,256]{2,1,0:T(8,128)(2,1)} %get-tuple-element.29), calls=%async_computation | async-start | bytes 2359296 | tf_op jit(solution)/shard_map/all_to_all | solution.py:267
  17.3 5.0 %collective-permute-start.1 = (bf16[2,16,1024]{2,1,0:T(8,128)(2,1)S(1)}, bf16[2,16,1024]{2,1,0:T(8,128)(2,1)S(1)}, u32[]{:S(2)}, u32[]{:S(2)}) collective-permute-start(bf16[2,16,1024]{2,1,0:T(8,128)(2,1)S(1)} %pad_maximum_fusion), channel_id=1, source_target_pairs={{0,16},{16,32},{32,48},{48,0},{64,80},{80,96},{96,112},{112,64},{1... | collective-permute-start | bytes 196616 | tf_op jit(solution)/shard_map/ppermute | solution.py:290
  18.7 3.6 %collective-permute-start.2 = (bf16[2,16,1024]{2,1,0:T(8,128)(2,1)S(1)}, bf16[2,16,1024]{2,1,0:T(8,128)(2,1)S(1)}, u32[]{:S(2)}, u32[]{:S(2)}) collective-permute-start(bf16[2,16,1024]{2,1,0:T(8,128)(2,1)S(1)} %pad_maximum_fusion.1), channel_id=1, source_target_pairs={{0,48},{16,0},{32,16},{48,32},{64,112},{80,64},{96,80},{112,96},{1... | collective-permute-start | bytes 196616 | tf_op jit(solution)/shard_map/ppermute | solution.py:290
  20.2 5.0 %collective-permute-start.3 = (bf16[2,16,1024]{2,1,0:T(8,128)(2,1)S(1)}, bf16[2,16,1024]{2,1,0:T(8,128)(2,1)S(1)}, u32[]{:S(2)}, u32[]{:S(2)}) collective-permute-start(bf16[2,16,1024]{2,1,0:T(8,128)(2,1)S(1)} %pad_maximum_fusion.2), channel_id=1, source_target_pairs={{0,32},{16,48},{32,0},{48,16},{64,96},{80,112},{96,64},{112,80},{1... | collective-permute-start | bytes 196616 | tf_op jit(solution)/shard_map/ppermute | solution.py:290
  36.9 19.8 %copy-start.8 = (bf16[1024,256]{1,0:T(8,128)(2,1)}, bf16[1024,256]{1,0:T(8,128)(2,1)S(1)}, u32[]{:S(2)}) copy-start(bf16[1024,256]{1,0:T(8,128)(2,1)S(1)} %get-tuple-element.31.refs_0_) | copy-start | bytes 1572868
  36.9 17.6 %collective-permute-start.6 = (bf16[1024,256]{1,0:T(8,128)(2,1)S(1)}, bf16[1024,256]{1,0:T(8,128)(2,1)S(1)}, u32[]{:S(2)}, u32[]{:S(2)}) collective-permute-start(bf16[1024,256]{1,0:T(8,128)(2,1)S(1)} %get-tuple-element.31.refs_0_), channel_id=1, source_target_pairs={{0,48},{16,0},{32,16},{48,32},{64,112},{80,64},{96,80},{112,96},{1... | collective-permute-start | bytes 1572872 | tf_op jit(solution)/shard_map/ppermute | solution.py:290
  39.6 14.8 %collective-permute-start.5 = (bf16[1024,256]{1,0:T(8,128)(2,1)S(1)}, bf16[1024,256]{1,0:T(8,128)(2,1)}, u32[]{:S(2)}, u32[]{:S(2)}) collective-permute-start(bf16[1024,256]{1,0:T(8,128)(2,1)S(1)} %get-tuple-element.31.refs_0_), channel_id=1, source_target_pairs={{0,16},{16,32},{32,48},{48,0},{64,80},{80,96},{96,112},{112,64},{1... | collective-permute-start | bytes 1572872 | tf_op jit(solution)/shard_map/ppermute | solution.py:290
  39.6 14.8 %collective-permute-start.4 = (bf16[1024,256]{1,0:T(8,128)(2,1)S(1)}, bf16[1024,256]{1,0:T(8,128)(2,1)}, u32[]{:S(2)}, u32[]{:S(2)}) collective-permute-start(bf16[1024,256]{1,0:T(8,128)(2,1)S(1)} %get-tuple-element.31.refs_0_), channel_id=1, source_target_pairs={{0,64},{16,80},{32,96},{48,112},{64,0},{80,16},{96,32},{112,48},{1... | collective-permute-start | bytes 1572872 | tf_op jit(solution)/shard_map/ppermute | solution.py:290
  40.0 14.5 %all-to-all-start.1 = ((bf16[8,16,320]{2,1,0:T(8,128)(2,1)}), bf16[8,16,320]{2,1,0:T(8,128)(2,1)S(1)}, u32[]{:S(2)}, u32[]{:S(2)}) async-start(bf16[8,16,320]{2,1,0:T(8,128)(2,1)} %get-tuple-element.30), calls=%async_computation.1 | async-start | bytes 196608 | tf_op jit(solution)/shard_map/all_to_all | solution.py:267
  54.5 2.3 %copy-start.2 = (bf16[1024,256]{1,0:T(8,128)(2,1)}, bf16[1024,256]{1,0:T(8,128)(2,1)S(1)}, u32[]{:S(2)}) copy-start(bf16[1024,256]{1,0:T(8,128)(2,1)S(1)} %collective-permute-done.6.refs_3_.refs_1_) | copy-start | bytes 1572868
  55.3 29.2 %collective-permute-start.8 = (bf16[1024,256]{1,0:T(8,128)(2,1)}, bf16[1024,256]{1,0:T(8,128)(2,1)S(1)}, u32[]{:S(2)}, u32[]{:S(2)}) collective-permute-start(bf16[1024,256]{1,0:T(8,128)(2,1)} %get-tuple-element.33.refs_1_), channel_id=1, source_target_pairs={{0,48},{16,0},{32,16},{48,32},{64,112},{80,64},{96,80},{112,96},{1... | collective-permute-start | bytes 1572872 | tf_op jit(solution)/shard_map/ppermute | solution.py:290
  56.2 28.3 %collective-permute-start.7 = (bf16[1024,256]{1,0:T(8,128)(2,1)}, bf16[1024,256]{1,0:T(8,128)(2,1)}, u32[]{:S(2)}, u32[]{:S(2)}) collective-permute-start(bf16[1024,256]{1,0:T(8,128)(2,1)} %get-tuple-element.33.refs_1_), channel_id=1, source_target_pairs={{0,16},{16,32},{32,48},{48,0},{64,80},{80,96},{96,112},{112,64},{1... | collective-permute-start | bytes 1572872 | tf_op jit(solution)/shard_map/ppermute | solution.py:290
  56.7 27.7 %collective-permute-start.11 = (bf16[320,1024]{1,0:T(8,128)(2,1)S(1)}, bf16[320,1024]{1,0:T(8,128)(2,1)S(1)}, u32[]{:S(2)}, u32[]{:S(2)}) collective-permute-start(bf16[320,1024]{1,0:T(8,128)(2,1)S(1)} %get-tuple-element.34.refs_0_), channel_id=1, source_target_pairs={{0,64},{16,80},{32,96},{48,112},{64,0},{80,16},{96,32},{112,48},{1... | collective-permute-start | bytes 1966088 | tf_op jit(solution)/shard_map/ppermute | solution.py:290
  57.1 27.4 %collective-permute-start.10 = (bf16[320,1024]{1,0:T(8,128)(2,1)S(1)}, bf16[320,1024]{1,0:T(8,128)(2,1)S(1)}, u32[]{:S(2)}, u32[]{:S(2)}) collective-permute-start(bf16[320,1024]{1,0:T(8,128)(2,1)S(1)} %get-tuple-element.34.refs_0_), channel_id=1, source_target_pairs={{0,48},{16,0},{32,16},{48,32},{64,112},{80,64},{96,80},{112,96},{1... | collective-permute-start | bytes 1966088 | tf_op jit(solution)/shard_map/ppermute | solution.py:290
  59.2 25.3 %collective-permute-start.9 = (bf16[320,1024]{1,0:T(8,128)(2,1)S(1)}, bf16[320,1024]{1,0:T(8,128)(2,1)S(1)}, u32[]{:S(2)}, u32[]{:S(2)}) collective-permute-start(bf16[320,1024]{1,0:T(8,128)(2,1)S(1)} %get-tuple-element.34.refs_0_), channel_id=1, source_target_pairs={{0,16},{16,32},{32,48},{48,0},{64,80},{80,96},{96,112},{112,64},{1... | collective-permute-start | bytes 1966088 | tf_op jit(solution)/shard_map/ppermute | solution.py:290
  59.3 17.5 %all-to-all-start.2 = ((bf16[16,16,320]{2,1,0:T(8,128)(2,1)}), bf16[16,16,320]{2,1,0:T(8,128)(2,1)S(1)}, u32[]{:S(2)}, u32[]{:S(2)}) async-start(bf16[16,16,320]{2,1,0:T(8,128)(2,1)} %get-tuple-element.32), calls=%async_computation.2 | async-start | bytes 393216 | tf_op jit(solution)/shard_map/all_to_all | solution.py:267
  66.4 3.3 %copy-start.3 = (bf16[1024,256]{1,0:T(8,128)(2,1)S(1)}, bf16[1024,256]{1,0:T(8,128)(2,1)}, u32[]{:S(2)}) copy-start(bf16[1024,256]{1,0:T(8,128)(2,1)} %copy-done.2) | copy-start | bytes 1572868
  66.6 1.0 copy-start.9
  76.8 1.6 %copy-start.4 = (bf16[8,256,512]{2,1,0:T(8,128)(2,1)S(1)}, bf16[8,256,512]{2,1,0:T(8,128)(2,1)}, u32[]{:S(2)}) copy-start(bf16[8,256,512]{2,1,0:T(8,128)(2,1)} %refs_4_.1) | copy-start | bytes 6291460
  78.4 1.6 %copy-start.5 = (bf16[8,256,512]{2,1,0:T(8,128)(2,1)S(1)}, bf16[8,256,512]{2,1,0:T(8,128)(2,1)}, u32[]{:S(2)}) copy-start(bf16[8,256,512]{2,1,0:T(8,128)(2,1)} %refs_5_.1) | copy-start | bytes 6291460
  84.5 0.8 copy-start
  85.3 21.3 %collective-permute-start.14 = (bf16[320,1024]{1,0:T(8,128)(2,1)S(1)}, bf16[320,1024]{1,0:T(8,128)(2,1)S(1)}, u32[]{:S(2)}, u32[]{:S(2)}) collective-permute-start(bf16[320,1024]{1,0:T(8,128)(2,1)S(1)} %get-tuple-element.37.refs_1_), channel_id=1, source_target_pairs={{0,64},{16,80},{32,96},{48,112},{64,0},{80,16},{96,32},{112,48},{1... | collective-permute-start | bytes 1966088 | tf_op jit(solution)/shard_map/ppermute | solution.py:290
  85.4 21.3 %collective-permute-start.12 = (bf16[1024,256]{1,0:T(8,128)(2,1)}, bf16[1024,256]{1,0:T(8,128)(2,1)}, u32[]{:S(2)}, u32[]{:S(2)}) collective-permute-start(bf16[1024,256]{1,0:T(8,128)(2,1)} %collective-permute-done.5.refs_2_.refs_0_), channel_id=1, source_target_pairs={{0,16},{16,32},{32,48},{48,0},{64,80},{80,96},{96,112},{112,64},{1... | collective-permute-start | bytes 1572872 | tf_op jit(solution)/shard_map/ppermute | solution.py:290
  85.4 21.2 %collective-permute-start.13 = (bf16[1024,256]{1,0:T(8,128)(2,1)S(1)}, bf16[1024,256]{1,0:T(8,128)(2,1)}, u32[]{:S(2)}, u32[]{:S(2)}) collective-permute-start(bf16[1024,256]{1,0:T(8,128)(2,1)S(1)} %get-tuple-element.36.refs_1_), channel_id=1, source_target_pairs={{0,48},{16,0},{32,16},{48,32},{64,112},{80,64},{96,80},{112,96},{1... | collective-permute-start | bytes 1572872 | tf_op jit(solution)/shard_map/ppermute | solution.py:290
  88.0 18.3 %all-to-all-start.3 = ((bf16[16,48,128]{2,1,0:T(8,128)(2,1)}), bf16[16,48,128]{2,1,0:T(8,128)(2,1)S(1)}, u32[]{:S(2)}, u32[]{:S(2)}) async-start(bf16[16,48,128]{2,1,0:T(8,128)(2,1)} %get-tuple-element.35), calls=%async_computation.3 | async-start | bytes 393216 | tf_op jit(solution)/shard_map/all_to_all | solution.py:267
  95.0 1.1 copy-start.1
  106.7 15.5 %collective-permute-start.17 = (bf16[320,1024]{1,0:T(8,128)(2,1)S(1)}, bf16[320,1024]{1,0:T(8,128)(2,1)S(1)}, u32[]{:S(2)}, u32[]{:S(2)}) collective-permute-start(bf16[320,1024]{1,0:T(8,128)(2,1)S(1)} %get-tuple-element.47.refs_2_), channel_id=1, source_target_pairs={{0,48},{16,0},{32,16},{48,32},{64,112},{80,64},{96,80},{112,96},{1... | collective-permute-start | bytes 1966088 | tf_op jit(solution)/shard_map/ppermute | solution.py:290
  108.9 15.1 %collective-permute-start.16 = (bf16[320,1024]{1,0:T(8,128)(2,1)S(1)}, bf16[320,1024]{1,0:T(8,128)(2,1)}, u32[]{:S(2)}, u32[]{:S(2)}) collective-permute-start(bf16[320,1024]{1,0:T(8,128)(2,1)S(1)} %get-tuple-element.46.refs_0_), channel_id=1, source_target_pairs={{0,64},{16,80},{32,96},{48,112},{64,0},{80,16},{96,32},{112,48},{1... | collective-permute-start | bytes 1966088 | tf_op jit(solution)/shard_map/ppermute | solution.py:290
  108.9 16.3 %collective-permute-start.15 = (bf16[320,1024]{1,0:T(8,128)(2,1)S(1)}, bf16[320,1024]{1,0:T(8,128)(2,1)}, u32[]{:S(2)}, u32[]{:S(2)}) collective-permute-start(bf16[320,1024]{1,0:T(8,128)(2,1)S(1)} %get-tuple-element.46.refs_0_), channel_id=1, source_target_pairs={{0,16},{16,32},{32,48},{48,0},{64,80},{80,96},{96,112},{112,64},{1... | collective-permute-start | bytes 1966088 | tf_op jit(solution)/shard_map/ppermute | solution.py:290
  115.2 14.2 %all-to-all-start.4 = ((bf16[16,16,512]{2,1,0:T(8,128)(2,1)}), bf16[16,16,512]{2,1,0:T(8,128)(2,1)S(1)}, u32[]{:S(2)}, u32[]{:S(2)}) async-start(bf16[16,16,512]{2,1,0:T(8,128)(2,1)} %bitcast.10), calls=%async_computation.4 | async-start | bytes 524288 | tf_op jit(solution)/shard_map/all_to_all | solution.py:267
  129.5 0.7 copy-start.13

commit v5 on v4

--- a/solution.py
+++ b/solution.py
@@ -329,19 +329,19 @@
         compiler_params=pltpu.CompilerParams(vmem_limit_bytes=4 << 20),
         name="turn",
     )(packed)
-    moved = (out_across, own_qkv)
-    projected, out_across, own_qkv = pl.pallas_call(
-        lambda terms_ref, bias_ref, *refs: sum_kernel(groups, terms_ref, bias_ref, refs[4]),
+    moved = (out_across,)
+    projected, out_across = pl.pallas_call(
+        lambda terms_ref, bias_ref, *refs: sum_kernel(groups, terms_ref, bias_ref, refs[1]),
         out_shape=(
             jax.ShapeDtypeStruct((groups, slots, group_width), jnp.bfloat16),
             *(jax.ShapeDtypeStruct(v.shape, v.dtype) for v in moved),
         ),
-        in_specs=[vmem] * 2 + [anywhere] * 4,
-        out_specs=(vmem,) + (anywhere,) * 2,
-        input_output_aliases={2: 1, 3: 2},
+        in_specs=[vmem] * 2 + [anywhere],
+        out_specs=(vmem,) + (anywhere,),
+        input_output_aliases={2: 1},
         compiler_params=pltpu.CompilerParams(vmem_limit_bytes=3 << 20),
         name="sum",
-    )(terms, qkv_bias.reshape(1, group_width), *moved, out_low, out_high)
+    )(terms, qkv_bias.reshape(1, group_width), *moved)
     gathered = exchange(projected, "tensor")
 
     out_cross_low, out_cross_high = send(out_across, ahead), send(out_across, behind)
@@ -400,9 +400,6 @@
         compiler_params=pltpu.CompilerParams(vmem_limit_bytes=3 << 20),
         name="merge",
     )(message)
-    attended, out_far, out_cross_far, qkv_cross_high, qkv_low, grouped_out, grouped_qkv = hold(
-        attended, out_far, out_cross_far, qkv_cross_high, qkv_low, grouped_out, grouped_qkv
-    )
     grouped_out = place(
         grouped_out,
         [out_far, out_cross_far],

time: 133 us -> 127 us (0.955)
  waiting for transfers between devices: 40.3 us -> 32.5 us
  Pallas kernels: 23.2 us -> 24.7 us
    all_to_all x5, waiting for transfers between devices: 33.8 us -> 20.1 us  [exchange(): return lax.all_to_all(blocks, axis, split_axis=0, concat_axis=0, tiled=True)]
    ppermute x18, waiting for transfers between devices: 6.45 us -> 12.4 us  [send(): return lax.ppermute(value, 'dp', pairs)]
    all_to_all x5, starting transfers between devices: 33.6 us -> 31.5 us  [exchange(): return lax.all_to_all(blocks, axis, split_axis=0, concat_axis=0, tiled=True)]
    ppermute x18, starting transfers between devices: 18.6 us -> 20.4 us  [send(): return lax.ppermute(value, 'dp', pairs)]
    pallas_call x7, Pallas kernels: 13.2 us -> 14.6 us  [place(): pl.pallas_call(lambda *refs: place_kernel(axis, where, *refs), out_shape=...]
    unnamed x30 -> x26, local copies, waits for them, and re-layouts: 10.6 us -> 11.4 us
  transfers between devices with their start and end apart: 23 -> 23, of which waited for: 10 -> 10; matrix products, arithmetic and copies ran while one was open for 3% -> 4% of each run, Pallas kernels for 15% -> 17%
where the time goes in v5:
time: 127 us; the launch traced here: 126 us
  starting transfers between devices  51.8 us (41%)
  waiting for transfers between devices  32.5 us (26%)
  Pallas kernels  24.7 us (19%)
  local copies, waits for them, and re-layouts  12.2 us (10%)
  matrix products  3.38 us (3%)
    all_to_all x5, starting transfers between devices, exchange(): return lax.all_to_all(blocks, axis, split_axis=0, concat_axis=0, tiled=True)  31.5 us
    ppermute x18, starting transfers between devices, send(): return lax.ppermute(value, 'dp', pairs)  20.4 us
    all_to_all x5, waiting for transfers between devices, exchange(): return lax.all_to_all(blocks, axis, split_axis=0, concat_axis=0, tiled=True)  20.1 us
    pallas_call x7, Pallas kernels, place(): pl.pallas_call(lambda *refs: place_kernel(axis, where, *refs), out_shape=...  14.6 us
    ppermute x18, waiting for transfers between devices, send(): return lax.ppermute(value, 'dp', pairs)  12.4 us
    unnamed x26, local copies, waits for them, and re-layouts  11.4 us
    pallas_call x1, Pallas kernels, on_device(): pl.pallas_call(lambda *refs: attend_kernel(score_scale, *refs), out_shape...  4.48 us
    dot_general x1, matrix products, on_device(): jnp.dot(attended, grouped_out.T, preferred_element_type=jnp.float32)  3.38 us
  transfers between devices with their start and end apart: 23, of which 10 were waited for; matrix products, arithmetic and copies ran while one was open for 4% of the time, Pallas kernels for 17%

profile of v5, /device:TPU:1, one launch (start us, length us, event | category | flops | bytes accessed | tf_op | source)
XLA Modules:
  0.0 125.7 jit_solution(3147379335664130055)
XLA Ops:
  0.6 0.9 copy-done.8
  2.5 2.1 %collective-permute-start = (bf16[4,16,1024]{2,1,0:T(8,128)(2,1)S(1)}, bf16[4,16,1024]{2,1,0:T(8,128)(2,1)S(1)}, u32[]{:S(2)}, u32[]{:S(2)}) collective-permute-start(bf16[4,16,1024]{2,1,0:T(8,128)(2,1)S(1)} %get-tuple-element.19), channel_id=1, source_target_pairs={{0,64},{16,80},{32,96},{48,112},{64,0},{80,16},{96,32},{112,48},{1... | collective-permute-start | bytes 393224 | tf_op jit(solution)/shard_map/ppermute | solution.py:290
  4.7 1.1 copy-done.6
  5.8 1.0 copy-done.7
  6.8 1.3 %pack.1.refs_0_ = bf16[16,144,256]{2,1,0:T(8,128)(2,1)} custom-call(bf16[4,16,1024]{2,1,0:T(8,128)(2,1)S(1)} %get-tuple-element.18.refs_0_.own, bf16[64,5120]{1,0:T(8,128)(2,1)S(1)} %copy-done.6, bf16[64,4096]{1,0:T(8,128)(2,1)S(1)} %copy-done.7), custom_call_target="tpu_custom_call" | custom-call | tf_op jit(solution)/shard_map/pack/pallas_call | solution.py:300
  8.1 9.1 %all-to-all-start = ((bf16[16,144,256]{2,1,0:T(8,128)(2,1)}), bf16[16,144,256]{2,1,0:T(8,128)(2,1)S(1)}, u32[]{:S(2)}, u32[]{:S(2)}) async-start(bf16[16,144,256]{2,1,0:T(8,128)(2,1)} %get-tuple-element.21), calls=%async_computation | async-start | bytes 2359296 | tf_op jit(solution)/shard_map/all_to_all | solution.py:267
  17.2 3.0 %collective-permute-start.3 = (bf16[2,16,1024]{2,1,0:T(8,128)(2,1)S(1)}, bf16[2,16,1024]{2,1,0:T(8,128)(2,1)S(1)}, u32[]{:S(2)}, u32[]{:S(2)}) collective-permute-start(bf16[2,16,1024]{2,1,0:T(8,128)(2,1)S(1)} %pad_maximum_fusion.2), channel_id=1, source_target_pairs={{0,32},{16,48},{32,0},{48,16},{64,96},{80,112},{96,64},{112,80},{1... | collective-permute-start | bytes 196616 | tf_op jit(solution)/shard_map/ppermute | solution.py:290
  20.2 0.8 collective-permute-start.2
  21.1 0.8 collective-permute-start.1
  22.4 1.7 %collective-permute-done.2.high = bf16[2,16,1024]{2,1,0:T(8,128)(2,1)S(1)} collective-permute-done((bf16[2,16,1024]{2,1,0:T(8,128)(2,1)S(1)}, bf16[2,16,1024]{2,1,0:T(8,128)(2,1)S(1)}, u32[]{:S(2)}, u32[]{:S(2)}) %collective-permute-start.2) | collective-permute-done | bytes 65568 | tf_op jit(solution)/shard_map/ppermute | solution.py:290
  24.1 1.6 %collective-permute-done.1.low = bf16[2,16,1024]{2,1,0:T(8,128)(2,1)S(1)} collective-permute-done((bf16[2,16,1024]{2,1,0:T(8,128)(2,1)S(1)}, bf16[2,16,1024]{2,1,0:T(8,128)(2,1)S(1)}, u32[]{:S(2)}, u32[]{:S(2)}) %collective-permute-start.1) | collective-permute-done | bytes 65568 | tf_op jit(solution)/shard_map/ppermute | solution.py:290
  25.8 10.0 %all-to-all-done.packed_ref = bf16[16,144,256]{2,1,0:T(8,128)(2,1)S(1)} async-done(((bf16[16,144,256]{2,1,0:T(8,128)(2,1)}), bf16[16,144,256]{2,1,0:T(8,128)(2,1)S(1)}, u32[]{:S(2)}, u32[]{:S(2)}) %all-to-all-start) | async-done | bytes 1179680 | tf_op jit(solution)/shard_map/all_to_all | solution.py:267
  35.8 1.1 terms.1
  37.2 1.3 %collective-permute-start.10 = (bf16[1024,256]{1,0:T(8,128)(2,1)}, bf16[1024,256]{1,0:T(8,128)(2,1)}, u32[]{:S(2)}, u32[]{:S(2)}) collective-permute-start(bf16[1024,256]{1,0:T(8,128)(2,1)} %get-tuple-element.23.refs_0_), channel_id=1, source_target_pairs={{0,16},{16,32},{32,48},{48,0},{64,80},{80,96},{96,112},{112,64},{1... | collective-permute-start | bytes 1572872 | tf_op jit(solution)/shard_map/ppermute | solution.py:290
  38.5 1.4 %collective-permute-start.11 = (bf16[1024,256]{1,0:T(8,128)(2,1)}, bf16[1024,256]{1,0:T(8,128)(2,1)}, u32[]{:S(2)}, u32[]{:S(2)}) collective-permute-start(bf16[1024,256]{1,0:T(8,128)(2,1)} %get-tuple-element.23.refs_0_), channel_id=1, source_target_pairs={{0,48},{16,0},{32,16},{48,32},{64,112},{80,64},{96,80},{112,96},{1... | collective-permute-start | bytes 1572872 | tf_op jit(solution)/shard_map/ppermute | solution.py:290
  40.0 3.8 %all-to-all-start.1 = ((bf16[8,16,320]{2,1,0:T(8,128)(2,1)}), bf16[8,16,320]{2,1,0:T(8,128)(2,1)S(1)}, u32[]{:S(2)}, u32[]{:S(2)}) async-start(bf16[8,16,320]{2,1,0:T(8,128)(2,1)} %get-tuple-element.22), calls=%async_computation.1 | async-start | bytes 196608 | tf_op jit(solution)/shard_map/all_to_all | solution.py:267
  44.1 1.5 %collective-permute-start.7 = (bf16[320,1024]{1,0:T(8,128)(2,1)S(1)}, bf16[320,1024]{1,0:T(8,128)(2,1)S(1)}, u32[]{:S(2)}, u32[]{:S(2)}) collective-permute-start(bf16[320,1024]{1,0:T(8,128)(2,1)S(1)} %turn.1.refs_0_), channel_id=1, source_target_pairs={{0,16},{16,32},{32,48},{48,0},{64,80},{80,96},{96,112},{112,64},{1... | collective-permute-start | bytes 1966088 | tf_op jit(solution)/shard_map/ppermute | solution.py:290
  45.6 1.3 %collective-permute-start.8 = (bf16[320,1024]{1,0:T(8,128)(2,1)S(1)}, bf16[320,1024]{1,0:T(8,128)(2,1)S(1)}, u32[]{:S(2)}, u32[]{:S(2)}) collective-permute-start(bf16[320,1024]{1,0:T(8,128)(2,1)S(1)} %turn.1.refs_0_), channel_id=1, source_target_pairs={{0,48},{16,0},{32,16},{48,32},{64,112},{80,64},{96,80},{112,96},{1... | collective-permute-start | bytes 1966088 | tf_op jit(solution)/shard_map/ppermute | solution.py:290
  46.9 2.8 %collective-permute-done.4.refs_0_ = bf16[1024,256]{1,0:T(8,128)(2,1)S(1)} collective-permute-done((bf16[1024,256]{1,0:T(8,128)(2,1)}, bf16[1024,256]{1,0:T(8,128)(2,1)S(1)}, u32[]{:S(2)}, u32[]{:S(2)}) %collective-permute-start.4) | collective-permute-done | bytes 524320 | tf_op jit(solution)/shard_map/ppermute | solution.py:290
  49.7 0.8 copy-done.2
  50.8 1.8 %all-to-all-done.1.terms_ref = bf16[8,16,320]{2,1,0:T(8,128)(2,1)S(1)} async-done(((bf16[8,16,320]{2,1,0:T(8,128)(2,1)}), bf16[8,16,320]{2,1,0:T(8,128)(2,1)S(1)}, u32[]{:S(2)}, u32[]{:S(2)}) %all-to-all-start.1) | async-done | bytes 81952 | tf_op jit(solution)/shard_map/all_to_all | solution.py:267
  52.6 1.0 copy-done.3
  54.4 0.8 copy-done.4
  55.7 2.1 %collective-permute-start.6 = (bf16[1024,256]{1,0:T(8,128)(2,1)}, bf16[1024,256]{1,0:T(8,128)(2,1)}, u32[]{:S(2)}, u32[]{:S(2)}) collective-permute-start(bf16[1024,256]{1,0:T(8,128)(2,1)} %copy-done.4), channel_id=1, source_target_pairs={{0,48},{16,0},{32,16},{48,32},{64,112},{80,64},{96,80},{112,96},{1... | collective-permute-start | bytes 1572872 | tf_op jit(solution)/shard_map/ppermute | solution.py:290
  58.0 8.0 %all-to-all-start.2 = ((bf16[16,16,320]{2,1,0:T(8,128)(2,1)}), bf16[16,16,320]{2,1,0:T(8,128)(2,1)S(1)}, u32[]{:S(2)}, u32[]{:S(2)}) async-start(bf16[16,16,320]{2,1,0:T(8,128)(2,1)} %get-tuple-element.24), calls=%async_computation.2 | async-start | bytes 393216 | tf_op jit(solution)/shard_map/all_to_all | solution.py:267
  66.2 1.0 copy-done.5
  67.2 2.0 %place.7.refs_2_ = bf16[8192,256]{1,0:T(8,128)(2,1)} custom-call(bf16[1024,256]{1,0:T(8,128)(2,1)} %get-tuple-element.23.refs_0_, bf16[1024,256]{1,0:T(8,128)(2,1)S(1)} %copy-done.5), custom_call_target="tpu_custom_call" | custom-call | tf_op jit(solution)/shard_map/place/pallas_call | solution.py:151
  69.2 2.2 %place.8.refs_6_ = bf16[8192,256]{1,0:T(8,128)(2,1)} custom-call(bf16[1024,256]{1,0:T(8,128)(2,1)} %collective-permute-done.10.refs_0_, bf16[1024,256]{1,0:T(8,128)(2,1)} %collective-permute-done.11.refs_1_, bf16[8192,256]{1,0:T(8,128)(2,1)} %place.7.refs_2_), custom_call_target="tpu_custom_call", output_to_operand_aliasing={{}: (2, {})} | custom-call | tf_op jit(solution)/shard_map/place/pallas_call | solution.py:151
  71.4 2.8 %all-to-all-done.2.refs_3_ = bf16[16,16,320]{2,1,0:T(8,128)(2,1)S(1)} async-done(((bf16[16,16,320]{2,1,0:T(8,128)(2,1)}), bf16[16,16,320]{2,1,0:T(8,128)(2,1)S(1)}, u32[]{:S(2)}, u32[]{:S(2)}) %all-to-all-start.2) | async-done | bytes 163872 | tf_op jit(solution)/shard_map/all_to_all | solution.py:267
  74.2 1.6 %copy-done = bf16[8,256,512]{2,1,0:T(8,128)(2,1)S(1)} copy-done((bf16[8,256,512]{2,1,0:T(8,128)(2,1)S(1)}, bf16[8,256,512]{2,1,0:T(8,128)(2,1)}, u32[]{:S(2)}) %copy-start) | copy-done | bytes 2097176
  75.8 1.6 %copy-done.1 = bf16[8,256,512]{2,1,0:T(8,128)(2,1)S(1)} copy-done((bf16[8,256,512]{2,1,0:T(8,128)(2,1)S(1)}, bf16[8,256,512]{2,1,0:T(8,128)(2,1)}, u32[]{:S(2)}) %copy-start.1) | copy-done | bytes 2097176
  77.4 4.5 %attend.1.refs_0_ = bf16[16,48,128]{2,1,0:T(8,128)(2,1)} custom-call(s32[8]{0:T(128)S(1)} %copy-done.10, f32[16,128]{1,0:T(8,128)S(1)} %get-tuple-element.42.refs_1_, f32[16,128]{1,0:T(8,128)S(1)} %get-tuple-element.43.refs_2_, bf16[16,16,320]{2,1,0:T(8,128)(2,1)S(1)} %all-to-all-done.2.refs_3_, bf16[8,256,512]{2,1,0:T(8,128)(2,1)S(1)} %copy-done, ...), custom_call_target="tpu_custom_call" | custom-call | tf_op jit(solution)/shard_map/attend/pallas_call | solution.py:370
  81.9 1.2 collective-permute-start.16
  83.3 2.5 %collective-permute-start.13 = (bf16[1024,256]{1,0:T(8,128)(2,1)}, bf16[1024,256]{1,0:T(8,128)(2,1)}, u32[]{:S(2)}, u32[]{:S(2)}) collective-permute-start(bf16[1024,256]{1,0:T(8,128)(2,1)} %get-tuple-element.27.refs_1_), channel_id=1, source_target_pairs={{0,48},{16,0},{32,16},{48,32},{64,112},{80,64},{96,80},{112,96},{1... | collective-permute-start | bytes 1572872 | tf_op jit(solution)/shard_map/ppermute | solution.py:290
  85.8 6.0 %all-to-all-start.3 = ((bf16[16,48,128]{2,1,0:T(8,128)(2,1)}), bf16[16,48,128]{2,1,0:T(8,128)(2,1)S(1)}, u32[]{:S(2)}, u32[]{:S(2)}) async-start(bf16[16,48,128]{2,1,0:T(8,128)(2,1)} %get-tuple-element.26), calls=%async_computation.3 | async-start | bytes 393216 | tf_op jit(solution)/shard_map/all_to_all | solution.py:267
  91.9 5.6 %collective-permute-done.16.refs_2_ = bf16[320,1024]{1,0:T(8,128)(2,1)} collective-permute-done((bf16[320,1024]{1,0:T(8,128)(2,1)S(1)}, bf16[320,1024]{1,0:T(8,128)(2,1)}, u32[]{:S(2)}, u32[]{:S(2)}) %collective-permute-start.16) | collective-permute-done | bytes 655392 | tf_op jit(solution)/shard_map/ppermute | solution.py:290
  97.5 0.8 collective-permute-start.17
  98.3 2.0 %place.9.refs_2_ = bf16[8192,256]{1,0:T(8,128)(2,1)} custom-call(bf16[1024,256]{1,0:T(8,128)(2,1)S(1)} %get-tuple-element.28.refs_0_, bf16[1024,256]{1,0:T(8,128)(2,1)} %get-tuple-element.27.refs_1_, bf16[8192,256]{1,0:T(8,128)(2,1)} %get-tuple-element.29.refs_2_), custom_call_target="tpu_custom_call", output_to_operand_aliasing={{}: (2, {})} | custom-call | tf_op jit(solution)/shard_map/place/pallas_call | solution.py:151
  100.3 3.1 %all-to-all-done.3.message_ref = bf16[16,48,128]{2,1,0:T(8,128)(2,1)S(1)} async-done(((bf16[16,48,128]{2,1,0:T(8,128)(2,1)}), bf16[16,48,128]{2,1,0:T(8,128)(2,1)S(1)}, u32[]{:S(2)}, u32[]{:S(2)}) %all-to-all-start.3) | async-done | bytes 196640 | tf_op jit(solution)/shard_map/all_to_all | solution.py:267
  103.8 2.2 %place.10 = bf16[8192,256]{1,0:T(8,128)(2,1)} custom-call(bf16[1024,256]{1,0:T(8,128)(2,1)} %collective-permute-done.12.refs_0_, bf16[1024,256]{1,0:T(8,128)(2,1)} %collective-permute-done.13.refs_1_, bf16[8192,256]{1,0:T(8,128)(2,1)} %place.9.refs_2_), custom_call_target="tpu_custom_call", output_to_operand_aliasing={{}: (2, {})} | custom-call | tf_op jit(solution)/shard_map/place/pallas_call | solution.py:151
  106.0 3.4 %convolution_convert_fusion = bf16[16,8192]{1,0:T(8,128)(2,1)S(1)} fusion(bf16[16,256]{1,0:T(8,128)(2,1)S(1)} %merge.1, bf16[8192,256]{1,0:T(8,128)(2,1)} %place.10), kind=kOutput, calls=%fused_computation | convolution fusion | flops 67239936 | bytes 4464640 | tf_op jit(solution)/shard_map/dot_general | solution.py:427
  109.4 0.7 copy.29
  110.1 4.6 %all-to-all-start.4 = ((bf16[16,16,512]{2,1,0:T(8,128)(2,1)}), bf16[16,16,512]{2,1,0:T(8,128)(2,1)S(1)}, u32[]{:S(2)}, u32[]{:S(2)}) async-start(bf16[16,16,512]{2,1,0:T(8,128)(2,1)} %bitcast.10), calls=%async_computation.4 | async-start | bytes 524288 | tf_op jit(solution)/shard_map/all_to_all | solution.py:267
  114.8 1.1 place.11.refs_3_
  115.8 2.4 %place.12.refs_3_ = bf16[320,8192]{1,0:T(8,128)(2,1)} custom-call(bf16[320,1024]{1,0:T(8,128)(2,1)S(1)} %get-tuple-element.30.refs_0_, bf16[320,1024]{1,0:T(8,128)(2,1)S(1)} %get-tuple-element.31.refs_1_, bf16[320,1024]{1,0:T(8,128)(2,1)} %collective-permute-done.16.refs_2_, bf16[320,8192]{1,0:T(8,128)(2,1)} %place.11.refs_3_), custom_call_target="tpu_custom_call", output_to_operand_aliasing={{}: (3, {})} | custom-call | tf_op jit(solution)/shard_map/place/pallas_call | solution.py:151
  118.3 2.8 %place.13.after_ref = bf16[320,8192]{1,0:T(8,128)(2,1)} custom-call(bf16[320,1024]{1,0:T(8,128)(2,1)} %collective-permute-done.14.refs_0_, bf16[320,1024]{1,0:T(8,128)(2,1)} %collective-permute-done.15.refs_1_, bf16[320,1024]{1,0:T(8,128)(2,1)} %collective-permute-done.17.refs_2_, bf16[320,8192]{1,0:T(8,128)(2,1)} %place.12.refs_3_), custom_call_target="tpu_custom_call", output_to_operand_aliasing={{}: (3, {})} | custom-call | tf_op jit(solution)/shard_map/place/pallas_call | solution.py:151
  121.0 2.4 %all-to-all-done.4.terms_ref = bf16[16,16,512]{2,1,0:T(8,128)(2,1)S(1)} async-done(((bf16[16,16,512]{2,1,0:T(8,128)(2,1)}), bf16[16,16,512]{2,1,0:T(8,128)(2,1)S(1)}, u32[]{:S(2)}, u32[]{:S(2)}) %all-to-all-start.4) | async-done | bytes 262176 | tf_op jit(solution)/shard_map/all_to_all | solution.py:267
  124.1 1.6 %total.1 = bf16[16,512]{1,0:T(8,128)(2,1)} custom-call(bf16[16,16,512]{2,1,0:T(8,128)(2,1)} %copy-done.11, bf16[320,8192]{1,0:T(8,128)(2,1)} %place.13.after_ref), custom_call_target="tpu_custom_call" | custom-call | tf_op jit(solution)/shard_map/total/pallas_call | solution.py:430
  (54 shorter events, 5.5 us)
Async XLA Ops:
  0.6 1.0 copy-start.8
  1.6 0.7 copy-start.9
  2.5 5.5 %collective-permute-start = (bf16[4,16,1024]{2,1,0:T(8,128)(2,1)S(1)}, bf16[4,16,1024]{2,1,0:T(8,128)(2,1)S(1)}, u32[]{:S(2)}, u32[]{:S(2)}) collective-permute-start(bf16[4,16,1024]{2,1,0:T(8,128)(2,1)S(1)} %get-tuple-element.19), channel_id=1, source_target_pairs={{0,64},{16,80},{32,96},{48,112},{64,0},{80,16},{96,32},{112,48},{1... | collective-permute-start | bytes 393224 | tf_op jit(solution)/shard_map/ppermute | solution.py:290
  4.7 1.1 copy-start.6
  5.8 1.0 copy-start.7
  6.8 37.0 %copy-start.12 = (bf16[320]{0:T(512)(128)(2,1)S(1)}, bf16[320]{0:T(512)(128)(2,1)}, u32[]{:S(2)}) copy-start(bf16[320]{0:T(512)(128)(2,1)} %param.10) | copy-start | bytes 1924
  8.1 49.8 %copy-start.10 = (s32[8]{0:T(128)S(1)}, s32[8]{0:T(128)}, u32[]{:S(2)}) copy-start(s32[8]{0:T(128)} %refs_0_.1) | copy-start | bytes 100
  8.1 27.7 %all-to-all-start = ((bf16[16,144,256]{2,1,0:T(8,128)(2,1)}), bf16[16,144,256]{2,1,0:T(8,128)(2,1)S(1)}, u32[]{:S(2)}, u32[]{:S(2)}) async-start(bf16[16,144,256]{2,1,0:T(8,128)(2,1)} %get-tuple-element.21), calls=%async_computation | async-start | bytes 2359296 | tf_op jit(solution)/shard_map/all_to_all | solution.py:267
  17.2 5.2 %collective-permute-start.3 = (bf16[2,16,1024]{2,1,0:T(8,128)(2,1)S(1)}, bf16[2,16,1024]{2,1,0:T(8,128)(2,1)S(1)}, u32[]{:S(2)}, u32[]{:S(2)}) collective-permute-start(bf16[2,16,1024]{2,1,0:T(8,128)(2,1)S(1)} %pad_maximum_fusion.2), channel_id=1, source_target_pairs={{0,32},{16,48},{32,0},{48,16},{64,96},{80,112},{96,64},{112,80},{1... | collective-permute-start | bytes 196616 | tf_op jit(solution)/shard_map/ppermute | solution.py:290
  20.2 3.9 %collective-permute-start.2 = (bf16[2,16,1024]{2,1,0:T(8,128)(2,1)S(1)}, bf16[2,16,1024]{2,1,0:T(8,128)(2,1)S(1)}, u32[]{:S(2)}, u32[]{:S(2)}) collective-permute-start(bf16[2,16,1024]{2,1,0:T(8,128)(2,1)S(1)} %pad_maximum_fusion.1), channel_id=1, source_target_pairs={{0,48},{16,0},{32,16},{48,32},{64,112},{80,64},{96,80},{112,96},{1... | collective-permute-start | bytes 196616 | tf_op jit(solution)/shard_map/ppermute | solution.py:290
  21.1 4.7 %collective-permute-start.1 = (bf16[2,16,1024]{2,1,0:T(8,128)(2,1)S(1)}, bf16[2,16,1024]{2,1,0:T(8,128)(2,1)S(1)}, u32[]{:S(2)}, u32[]{:S(2)}) collective-permute-start(bf16[2,16,1024]{2,1,0:T(8,128)(2,1)S(1)} %pad_maximum_fusion), channel_id=1, source_target_pairs={{0,16},{16,32},{32,48},{48,0},{64,80},{80,96},{96,112},{112,64},{1... | collective-permute-start | bytes 196616 | tf_op jit(solution)/shard_map/ppermute | solution.py:290
  36.9 12.8 %collective-permute-start.4 = (bf16[1024,256]{1,0:T(8,128)(2,1)}, bf16[1024,256]{1,0:T(8,128)(2,1)S(1)}, u32[]{:S(2)}, u32[]{:S(2)}) collective-permute-start(bf16[1024,256]{1,0:T(8,128)(2,1)} %get-tuple-element.23.refs_0_), channel_id=1, source_target_pairs={{0,64},{16,80},{32,96},{48,112},{64,0},{80,16},{96,32},{112,48},{1... | collective-permute-start | bytes 1572872 | tf_op jit(solution)/shard_map/ppermute | solution.py:290
  37.2 18.0 %collective-permute-start.10 = (bf16[1024,256]{1,0:T(8,128)(2,1)}, bf16[1024,256]{1,0:T(8,128)(2,1)}, u32[]{:S(2)}, u32[]{:S(2)}) collective-permute-start(bf16[1024,256]{1,0:T(8,128)(2,1)} %get-tuple-element.23.refs_0_), channel_id=1, source_target_pairs={{0,16},{16,32},{32,48},{48,0},{64,80},{80,96},{96,112},{112,64},{1... | collective-permute-start | bytes 1572872 | tf_op jit(solution)/shard_map/ppermute | solution.py:290
  38.5 17.2 %collective-permute-start.11 = (bf16[1024,256]{1,0:T(8,128)(2,1)}, bf16[1024,256]{1,0:T(8,128)(2,1)}, u32[]{:S(2)}, u32[]{:S(2)}) collective-permute-start(bf16[1024,256]{1,0:T(8,128)(2,1)} %get-tuple-element.23.refs_0_), channel_id=1, source_target_pairs={{0,48},{16,0},{32,16},{48,32},{64,112},{80,64},{96,80},{112,96},{1... | collective-permute-start | bytes 1572872 | tf_op jit(solution)/shard_map/ppermute | solution.py:290
  40.0 12.7 %all-to-all-start.1 = ((bf16[8,16,320]{2,1,0:T(8,128)(2,1)}), bf16[8,16,320]{2,1,0:T(8,128)(2,1)S(1)}, u32[]{:S(2)}, u32[]{:S(2)}) async-start(bf16[8,16,320]{2,1,0:T(8,128)(2,1)} %get-tuple-element.22), calls=%async_computation.1 | async-start | bytes 196608 | tf_op jit(solution)/shard_map/all_to_all | solution.py:267
  44.1 37.8 %collective-permute-start.7 = (bf16[320,1024]{1,0:T(8,128)(2,1)S(1)}, bf16[320,1024]{1,0:T(8,128)(2,1)S(1)}, u32[]{:S(2)}, u32[]{:S(2)}) collective-permute-start(bf16[320,1024]{1,0:T(8,128)(2,1)S(1)} %turn.1.refs_0_), channel_id=1, source_target_pairs={{0,16},{16,32},{32,48},{48,0},{64,80},{80,96},{96,112},{112,64},{1... | collective-permute-start | bytes 1966088 | tf_op jit(solution)/shard_map/ppermute | solution.py:290
  45.6 36.3 %collective-permute-start.8 = (bf16[320,1024]{1,0:T(8,128)(2,1)S(1)}, bf16[320,1024]{1,0:T(8,128)(2,1)S(1)}, u32[]{:S(2)}, u32[]{:S(2)}) collective-permute-start(bf16[320,1024]{1,0:T(8,128)(2,1)S(1)} %turn.1.refs_0_), channel_id=1, source_target_pairs={{0,48},{16,0},{32,16},{48,32},{64,112},{80,64},{96,80},{112,96},{1... | collective-permute-start | bytes 1966088 | tf_op jit(solution)/shard_map/ppermute | solution.py:290
  49.7 0.8 copy-start.2
  50.5 31.3 %collective-permute-start.9 = (bf16[320,1024]{1,0:T(8,128)(2,1)S(1)}, bf16[320,1024]{1,0:T(8,128)(2,1)S(1)}, u32[]{:S(2)}, u32[]{:S(2)}) collective-permute-start(bf16[320,1024]{1,0:T(8,128)(2,1)S(1)} %turn.1.refs_0_), channel_id=1, source_target_pairs={{0,64},{16,80},{32,96},{48,112},{64,0},{80,16},{96,32},{112,48},{1... | collective-permute-start | bytes 1966088 | tf_op jit(solution)/shard_map/ppermute | solution.py:290
  52.6 1.0 copy-start.3
  54.4 0.8 copy-start.4
  55.2 26.7 %collective-permute-start.5 = (bf16[1024,256]{1,0:T(8,128)(2,1)}, bf16[1024,256]{1,0:T(8,128)(2,1)S(1)}, u32[]{:S(2)}, u32[]{:S(2)}) collective-permute-start(bf16[1024,256]{1,0:T(8,128)(2,1)} %copy-done.4), channel_id=1, source_target_pairs={{0,16},{16,32},{32,48},{48,0},{64,80},{80,96},{96,112},{112,64},{1... | collective-permute-start | bytes 1572872 | tf_op jit(solution)/shard_map/ppermute | solution.py:290
  55.7 26.1 %collective-permute-start.6 = (bf16[1024,256]{1,0:T(8,128)(2,1)}, bf16[1024,256]{1,0:T(8,128)(2,1)}, u32[]{:S(2)}, u32[]{:S(2)}) collective-permute-start(bf16[1024,256]{1,0:T(8,128)(2,1)} %copy-done.4), channel_id=1, source_target_pairs={{0,48},{16,0},{32,16},{48,32},{64,112},{80,64},{96,80},{112,96},{1... | collective-permute-start | bytes 1572872 | tf_op jit(solution)/shard_map/ppermute | solution.py:290
  58.0 16.2 %all-to-all-start.2 = ((bf16[16,16,320]{2,1,0:T(8,128)(2,1)}), bf16[16,16,320]{2,1,0:T(8,128)(2,1)S(1)}, u32[]{:S(2)}, u32[]{:S(2)}) async-start(bf16[16,16,320]{2,1,0:T(8,128)(2,1)} %get-tuple-element.24), calls=%async_computation.2 | async-start | bytes 393216 | tf_op jit(solution)/shard_map/all_to_all | solution.py:267
  66.2 1.0 copy-start.5
  74.2 1.6 %copy-start = (bf16[8,256,512]{2,1,0:T(8,128)(2,1)S(1)}, bf16[8,256,512]{2,1,0:T(8,128)(2,1)}, u32[]{:S(2)}) copy-start(bf16[8,256,512]{2,1,0:T(8,128)(2,1)} %refs_4_.1) | copy-start | bytes 6291460
  75.8 1.6 %copy-start.1 = (bf16[8,256,512]{2,1,0:T(8,128)(2,1)S(1)}, bf16[8,256,512]{2,1,0:T(8,128)(2,1)}, u32[]{:S(2)}) copy-start(bf16[8,256,512]{2,1,0:T(8,128)(2,1)} %refs_5_.1) | copy-start | bytes 6291460
  81.9 15.6 %collective-permute-start.16 = (bf16[320,1024]{1,0:T(8,128)(2,1)S(1)}, bf16[320,1024]{1,0:T(8,128)(2,1)}, u32[]{:S(2)}, u32[]{:S(2)}) collective-permute-start(bf16[320,1024]{1,0:T(8,128)(2,1)S(1)} %get-tuple-element.31.refs_1_), channel_id=1, source_target_pairs={{0,64},{16,80},{32,96},{48,112},{64,0},{80,16},{96,32},{112,48},{1... | collective-permute-start | bytes 1966088 | tf_op jit(solution)/shard_map/ppermute | solution.py:290
  83.1 20.7 %collective-permute-start.12 = (bf16[1024,256]{1,0:T(8,128)(2,1)}, bf16[1024,256]{1,0:T(8,128)(2,1)}, u32[]{:S(2)}, u32[]{:S(2)}) collective-permute-start(bf16[1024,256]{1,0:T(8,128)(2,1)} %collective-permute-done.10.refs_0_), channel_id=1, source_target_pairs={{0,16},{16,32},{32,48},{48,0},{64,80},{80,96},{96,112},{112,64},{1... | collective-permute-start | bytes 1572872 | tf_op jit(solution)/shard_map/ppermute | solution.py:290
  83.3 20.5 %collective-permute-start.13 = (bf16[1024,256]{1,0:T(8,128)(2,1)}, bf16[1024,256]{1,0:T(8,128)(2,1)}, u32[]{:S(2)}, u32[]{:S(2)}) collective-permute-start(bf16[1024,256]{1,0:T(8,128)(2,1)} %get-tuple-element.27.refs_1_), channel_id=1, source_target_pairs={{0,48},{16,0},{32,16},{48,32},{64,112},{80,64},{96,80},{112,96},{1... | collective-permute-start | bytes 1572872 | tf_op jit(solution)/shard_map/ppermute | solution.py:290
  85.8 17.6 %all-to-all-start.3 = ((bf16[16,48,128]{2,1,0:T(8,128)(2,1)}), bf16[16,48,128]{2,1,0:T(8,128)(2,1)S(1)}, u32[]{:S(2)}, u32[]{:S(2)}) async-start(bf16[16,48,128]{2,1,0:T(8,128)(2,1)} %get-tuple-element.26), calls=%async_computation.3 | async-start | bytes 393216 | tf_op jit(solution)/shard_map/all_to_all | solution.py:267
  91.8 26.5 %collective-permute-start.14 = (bf16[320,1024]{1,0:T(8,128)(2,1)S(1)}, bf16[320,1024]{1,0:T(8,128)(2,1)}, u32[]{:S(2)}, u32[]{:S(2)}) collective-permute-start(bf16[320,1024]{1,0:T(8,128)(2,1)S(1)} %get-tuple-element.30.refs_0_), channel_id=1, source_target_pairs={{0,16},{16,32},{32,48},{48,0},{64,80},{80,96},{96,112},{112,64},{1... | collective-permute-start | bytes 1966088 | tf_op jit(solution)/shard_map/ppermute | solution.py:290
  91.8 26.5 %collective-permute-start.15 = (bf16[320,1024]{1,0:T(8,128)(2,1)S(1)}, bf16[320,1024]{1,0:T(8,128)(2,1)}, u32[]{:S(2)}, u32[]{:S(2)}) collective-permute-start(bf16[320,1024]{1,0:T(8,128)(2,1)S(1)} %get-tuple-element.30.refs_0_), channel_id=1, source_target_pairs={{0,64},{16,80},{32,96},{48,112},{64,0},{80,16},{96,32},{112,48},{1... | collective-permute-start | bytes 1966088 | tf_op jit(solution)/shard_map/ppermute | solution.py:290
  97.5 20.8 %collective-permute-start.17 = (bf16[320,1024]{1,0:T(8,128)(2,1)}, bf16[320,1024]{1,0:T(8,128)(2,1)}, u32[]{:S(2)}, u32[]{:S(2)}) collective-permute-start(bf16[320,1024]{1,0:T(8,128)(2,1)} %collective-permute-done.16.refs_2_), channel_id=1, source_target_pairs={{0,48},{16,0},{32,16},{48,32},{64,112},{80,64},{96,80},{112,96},{1... | collective-permute-start | bytes 1966088 | tf_op jit(solution)/shard_map/ppermute | solution.py:290
  110.1 13.3 %all-to-all-start.4 = ((bf16[16,16,512]{2,1,0:T(8,128)(2,1)}), bf16[16,16,512]{2,1,0:T(8,128)(2,1)S(1)}, u32[]{:S(2)}, u32[]{:S(2)}) async-start(bf16[16,16,512]{2,1,0:T(8,128)(2,1)} %bitcast.10), calls=%async_computation.4 | async-start | bytes 524288 | tf_op jit(solution)/shard_map/all_to_all | solution.py:267
  123.4 0.7 copy-start.11

commit v6 on v5

--- a/solution.py
+++ b/solution.py
@@ -126,10 +126,13 @@
     turned_ref[width:] = pairs.T
 
 
-def place_kernel(axis, where, *refs):
+def place_kernel(axis, where, mark, *refs):
     parts = refs[: len(where)]
     replica = lax.axis_index("dp")
     whole_ref, sems = refs[-2:]
+    if mark:
+        whole_ref, mark_ref, sems = refs[-3:]
+        mark_ref[...] = jnp.zeros_like(mark_ref)
     copies = []
     for i, (part, (c, y)) in enumerate(zip(parts, where)):
         size = part.shape[axis]
@@ -143,16 +146,19 @@
         copy.wait()
 
 
-def place(whole, parts, where, axis, shape):
+def place(whole, parts, where, axis, shape, mark=False):
     count = len(parts)
     continued = whole is not None
+    whole_shape = jax.ShapeDtypeStruct(shape, parts[0].dtype)
     vmem = pl.BlockSpec(memory_space=pltpu.VMEM)
     anywhere = pl.BlockSpec(memory_space=pl.ANY)
     return pl.pallas_call(
-        lambda *refs: place_kernel(axis, where, *refs),
-        out_shape=jax.ShapeDtypeStruct(shape, parts[0].dtype),
+        lambda *refs: place_kernel(axis, where, mark, *refs),
+        out_shape=(whole_shape, jax.ShapeDtypeStruct((8, 128), jnp.float32))
+        if mark
+        else whole_shape,
         in_specs=[vmem] * count + ([anywhere] if continued else []),
-        out_specs=anywhere,
+        out_specs=(anywhere, vmem) if mark else anywhere,
         scratch_shapes=[pltpu.SemaphoreType.DMA((count,))],
         input_output_aliases={count: 0} if continued else {},
         compiler_params=pltpu.CompilerParams(vmem_limit_bytes=4 << 20),
@@ -416,12 +422,13 @@
         1,
         qkv_shape,
     )
-    grouped_qkv = place(
+    grouped_qkv, placed = place(
         grouped_qkv,
         [qkv_far, qkv_cross_low, qkv_cross_far],
         [(0, 2), (1, -1), (1, 2)],
         1,
         qkv_shape,
+        mark=True,
     )
 
     term_sums = jnp.dot(attended, grouped_out.T, preferred_element_type=jnp.float32)
@@ -431,9 +438,9 @@
         total_kernel,
         out_shape=jax.ShapeDtypeStruct((slots, feature_width // groups), jnp.bfloat16),
         in_specs=[vmem, anywhere],
-        compiler_params=pltpu.CompilerParams(vmem_limit_bytes=56 << 20),
+        compiler_params=pltpu.CompilerParams(vmem_limit_bytes=2 << 20),
         name="total",
-    )(term_sums, grouped_qkv)
+    )(term_sums, placed)
     attn_output = attn_output.reshape(step_count, row_count, -1)
     return (attn_output, grouped_qkv.T, grouped_out)
 

time: 127 us -> 124 us (0.976)
  local copies, waits for them, and re-layouts: 12.2 us -> 9.68 us
    unnamed x26 -> x20, local copies, waits for them, and re-layouts: 11.4 us -> 8.81 us
  transfers between devices with their start and end apart: 23 -> 23, of which waited for: 10 -> 10; matrix products, arithmetic and copies ran while one was open for 4% -> 4% of each run, Pallas kernels for 17% -> 18%
where the time goes in v6:
time: 124 us; the launch traced here: 123 us
  starting transfers between devices  51.8 us (42%)
  waiting for transfers between devices  33.3 us (27%)
  Pallas kernels  23.8 us (19%)
  local copies, waits for them, and re-layouts  9.68 us (8%)
  matrix products  3.38 us (3%)
    all_to_all x5, starting transfers between devices, exchange(): return lax.all_to_all(blocks, axis, split_axis=0, concat_axis=0, tiled=True)  31.5 us
    all_to_all x5, waiting for transfers between devices, exchange(): return lax.all_to_all(blocks, axis, split_axis=0, concat_axis=0, tiled=True)  20.9 us
    ppermute x18, starting transfers between devices, send(): return lax.ppermute(value, 'dp', pairs)  20.3 us
    pallas_call x7, Pallas kernels, place(): pl.pallas_call(lambda *refs: place_kernel(axis, where, mark, *refs), out_...  14.6 us
    ppermute x18, waiting for transfers between devices, send(): return lax.ppermute(value, 'dp', pairs)  12.4 us
    unnamed x20, local copies, waits for them, and re-layouts  8.81 us
    pallas_call x1, Pallas kernels, on_device(): pl.pallas_call(lambda *refs: attend_kernel(score_scale, *refs), out_shape...  4.48 us
    dot_general x1, matrix products, on_device(): jnp.dot(attended, grouped_out.T, preferred_element_type=jnp.float32)  3.38 us
  transfers between devices with their start and end apart: 23, of which 10 were waited for; matrix products, arithmetic and copies ran while one was open for 4% of the time, Pallas kernels for 18%

profile of v6, /device:TPU:1, one launch (start us, length us, event | category | flops | bytes accessed | tf_op | source)
XLA Modules:
  0.0 123.0 jit_solution(9036093382739470877)
XLA Ops:
  0.6 0.9 copy-done.6
  1.6 0.7 copy-done.7
  2.5 2.1 %collective-permute-start = (bf16[4,16,1024]{2,1,0:T(8,128)(2,1)S(1)}, bf16[4,16,1024]{2,1,0:T(8,128)(2,1)S(1)}, u32[]{:S(2)}, u32[]{:S(2)}) collective-permute-start(bf16[4,16,1024]{2,1,0:T(8,128)(2,1)S(1)} %get-tuple-element.21), channel_id=1, source_target_pairs={{0,64},{16,80},{32,96},{48,112},{64,0},{80,16},{96,32},{112,48},{1... | collective-permute-start | bytes 393224 | tf_op jit(solution)/shard_map/ppermute | solution.py:296
  4.7 1.1 copy-done.4
  5.8 1.0 copy-done.5
  6.8 1.3 %pack.1.refs_0_ = bf16[16,144,256]{2,1,0:T(8,128)(2,1)} custom-call(bf16[4,16,1024]{2,1,0:T(8,128)(2,1)S(1)} %get-tuple-element.20.refs_0_.own, bf16[64,5120]{1,0:T(8,128)(2,1)S(1)} %copy-done.4, bf16[64,4096]{1,0:T(8,128)(2,1)S(1)} %copy-done.5), custom_call_target="tpu_custom_call" | custom-call | tf_op jit(solution)/shard_map/pack/pallas_call | solution.py:306
  8.1 9.1 %all-to-all-start = ((bf16[16,144,256]{2,1,0:T(8,128)(2,1)}), bf16[16,144,256]{2,1,0:T(8,128)(2,1)S(1)}, u32[]{:S(2)}, u32[]{:S(2)}) async-start(bf16[16,144,256]{2,1,0:T(8,128)(2,1)} %get-tuple-element.23), calls=%async_computation | async-start | bytes 2359296 | tf_op jit(solution)/shard_map/all_to_all | solution.py:273
  17.2 3.0 %collective-permute-start.3 = (bf16[2,16,1024]{2,1,0:T(8,128)(2,1)S(1)}, bf16[2,16,1024]{2,1,0:T(8,128)(2,1)S(1)}, u32[]{:S(2)}, u32[]{:S(2)}) collective-permute-start(bf16[2,16,1024]{2,1,0:T(8,128)(2,1)S(1)} %pad_maximum_fusion.2), channel_id=1, source_target_pairs={{0,32},{16,48},{32,0},{48,16},{64,96},{80,112},{96,64},{112,80},{1... | collective-permute-start | bytes 196616 | tf_op jit(solution)/shard_map/ppermute | solution.py:296
  20.2 0.8 collective-permute-start.2
  21.1 0.8 collective-permute-start.1
  22.4 1.7 %collective-permute-done.2.high = bf16[2,16,1024]{2,1,0:T(8,128)(2,1)S(1)} collective-permute-done((bf16[2,16,1024]{2,1,0:T(8,128)(2,1)S(1)}, bf16[2,16,1024]{2,1,0:T(8,128)(2,1)S(1)}, u32[]{:S(2)}, u32[]{:S(2)}) %collective-permute-start.2) | collective-permute-done | bytes 65568 | tf_op jit(solution)/shard_map/ppermute | solution.py:296
  24.1 1.6 %collective-permute-done.1.low = bf16[2,16,1024]{2,1,0:T(8,128)(2,1)S(1)} collective-permute-done((bf16[2,16,1024]{2,1,0:T(8,128)(2,1)S(1)}, bf16[2,16,1024]{2,1,0:T(8,128)(2,1)S(1)}, u32[]{:S(2)}, u32[]{:S(2)}) %collective-permute-start.1) | collective-permute-done | bytes 65568 | tf_op jit(solution)/shard_map/ppermute | solution.py:296
  25.8 10.0 %all-to-all-done.packed_ref = bf16[16,144,256]{2,1,0:T(8,128)(2,1)S(1)} async-done(((bf16[16,144,256]{2,1,0:T(8,128)(2,1)}), bf16[16,144,256]{2,1,0:T(8,128)(2,1)S(1)}, u32[]{:S(2)}, u32[]{:S(2)}) %all-to-all-start) | async-done | bytes 1179680 | tf_op jit(solution)/shard_map/all_to_all | solution.py:273
  35.8 1.1 terms.1
  37.2 1.3 %collective-permute-start.10 = (bf16[1024,256]{1,0:T(8,128)(2,1)}, bf16[1024,256]{1,0:T(8,128)(2,1)}, u32[]{:S(2)}, u32[]{:S(2)}) collective-permute-start(bf16[1024,256]{1,0:T(8,128)(2,1)} %get-tuple-element.25.refs_0_), channel_id=1, source_target_pairs={{0,16},{16,32},{32,48},{48,0},{64,80},{80,96},{96,112},{112,64},{1... | collective-permute-start | bytes 1572872 | tf_op jit(solution)/shard_map/ppermute | solution.py:296
  38.5 1.4 %collective-permute-start.11 = (bf16[1024,256]{1,0:T(8,128)(2,1)}, bf16[1024,256]{1,0:T(8,128)(2,1)}, u32[]{:S(2)}, u32[]{:S(2)}) collective-permute-start(bf16[1024,256]{1,0:T(8,128)(2,1)} %get-tuple-element.25.refs_0_), channel_id=1, source_target_pairs={{0,48},{16,0},{32,16},{48,32},{64,112},{80,64},{96,80},{112,96},{1... | collective-permute-start | bytes 1572872 | tf_op jit(solution)/shard_map/ppermute | solution.py:296
  40.0 3.8 %all-to-all-start.1 = ((bf16[8,16,320]{2,1,0:T(8,128)(2,1)}), bf16[8,16,320]{2,1,0:T(8,128)(2,1)S(1)}, u32[]{:S(2)}, u32[]{:S(2)}) async-start(bf16[8,16,320]{2,1,0:T(8,128)(2,1)} %get-tuple-element.24), calls=%async_computation.1 | async-start | bytes 196608 | tf_op jit(solution)/shard_map/all_to_all | solution.py:273
  44.1 1.5 %collective-permute-start.7 = (bf16[320,1024]{1,0:T(8,128)(2,1)S(1)}, bf16[320,1024]{1,0:T(8,128)(2,1)S(1)}, u32[]{:S(2)}, u32[]{:S(2)}) collective-permute-start(bf16[320,1024]{1,0:T(8,128)(2,1)S(1)} %turn.1.refs_0_), channel_id=1, source_target_pairs={{0,16},{16,32},{32,48},{48,0},{64,80},{80,96},{96,112},{112,64},{1... | collective-permute-start | bytes 1966088 | tf_op jit(solution)/shard_map/ppermute | solution.py:296
  45.6 1.3 %collective-permute-start.8 = (bf16[320,1024]{1,0:T(8,128)(2,1)S(1)}, bf16[320,1024]{1,0:T(8,128)(2,1)S(1)}, u32[]{:S(2)}, u32[]{:S(2)}) collective-permute-start(bf16[320,1024]{1,0:T(8,128)(2,1)S(1)} %turn.1.refs_0_), channel_id=1, source_target_pairs={{0,48},{16,0},{32,16},{48,32},{64,112},{80,64},{96,80},{112,96},{1... | collective-permute-start | bytes 1966088 | tf_op jit(solution)/shard_map/ppermute | solution.py:296
  46.9 2.8 %collective-permute-done.4.refs_0_ = bf16[1024,256]{1,0:T(8,128)(2,1)S(1)} collective-permute-done((bf16[1024,256]{1,0:T(8,128)(2,1)}, bf16[1024,256]{1,0:T(8,128)(2,1)S(1)}, u32[]{:S(2)}, u32[]{:S(2)}) %collective-permute-start.4) | collective-permute-done | bytes 524320 | tf_op jit(solution)/shard_map/ppermute | solution.py:296
  50.0 2.6 %all-to-all-done.1.terms_ref = bf16[8,16,320]{2,1,0:T(8,128)(2,1)S(1)} async-done(((bf16[8,16,320]{2,1,0:T(8,128)(2,1)}), bf16[8,16,320]{2,1,0:T(8,128)(2,1)S(1)}, u32[]{:S(2)}, u32[]{:S(2)}) %all-to-all-start.1) | async-done | bytes 81952 | tf_op jit(solution)/shard_map/all_to_all | solution.py:273
  52.6 0.7 sum.1
  53.3 0.8 copy-done.2
  54.7 2.1 %collective-permute-start.6 = (bf16[1024,256]{1,0:T(8,128)(2,1)}, bf16[1024,256]{1,0:T(8,128)(2,1)}, u32[]{:S(2)}, u32[]{:S(2)}) collective-permute-start(bf16[1024,256]{1,0:T(8,128)(2,1)} %copy-done.2), channel_id=1, source_target_pairs={{0,48},{16,0},{32,16},{48,32},{64,112},{80,64},{96,80},{112,96},{1... | collective-permute-start | bytes 1572872 | tf_op jit(solution)/shard_map/ppermute | solution.py:296
  56.9 8.0 %all-to-all-start.2 = ((bf16[16,16,320]{2,1,0:T(8,128)(2,1)}), bf16[16,16,320]{2,1,0:T(8,128)(2,1)S(1)}, u32[]{:S(2)}, u32[]{:S(2)}) async-start(bf16[16,16,320]{2,1,0:T(8,128)(2,1)} %get-tuple-element.26), calls=%async_computation.2 | async-start | bytes 393216 | tf_op jit(solution)/shard_map/all_to_all | solution.py:273
  65.1 1.0 copy-done.3
  66.1 2.0 %place.7.refs_2_ = bf16[8192,256]{1,0:T(8,128)(2,1)} custom-call(bf16[1024,256]{1,0:T(8,128)(2,1)} %get-tuple-element.25.refs_0_, bf16[1024,256]{1,0:T(8,128)(2,1)S(1)} %copy-done.3), custom_call_target="tpu_custom_call" | custom-call | tf_op jit(solution)/shard_map/place/pallas_call | solution.py:155
  68.2 2.2 %place.8.refs_6_ = bf16[8192,256]{1,0:T(8,128)(2,1)} custom-call(bf16[1024,256]{1,0:T(8,128)(2,1)} %collective-permute-done.10.refs_0_, bf16[1024,256]{1,0:T(8,128)(2,1)} %collective-permute-done.11.refs_1_, bf16[8192,256]{1,0:T(8,128)(2,1)} %place.7.refs_2_), custom_call_target="tpu_custom_call", output_to_operand_aliasing={{}: (2, {})} | custom-call | tf_op jit(solution)/shard_map/place/pallas_call | solution.py:155
  70.4 2.8 %all-to-all-done.2.refs_3_ = bf16[16,16,320]{2,1,0:T(8,128)(2,1)S(1)} async-done(((bf16[16,16,320]{2,1,0:T(8,128)(2,1)}), bf16[16,16,320]{2,1,0:T(8,128)(2,1)S(1)}, u32[]{:S(2)}, u32[]{:S(2)}) %all-to-all-start.2) | async-done | bytes 163872 | tf_op jit(solution)/shard_map/all_to_all | solution.py:273
  73.1 1.6 %copy-done = bf16[8,256,512]{2,1,0:T(8,128)(2,1)S(1)} copy-done((bf16[8,256,512]{2,1,0:T(8,128)(2,1)S(1)}, bf16[8,256,512]{2,1,0:T(8,128)(2,1)}, u32[]{:S(2)}) %copy-start) | copy-done | bytes 2097176
  74.7 1.6 %copy-done.1 = bf16[8,256,512]{2,1,0:T(8,128)(2,1)S(1)} copy-done((bf16[8,256,512]{2,1,0:T(8,128)(2,1)S(1)}, bf16[8,256,512]{2,1,0:T(8,128)(2,1)}, u32[]{:S(2)}) %copy-start.1) | copy-done | bytes 2097176
  76.3 4.5 %attend.1.refs_0_ = bf16[16,48,128]{2,1,0:T(8,128)(2,1)} custom-call(s32[8]{0:T(128)S(1)} %copy-done.8, f32[16,128]{1,0:T(8,128)S(1)} %get-tuple-element.46.refs_1_, f32[16,128]{1,0:T(8,128)S(1)} %get-tuple-element.47.refs_2_, bf16[16,16,320]{2,1,0:T(8,128)(2,1)S(1)} %all-to-all-done.2.refs_3_, bf16[8,256,512]{2,1,0:T(8,128)(2,1)S(1)} %copy-done, ...), custom_call_target="tpu_custom_call" | custom-call | tf_op jit(solution)/shard_map/attend/pallas_call | solution.py:376
  80.8 1.2 collective-permute-start.16
  82.3 2.5 %collective-permute-start.13 = (bf16[1024,256]{1,0:T(8,128)(2,1)}, bf16[1024,256]{1,0:T(8,128)(2,1)}, u32[]{:S(2)}, u32[]{:S(2)}) collective-permute-start(bf16[1024,256]{1,0:T(8,128)(2,1)} %get-tuple-element.29.refs_1_), channel_id=1, source_target_pairs={{0,48},{16,0},{32,16},{48,32},{64,112},{80,64},{96,80},{112,96},{1... | collective-permute-start | bytes 1572872 | tf_op jit(solution)/shard_map/ppermute | solution.py:296
  84.7 6.0 %all-to-all-start.3 = ((bf16[16,48,128]{2,1,0:T(8,128)(2,1)}), bf16[16,48,128]{2,1,0:T(8,128)(2,1)S(1)}, u32[]{:S(2)}, u32[]{:S(2)}) async-start(bf16[16,48,128]{2,1,0:T(8,128)(2,1)} %get-tuple-element.28), calls=%async_computation.3 | async-start | bytes 393216 | tf_op jit(solution)/shard_map/all_to_all | solution.py:273
  90.8 5.6 %collective-permute-done.16.refs_2_ = bf16[320,1024]{1,0:T(8,128)(2,1)} collective-permute-done((bf16[320,1024]{1,0:T(8,128)(2,1)S(1)}, bf16[320,1024]{1,0:T(8,128)(2,1)}, u32[]{:S(2)}, u32[]{:S(2)}) %collective-permute-start.16) | collective-permute-done | bytes 655392 | tf_op jit(solution)/shard_map/ppermute | solution.py:296
  96.5 0.7 collective-permute-start.17
  97.2 2.0 %place.9.refs_2_ = bf16[8192,256]{1,0:T(8,128)(2,1)} custom-call(bf16[1024,256]{1,0:T(8,128)(2,1)S(1)} %get-tuple-element.30.refs_0_, bf16[1024,256]{1,0:T(8,128)(2,1)} %get-tuple-element.29.refs_1_, bf16[8192,256]{1,0:T(8,128)(2,1)} %get-tuple-element.31.refs_2_), custom_call_target="tpu_custom_call", output_to_operand_aliasing={{}: (2, {})} | custom-call | tf_op jit(solution)/shard_map/place/pallas_call | solution.py:155
  99.2 3.2 %all-to-all-done.3.message_ref = bf16[16,48,128]{2,1,0:T(8,128)(2,1)S(1)} async-done(((bf16[16,48,128]{2,1,0:T(8,128)(2,1)}), bf16[16,48,128]{2,1,0:T(8,128)(2,1)S(1)}, u32[]{:S(2)}, u32[]{:S(2)}) %all-to-all-start.3) | async-done | bytes 196640 | tf_op jit(solution)/shard_map/all_to_all | solution.py:273
  102.8 2.2 %place.10 = bf16[8192,256]{1,0:T(8,128)(2,1)} custom-call(bf16[1024,256]{1,0:T(8,128)(2,1)} %collective-permute-done.12.refs_0_, bf16[1024,256]{1,0:T(8,128)(2,1)} %collective-permute-done.13.refs_1_, bf16[8192,256]{1,0:T(8,128)(2,1)} %place.9.refs_2_), custom_call_target="tpu_custom_call", output_to_operand_aliasing={{}: (2, {})} | custom-call | tf_op jit(solution)/shard_map/place/pallas_call | solution.py:155
  105.0 3.4 %convolution_convert_fusion = bf16[16,8192]{1,0:T(8,128)(2,1)S(1)} fusion(bf16[16,256]{1,0:T(8,128)(2,1)S(1)} %merge.1, bf16[8192,256]{1,0:T(8,128)(2,1)} %place.10), kind=kOutput, calls=%fused_computation | convolution fusion | flops 67239936 | bytes 4464640 | tf_op jit(solution)/shard_map/dot_general | solution.py:434
  108.3 0.8 copy.29
  109.1 4.6 %all-to-all-start.4 = ((bf16[16,16,512]{2,1,0:T(8,128)(2,1)}), bf16[16,16,512]{2,1,0:T(8,128)(2,1)S(1)}, u32[]{:S(2)}, u32[]{:S(2)}) async-start(bf16[16,16,512]{2,1,0:T(8,128)(2,1)} %bitcast.10), calls=%async_computation.4 | async-start | bytes 524288 | tf_op jit(solution)/shard_map/all_to_all | solution.py:273
  113.7 1.1 place.11.refs_3_
  114.8 2.4 %place.12.refs_3_ = bf16[320,8192]{1,0:T(8,128)(2,1)} custom-call(bf16[320,1024]{1,0:T(8,128)(2,1)S(1)} %get-tuple-element.32.refs_0_, bf16[320,1024]{1,0:T(8,128)(2,1)S(1)} %get-tuple-element.33.refs_1_, bf16[320,1024]{1,0:T(8,128)(2,1)} %collective-permute-done.16.refs_2_, bf16[320,8192]{1,0:T(8,128)(2,1)} %place.11.refs_3_), custom_call_target="tpu_custom_call", output_to_operand_aliasing={{}: (3, {})} | custom-call | tf_op jit(solution)/shard_map/place/pallas_call | solution.py:155
  117.2 2.8 %place.13 = (bf16[320,8192]{1,0:T(8,128)(2,1)}, f32[8,128]{1,0:T(8,128)S(1)}) custom-call(bf16[320,1024]{1,0:T(8,128)(2,1)} %collective-permute-done.14.refs_0_, bf16[320,1024]{1,0:T(8,128)(2,1)} %collective-permute-done.15.refs_1_, bf16[320,1024]{1,0:T(8,128)(2,1)} %collective-permute-done.17.refs_2_, ...), custom_call_target="tpu_custom_call", output_to_operand_aliasing={{0}: (3, {})} | custom-call | tf_op jit(solution)/shard_map/place/pallas_call | solution.py:155
  120.0 2.4 %all-to-all-done.4.terms_ref = bf16[16,16,512]{2,1,0:T(8,128)(2,1)S(1)} async-done(((bf16[16,16,512]{2,1,0:T(8,128)(2,1)}), bf16[16,16,512]{2,1,0:T(8,128)(2,1)S(1)}, u32[]{:S(2)}, u32[]{:S(2)}) %all-to-all-start.4) | async-done | bytes 262176 | tf_op jit(solution)/shard_map/all_to_all | solution.py:273
  122.4 0.6 total.1
  (48 shorter events, 3.4 us)
Async XLA Ops:
  0.6 1.0 copy-start.6
  1.6 0.7 copy-start.7
  2.5 5.5 %collective-permute-start = (bf16[4,16,1024]{2,1,0:T(8,128)(2,1)S(1)}, bf16[4,16,1024]{2,1,0:T(8,128)(2,1)S(1)}, u32[]{:S(2)}, u32[]{:S(2)}) collective-permute-start(bf16[4,16,1024]{2,1,0:T(8,128)(2,1)S(1)} %get-tuple-element.21), channel_id=1, source_target_pairs={{0,64},{16,80},{32,96},{48,112},{64,0},{80,16},{96,32},{112,48},{1... | collective-permute-start | bytes 393224 | tf_op jit(solution)/shard_map/ppermute | solution.py:296
  4.7 1.1 copy-start.4
  5.8 1.0 copy-start.5
  6.8 37.0 %copy-start.9 = (bf16[320]{0:T(512)(128)(2,1)S(1)}, bf16[320]{0:T(512)(128)(2,1)}, u32[]{:S(2)}) copy-start(bf16[320]{0:T(512)(128)(2,1)} %param.10) | copy-start | bytes 1924
  8.1 48.7 %copy-start.8 = (s32[8]{0:T(128)S(1)}, s32[8]{0:T(128)}, u32[]{:S(2)}) copy-start(s32[8]{0:T(128)} %refs_0_.1) | copy-start | bytes 100
  8.1 27.7 %all-to-all-start = ((bf16[16,144,256]{2,1,0:T(8,128)(2,1)}), bf16[16,144,256]{2,1,0:T(8,128)(2,1)S(1)}, u32[]{:S(2)}, u32[]{:S(2)}) async-start(bf16[16,144,256]{2,1,0:T(8,128)(2,1)} %get-tuple-element.23), calls=%async_computation | async-start | bytes 2359296 | tf_op jit(solution)/shard_map/all_to_all | solution.py:273
  17.2 5.2 %collective-permute-start.3 = (bf16[2,16,1024]{2,1,0:T(8,128)(2,1)S(1)}, bf16[2,16,1024]{2,1,0:T(8,128)(2,1)S(1)}, u32[]{:S(2)}, u32[]{:S(2)}) collective-permute-start(bf16[2,16,1024]{2,1,0:T(8,128)(2,1)S(1)} %pad_maximum_fusion.2), channel_id=1, source_target_pairs={{0,32},{16,48},{32,0},{48,16},{64,96},{80,112},{96,64},{112,80},{1... | collective-permute-start | bytes 196616 | tf_op jit(solution)/shard_map/ppermute | solution.py:296
  20.2 3.9 %collective-permute-start.2 = (bf16[2,16,1024]{2,1,0:T(8,128)(2,1)S(1)}, bf16[2,16,1024]{2,1,0:T(8,128)(2,1)S(1)}, u32[]{:S(2)}, u32[]{:S(2)}) collective-permute-start(bf16[2,16,1024]{2,1,0:T(8,128)(2,1)S(1)} %pad_maximum_fusion.1), channel_id=1, source_target_pairs={{0,48},{16,0},{32,16},{48,32},{64,112},{80,64},{96,80},{112,96},{1... | collective-permute-start | bytes 196616 | tf_op jit(solution)/shard_map/ppermute | solution.py:296
  21.1 4.7 %collective-permute-start.1 = (bf16[2,16,1024]{2,1,0:T(8,128)(2,1)S(1)}, bf16[2,16,1024]{2,1,0:T(8,128)(2,1)S(1)}, u32[]{:S(2)}, u32[]{:S(2)}) collective-permute-start(bf16[2,16,1024]{2,1,0:T(8,128)(2,1)S(1)} %pad_maximum_fusion), channel_id=1, source_target_pairs={{0,16},{16,32},{32,48},{48,0},{64,80},{80,96},{96,112},{112,64},{1... | collective-permute-start | bytes 196616 | tf_op jit(solution)/shard_map/ppermute | solution.py:296
  36.9 12.8 %collective-permute-start.4 = (bf16[1024,256]{1,0:T(8,128)(2,1)}, bf16[1024,256]{1,0:T(8,128)(2,1)S(1)}, u32[]{:S(2)}, u32[]{:S(2)}) collective-permute-start(bf16[1024,256]{1,0:T(8,128)(2,1)} %get-tuple-element.25.refs_0_), channel_id=1, source_target_pairs={{0,64},{16,80},{32,96},{48,112},{64,0},{80,16},{96,32},{112,48},{1... | collective-permute-start | bytes 1572872 | tf_op jit(solution)/shard_map/ppermute | solution.py:296
  37.2 16.9 %collective-permute-start.10 = (bf16[1024,256]{1,0:T(8,128)(2,1)}, bf16[1024,256]{1,0:T(8,128)(2,1)}, u32[]{:S(2)}, u32[]{:S(2)}) collective-permute-start(bf16[1024,256]{1,0:T(8,128)(2,1)} %get-tuple-element.25.refs_0_), channel_id=1, source_target_pairs={{0,16},{16,32},{32,48},{48,0},{64,80},{80,96},{96,112},{112,64},{1... | collective-permute-start | bytes 1572872 | tf_op jit(solution)/shard_map/ppermute | solution.py:296
  38.5 16.2 %collective-permute-start.11 = (bf16[1024,256]{1,0:T(8,128)(2,1)}, bf16[1024,256]{1,0:T(8,128)(2,1)}, u32[]{:S(2)}, u32[]{:S(2)}) collective-permute-start(bf16[1024,256]{1,0:T(8,128)(2,1)} %get-tuple-element.25.refs_0_), channel_id=1, source_target_pairs={{0,48},{16,0},{32,16},{48,32},{64,112},{80,64},{96,80},{112,96},{1... | collective-permute-start | bytes 1572872 | tf_op jit(solution)/shard_map/ppermute | solution.py:296
  40.0 12.7 %all-to-all-start.1 = ((bf16[8,16,320]{2,1,0:T(8,128)(2,1)}), bf16[8,16,320]{2,1,0:T(8,128)(2,1)S(1)}, u32[]{:S(2)}, u32[]{:S(2)}) async-start(bf16[8,16,320]{2,1,0:T(8,128)(2,1)} %get-tuple-element.24), calls=%async_computation.1 | async-start | bytes 196608 | tf_op jit(solution)/shard_map/all_to_all | solution.py:273
  44.1 36.7 %collective-permute-start.7 = (bf16[320,1024]{1,0:T(8,128)(2,1)S(1)}, bf16[320,1024]{1,0:T(8,128)(2,1)S(1)}, u32[]{:S(2)}, u32[]{:S(2)}) collective-permute-start(bf16[320,1024]{1,0:T(8,128)(2,1)S(1)} %turn.1.refs_0_), channel_id=1, source_target_pairs={{0,16},{16,32},{32,48},{48,0},{64,80},{80,96},{96,112},{112,64},{1... | collective-permute-start | bytes 1966088 | tf_op jit(solution)/shard_map/ppermute | solution.py:296
  45.6 35.2 %collective-permute-start.8 = (bf16[320,1024]{1,0:T(8,128)(2,1)S(1)}, bf16[320,1024]{1,0:T(8,128)(2,1)S(1)}, u32[]{:S(2)}, u32[]{:S(2)}) collective-permute-start(bf16[320,1024]{1,0:T(8,128)(2,1)S(1)} %turn.1.refs_0_), channel_id=1, source_target_pairs={{0,48},{16,0},{32,16},{48,32},{64,112},{80,64},{96,80},{112,96},{1... | collective-permute-start | bytes 1966088 | tf_op jit(solution)/shard_map/ppermute | solution.py:296
  49.7 31.1 %collective-permute-start.9 = (bf16[320,1024]{1,0:T(8,128)(2,1)S(1)}, bf16[320,1024]{1,0:T(8,128)(2,1)S(1)}, u32[]{:S(2)}, u32[]{:S(2)}) collective-permute-start(bf16[320,1024]{1,0:T(8,128)(2,1)S(1)} %turn.1.refs_0_), channel_id=1, source_target_pairs={{0,64},{16,80},{32,96},{48,112},{64,0},{80,16},{96,32},{112,48},{1... | collective-permute-start | bytes 1966088 | tf_op jit(solution)/shard_map/ppermute | solution.py:296
  53.3 0.8 copy-start.2
  54.1 26.7 %collective-permute-start.5 = (bf16[1024,256]{1,0:T(8,128)(2,1)}, bf16[1024,256]{1,0:T(8,128)(2,1)S(1)}, u32[]{:S(2)}, u32[]{:S(2)}) collective-permute-start(bf16[1024,256]{1,0:T(8,128)(2,1)} %copy-done.2), channel_id=1, source_target_pairs={{0,16},{16,32},{32,48},{48,0},{64,80},{80,96},{96,112},{112,64},{1... | collective-permute-start | bytes 1572872 | tf_op jit(solution)/shard_map/ppermute | solution.py:296
  54.7 26.1 %collective-permute-start.6 = (bf16[1024,256]{1,0:T(8,128)(2,1)}, bf16[1024,256]{1,0:T(8,128)(2,1)}, u32[]{:S(2)}, u32[]{:S(2)}) collective-permute-start(bf16[1024,256]{1,0:T(8,128)(2,1)} %copy-done.2), channel_id=1, source_target_pairs={{0,48},{16,0},{32,16},{48,32},{64,112},{80,64},{96,80},{112,96},{1... | collective-permute-start | bytes 1572872 | tf_op jit(solution)/shard_map/ppermute | solution.py:296
  56.9 16.2 %all-to-all-start.2 = ((bf16[16,16,320]{2,1,0:T(8,128)(2,1)}), bf16[16,16,320]{2,1,0:T(8,128)(2,1)S(1)}, u32[]{:S(2)}, u32[]{:S(2)}) async-start(bf16[16,16,320]{2,1,0:T(8,128)(2,1)} %get-tuple-element.26), calls=%async_computation.2 | async-start | bytes 393216 | tf_op jit(solution)/shard_map/all_to_all | solution.py:273
  65.1 1.0 copy-start.3
  73.1 1.6 %copy-start = (bf16[8,256,512]{2,1,0:T(8,128)(2,1)S(1)}, bf16[8,256,512]{2,1,0:T(8,128)(2,1)}, u32[]{:S(2)}) copy-start(bf16[8,256,512]{2,1,0:T(8,128)(2,1)} %refs_4_.1) | copy-start | bytes 6291460
  74.7 1.6 %copy-start.1 = (bf16[8,256,512]{2,1,0:T(8,128)(2,1)S(1)}, bf16[8,256,512]{2,1,0:T(8,128)(2,1)}, u32[]{:S(2)}) copy-start(bf16[8,256,512]{2,1,0:T(8,128)(2,1)} %refs_5_.1) | copy-start | bytes 6291460
  80.8 15.6 %collective-permute-start.16 = (bf16[320,1024]{1,0:T(8,128)(2,1)S(1)}, bf16[320,1024]{1,0:T(8,128)(2,1)}, u32[]{:S(2)}, u32[]{:S(2)}) collective-permute-start(bf16[320,1024]{1,0:T(8,128)(2,1)S(1)} %get-tuple-element.33.refs_1_), channel_id=1, source_target_pairs={{0,64},{16,80},{32,96},{48,112},{64,0},{80,16},{96,32},{112,48},{1... | collective-permute-start | bytes 1966088 | tf_op jit(solution)/shard_map/ppermute | solution.py:296
  82.1 20.7 %collective-permute-start.12 = (bf16[1024,256]{1,0:T(8,128)(2,1)}, bf16[1024,256]{1,0:T(8,128)(2,1)}, u32[]{:S(2)}, u32[]{:S(2)}) collective-permute-start(bf16[1024,256]{1,0:T(8,128)(2,1)} %collective-permute-done.10.refs_0_), channel_id=1, source_target_pairs={{0,16},{16,32},{32,48},{48,0},{64,80},{80,96},{96,112},{112,64},{1... | collective-permute-start | bytes 1572872 | tf_op jit(solution)/shard_map/ppermute | solution.py:296
  82.3 20.5 %collective-permute-start.13 = (bf16[1024,256]{1,0:T(8,128)(2,1)}, bf16[1024,256]{1,0:T(8,128)(2,1)}, u32[]{:S(2)}, u32[]{:S(2)}) collective-permute-start(bf16[1024,256]{1,0:T(8,128)(2,1)} %get-tuple-element.29.refs_1_), channel_id=1, source_target_pairs={{0,48},{16,0},{32,16},{48,32},{64,112},{80,64},{96,80},{112,96},{1... | collective-permute-start | bytes 1572872 | tf_op jit(solution)/shard_map/ppermute | solution.py:296
  84.7 17.6 %all-to-all-start.3 = ((bf16[16,48,128]{2,1,0:T(8,128)(2,1)}), bf16[16,48,128]{2,1,0:T(8,128)(2,1)S(1)}, u32[]{:S(2)}, u32[]{:S(2)}) async-start(bf16[16,48,128]{2,1,0:T(8,128)(2,1)} %get-tuple-element.28), calls=%async_computation.3 | async-start | bytes 393216 | tf_op jit(solution)/shard_map/all_to_all | solution.py:273
  90.7 26.5 %collective-permute-start.14 = (bf16[320,1024]{1,0:T(8,128)(2,1)S(1)}, bf16[320,1024]{1,0:T(8,128)(2,1)}, u32[]{:S(2)}, u32[]{:S(2)}) collective-permute-start(bf16[320,1024]{1,0:T(8,128)(2,1)S(1)} %get-tuple-element.32.refs_0_), channel_id=1, source_target_pairs={{0,16},{16,32},{32,48},{48,0},{64,80},{80,96},{96,112},{112,64},{1... | collective-permute-start | bytes 1966088 | tf_op jit(solution)/shard_map/ppermute | solution.py:296
  90.7 26.5 %collective-permute-start.15 = (bf16[320,1024]{1,0:T(8,128)(2,1)S(1)}, bf16[320,1024]{1,0:T(8,128)(2,1)}, u32[]{:S(2)}, u32[]{:S(2)}) collective-permute-start(bf16[320,1024]{1,0:T(8,128)(2,1)S(1)} %get-tuple-element.32.refs_0_), channel_id=1, source_target_pairs={{0,64},{16,80},{32,96},{48,112},{64,0},{80,16},{96,32},{112,48},{1... | collective-permute-start | bytes 1966088 | tf_op jit(solution)/shard_map/ppermute | solution.py:296
  96.5 20.8 %collective-permute-start.17 = (bf16[320,1024]{1,0:T(8,128)(2,1)}, bf16[320,1024]{1,0:T(8,128)(2,1)}, u32[]{:S(2)}, u32[]{:S(2)}) collective-permute-start(bf16[320,1024]{1,0:T(8,128)(2,1)} %collective-permute-done.16.refs_2_), channel_id=1, source_target_pairs={{0,48},{16,0},{32,16},{48,32},{64,112},{80,64},{96,80},{112,96},{1... | collective-permute-start | bytes 1966088 | tf_op jit(solution)/shard_map/ppermute | solution.py:296
  109.1 13.3 %all-to-all-start.4 = ((bf16[16,16,512]{2,1,0:T(8,128)(2,1)}), bf16[16,16,512]{2,1,0:T(8,128)(2,1)S(1)}, u32[]{:S(2)}, u32[]{:S(2)}) async-start(bf16[16,16,512]{2,1,0:T(8,128)(2,1)} %bitcast.10), calls=%async_computation.4 | async-start | bytes 524288 | tf_op jit(solution)/shard_map/all_to_all | solution.py:273

commit v7 on v6

--- a/solution.py
+++ b/solution.py
@@ -15,11 +15,18 @@
 FLOOR = -1e30
 
 
-def pack_kernel(groups, after_ref, qkv_ref, out_ref, packed_ref):
+def pack_kernel(groups, after_ref, qkv_in, out_in, packed_ref, qkv_ref, out_ref, sems):
     query_width = QH * HD // groups
     kv_width = KVH * HD // groups
     rows = qkv_ref.shape[0]
     quarter = rows // 4
+    copies = []
+    for i, (source, target) in enumerate(((qkv_in, qkv_ref), (out_in, out_ref))):
+        copies.append(pltpu.make_async_copy(source, target, sems.at[i]))
+    for copy in copies:
+        copy.start()
+    for copy in copies:
+        copy.wait()
     for g in range(groups):
         keys_at = QH * HD + g * kv_width
         values_at = QH * HD + KVH * HD + g * kv_width
@@ -54,7 +61,15 @@
     return queries, pairs
 
 
-def norm_kernel(states_ref, gain_ref, own_ref, send_ref):
+def norm_kernel(states_in, gain_in, own_ref, send_ref, states_ref, gain_ref, sems):
+    copies = [
+        pltpu.make_async_copy(states_in, states_ref, sems.at[0]),
+        pltpu.make_async_copy(gain_in, gain_ref, sems.at[1]),
+    ]
+    for copy in copies:
+        copy.start()
+    for copy in copies:
+        copy.wait()
     states = jnp.concatenate([states_ref[0], states_ref[1]], 0).astype(jnp.float32)
     normed = (
         states
@@ -166,10 +181,22 @@
     )(*parts, *((whole,) if continued else ()))
 
 
-def attend_kernel(scale, lengths_ref, cosine_ref, sine_ref, new_ref, key_ref, value_ref, message_ref, query_s, message_s):
+def attend_kernel(scale, lengths_ref, cosine_ref, sine_ref, new_ref, key_ref, value_ref, message_ref, query_s, message_s, key_s, value_s, sems):
     groups, slots, _ = new_ref.shape
     rows, span, _ = key_ref.shape
     per_row = query_s.shape[0] // rows
+    key_copies, value_copies = (
+        [
+            pltpu.make_async_copy(
+                ref.at[pl.ds(r, 4)], scratch.at[pl.ds(r, 4)], sems.at[i, r]
+            )
+            for r in range(0, rows, 4)
+        ]
+        for i, (ref, scratch) in enumerate(((key_ref, key_s), (value_ref, value_s)))
+    )
+    for key_copy, value_copy in zip(key_copies, value_copies):
+        key_copy.start()
+        value_copy.start()
     cosine, sine = cosine_ref[...], sine_ref[...]
 
     def turned(values):
@@ -213,7 +240,9 @@
             )
 
         valid = position < lengths_ref[r]
-        scores = jnp.where(valid, product(key_ref[r]), FLOOR)
+        if r % 4 == 0:
+            key_copies[r // 4].wait()
+        scores = jnp.where(valid, product(key_s[r]), FLOOR)
         fresh = (slot % rows == r) & (slot // rows <= step) & (member == 0)
         fresh_scores = jnp.where(fresh, product(new_keys), FLOOR)
         highest = jnp.maximum(
@@ -225,8 +254,10 @@
         weights = jnp.where(valid, jnp.exp(scores - highest), 0.0)
         fresh_weights = jnp.where(fresh, jnp.exp(fresh_scores - highest), 0.0)
         total = jnp.sum(weights, 1, keepdims=True) + jnp.sum(fresh_weights, 1, keepdims=True)
+        if r % 4 == 0:
+            value_copies[r // 4].wait()
         mixed = jnp.dot(
-            weights.astype(jnp.bfloat16), value_ref[r], preferred_element_type=jnp.float32
+            weights.astype(jnp.bfloat16), value_s[r], preferred_element_type=jnp.float32
         ) + jnp.dot(
             fresh_weights.astype(jnp.bfloat16), new_values, preferred_element_type=jnp.float32
         )
@@ -287,6 +318,11 @@
     vmem = pl.BlockSpec(memory_space=pltpu.VMEM)
     smem = pl.BlockSpec(memory_space=pltpu.SMEM)
     anywhere = pl.BlockSpec(memory_space=pl.ANY)
+    in_hbm = pl.BlockSpec(memory_space=pltpu.HBM)
+
+    def stay(value):
+        return pltpu.with_memory_space_constraint(value, pltpu.HBM)
+
     across = [(i, i ^ 4) for i in range(replicas)]
     ahead = [(i, (i & 4) | ((i + 1) & 3)) for i in range(replicas)]
     behind = [(i, (i & 4) | ((i + 3) & 3)) for i in range(replicas)]
@@ -299,17 +335,28 @@
     own_states, other_states = pl.pallas_call(
         norm_kernel,
         out_shape=(jax.ShapeDtypeStruct((replicas // 2, slots, share), jnp.bfloat16),) * 2,
+        in_specs=[in_hbm] * 2,
+        scratch_shapes=[
+            pltpu.VMEM(hidden.shape, hidden.dtype),
+            pltpu.VMEM(norm_gain.shape, norm_gain.dtype),
+            pltpu.SemaphoreType.DMA((2,)),
+        ],
         compiler_params=pltpu.CompilerParams(vmem_limit_bytes=6 << 20),
         name="norm",
-    )(hidden, norm_gain)
+    )(stay(hidden), stay(norm_gain))
     cross_states = send(other_states, across)
     packed = pl.pallas_call(
         lambda *refs: pack_kernel(groups, *refs),
         out_shape=jax.ShapeDtypeStruct((groups, fresh_qkv.shape[0] * 9 // 4, query_width), fresh_qkv.dtype),
-        in_specs=[anywhere] + [vmem] * 2,
+        in_specs=[anywhere] + [in_hbm] * 2,
+        scratch_shapes=[
+            pltpu.VMEM(fresh_qkv.shape, fresh_qkv.dtype),
+            pltpu.VMEM(fresh_out.shape, fresh_out.dtype),
+            pltpu.SemaphoreType.DMA((2,)),
+        ],
         compiler_params=pltpu.CompilerParams(vmem_limit_bytes=6 << 20),
         name="pack",
-    )(own_states, fresh_qkv, fresh_out)
+    )(own_states, stay(fresh_qkv), stay(fresh_out))
     packed, cross_states = hold(packed, cross_states)
     packed = exchange(packed, "tensor")
 
@@ -342,12 +389,12 @@
             jax.ShapeDtypeStruct((groups, slots, group_width), jnp.bfloat16),
             *(jax.ShapeDtypeStruct(v.shape, v.dtype) for v in moved),
         ),
-        in_specs=[vmem] * 2 + [anywhere],
-        out_specs=(vmem,) + (anywhere,),
+        in_specs=[vmem] * 2 + [in_hbm],
+        out_specs=(vmem, in_hbm),
         input_output_aliases={2: 1},
         compiler_params=pltpu.CompilerParams(vmem_limit_bytes=3 << 20),
         name="sum",
-    )(terms, qkv_bias.reshape(1, group_width), *moved)
+    )(terms, qkv_bias.reshape(1, group_width), stay(out_across))
     gathered = exchange(projected, "tensor")
 
     out_cross_low, out_cross_high = send(out_across, ahead), send(out_across, behind)
@@ -376,14 +423,17 @@
     message = pl.pallas_call(
         lambda *refs: attend_kernel(score_scale, *refs),
         out_shape=jax.ShapeDtypeStruct((groups, 3 * slots, HD), jnp.bfloat16),
-        in_specs=[smem] + [vmem] * 5,
+        in_specs=[smem] + [vmem] * 3 + [in_hbm] * 2,
         scratch_shapes=[
             pltpu.VMEM((slots * QH, HD), jnp.float32),
             pltpu.VMEM((groups, 3 * slots, HD), jnp.float32),
+            pltpu.VMEM(key_cache.shape, key_cache.dtype),
+            pltpu.VMEM(value_cache.shape, value_cache.dtype),
+            pltpu.SemaphoreType.DMA((2, row_count)),
         ],
         compiler_params=pltpu.CompilerParams(vmem_limit_bytes=14 << 20),
         name="attend",
-    )(lengths, cosine, sine, gathered, key_cache, value_cache)
+    )(lengths, cosine, sine, gathered, stay(key_cache), stay(value_cache))
     message, out_cross_low, out_cross_high, qkv_low, qkv_high, qkv_across, grouped_out = hold(
         message, out_cross_low, out_cross_high, qkv_low, qkv_high, qkv_across, grouped_out
     )

time: 124 us -> 122 us (0.984)
  local copies, waits for them, and re-layouts: 9.68 us -> 1.91 us
  Pallas kernels: 23.8 us -> 27.6 us
    unnamed x20 -> x8, local copies, waits for them, and re-layouts: 8.81 us -> 1.06 us
    all_to_all x5, starting transfers between devices: 31.5 us -> 33.3 us  [exchange(): return lax.all_to_all(blocks, axis, split_axis=0, concat_axis=0, tiled=True)]
    pallas_call x1, Pallas kernels: 4.48 us -> 6.1 us  [on_device(): pl.pallas_call(lambda *refs: attend_kernel(score_scale, *refs), out_shape...]
    pallas_call x1, Pallas kernels: 1.28 us -> 2.54 us  [on_device(): pl.pallas_call(lambda *refs: pack_kernel(groups, *refs), out_shape=jax.Sh...]
  transfers between devices with their start and end apart: 23 -> 23, of which waited for: 10 -> 11; matrix products, arithmetic and copies ran while one was open for 4% -> 4% of each run, Pallas kernels for 18% -> 20%
where the time goes in v7:
time: 122 us; the launch traced here: 121 us
  starting transfers between devices  52.9 us (43%)
  waiting for transfers between devices  34.2 us (28%)
  Pallas kernels  27.6 us (23%)
  matrix products  3.38 us (3%)
  local copies, waits for them, and re-layouts  1.91 us (2%)
    all_to_all x5, starting transfers between devices, exchange(): return lax.all_to_all(blocks, axis, split_axis=0, concat_axis=0, tiled=True)  33.3 us
    all_to_all x5, waiting for transfers between devices, exchange(): return lax.all_to_all(blocks, axis, split_axis=0, concat_axis=0, tiled=True)  21.8 us
    ppermute x18, starting transfers between devices, send(): return lax.ppermute(value, 'dp', pairs)  19.6 us
    pallas_call x7, Pallas kernels, place(): pl.pallas_call(lambda *refs: place_kernel(axis, where, mark, *refs), out_...  14.6 us
    ppermute x18, waiting for transfers between devices, send(): return lax.ppermute(value, 'dp', pairs)  12.5 us
    pallas_call x1, Pallas kernels, on_device(): pl.pallas_call(lambda *refs: attend_kernel(score_scale, *refs), out_shape...  6.1 us
    dot_general x1, matrix products, on_device(): jnp.dot(attended, grouped_out.T, preferred_element_type=jnp.float32)  3.38 us
    pallas_call x1, Pallas kernels, on_device(): pl.pallas_call(lambda *refs: pack_kernel(groups, *refs), out_shape=jax.Sh...  2.54 us
  transfers between devices with their start and end apart: 23, of which 11 were waited for; matrix products, arithmetic and copies ran while one was open for 4% of the time, Pallas kernels for 20%

profile of v7, /device:TPU:1, one launch (start us, length us, event | category | flops | bytes accessed | tf_op | source)
XLA Modules:
  0.0 121.1 jit_solution(5510258278152580956)
XLA Ops:
  0.6 1.2 norm.1
  1.8 2.1 %collective-permute-start = (bf16[4,16,1024]{2,1,0:T(8,128)(2,1)S(1)}, bf16[4,16,1024]{2,1,0:T(8,128)(2,1)S(1)}, u32[]{:S(2)}, u32[]{:S(2)}) collective-permute-start(bf16[4,16,1024]{2,1,0:T(8,128)(2,1)S(1)} %get-tuple-element.21), channel_id=1, source_target_pairs={{0,64},{16,80},{32,96},{48,112},{64,0},{80,16},{96,32},{112,48},{1... | collective-permute-start | bytes 393224 | tf_op jit(solution)/shard_map/ppermute | solution.py:332
  4.0 2.5 %pack.1.refs_0_ = bf16[16,144,256]{2,1,0:T(8,128)(2,1)} custom-call(bf16[4,16,1024]{2,1,0:T(8,128)(2,1)S(1)} %get-tuple-element.20.refs_0_.own, bf16[64,5120]{1,0:T(8,128)(2,1)} %refs_1_.1, bf16[64,4096]{1,0:T(8,128)(2,1)} %refs_2_.1), custom_call_target="tpu_custom_call" | custom-call | tf_op jit(solution)/shard_map/pack/pallas_call | solution.py:348
  6.7 9.8 %all-to-all-start = ((bf16[16,144,256]{2,1,0:T(8,128)(2,1)}), bf16[16,144,256]{2,1,0:T(8,128)(2,1)S(1)}, u32[]{:S(2)}, u32[]{:S(2)}) async-start(bf16[16,144,256]{2,1,0:T(8,128)(2,1)} %get-tuple-element.23), calls=%async_computation | async-start | bytes 2359296 | tf_op jit(solution)/shard_map/all_to_all | solution.py:304
  16.5 3.0 %collective-permute-start.3 = (bf16[2,16,1024]{2,1,0:T(8,128)(2,1)S(1)}, bf16[2,16,1024]{2,1,0:T(8,128)(2,1)S(1)}, u32[]{:S(2)}, u32[]{:S(2)}) collective-permute-start(bf16[2,16,1024]{2,1,0:T(8,128)(2,1)S(1)} %pad_maximum_fusion.2), channel_id=1, source_target_pairs={{0,32},{16,48},{32,0},{48,16},{64,96},{80,112},{96,64},{112,80},{1... | collective-permute-start | bytes 196616 | tf_op jit(solution)/shard_map/ppermute | solution.py:332
  19.5 0.8 collective-permute-start.2
  20.4 0.8 collective-permute-start.1
  21.1 0.6 collective-permute-done.3.far
  21.7 1.7 %collective-permute-done.2.high = bf16[2,16,1024]{2,1,0:T(8,128)(2,1)S(1)} collective-permute-done((bf16[2,16,1024]{2,1,0:T(8,128)(2,1)S(1)}, bf16[2,16,1024]{2,1,0:T(8,128)(2,1)S(1)}, u32[]{:S(2)}, u32[]{:S(2)}) %collective-permute-start.2) | collective-permute-done | bytes 65568 | tf_op jit(solution)/shard_map/ppermute | solution.py:332
  23.4 1.6 %collective-permute-done.1.low = bf16[2,16,1024]{2,1,0:T(8,128)(2,1)S(1)} collective-permute-done((bf16[2,16,1024]{2,1,0:T(8,128)(2,1)S(1)}, bf16[2,16,1024]{2,1,0:T(8,128)(2,1)S(1)}, u32[]{:S(2)}, u32[]{:S(2)}) %collective-permute-start.1) | collective-permute-done | bytes 65568 | tf_op jit(solution)/shard_map/ppermute | solution.py:332
  25.1 10.0 %all-to-all-done.packed_ref = bf16[16,144,256]{2,1,0:T(8,128)(2,1)S(1)} async-done(((bf16[16,144,256]{2,1,0:T(8,128)(2,1)}), bf16[16,144,256]{2,1,0:T(8,128)(2,1)S(1)}, u32[]{:S(2)}, u32[]{:S(2)}) %all-to-all-start) | async-done | bytes 1179680 | tf_op jit(solution)/shard_map/all_to_all | solution.py:304
  35.1 1.1 terms.1
  36.2 0.3 collective-permute-start.4
  36.5 1.3 %collective-permute-start.10 = (bf16[1024,256]{1,0:T(8,128)(2,1)}, bf16[1024,256]{1,0:T(8,128)(2,1)}, u32[]{:S(2)}, u32[]{:S(2)}) collective-permute-start(bf16[1024,256]{1,0:T(8,128)(2,1)} %get-tuple-element.25.refs_0_), channel_id=1, source_target_pairs={{0,16},{16,32},{32,48},{48,0},{64,80},{80,96},{96,112},{112,64},{1... | collective-permute-start | bytes 1572872 | tf_op jit(solution)/shard_map/ppermute | solution.py:332
  37.8 1.4 %collective-permute-start.11 = (bf16[1024,256]{1,0:T(8,128)(2,1)}, bf16[1024,256]{1,0:T(8,128)(2,1)}, u32[]{:S(2)}, u32[]{:S(2)}) collective-permute-start(bf16[1024,256]{1,0:T(8,128)(2,1)} %get-tuple-element.25.refs_0_), channel_id=1, source_target_pairs={{0,48},{16,0},{32,16},{48,32},{64,112},{80,64},{96,80},{112,96},{1... | collective-permute-start | bytes 1572872 | tf_op jit(solution)/shard_map/ppermute | solution.py:332
  39.3 3.8 %all-to-all-start.1 = ((bf16[8,16,320]{2,1,0:T(8,128)(2,1)}), bf16[8,16,320]{2,1,0:T(8,128)(2,1)S(1)}, u32[]{:S(2)}, u32[]{:S(2)}) async-start(bf16[8,16,320]{2,1,0:T(8,128)(2,1)} %get-tuple-element.24), calls=%async_computation.1 | async-start | bytes 196608 | tf_op jit(solution)/shard_map/all_to_all | solution.py:304
  43.1 0.3 turn.1.refs_0_
  43.4 1.5 %collective-permute-start.7 = (bf16[320,1024]{1,0:T(8,128)(2,1)S(1)}, bf16[320,1024]{1,0:T(8,128)(2,1)S(1)}, u32[]{:S(2)}, u32[]{:S(2)}) collective-permute-start(bf16[320,1024]{1,0:T(8,128)(2,1)S(1)} %turn.1.refs_0_), channel_id=1, source_target_pairs={{0,16},{16,32},{32,48},{48,0},{64,80},{80,96},{96,112},{112,64},{1... | collective-permute-start | bytes 1966088 | tf_op jit(solution)/shard_map/ppermute | solution.py:332
  44.9 1.3 %collective-permute-start.8 = (bf16[320,1024]{1,0:T(8,128)(2,1)S(1)}, bf16[320,1024]{1,0:T(8,128)(2,1)S(1)}, u32[]{:S(2)}, u32[]{:S(2)}) collective-permute-start(bf16[320,1024]{1,0:T(8,128)(2,1)S(1)} %turn.1.refs_0_), channel_id=1, source_target_pairs={{0,48},{16,0},{32,16},{48,32},{64,112},{80,64},{96,80},{112,96},{1... | collective-permute-start | bytes 1966088 | tf_op jit(solution)/shard_map/ppermute | solution.py:332
  46.2 2.8 %collective-permute-done.4.refs_0_ = bf16[1024,256]{1,0:T(8,128)(2,1)S(1)} collective-permute-done((bf16[1024,256]{1,0:T(8,128)(2,1)}, bf16[1024,256]{1,0:T(8,128)(2,1)S(1)}, u32[]{:S(2)}, u32[]{:S(2)}) %collective-permute-start.4) | collective-permute-done | bytes 524320 | tf_op jit(solution)/shard_map/ppermute | solution.py:332
  49.0 0.3 collective-permute-start.9
  49.4 2.6 %all-to-all-done.1.terms_ref = bf16[8,16,320]{2,1,0:T(8,128)(2,1)S(1)} async-done(((bf16[8,16,320]{2,1,0:T(8,128)(2,1)}), bf16[8,16,320]{2,1,0:T(8,128)(2,1)S(1)}, u32[]{:S(2)}, u32[]{:S(2)}) %all-to-all-start.1) | async-done | bytes 81952 | tf_op jit(solution)/shard_map/all_to_all | solution.py:304
  52.0 0.7 sum.1
  52.7 0.5 collective-permute-start.5
  53.2 2.1 %collective-permute-start.6 = (bf16[1024,256]{1,0:T(8,128)(2,1)}, bf16[1024,256]{1,0:T(8,128)(2,1)}, u32[]{:S(2)}, u32[]{:S(2)}) collective-permute-start(bf16[1024,256]{1,0:T(8,128)(2,1)} %get-tuple-element.27.refs_1_), channel_id=1, source_target_pairs={{0,48},{16,0},{32,16},{48,32},{64,112},{80,64},{96,80},{112,96},{1... | collective-permute-start | bytes 1572872 | tf_op jit(solution)/shard_map/ppermute | solution.py:332
  55.4 8.0 %all-to-all-start.2 = ((bf16[16,16,320]{2,1,0:T(8,128)(2,1)}), bf16[16,16,320]{2,1,0:T(8,128)(2,1)S(1)}, u32[]{:S(2)}, u32[]{:S(2)}) async-start(bf16[16,16,320]{2,1,0:T(8,128)(2,1)} %get-tuple-element.26), calls=%async_computation.2 | async-start | bytes 393216 | tf_op jit(solution)/shard_map/all_to_all | solution.py:304
  63.6 1.0 copy-done.1
  64.7 2.0 %place.7.refs_2_ = bf16[8192,256]{1,0:T(8,128)(2,1)} custom-call(bf16[1024,256]{1,0:T(8,128)(2,1)} %get-tuple-element.25.refs_0_, bf16[1024,256]{1,0:T(8,128)(2,1)S(1)} %copy-done.1), custom_call_target="tpu_custom_call" | custom-call | tf_op jit(solution)/shard_map/place/pallas_call | solution.py:170
  66.7 2.2 %place.8.refs_6_ = bf16[8192,256]{1,0:T(8,128)(2,1)} custom-call(bf16[1024,256]{1,0:T(8,128)(2,1)} %collective-permute-done.10.refs_0_, bf16[1024,256]{1,0:T(8,128)(2,1)} %collective-permute-done.11.refs_1_, bf16[8192,256]{1,0:T(8,128)(2,1)} %place.7.refs_2_), custom_call_target="tpu_custom_call", output_to_operand_aliasing={{}: (2, {})} | custom-call | tf_op jit(solution)/shard_map/place/pallas_call | solution.py:170
  68.9 2.8 %all-to-all-done.2.refs_3_ = bf16[16,16,320]{2,1,0:T(8,128)(2,1)S(1)} async-done(((bf16[16,16,320]{2,1,0:T(8,128)(2,1)}), bf16[16,16,320]{2,1,0:T(8,128)(2,1)S(1)}, u32[]{:S(2)}, u32[]{:S(2)}) %all-to-all-start.2) | async-done | bytes 163872 | tf_op jit(solution)/shard_map/all_to_all | solution.py:304
  71.6 6.1 %attend.1.refs_0_ = bf16[16,48,128]{2,1,0:T(8,128)(2,1)} custom-call(s32[8]{0:T(128)S(1)} %copy-done.2, f32[16,128]{1,0:T(8,128)S(1)} %get-tuple-element.46.refs_1_, f32[16,128]{1,0:T(8,128)S(1)} %get-tuple-element.47.refs_2_, bf16[16,16,320]{2,1,0:T(8,128)(2,1)S(1)} %all-to-all-done.2.refs_3_, bf16[8,256,512]{2,1,0:T(8,128)(2,1)} %refs_4_.1, ...), custom_call_target="tpu_custom_call" | custom-call | tf_op jit(solution)/shard_map/attend/pallas_call | solution.py:423
  77.8 1.2 %collective-permute-start.16 = (bf16[320,1024]{1,0:T(8,128)(2,1)S(1)}, bf16[320,1024]{1,0:T(8,128)(2,1)}, u32[]{:S(2)}, u32[]{:S(2)}) collective-permute-start(bf16[320,1024]{1,0:T(8,128)(2,1)S(1)} %get-tuple-element.33.refs_1_), channel_id=1, source_target_pairs={{0,64},{16,80},{32,96},{48,112},{64,0},{80,16},{96,32},{112,48},{1... | collective-permute-start | bytes 1966088 | tf_op jit(solution)/shard_map/ppermute | solution.py:332
  79.1 0.2 collective-permute-start.12
  79.2 2.5 %collective-permute-start.13 = (bf16[1024,256]{1,0:T(8,128)(2,1)}, bf16[1024,256]{1,0:T(8,128)(2,1)}, u32[]{:S(2)}, u32[]{:S(2)}) collective-permute-start(bf16[1024,256]{1,0:T(8,128)(2,1)} %get-tuple-element.29.refs_1_), channel_id=1, source_target_pairs={{0,48},{16,0},{32,16},{48,32},{64,112},{80,64},{96,80},{112,96},{1... | collective-permute-start | bytes 1572872 | tf_op jit(solution)/shard_map/ppermute | solution.py:332
  81.7 6.0 %all-to-all-start.3 = ((bf16[16,48,128]{2,1,0:T(8,128)(2,1)}), bf16[16,48,128]{2,1,0:T(8,128)(2,1)S(1)}, u32[]{:S(2)}, u32[]{:S(2)}) async-start(bf16[16,48,128]{2,1,0:T(8,128)(2,1)} %get-tuple-element.28), calls=%async_computation.3 | async-start | bytes 393216 | tf_op jit(solution)/shard_map/all_to_all | solution.py:304
  87.8 5.5 %collective-permute-done.16.refs_2_ = bf16[320,1024]{1,0:T(8,128)(2,1)} collective-permute-done((bf16[320,1024]{1,0:T(8,128)(2,1)S(1)}, bf16[320,1024]{1,0:T(8,128)(2,1)}, u32[]{:S(2)}, u32[]{:S(2)}) %collective-permute-start.16) | collective-permute-done | bytes 655392 | tf_op jit(solution)/shard_map/ppermute | solution.py:332
  93.3 2.0 %place.9.refs_2_ = bf16[8192,256]{1,0:T(8,128)(2,1)} custom-call(bf16[1024,256]{1,0:T(8,128)(2,1)S(1)} %get-tuple-element.30.refs_0_, bf16[1024,256]{1,0:T(8,128)(2,1)} %get-tuple-element.29.refs_1_, bf16[8192,256]{1,0:T(8,128)(2,1)} %get-tuple-element.31.refs_2_), custom_call_target="tpu_custom_call", output_to_operand_aliasing={{}: (2, {})} | custom-call | tf_op jit(solution)/shard_map/place/pallas_call | solution.py:170
  95.4 4.0 %all-to-all-done.3.message_ref = bf16[16,48,128]{2,1,0:T(8,128)(2,1)S(1)} async-done(((bf16[16,48,128]{2,1,0:T(8,128)(2,1)}), bf16[16,48,128]{2,1,0:T(8,128)(2,1)S(1)}, u32[]{:S(2)}, u32[]{:S(2)}) %all-to-all-start.3) | async-done | bytes 196640 | tf_op jit(solution)/shard_map/all_to_all | solution.py:304
  99.4 0.4 merge.1
  99.8 2.2 %place.10 = bf16[8192,256]{1,0:T(8,128)(2,1)} custom-call(bf16[1024,256]{1,0:T(8,128)(2,1)} %collective-permute-done.12.refs_0_, bf16[1024,256]{1,0:T(8,128)(2,1)} %collective-permute-done.13.refs_1_, bf16[8192,256]{1,0:T(8,128)(2,1)} %place.9.refs_2_), custom_call_target="tpu_custom_call", output_to_operand_aliasing={{}: (2, {})} | custom-call | tf_op jit(solution)/shard_map/place/pallas_call | solution.py:170
  101.9 3.4 %convolution_convert_fusion = bf16[16,8192]{1,0:T(8,128)(2,1)S(1)} fusion(bf16[16,256]{1,0:T(8,128)(2,1)S(1)} %merge.1, bf16[8192,256]{1,0:T(8,128)(2,1)} %place.10), kind=kOutput, calls=%fused_computation | convolution fusion | flops 67239936 | bytes 4464640 | tf_op jit(solution)/shard_map/dot_general | solution.py:484
  105.3 0.7 copy.29
  106.1 5.7 %all-to-all-start.4 = ((bf16[16,16,512]{2,1,0:T(8,128)(2,1)}), bf16[16,16,512]{2,1,0:T(8,128)(2,1)S(1)}, u32[]{:S(2)}, u32[]{:S(2)}) async-start(bf16[16,16,512]{2,1,0:T(8,128)(2,1)} %bitcast.10), calls=%async_computation.4 | async-start | bytes 524288 | tf_op jit(solution)/shard_map/all_to_all | solution.py:304
  111.8 1.1 place.11.refs_3_
  112.9 2.4 %place.12.refs_3_ = bf16[320,8192]{1,0:T(8,128)(2,1)} custom-call(bf16[320,1024]{1,0:T(8,128)(2,1)S(1)} %get-tuple-element.32.refs_0_, bf16[320,1024]{1,0:T(8,128)(2,1)S(1)} %get-tuple-element.33.refs_1_, bf16[320,1024]{1,0:T(8,128)(2,1)} %collective-permute-done.16.refs_2_, bf16[320,8192]{1,0:T(8,128)(2,1)} %place.11.refs_3_), custom_call_target="tpu_custom_call", output_to_operand_aliasing={{}: (3, {})} | custom-call | tf_op jit(solution)/shard_map/place/pallas_call | solution.py:170
  115.3 2.8 %place.13 = (bf16[320,8192]{1,0:T(8,128)(2,1)}, f32[8,128]{1,0:T(8,128)S(1)}) custom-call(bf16[320,1024]{1,0:T(8,128)(2,1)} %collective-permute-done.14.refs_0_, bf16[320,1024]{1,0:T(8,128)(2,1)} %collective-permute-done.15.refs_1_, bf16[320,1024]{1,0:T(8,128)(2,1)} %collective-permute-done.17.refs_2_, ...), custom_call_target="tpu_custom_call", output_to_operand_aliasing={{0}: (3, {})} | custom-call | tf_op jit(solution)/shard_map/place/pallas_call | solution.py:170
  118.1 2.4 %all-to-all-done.4.terms_ref = bf16[16,16,512]{2,1,0:T(8,128)(2,1)S(1)} async-done(((bf16[16,16,512]{2,1,0:T(8,128)(2,1)}), bf16[16,16,512]{2,1,0:T(8,128)(2,1)S(1)}, u32[]{:S(2)}, u32[]{:S(2)}) %all-to-all-start.4) | async-done | bytes 262176 | tf_op jit(solution)/shard_map/all_to_all | solution.py:304
  120.5 0.6 total.1
  (36 shorter events, 0.6 us)
Async XLA Ops:
  1.8 4.8 %collective-permute-start = (bf16[4,16,1024]{2,1,0:T(8,128)(2,1)S(1)}, bf16[4,16,1024]{2,1,0:T(8,128)(2,1)S(1)}, u32[]{:S(2)}, u32[]{:S(2)}) collective-permute-start(bf16[4,16,1024]{2,1,0:T(8,128)(2,1)S(1)} %get-tuple-element.21), channel_id=1, source_target_pairs={{0,64},{16,80},{32,96},{48,112},{64,0},{80,16},{96,32},{112,48},{1... | collective-permute-start | bytes 393224 | tf_op jit(solution)/shard_map/ppermute | solution.py:332
  4.0 39.1 %copy-start.3 = (bf16[320]{0:T(512)(128)(2,1)S(1)}, bf16[320]{0:T(512)(128)(2,1)}, u32[]{:S(2)}) copy-start(bf16[320]{0:T(512)(128)(2,1)} %param.10) | copy-start | bytes 1924
  6.5 48.8 %copy-start.2 = (s32[8]{0:T(128)S(1)}, s32[8]{0:T(128)}, u32[]{:S(2)}) copy-start(s32[8]{0:T(128)} %refs_0_.1) | copy-start | bytes 100
  6.7 28.4 %all-to-all-start = ((bf16[16,144,256]{2,1,0:T(8,128)(2,1)}), bf16[16,144,256]{2,1,0:T(8,128)(2,1)S(1)}, u32[]{:S(2)}, u32[]{:S(2)}) async-start(bf16[16,144,256]{2,1,0:T(8,128)(2,1)} %get-tuple-element.23), calls=%async_computation | async-start | bytes 2359296 | tf_op jit(solution)/shard_map/all_to_all | solution.py:304
  16.5 5.2 %collective-permute-start.3 = (bf16[2,16,1024]{2,1,0:T(8,128)(2,1)S(1)}, bf16[2,16,1024]{2,1,0:T(8,128)(2,1)S(1)}, u32[]{:S(2)}, u32[]{:S(2)}) collective-permute-start(bf16[2,16,1024]{2,1,0:T(8,128)(2,1)S(1)} %pad_maximum_fusion.2), channel_id=1, source_target_pairs={{0,32},{16,48},{32,0},{48,16},{64,96},{80,112},{96,64},{112,80},{1... | collective-permute-start | bytes 196616 | tf_op jit(solution)/shard_map/ppermute | solution.py:332
  19.5 3.9 %collective-permute-start.2 = (bf16[2,16,1024]{2,1,0:T(8,128)(2,1)S(1)}, bf16[2,16,1024]{2,1,0:T(8,128)(2,1)S(1)}, u32[]{:S(2)}, u32[]{:S(2)}) collective-permute-start(bf16[2,16,1024]{2,1,0:T(8,128)(2,1)S(1)} %pad_maximum_fusion.1), channel_id=1, source_target_pairs={{0,48},{16,0},{32,16},{48,32},{64,112},{80,64},{96,80},{112,96},{1... | collective-permute-start | bytes 196616 | tf_op jit(solution)/shard_map/ppermute | solution.py:332
  20.4 4.7 %collective-permute-start.1 = (bf16[2,16,1024]{2,1,0:T(8,128)(2,1)S(1)}, bf16[2,16,1024]{2,1,0:T(8,128)(2,1)S(1)}, u32[]{:S(2)}, u32[]{:S(2)}) collective-permute-start(bf16[2,16,1024]{2,1,0:T(8,128)(2,1)S(1)} %pad_maximum_fusion), channel_id=1, source_target_pairs={{0,16},{16,32},{32,48},{48,0},{64,80},{80,96},{96,112},{112,64},{1... | collective-permute-start | bytes 196616 | tf_op jit(solution)/shard_map/ppermute | solution.py:332
  36.2 12.8 %collective-permute-start.4 = (bf16[1024,256]{1,0:T(8,128)(2,1)}, bf16[1024,256]{1,0:T(8,128)(2,1)S(1)}, u32[]{:S(2)}, u32[]{:S(2)}) collective-permute-start(bf16[1024,256]{1,0:T(8,128)(2,1)} %get-tuple-element.25.refs_0_), channel_id=1, source_target_pairs={{0,64},{16,80},{32,96},{48,112},{64,0},{80,16},{96,32},{112,48},{1... | collective-permute-start | bytes 1572872 | tf_op jit(solution)/shard_map/ppermute | solution.py:332
  36.5 16.1 %collective-permute-start.10 = (bf16[1024,256]{1,0:T(8,128)(2,1)}, bf16[1024,256]{1,0:T(8,128)(2,1)}, u32[]{:S(2)}, u32[]{:S(2)}) collective-permute-start(bf16[1024,256]{1,0:T(8,128)(2,1)} %get-tuple-element.25.refs_0_), channel_id=1, source_target_pairs={{0,16},{16,32},{32,48},{48,0},{64,80},{80,96},{96,112},{112,64},{1... | collective-permute-start | bytes 1572872 | tf_op jit(solution)/shard_map/ppermute | solution.py:332
  37.8 15.4 %collective-permute-start.11 = (bf16[1024,256]{1,0:T(8,128)(2,1)}, bf16[1024,256]{1,0:T(8,128)(2,1)}, u32[]{:S(2)}, u32[]{:S(2)}) collective-permute-start(bf16[1024,256]{1,0:T(8,128)(2,1)} %get-tuple-element.25.refs_0_), channel_id=1, source_target_pairs={{0,48},{16,0},{32,16},{48,32},{64,112},{80,64},{96,80},{112,96},{1... | collective-permute-start | bytes 1572872 | tf_op jit(solution)/shard_map/ppermute | solution.py:332
  39.3 12.7 %all-to-all-start.1 = ((bf16[8,16,320]{2,1,0:T(8,128)(2,1)}), bf16[8,16,320]{2,1,0:T(8,128)(2,1)S(1)}, u32[]{:S(2)}, u32[]{:S(2)}) async-start(bf16[8,16,320]{2,1,0:T(8,128)(2,1)} %get-tuple-element.24), calls=%async_computation.1 | async-start | bytes 196608 | tf_op jit(solution)/shard_map/all_to_all | solution.py:304
  43.4 34.4 %collective-permute-start.7 = (bf16[320,1024]{1,0:T(8,128)(2,1)S(1)}, bf16[320,1024]{1,0:T(8,128)(2,1)S(1)}, u32[]{:S(2)}, u32[]{:S(2)}) collective-permute-start(bf16[320,1024]{1,0:T(8,128)(2,1)S(1)} %turn.1.refs_0_), channel_id=1, source_target_pairs={{0,16},{16,32},{32,48},{48,0},{64,80},{80,96},{96,112},{112,64},{1... | collective-permute-start | bytes 1966088 | tf_op jit(solution)/shard_map/ppermute | solution.py:332
  44.9 32.9 %collective-permute-start.8 = (bf16[320,1024]{1,0:T(8,128)(2,1)S(1)}, bf16[320,1024]{1,0:T(8,128)(2,1)S(1)}, u32[]{:S(2)}, u32[]{:S(2)}) collective-permute-start(bf16[320,1024]{1,0:T(8,128)(2,1)S(1)} %turn.1.refs_0_), channel_id=1, source_target_pairs={{0,48},{16,0},{32,16},{48,32},{64,112},{80,64},{96,80},{112,96},{1... | collective-permute-start | bytes 1966088 | tf_op jit(solution)/shard_map/ppermute | solution.py:332
  49.0 2.9 %copy-start = (bf16[1024,256]{1,0:T(8,128)(2,1)}, bf16[1024,256]{1,0:T(8,128)(2,1)S(1)}, u32[]{:S(2)}) copy-start(bf16[1024,256]{1,0:T(8,128)(2,1)S(1)} %collective-permute-done.4.refs_0_) | copy-start | bytes 1572868
  49.0 28.7 %collective-permute-start.9 = (bf16[320,1024]{1,0:T(8,128)(2,1)S(1)}, bf16[320,1024]{1,0:T(8,128)(2,1)S(1)}, u32[]{:S(2)}, u32[]{:S(2)}) collective-permute-start(bf16[320,1024]{1,0:T(8,128)(2,1)S(1)} %turn.1.refs_0_), channel_id=1, source_target_pairs={{0,64},{16,80},{32,96},{48,112},{64,0},{80,16},{96,32},{112,48},{1... | collective-permute-start | bytes 1966088 | tf_op jit(solution)/shard_map/ppermute | solution.py:332
  52.7 25.1 %collective-permute-start.5 = (bf16[1024,256]{1,0:T(8,128)(2,1)}, bf16[1024,256]{1,0:T(8,128)(2,1)S(1)}, u32[]{:S(2)}, u32[]{:S(2)}) collective-permute-start(bf16[1024,256]{1,0:T(8,128)(2,1)} %get-tuple-element.27.refs_1_), channel_id=1, source_target_pairs={{0,16},{16,32},{32,48},{48,0},{64,80},{80,96},{96,112},{112,64},{1... | collective-permute-start | bytes 1572872 | tf_op jit(solution)/shard_map/ppermute | solution.py:332
  53.2 24.6 %collective-permute-start.6 = (bf16[1024,256]{1,0:T(8,128)(2,1)}, bf16[1024,256]{1,0:T(8,128)(2,1)}, u32[]{:S(2)}, u32[]{:S(2)}) collective-permute-start(bf16[1024,256]{1,0:T(8,128)(2,1)} %get-tuple-element.27.refs_1_), channel_id=1, source_target_pairs={{0,48},{16,0},{32,16},{48,32},{64,112},{80,64},{96,80},{112,96},{1... | collective-permute-start | bytes 1572872 | tf_op jit(solution)/shard_map/ppermute | solution.py:332
  55.4 16.2 %all-to-all-start.2 = ((bf16[16,16,320]{2,1,0:T(8,128)(2,1)}), bf16[16,16,320]{2,1,0:T(8,128)(2,1)S(1)}, u32[]{:S(2)}, u32[]{:S(2)}) async-start(bf16[16,16,320]{2,1,0:T(8,128)(2,1)} %get-tuple-element.26), calls=%async_computation.2 | async-start | bytes 393216 | tf_op jit(solution)/shard_map/all_to_all | solution.py:304
  63.6 1.0 copy-start.1
  77.8 15.5 %collective-permute-start.16 = (bf16[320,1024]{1,0:T(8,128)(2,1)S(1)}, bf16[320,1024]{1,0:T(8,128)(2,1)}, u32[]{:S(2)}, u32[]{:S(2)}) collective-permute-start(bf16[320,1024]{1,0:T(8,128)(2,1)S(1)} %get-tuple-element.33.refs_1_), channel_id=1, source_target_pairs={{0,64},{16,80},{32,96},{48,112},{64,0},{80,16},{96,32},{112,48},{1... | collective-permute-start | bytes 1966088 | tf_op jit(solution)/shard_map/ppermute | solution.py:332
  79.1 20.7 %collective-permute-start.12 = (bf16[1024,256]{1,0:T(8,128)(2,1)}, bf16[1024,256]{1,0:T(8,128)(2,1)}, u32[]{:S(2)}, u32[]{:S(2)}) collective-permute-start(bf16[1024,256]{1,0:T(8,128)(2,1)} %collective-permute-done.10.refs_0_), channel_id=1, source_target_pairs={{0,16},{16,32},{32,48},{48,0},{64,80},{80,96},{96,112},{112,64},{1... | collective-permute-start | bytes 1572872 | tf_op jit(solution)/shard_map/ppermute | solution.py:332
  79.2 20.5 %collective-permute-start.13 = (bf16[1024,256]{1,0:T(8,128)(2,1)}, bf16[1024,256]{1,0:T(8,128)(2,1)}, u32[]{:S(2)}, u32[]{:S(2)}) collective-permute-start(bf16[1024,256]{1,0:T(8,128)(2,1)} %get-tuple-element.29.refs_1_), channel_id=1, source_target_pairs={{0,48},{16,0},{32,16},{48,32},{64,112},{80,64},{96,80},{112,96},{1... | collective-permute-start | bytes 1572872 | tf_op jit(solution)/shard_map/ppermute | solution.py:332
  81.7 17.6 %all-to-all-start.3 = ((bf16[16,48,128]{2,1,0:T(8,128)(2,1)}), bf16[16,48,128]{2,1,0:T(8,128)(2,1)S(1)}, u32[]{:S(2)}, u32[]{:S(2)}) async-start(bf16[16,48,128]{2,1,0:T(8,128)(2,1)} %get-tuple-element.28), calls=%async_computation.3 | async-start | bytes 393216 | tf_op jit(solution)/shard_map/all_to_all | solution.py:304
  87.7 27.6 %collective-permute-start.14 = (bf16[320,1024]{1,0:T(8,128)(2,1)S(1)}, bf16[320,1024]{1,0:T(8,128)(2,1)}, u32[]{:S(2)}, u32[]{:S(2)}) collective-permute-start(bf16[320,1024]{1,0:T(8,128)(2,1)S(1)} %get-tuple-element.32.refs_0_), channel_id=1, source_target_pairs={{0,16},{16,32},{32,48},{48,0},{64,80},{80,96},{96,112},{112,64},{1... | collective-permute-start | bytes 1966088 | tf_op jit(solution)/shard_map/ppermute | solution.py:332
  87.7 27.6 %collective-permute-start.15 = (bf16[320,1024]{1,0:T(8,128)(2,1)S(1)}, bf16[320,1024]{1,0:T(8,128)(2,1)}, u32[]{:S(2)}, u32[]{:S(2)}) collective-permute-start(bf16[320,1024]{1,0:T(8,128)(2,1)S(1)} %get-tuple-element.32.refs_0_), channel_id=1, source_target_pairs={{0,64},{16,80},{32,96},{48,112},{64,0},{80,16},{96,32},{112,48},{1... | collective-permute-start | bytes 1966088 | tf_op jit(solution)/shard_map/ppermute | solution.py:332
  93.3 22.0 %collective-permute-start.17 = (bf16[320,1024]{1,0:T(8,128)(2,1)}, bf16[320,1024]{1,0:T(8,128)(2,1)}, u32[]{:S(2)}, u32[]{:S(2)}) collective-permute-start(bf16[320,1024]{1,0:T(8,128)(2,1)} %collective-permute-done.16.refs_2_), channel_id=1, source_target_pairs={{0,48},{16,0},{32,16},{48,32},{64,112},{80,64},{96,80},{112,96},{1... | collective-permute-start | bytes 1966088 | tf_op jit(solution)/shard_map/ppermute | solution.py:332
  106.1 14.4 %all-to-all-start.4 = ((bf16[16,16,512]{2,1,0:T(8,128)(2,1)}), bf16[16,16,512]{2,1,0:T(8,128)(2,1)S(1)}, u32[]{:S(2)}, u32[]{:S(2)}) async-start(bf16[16,16,512]{2,1,0:T(8,128)(2,1)} %bitcast.10), calls=%async_computation.4 | async-start | bytes 524288 | tf_op jit(solution)/shard_map/all_to_all | solution.py:304

commit v8 on v7

--- a/solution.py
+++ b/solution.py
@@ -184,7 +184,7 @@
 def attend_kernel(scale, lengths_ref, cosine_ref, sine_ref, new_ref, key_ref, value_ref, message_ref, query_s, message_s, key_s, value_s, sems):
     groups, slots, _ = new_ref.shape
     rows, span, _ = key_ref.shape
-    per_row = query_s.shape[0] // rows
+    per_row = 4 * groups
     key_copies, value_copies = (
         [
             pltpu.make_async_copy(
@@ -194,9 +194,8 @@
         ]
         for i, (ref, scratch) in enumerate(((key_ref, key_s), (value_ref, value_s)))
     )
-    for key_copy, value_copy in zip(key_copies, value_copies):
-        key_copy.start()
-        value_copy.start()
+    for copy in key_copies + value_copies:
+        copy.start()
     cosine, sine = cosine_ref[...], sine_ref[...]
 
     def turned(values):
@@ -220,63 +219,79 @@
     )
 
     member = lax.axis_index("tensor")
-    kv_of = lax.broadcasted_iota(jnp.int32, (per_row, 1), 0) // (per_row // KVH)
-    position = lax.broadcasted_iota(jnp.int32, (per_row, span), 1) + member * span
-    slot = lax.broadcasted_iota(jnp.int32, (per_row, slots), 1)
-    step = lax.broadcasted_iota(jnp.int32, (per_row, slots), 0) % 2
-    lane = lax.broadcasted_iota(jnp.int32, (per_row, HD), 1)
+    total_rows = rows * per_row
+    row = lax.broadcasted_iota(jnp.int32, (total_rows, 1), 0)
+    kv_of = row[:per_row] // (per_row // KVH)
+    position = lax.broadcasted_iota(jnp.int32, (total_rows, span), 1) + member * span
+    slot = lax.broadcasted_iota(jnp.int32, (total_rows, slots), 1)
+    lane = lax.broadcasted_iota(jnp.int32, (total_rows, HD), 1)
+
+    def product(left, right):
+        return lax.dot_general(
+            left, right, (((1,), (1,)), ((), ())), preferred_element_type=jnp.float32
+        )
+
+    def diagonal(values):
+        own = values[:, :HD]
+        for k in range(1, KVH):
+            own = jnp.where(kv_of == k, values[:, k * HD : (k + 1) * HD], own)
+        return own
+
+    def of_row(values, r):
+        return values[r * per_row : (r + 1) * per_row]
+
+    queries = []
     for r in range(rows):
         query = query_s[r * per_row : (r + 1) * per_row, :].astype(jnp.bfloat16)
-        query = jnp.concatenate(
-            [jnp.where(kv_of == k, query, jnp.zeros_like(query)) for k in range(KVH)], 1
+        queries.append(
+            jnp.concatenate(
+                [jnp.where(kv_of == k, query, jnp.zeros_like(query)) for k in range(KVH)], 1
+            )
         )
-
-        def product(keys):
-            return (
-                lax.dot_general(
-                    query, keys, (((1,), (1,)), ((), ())), preferred_element_type=jnp.float32
-                )
-                * scale
-            )
-
-        valid = position < lengths_ref[r]
-        if r % 4 == 0:
-            key_copies[r // 4].wait()
-        scores = jnp.where(valid, product(key_s[r]), FLOOR)
-        fresh = (slot % rows == r) & (slot // rows <= step) & (member == 0)
-        fresh_scores = jnp.where(fresh, product(new_keys), FLOOR)
-        highest = jnp.maximum(
-            jnp.max(scores, 1, keepdims=True), jnp.max(fresh_scores, 1, keepdims=True)
-        )
-        upper = highest.astype(jnp.bfloat16).astype(jnp.float32)
-        lower = (highest - upper).astype(jnp.bfloat16).astype(jnp.float32)
-        highest = upper + lower
-        weights = jnp.where(valid, jnp.exp(scores - highest), 0.0)
-        fresh_weights = jnp.where(fresh, jnp.exp(fresh_scores - highest), 0.0)
-        total = jnp.sum(weights, 1, keepdims=True) + jnp.sum(fresh_weights, 1, keepdims=True)
-        if r % 4 == 0:
-            value_copies[r // 4].wait()
-        mixed = jnp.dot(
-            weights.astype(jnp.bfloat16), value_s[r], preferred_element_type=jnp.float32
-        ) + jnp.dot(
-            fresh_weights.astype(jnp.bfloat16), new_values, preferred_element_type=jnp.float32
-        )
-        own = jnp.zeros((per_row, HD), jnp.float32)
-        for k in range(KVH):
-            own = jnp.where(kv_of == k, mixed[:, k * HD : (k + 1) * HD], own)
-        total_upper = total.astype(jnp.bfloat16).astype(jnp.float32)
-        total_lower = total - total_upper
-        part = lane // 16 % 4
-        facts = jnp.where(
-            part < 2,
-            jnp.where(part == 0, upper, lower),
-            jnp.where(part == 2, total_upper, total_lower),
-        )
-        facts = jnp.where(lane < 64, facts, pltpu.roll(facts, per_row - 2, 0))
+    fresh = (slot % rows == row // per_row) & (slot // rows <= row % 2) & (member == 0)
+    fresh_scores = jnp.where(
+        fresh, product(jnp.concatenate(queries, 0), new_keys) * scale, FLOOR
+    )
+    for copy in key_copies:
+        copy.wait()
+    scores = jnp.concatenate([product(queries[r], key_s[r]) for r in range(rows)], 0) * scale
+    length = jnp.concatenate(
+        [jnp.full((per_row, 1), lengths_ref[r], jnp.int32) for r in range(rows)], 0
+    )
+    valid = position < length
+    scores = jnp.where(valid, scores, FLOOR)
+    highest = jnp.maximum(
+        jnp.max(scores, 1, keepdims=True), jnp.max(fresh_scores, 1, keepdims=True)
+    )
+    upper = highest.astype(jnp.bfloat16).astype(jnp.float32)
+    lower = (highest - upper).astype(jnp.bfloat16).astype(jnp.float32)
+    highest = upper + lower
+    weights = jnp.where(valid, jnp.exp(scores - highest), 0.0)
+    fresh_weights = jnp.where(fresh, jnp.exp(fresh_scores - highest), 0.0)
+    total = jnp.sum(weights, 1, keepdims=True) + jnp.sum(fresh_weights, 1, keepdims=True)
+    weights = weights.astype(jnp.bfloat16)
+    fresh_mixed = jnp.dot(
+        fresh_weights.astype(jnp.bfloat16), new_values, preferred_element_type=jnp.float32
+    )
+    total_upper = total.astype(jnp.bfloat16).astype(jnp.float32)
+    total_lower = total - total_upper
+    part = lane // 16 % 4
+    facts = jnp.where(
+        part < 2,
+        jnp.where(part == 0, upper, lower),
+        jnp.where(part == 2, total_upper, total_lower),
+    )
+    facts = jnp.where(lane < 64, facts, pltpu.roll(facts, total_rows - 2, 0))
+    for copy in value_copies:
+        copy.wait()
+    for r in range(rows):
+        mixed = jnp.dot(of_row(weights, r), value_s[r], preferred_element_type=jnp.float32)
+        own = diagonal(mixed + of_row(fresh_mixed, r))
+        own_facts = of_row(facts, r)
         for t in range(groups):
             message_s[t, pl.ds(r, 4, stride=rows), :] = own[t * 4 : (t + 1) * 4]
-            message_s[t, pl.ds(4 * rows + r, 2, stride=rows), :] = facts[t * 4 : t * 4 + 2]
-    message_ref[...] = message_s[...].astype(message_ref.dtype)
+            message_s[t, pl.ds(4 * rows + r, 2, stride=rows), :] = own_facts[t * 4 : t * 4 + 2]
+    message_ref[...] = message_s[:, : message_ref.shape[1], :].astype(message_ref.dtype)
 
 
 def merge_kernel(message_ref, attended_ref):
@@ -425,8 +440,8 @@
         out_shape=jax.ShapeDtypeStruct((groups, 3 * slots, HD), jnp.bfloat16),
         in_specs=[smem] + [vmem] * 3 + [in_hbm] * 2,
         scratch_shapes=[
-            pltpu.VMEM((slots * QH, HD), jnp.float32),
-            pltpu.VMEM((groups, 3 * slots, HD), jnp.float32),
+            pltpu.VMEM((slots * QH + 4 * groups, HD), jnp.float32),
+            pltpu.VMEM((groups, 4 * slots, HD), jnp.float32),
             pltpu.VMEM(key_cache.shape, key_cache.dtype),
             pltpu.VMEM(value_cache.shape, value_cache.dtype),
             pltpu.SemaphoreType.DMA((2, row_count)),

time: 122 us -> 122 us (level)
  starting transfers between devices: 52.9 us -> 56.4 us
  waiting for transfers between devices: 34.2 us -> 32.3 us
  Pallas kernels: 27.6 us -> 26.1 us
    ppermute x18, starting transfers between devices: 19.6 us -> 22 us  [send(): return lax.ppermute(value, 'dp', pairs)]
    pallas_call x1, Pallas kernels: 6.1 us -> 4.57 us  [on_device(): pl.pallas_call(lambda *refs: attend_kernel(score_scale, *refs), out_shape...]
    ppermute x18, waiting for transfers between devices: 12.5 us -> 11.1 us  [send(): return lax.ppermute(value, 'dp', pairs)]
  transfers between devices with their start and end apart: 23 -> 23, of which waited for: 11 -> 12; matrix products, arithmetic and copies ran while one was open for 4% -> 4% of each run, Pallas kernels for 20% -> 19%
where the time goes in v8:
time: 122 us; the launch traced here: 121 us
  starting transfers between devices  56.4 us (46%)
  waiting for transfers between devices  32.3 us (26%)
  Pallas kernels  26.1 us (21%)
  matrix products  3.38 us (3%)
  local copies, waits for them, and re-layouts  1.91 us (2%)
    all_to_all x5, starting transfers between devices, exchange(): return lax.all_to_all(blocks, axis, split_axis=0, concat_axis=0, tiled=True)  34.3 us
    ppermute x18, starting transfers between devices, send(): return lax.ppermute(value, 'dp', pairs)  22 us
    all_to_all x5, waiting for transfers between devices, exchange(): return lax.all_to_all(blocks, axis, split_axis=0, concat_axis=0, tiled=True)  21.2 us
    pallas_call x7, Pallas kernels, place(): pl.pallas_call(lambda *refs: place_kernel(axis, where, mark, *refs), out_...  14.6 us
    ppermute x18, waiting for transfers between devices, send(): return lax.ppermute(value, 'dp', pairs)  11.1 us
    pallas_call x1, Pallas kernels, on_device(): pl.pallas_call(lambda *refs: attend_kernel(score_scale, *refs), out_shape...  4.57 us
    dot_general x1, matrix products, on_device(): jnp.dot(attended, grouped_out.T, preferred_element_type=jnp.float32)  3.38 us
    pallas_call x1, Pallas kernels, on_device(): pl.pallas_call(lambda *refs: pack_kernel(groups, *refs), out_shape=jax.Sh...  2.54 us
  transfers between devices with their start and end apart: 23, of which 12 were waited for; matrix products, arithmetic and copies ran while one was open for 4% of the time, Pallas kernels for 19%

profile of v8, /device:TPU:1, one launch (start us, length us, event | category | flops | bytes accessed | tf_op | source)
XLA Modules:
  0.0 121.1 jit_solution(14121429704488368597)
XLA Ops:
  0.6 1.2 norm.1
  1.8 2.1 %collective-permute-start = (bf16[4,16,1024]{2,1,0:T(8,128)(2,1)S(1)}, bf16[4,16,1024]{2,1,0:T(8,128)(2,1)S(1)}, u32[]{:S(2)}, u32[]{:S(2)}) collective-permute-start(bf16[4,16,1024]{2,1,0:T(8,128)(2,1)S(1)} %get-tuple-element.21), channel_id=1, source_target_pairs={{0,64},{16,80},{32,96},{48,112},{64,0},{80,16},{96,32},{112,48},{1... | collective-permute-start | bytes 393224 | tf_op jit(solution)/shard_map/ppermute | solution.py:347
  4.0 2.5 %pack.1.refs_0_ = bf16[16,144,256]{2,1,0:T(8,128)(2,1)} custom-call(bf16[4,16,1024]{2,1,0:T(8,128)(2,1)S(1)} %get-tuple-element.20.refs_0_.own, bf16[64,5120]{1,0:T(8,128)(2,1)} %refs_1_.1, bf16[64,4096]{1,0:T(8,128)(2,1)} %refs_2_.1), custom_call_target="tpu_custom_call" | custom-call | tf_op jit(solution)/shard_map/pack/pallas_call | solution.py:363
  6.7 9.8 %all-to-all-start = ((bf16[16,144,256]{2,1,0:T(8,128)(2,1)}), bf16[16,144,256]{2,1,0:T(8,128)(2,1)S(1)}, u32[]{:S(2)}, u32[]{:S(2)}) async-start(bf16[16,144,256]{2,1,0:T(8,128)(2,1)} %get-tuple-element.23), calls=%async_computation | async-start | bytes 2359296 | tf_op jit(solution)/shard_map/all_to_all | solution.py:319
  16.5 3.0 %collective-permute-start.3 = (bf16[2,16,1024]{2,1,0:T(8,128)(2,1)S(1)}, bf16[2,16,1024]{2,1,0:T(8,128)(2,1)S(1)}, u32[]{:S(2)}, u32[]{:S(2)}) collective-permute-start(bf16[2,16,1024]{2,1,0:T(8,128)(2,1)S(1)} %pad_maximum_fusion.2), channel_id=1, source_target_pairs={{0,32},{16,48},{32,0},{48,16},{64,96},{80,112},{96,64},{112,80},{1... | collective-permute-start | bytes 196616 | tf_op jit(solution)/shard_map/ppermute | solution.py:347
  19.5 0.8 collective-permute-start.2
  20.4 0.8 collective-permute-start.1
  21.1 0.6 collective-permute-done.3.far
  21.7 1.7 %collective-permute-done.2.high = bf16[2,16,1024]{2,1,0:T(8,128)(2,1)S(1)} collective-permute-done((bf16[2,16,1024]{2,1,0:T(8,128)(2,1)S(1)}, bf16[2,16,1024]{2,1,0:T(8,128)(2,1)S(1)}, u32[]{:S(2)}, u32[]{:S(2)}) %collective-permute-start.2) | collective-permute-done | bytes 65568 | tf_op jit(solution)/shard_map/ppermute | solution.py:347
  23.4 1.6 %collective-permute-done.1.low = bf16[2,16,1024]{2,1,0:T(8,128)(2,1)S(1)} collective-permute-done((bf16[2,16,1024]{2,1,0:T(8,128)(2,1)S(1)}, bf16[2,16,1024]{2,1,0:T(8,128)(2,1)S(1)}, u32[]{:S(2)}, u32[]{:S(2)}) %collective-permute-start.1) | collective-permute-done | bytes 65568 | tf_op jit(solution)/shard_map/ppermute | solution.py:347
  25.1 10.0 %all-to-all-done.packed_ref = bf16[16,144,256]{2,1,0:T(8,128)(2,1)S(1)} async-done(((bf16[16,144,256]{2,1,0:T(8,128)(2,1)}), bf16[16,144,256]{2,1,0:T(8,128)(2,1)S(1)}, u32[]{:S(2)}, u32[]{:S(2)}) %all-to-all-start) | async-done | bytes 1179680 | tf_op jit(solution)/shard_map/all_to_all | solution.py:319
  35.1 1.1 terms.1
  36.5 1.3 %collective-permute-start.10 = (bf16[1024,256]{1,0:T(8,128)(2,1)}, bf16[1024,256]{1,0:T(8,128)(2,1)}, u32[]{:S(2)}, u32[]{:S(2)}) collective-permute-start(bf16[1024,256]{1,0:T(8,128)(2,1)} %get-tuple-element.25.refs_0_), channel_id=1, source_target_pairs={{0,16},{16,32},{32,48},{48,0},{64,80},{80,96},{96,112},{112,64},{1... | collective-permute-start | bytes 1572872 | tf_op jit(solution)/shard_map/ppermute | solution.py:347
  37.8 1.4 %collective-permute-start.11 = (bf16[1024,256]{1,0:T(8,128)(2,1)}, bf16[1024,256]{1,0:T(8,128)(2,1)}, u32[]{:S(2)}, u32[]{:S(2)}) collective-permute-start(bf16[1024,256]{1,0:T(8,128)(2,1)} %get-tuple-element.25.refs_0_), channel_id=1, source_target_pairs={{0,48},{16,0},{32,16},{48,32},{64,112},{80,64},{96,80},{112,96},{1... | collective-permute-start | bytes 1572872 | tf_op jit(solution)/shard_map/ppermute | solution.py:347
  39.3 3.8 %all-to-all-start.1 = ((bf16[8,16,320]{2,1,0:T(8,128)(2,1)}), bf16[8,16,320]{2,1,0:T(8,128)(2,1)S(1)}, u32[]{:S(2)}, u32[]{:S(2)}) async-start(bf16[8,16,320]{2,1,0:T(8,128)(2,1)} %get-tuple-element.24), calls=%async_computation.1 | async-start | bytes 196608 | tf_op jit(solution)/shard_map/all_to_all | solution.py:319
  43.4 1.5 %collective-permute-start.7 = (bf16[320,1024]{1,0:T(8,128)(2,1)S(1)}, bf16[320,1024]{1,0:T(8,128)(2,1)S(1)}, u32[]{:S(2)}, u32[]{:S(2)}) collective-permute-start(bf16[320,1024]{1,0:T(8,128)(2,1)S(1)} %turn.1.refs_0_), channel_id=1, source_target_pairs={{0,16},{16,32},{32,48},{48,0},{64,80},{80,96},{96,112},{112,64},{1... | collective-permute-start | bytes 1966088 | tf_op jit(solution)/shard_map/ppermute | solution.py:347
  44.9 1.3 %collective-permute-start.8 = (bf16[320,1024]{1,0:T(8,128)(2,1)S(1)}, bf16[320,1024]{1,0:T(8,128)(2,1)S(1)}, u32[]{:S(2)}, u32[]{:S(2)}) collective-permute-start(bf16[320,1024]{1,0:T(8,128)(2,1)S(1)} %turn.1.refs_0_), channel_id=1, source_target_pairs={{0,48},{16,0},{32,16},{48,32},{64,112},{80,64},{96,80},{112,96},{1... | collective-permute-start | bytes 1966088 | tf_op jit(solution)/shard_map/ppermute | solution.py:347
  46.2 2.8 %collective-permute-done.4.refs_0_ = bf16[1024,256]{1,0:T(8,128)(2,1)S(1)} collective-permute-done((bf16[1024,256]{1,0:T(8,128)(2,1)}, bf16[1024,256]{1,0:T(8,128)(2,1)S(1)}, u32[]{:S(2)}, u32[]{:S(2)}) %collective-permute-start.4) | collective-permute-done | bytes 524320 | tf_op jit(solution)/shard_map/ppermute | solution.py:347
  49.4 2.6 %all-to-all-done.1.terms_ref = bf16[8,16,320]{2,1,0:T(8,128)(2,1)S(1)} async-done(((bf16[8,16,320]{2,1,0:T(8,128)(2,1)}), bf16[8,16,320]{2,1,0:T(8,128)(2,1)S(1)}, u32[]{:S(2)}, u32[]{:S(2)}) %all-to-all-start.1) | async-done | bytes 81952 | tf_op jit(solution)/shard_map/all_to_all | solution.py:319
  52.0 0.7 sum.1
  52.7 0.5 collective-permute-start.5
  53.2 2.1 %collective-permute-start.6 = (bf16[1024,256]{1,0:T(8,128)(2,1)}, bf16[1024,256]{1,0:T(8,128)(2,1)}, u32[]{:S(2)}, u32[]{:S(2)}) collective-permute-start(bf16[1024,256]{1,0:T(8,128)(2,1)} %get-tuple-element.27.refs_1_), channel_id=1, source_target_pairs={{0,48},{16,0},{32,16},{48,32},{64,112},{80,64},{96,80},{112,96},{1... | collective-permute-start | bytes 1572872 | tf_op jit(solution)/shard_map/ppermute | solution.py:347
  55.4 8.0 %all-to-all-start.2 = ((bf16[16,16,320]{2,1,0:T(8,128)(2,1)}), bf16[16,16,320]{2,1,0:T(8,128)(2,1)S(1)}, u32[]{:S(2)}, u32[]{:S(2)}) async-start(bf16[16,16,320]{2,1,0:T(8,128)(2,1)} %get-tuple-element.26), calls=%async_computation.2 | async-start | bytes 393216 | tf_op jit(solution)/shard_map/all_to_all | solution.py:319
  63.6 1.0 copy-done.1
  64.7 2.0 %place.7.refs_2_ = bf16[8192,256]{1,0:T(8,128)(2,1)} custom-call(bf16[1024,256]{1,0:T(8,128)(2,1)} %get-tuple-element.25.refs_0_, bf16[1024,256]{1,0:T(8,128)(2,1)S(1)} %copy-done.1), custom_call_target="tpu_custom_call" | custom-call | tf_op jit(solution)/shard_map/place/pallas_call | solution.py:170
  66.7 2.2 %place.8.refs_6_ = bf16[8192,256]{1,0:T(8,128)(2,1)} custom-call(bf16[1024,256]{1,0:T(8,128)(2,1)} %collective-permute-done.10.refs_0_, bf16[1024,256]{1,0:T(8,128)(2,1)} %collective-permute-done.11.refs_1_, bf16[8192,256]{1,0:T(8,128)(2,1)} %place.7.refs_2_), custom_call_target="tpu_custom_call", output_to_operand_aliasing={{}: (2, {})} | custom-call | tf_op jit(solution)/shard_map/place/pallas_call | solution.py:170
  68.9 2.8 %all-to-all-done.2.refs_3_ = bf16[16,16,320]{2,1,0:T(8,128)(2,1)S(1)} async-done(((bf16[16,16,320]{2,1,0:T(8,128)(2,1)}), bf16[16,16,320]{2,1,0:T(8,128)(2,1)S(1)}, u32[]{:S(2)}, u32[]{:S(2)}) %all-to-all-start.2) | async-done | bytes 163872 | tf_op jit(solution)/shard_map/all_to_all | solution.py:319
  71.6 4.6 %attend.1.refs_0_ = bf16[16,48,128]{2,1,0:T(8,128)(2,1)} custom-call(s32[8]{0:T(128)S(1)} %copy-done.2, f32[16,128]{1,0:T(8,128)S(1)} %get-tuple-element.46.refs_1_, f32[16,128]{1,0:T(8,128)S(1)} %get-tuple-element.47.refs_2_, bf16[16,16,320]{2,1,0:T(8,128)(2,1)S(1)} %all-to-all-done.2.refs_3_, bf16[8,256,512]{2,1,0:T(8,128)(2,1)} %refs_4_.1, ...), custom_call_target="tpu_custom_call" | custom-call | tf_op jit(solution)/shard_map/attend/pallas_call | solution.py:438
  76.3 0.4 collective-permute-done.5.refs_1_
  76.7 1.2 collective-permute-start.16
  77.8 1.0 collective-permute-start.12
  78.8 1.7 %collective-permute-start.13 = (bf16[1024,256]{1,0:T(8,128)(2,1)}, bf16[1024,256]{1,0:T(8,128)(2,1)}, u32[]{:S(2)}, u32[]{:S(2)}) collective-permute-start(bf16[1024,256]{1,0:T(8,128)(2,1)} %get-tuple-element.29.refs_1_), channel_id=1, source_target_pairs={{0,48},{16,0},{32,16},{48,32},{64,112},{80,64},{96,80},{112,96},{1... | collective-permute-start | bytes 1572872 | tf_op jit(solution)/shard_map/ppermute | solution.py:347
  80.5 6.3 %all-to-all-start.3 = ((bf16[16,48,128]{2,1,0:T(8,128)(2,1)}), bf16[16,48,128]{2,1,0:T(8,128)(2,1)S(1)}, u32[]{:S(2)}, u32[]{:S(2)}) async-start(bf16[16,48,128]{2,1,0:T(8,128)(2,1)} %get-tuple-element.28), calls=%async_computation.3 | async-start | bytes 393216 | tf_op jit(solution)/shard_map/all_to_all | solution.py:319
  86.9 0.3 collective-permute-start.15
  87.2 3.7 %collective-permute-done.16.refs_2_ = bf16[320,1024]{1,0:T(8,128)(2,1)} collective-permute-done((bf16[320,1024]{1,0:T(8,128)(2,1)S(1)}, bf16[320,1024]{1,0:T(8,128)(2,1)}, u32[]{:S(2)}, u32[]{:S(2)}) %collective-permute-start.16) | collective-permute-done | bytes 655392 | tf_op jit(solution)/shard_map/ppermute | solution.py:347
  90.9 2.2 %collective-permute-start.17 = (bf16[320,1024]{1,0:T(8,128)(2,1)}, bf16[320,1024]{1,0:T(8,128)(2,1)}, u32[]{:S(2)}, u32[]{:S(2)}) collective-permute-start(bf16[320,1024]{1,0:T(8,128)(2,1)} %collective-permute-done.16.refs_2_), channel_id=1, source_target_pairs={{0,48},{16,0},{32,16},{48,32},{64,112},{80,64},{96,80},{112,96},{1... | collective-permute-start | bytes 1966088 | tf_op jit(solution)/shard_map/ppermute | solution.py:347
  93.1 2.0 %place.9.refs_2_ = bf16[8192,256]{1,0:T(8,128)(2,1)} custom-call(bf16[1024,256]{1,0:T(8,128)(2,1)S(1)} %get-tuple-element.30.refs_0_, bf16[1024,256]{1,0:T(8,128)(2,1)} %get-tuple-element.29.refs_1_, bf16[8192,256]{1,0:T(8,128)(2,1)} %get-tuple-element.31.refs_2_), custom_call_target="tpu_custom_call", output_to_operand_aliasing={{}: (2, {})} | custom-call | tf_op jit(solution)/shard_map/place/pallas_call | solution.py:170
  95.1 3.5 %all-to-all-done.3.message_ref = bf16[16,48,128]{2,1,0:T(8,128)(2,1)S(1)} async-done(((bf16[16,48,128]{2,1,0:T(8,128)(2,1)}), bf16[16,48,128]{2,1,0:T(8,128)(2,1)S(1)}, u32[]{:S(2)}, u32[]{:S(2)}) %all-to-all-start.3) | async-done | bytes 196640 | tf_op jit(solution)/shard_map/all_to_all | solution.py:319
  98.6 0.4 merge.1
  99.0 2.2 %place.10 = bf16[8192,256]{1,0:T(8,128)(2,1)} custom-call(bf16[1024,256]{1,0:T(8,128)(2,1)} %collective-permute-done.12.refs_0_, bf16[1024,256]{1,0:T(8,128)(2,1)} %collective-permute-done.13.refs_1_, bf16[8192,256]{1,0:T(8,128)(2,1)} %place.9.refs_2_), custom_call_target="tpu_custom_call", output_to_operand_aliasing={{}: (2, {})} | custom-call | tf_op jit(solution)/shard_map/place/pallas_call | solution.py:170
  101.2 3.4 %convolution_convert_fusion = bf16[16,8192]{1,0:T(8,128)(2,1)S(1)} fusion(bf16[16,256]{1,0:T(8,128)(2,1)S(1)} %merge.1, bf16[8192,256]{1,0:T(8,128)(2,1)} %place.10), kind=kOutput, calls=%fused_computation | convolution fusion | flops 67239936 | bytes 4464640 | tf_op jit(solution)/shard_map/dot_general | solution.py:499
  104.5 0.7 copy.29
  105.3 6.5 %all-to-all-start.4 = ((bf16[16,16,512]{2,1,0:T(8,128)(2,1)}), bf16[16,16,512]{2,1,0:T(8,128)(2,1)S(1)}, u32[]{:S(2)}, u32[]{:S(2)}) async-start(bf16[16,16,512]{2,1,0:T(8,128)(2,1)} %bitcast.10), calls=%async_computation.4 | async-start | bytes 524288 | tf_op jit(solution)/shard_map/all_to_all | solution.py:319
  111.8 1.1 place.11.refs_3_
  112.9 2.4 %place.12.refs_3_ = bf16[320,8192]{1,0:T(8,128)(2,1)} custom-call(bf16[320,1024]{1,0:T(8,128)(2,1)S(1)} %get-tuple-element.32.refs_0_, bf16[320,1024]{1,0:T(8,128)(2,1)S(1)} %get-tuple-element.33.refs_1_, bf16[320,1024]{1,0:T(8,128)(2,1)} %collective-permute-done.16.refs_2_, bf16[320,8192]{1,0:T(8,128)(2,1)} %place.11.refs_3_), custom_call_target="tpu_custom_call", output_to_operand_aliasing={{}: (3, {})} | custom-call | tf_op jit(solution)/shard_map/place/pallas_call | solution.py:170
  115.3 2.8 %place.13 = (bf16[320,8192]{1,0:T(8,128)(2,1)}, f32[8,128]{1,0:T(8,128)S(1)}) custom-call(bf16[320,1024]{1,0:T(8,128)(2,1)} %collective-permute-done.14.refs_0_, bf16[320,1024]{1,0:T(8,128)(2,1)} %collective-permute-done.15.refs_1_, bf16[320,1024]{1,0:T(8,128)(2,1)} %collective-permute-done.17.refs_2_, ...), custom_call_target="tpu_custom_call", output_to_operand_aliasing={{0}: (3, {})} | custom-call | tf_op jit(solution)/shard_map/place/pallas_call | solution.py:170
  118.1 2.4 %all-to-all-done.4.terms_ref = bf16[16,16,512]{2,1,0:T(8,128)(2,1)S(1)} async-done(((bf16[16,16,512]{2,1,0:T(8,128)(2,1)}), bf16[16,16,512]{2,1,0:T(8,128)(2,1)S(1)}, u32[]{:S(2)}, u32[]{:S(2)}) %all-to-all-start.4) | async-done | bytes 262176 | tf_op jit(solution)/shard_map/all_to_all | solution.py:319
  120.5 0.6 total.1
  (36 shorter events, 1.5 us)
Async XLA Ops:
  1.8 4.8 %collective-permute-start = (bf16[4,16,1024]{2,1,0:T(8,128)(2,1)S(1)}, bf16[4,16,1024]{2,1,0:T(8,128)(2,1)S(1)}, u32[]{:S(2)}, u32[]{:S(2)}) collective-permute-start(bf16[4,16,1024]{2,1,0:T(8,128)(2,1)S(1)} %get-tuple-element.21), channel_id=1, source_target_pairs={{0,64},{16,80},{32,96},{48,112},{64,0},{80,16},{96,32},{112,48},{1... | collective-permute-start | bytes 393224 | tf_op jit(solution)/shard_map/ppermute | solution.py:347
  4.0 39.1 %copy-start.3 = (bf16[320]{0:T(512)(128)(2,1)S(1)}, bf16[320]{0:T(512)(128)(2,1)}, u32[]{:S(2)}) copy-start(bf16[320]{0:T(512)(128)(2,1)} %param.10) | copy-start | bytes 1924
  6.5 48.8 %copy-start.2 = (s32[8]{0:T(128)S(1)}, s32[8]{0:T(128)}, u32[]{:S(2)}) copy-start(s32[8]{0:T(128)} %refs_0_.1) | copy-start | bytes 100
  6.7 28.4 %all-to-all-start = ((bf16[16,144,256]{2,1,0:T(8,128)(2,1)}), bf16[16,144,256]{2,1,0:T(8,128)(2,1)S(1)}, u32[]{:S(2)}, u32[]{:S(2)}) async-start(bf16[16,144,256]{2,1,0:T(8,128)(2,1)} %get-tuple-element.23), calls=%async_computation | async-start | bytes 2359296 | tf_op jit(solution)/shard_map/all_to_all | solution.py:319
  16.5 5.2 %collective-permute-start.3 = (bf16[2,16,1024]{2,1,0:T(8,128)(2,1)S(1)}, bf16[2,16,1024]{2,1,0:T(8,128)(2,1)S(1)}, u32[]{:S(2)}, u32[]{:S(2)}) collective-permute-start(bf16[2,16,1024]{2,1,0:T(8,128)(2,1)S(1)} %pad_maximum_fusion.2), channel_id=1, source_target_pairs={{0,32},{16,48},{32,0},{48,16},{64,96},{80,112},{96,64},{112,80},{1... | collective-permute-start | bytes 196616 | tf_op jit(solution)/shard_map/ppermute | solution.py:347
  19.5 3.9 %collective-permute-start.2 = (bf16[2,16,1024]{2,1,0:T(8,128)(2,1)S(1)}, bf16[2,16,1024]{2,1,0:T(8,128)(2,1)S(1)}, u32[]{:S(2)}, u32[]{:S(2)}) collective-permute-start(bf16[2,16,1024]{2,1,0:T(8,128)(2,1)S(1)} %pad_maximum_fusion.1), channel_id=1, source_target_pairs={{0,48},{16,0},{32,16},{48,32},{64,112},{80,64},{96,80},{112,96},{1... | collective-permute-start | bytes 196616 | tf_op jit(solution)/shard_map/ppermute | solution.py:347
  20.4 4.7 %collective-permute-start.1 = (bf16[2,16,1024]{2,1,0:T(8,128)(2,1)S(1)}, bf16[2,16,1024]{2,1,0:T(8,128)(2,1)S(1)}, u32[]{:S(2)}, u32[]{:S(2)}) collective-permute-start(bf16[2,16,1024]{2,1,0:T(8,128)(2,1)S(1)} %pad_maximum_fusion), channel_id=1, source_target_pairs={{0,16},{16,32},{32,48},{48,0},{64,80},{80,96},{96,112},{112,64},{1... | collective-permute-start | bytes 196616 | tf_op jit(solution)/shard_map/ppermute | solution.py:347
  36.2 12.8 %collective-permute-start.4 = (bf16[1024,256]{1,0:T(8,128)(2,1)}, bf16[1024,256]{1,0:T(8,128)(2,1)S(1)}, u32[]{:S(2)}, u32[]{:S(2)}) collective-permute-start(bf16[1024,256]{1,0:T(8,128)(2,1)} %get-tuple-element.25.refs_0_), channel_id=1, source_target_pairs={{0,64},{16,80},{32,96},{48,112},{64,0},{80,16},{96,32},{112,48},{1... | collective-permute-start | bytes 1572872 | tf_op jit(solution)/shard_map/ppermute | solution.py:347
  36.5 16.1 %collective-permute-start.10 = (bf16[1024,256]{1,0:T(8,128)(2,1)}, bf16[1024,256]{1,0:T(8,128)(2,1)}, u32[]{:S(2)}, u32[]{:S(2)}) collective-permute-start(bf16[1024,256]{1,0:T(8,128)(2,1)} %get-tuple-element.25.refs_0_), channel_id=1, source_target_pairs={{0,16},{16,32},{32,48},{48,0},{64,80},{80,96},{96,112},{112,64},{1... | collective-permute-start | bytes 1572872 | tf_op jit(solution)/shard_map/ppermute | solution.py:347
  37.8 15.4 %collective-permute-start.11 = (bf16[1024,256]{1,0:T(8,128)(2,1)}, bf16[1024,256]{1,0:T(8,128)(2,1)}, u32[]{:S(2)}, u32[]{:S(2)}) collective-permute-start(bf16[1024,256]{1,0:T(8,128)(2,1)} %get-tuple-element.25.refs_0_), channel_id=1, source_target_pairs={{0,48},{16,0},{32,16},{48,32},{64,112},{80,64},{96,80},{112,96},{1... | collective-permute-start | bytes 1572872 | tf_op jit(solution)/shard_map/ppermute | solution.py:347
  39.3 12.7 %all-to-all-start.1 = ((bf16[8,16,320]{2,1,0:T(8,128)(2,1)}), bf16[8,16,320]{2,1,0:T(8,128)(2,1)S(1)}, u32[]{:S(2)}, u32[]{:S(2)}) async-start(bf16[8,16,320]{2,1,0:T(8,128)(2,1)} %get-tuple-element.24), calls=%async_computation.1 | async-start | bytes 196608 | tf_op jit(solution)/shard_map/all_to_all | solution.py:319
  43.4 32.9 %collective-permute-start.7 = (bf16[320,1024]{1,0:T(8,128)(2,1)S(1)}, bf16[320,1024]{1,0:T(8,128)(2,1)S(1)}, u32[]{:S(2)}, u32[]{:S(2)}) collective-permute-start(bf16[320,1024]{1,0:T(8,128)(2,1)S(1)} %turn.1.refs_0_), channel_id=1, source_target_pairs={{0,16},{16,32},{32,48},{48,0},{64,80},{80,96},{96,112},{112,64},{1... | collective-permute-start | bytes 1966088 | tf_op jit(solution)/shard_map/ppermute | solution.py:347
  44.9 31.3 %collective-permute-start.8 = (bf16[320,1024]{1,0:T(8,128)(2,1)S(1)}, bf16[320,1024]{1,0:T(8,128)(2,1)S(1)}, u32[]{:S(2)}, u32[]{:S(2)}) collective-permute-start(bf16[320,1024]{1,0:T(8,128)(2,1)S(1)} %turn.1.refs_0_), channel_id=1, source_target_pairs={{0,48},{16,0},{32,16},{48,32},{64,112},{80,64},{96,80},{112,96},{1... | collective-permute-start | bytes 1966088 | tf_op jit(solution)/shard_map/ppermute | solution.py:347
  49.0 2.9 %copy-start = (bf16[1024,256]{1,0:T(8,128)(2,1)}, bf16[1024,256]{1,0:T(8,128)(2,1)S(1)}, u32[]{:S(2)}) copy-start(bf16[1024,256]{1,0:T(8,128)(2,1)S(1)} %collective-permute-done.4.refs_0_) | copy-start | bytes 1572868
  49.0 27.2 %collective-permute-start.9 = (bf16[320,1024]{1,0:T(8,128)(2,1)S(1)}, bf16[320,1024]{1,0:T(8,128)(2,1)S(1)}, u32[]{:S(2)}, u32[]{:S(2)}) collective-permute-start(bf16[320,1024]{1,0:T(8,128)(2,1)S(1)} %turn.1.refs_0_), channel_id=1, source_target_pairs={{0,64},{16,80},{32,96},{48,112},{64,0},{80,16},{96,32},{112,48},{1... | collective-permute-start | bytes 1966088 | tf_op jit(solution)/shard_map/ppermute | solution.py:347
  52.7 24.0 %collective-permute-start.5 = (bf16[1024,256]{1,0:T(8,128)(2,1)}, bf16[1024,256]{1,0:T(8,128)(2,1)S(1)}, u32[]{:S(2)}, u32[]{:S(2)}) collective-permute-start(bf16[1024,256]{1,0:T(8,128)(2,1)} %get-tuple-element.27.refs_1_), channel_id=1, source_target_pairs={{0,16},{16,32},{32,48},{48,0},{64,80},{80,96},{96,112},{112,64},{1... | collective-permute-start | bytes 1572872 | tf_op jit(solution)/shard_map/ppermute | solution.py:347
  53.2 23.5 %collective-permute-start.6 = (bf16[1024,256]{1,0:T(8,128)(2,1)}, bf16[1024,256]{1,0:T(8,128)(2,1)}, u32[]{:S(2)}, u32[]{:S(2)}) collective-permute-start(bf16[1024,256]{1,0:T(8,128)(2,1)} %get-tuple-element.27.refs_1_), channel_id=1, source_target_pairs={{0,48},{16,0},{32,16},{48,32},{64,112},{80,64},{96,80},{112,96},{1... | collective-permute-start | bytes 1572872 | tf_op jit(solution)/shard_map/ppermute | solution.py:347
  55.4 16.2 %all-to-all-start.2 = ((bf16[16,16,320]{2,1,0:T(8,128)(2,1)}), bf16[16,16,320]{2,1,0:T(8,128)(2,1)S(1)}, u32[]{:S(2)}, u32[]{:S(2)}) async-start(bf16[16,16,320]{2,1,0:T(8,128)(2,1)} %get-tuple-element.26), calls=%async_computation.2 | async-start | bytes 393216 | tf_op jit(solution)/shard_map/all_to_all | solution.py:319
  63.6 1.0 copy-start.1
  76.7 14.2 %collective-permute-start.16 = (bf16[320,1024]{1,0:T(8,128)(2,1)S(1)}, bf16[320,1024]{1,0:T(8,128)(2,1)}, u32[]{:S(2)}, u32[]{:S(2)}) collective-permute-start(bf16[320,1024]{1,0:T(8,128)(2,1)S(1)} %get-tuple-element.33.refs_1_), channel_id=1, source_target_pairs={{0,64},{16,80},{32,96},{48,112},{64,0},{80,16},{96,32},{112,48},{1... | collective-permute-start | bytes 1966088 | tf_op jit(solution)/shard_map/ppermute | solution.py:347
  77.8 21.1 %collective-permute-start.12 = (bf16[1024,256]{1,0:T(8,128)(2,1)}, bf16[1024,256]{1,0:T(8,128)(2,1)}, u32[]{:S(2)}, u32[]{:S(2)}) collective-permute-start(bf16[1024,256]{1,0:T(8,128)(2,1)} %collective-permute-done.10.refs_0_), channel_id=1, source_target_pairs={{0,16},{16,32},{32,48},{48,0},{64,80},{80,96},{96,112},{112,64},{1... | collective-permute-start | bytes 1572872 | tf_op jit(solution)/shard_map/ppermute | solution.py:347
  78.8 20.1 %collective-permute-start.13 = (bf16[1024,256]{1,0:T(8,128)(2,1)}, bf16[1024,256]{1,0:T(8,128)(2,1)}, u32[]{:S(2)}, u32[]{:S(2)}) collective-permute-start(bf16[1024,256]{1,0:T(8,128)(2,1)} %get-tuple-element.29.refs_1_), channel_id=1, source_target_pairs={{0,48},{16,0},{32,16},{48,32},{64,112},{80,64},{96,80},{112,96},{1... | collective-permute-start | bytes 1572872 | tf_op jit(solution)/shard_map/ppermute | solution.py:347
  80.5 18.1 %all-to-all-start.3 = ((bf16[16,48,128]{2,1,0:T(8,128)(2,1)}), bf16[16,48,128]{2,1,0:T(8,128)(2,1)S(1)}, u32[]{:S(2)}, u32[]{:S(2)}) async-start(bf16[16,48,128]{2,1,0:T(8,128)(2,1)} %get-tuple-element.28), calls=%async_computation.3 | async-start | bytes 393216 | tf_op jit(solution)/shard_map/all_to_all | solution.py:319
  86.8 28.5 %collective-permute-start.14 = (bf16[320,1024]{1,0:T(8,128)(2,1)S(1)}, bf16[320,1024]{1,0:T(8,128)(2,1)}, u32[]{:S(2)}, u32[]{:S(2)}) collective-permute-start(bf16[320,1024]{1,0:T(8,128)(2,1)S(1)} %get-tuple-element.32.refs_0_), channel_id=1, source_target_pairs={{0,16},{16,32},{32,48},{48,0},{64,80},{80,96},{96,112},{112,64},{1... | collective-permute-start | bytes 1966088 | tf_op jit(solution)/shard_map/ppermute | solution.py:347
  86.9 28.4 %collective-permute-start.15 = (bf16[320,1024]{1,0:T(8,128)(2,1)S(1)}, bf16[320,1024]{1,0:T(8,128)(2,1)}, u32[]{:S(2)}, u32[]{:S(2)}) collective-permute-start(bf16[320,1024]{1,0:T(8,128)(2,1)S(1)} %get-tuple-element.32.refs_0_), channel_id=1, source_target_pairs={{0,64},{16,80},{32,96},{48,112},{64,0},{80,16},{96,32},{112,48},{1... | collective-permute-start | bytes 1966088 | tf_op jit(solution)/shard_map/ppermute | solution.py:347
  90.9 24.4 %collective-permute-start.17 = (bf16[320,1024]{1,0:T(8,128)(2,1)}, bf16[320,1024]{1,0:T(8,128)(2,1)}, u32[]{:S(2)}, u32[]{:S(2)}) collective-permute-start(bf16[320,1024]{1,0:T(8,128)(2,1)} %collective-permute-done.16.refs_2_), channel_id=1, source_target_pairs={{0,48},{16,0},{32,16},{48,32},{64,112},{80,64},{96,80},{112,96},{1... | collective-permute-start | bytes 1966088 | tf_op jit(solution)/shard_map/ppermute | solution.py:347
  105.3 15.2 %all-to-all-start.4 = ((bf16[16,16,512]{2,1,0:T(8,128)(2,1)}), bf16[16,16,512]{2,1,0:T(8,128)(2,1)S(1)}, u32[]{:S(2)}, u32[]{:S(2)}) async-start(bf16[16,16,512]{2,1,0:T(8,128)(2,1)} %bitcast.10), calls=%async_computation.4 | async-start | bytes 524288 | tf_op jit(solution)/shard_map/all_to_all | solution.py:319

commit v9 on v8

--- a/solution.py
+++ b/solution.py
@@ -309,6 +309,21 @@
     mixture = jnp.sum(message[:, :half] * rescale, 0)
     attended = (mixture / total).astype(attended_ref.dtype)
     attended_ref[...] = jnp.concatenate([attended[: half // 2], attended[half // 2 :]], 1)
+
+
+def place_and_merge_kernel(where, message_ref, first_ref, second_ref, _, whole_ref, attended_ref, sems):
+    replica = lax.axis_index("dp")
+    copies = []
+    for i, (part, (c, y)) in enumerate(zip((first_ref, second_ref), where)):
+        size = part.shape[0]
+        source = ((replica // 4) ^ c) * 4 + ((replica + y) & 3)
+        target = whole_ref.at[pl.ds(pl.multiple_of(source * size, size), size), :]
+        copies.append(pltpu.make_async_copy(part, target, sems.at[i]))
+    for copy in copies:
+        copy.start()
+    merge_kernel(message_ref, attended_ref)
+    for copy in copies:
+        copy.wait()
 
 
 def total_kernel(terms_ref, after_ref, output_ref):
@@ -465,19 +480,20 @@
     grouped_qkv = place(
         None, [own_qkv, qkv_across], [(0, 0), (1, 0)], 1, qkv_shape
     )
-    attended = pl.pallas_call(
-        merge_kernel,
-        out_shape=jax.ShapeDtypeStruct((slots, own_heads * HD), jnp.bfloat16),
-        compiler_params=pltpu.CompilerParams(vmem_limit_bytes=3 << 20),
-        name="merge",
-    )(message)
-    grouped_out = place(
-        grouped_out,
-        [out_far, out_cross_far],
-        [(0, 2), (1, 2)],
-        0,
-        out_shape,
-    )
+    far = ((0, 2), (1, 2))
+    grouped_out, attended = pl.pallas_call(
+        lambda *refs: place_and_merge_kernel(far, *refs),
+        out_shape=(
+            jax.ShapeDtypeStruct(out_shape, out_far.dtype),
+            jax.ShapeDtypeStruct((slots, own_heads * HD), jnp.bfloat16),
+        ),
+        in_specs=[vmem] * 3 + [anywhere],
+        out_specs=(anywhere, vmem),
+        scratch_shapes=[pltpu.SemaphoreType.DMA((2,))],
+        input_output_aliases={3: 0},
+        compiler_params=pltpu.CompilerParams(vmem_limit_bytes=6 << 20),
+        name="place_and_merge",
+    )(message, out_far, out_cross_far, grouped_out)
     qkv_far, qkv_cross_far = send(qkv_low, ahead), send(qkv_cross_high, behind)
     qkv_cross_low = send(qkv_low, across)
     grouped_qkv = place(

time: 122 us -> 122 us (level)
    pallas_call x7 -> x6, Pallas kernels: 14.6 us -> 12.5 us  [place(): pl.pallas_call(lambda *refs: place_kernel(axis, where, mark, *refs), out_...]
    pallas_call x1, Pallas kernels: 0.36 us -> 2.4 us  [on_device(): pl.pallas_call(lambda *refs: place_and_merge_kernel(far, *refs), out_shap...]
where the time goes in v9:
time: 122 us; the launch traced here: 121 us
  starting transfers between devices  56.4 us (46%)
  waiting for transfers between devices  32.3 us (26%)
  Pallas kernels  26 us (21%)
  matrix products  3.38 us (3%)
  local copies, waits for them, and re-layouts  1.91 us (2%)
    all_to_all x5, starting transfers between devices, exchange(): return lax.all_to_all(blocks, axis, split_axis=0, concat_axis=0, tiled=True)  34.4 us
    ppermute x18, starting transfers between devices, send(): return lax.ppermute(value, 'dp', pairs)  22 us
    all_to_all x5, waiting for transfers between devices, exchange(): return lax.all_to_all(blocks, axis, split_axis=0, concat_axis=0, tiled=True)  21.2 us
    pallas_call x6, Pallas kernels, place(): pl.pallas_call(lambda *refs: place_kernel(axis, where, mark, *refs), out_...  12.5 us
    ppermute x18, waiting for transfers between devices, send(): return lax.ppermute(value, 'dp', pairs)  11.1 us
    pallas_call x1, Pallas kernels, on_device(): pl.pallas_call(lambda *refs: attend_kernel(score_scale, *refs), out_shape...  4.57 us
    dot_general x1, matrix products, on_device(): jnp.dot(attended, grouped_out.T, preferred_element_type=jnp.float32)  3.38 us
    pallas_call x1, Pallas kernels, on_device(): pl.pallas_call(lambda *refs: pack_kernel(groups, *refs), out_shape=jax.Sh...  2.54 us
  transfers between devices with their start and end apart: 23, of which 12 were waited for; matrix products, arithmetic and copies ran while one was open for 4% of the time, Pallas kernels for 19%

profile of v9, /device:TPU:1, one launch (start us, length us, event | category | flops | bytes accessed | tf_op | source)
XLA Modules:
  0.0 121.0 jit_solution(14810725896252071587)
XLA Ops:
  0.6 1.2 %norm.1 = (bf16[4,16,1024]{2,1,0:T(8,128)(2,1)S(1)}, bf16[4,16,1024]{2,1,0:T(8,128)(2,1)S(1)}) custom-call(bf16[2,8,8192]{2,1,0:T(8,128)(2,1)} %states_in.1, bf16[8192]{0:T(1024)(128)(2,1)} %gain_in.1), custom_call_target="tpu_custom_call" | custom-call | tf_op jit(solution)/shard_map/norm/pallas_call | solution.py:365
  1.8 2.1 %collective-permute-start = (bf16[4,16,1024]{2,1,0:T(8,128)(2,1)S(1)}, bf16[4,16,1024]{2,1,0:T(8,128)(2,1)S(1)}, u32[]{:S(2)}, u32[]{:S(2)}) collective-permute-start(bf16[4,16,1024]{2,1,0:T(8,128)(2,1)S(1)} %get-tuple-element.23), channel_id=1, source_target_pairs={{0,64},{16,80},{32,96},{48,112},{64,0},{80,16},{96,32},{112,48},{1... | collective-permute-start | bytes 393224 | tf_op jit(solution)/shard_map/ppermute | solution.py:362
  4.0 2.5 %pack.1.refs_0_ = bf16[16,144,256]{2,1,0:T(8,128)(2,1)} custom-call(bf16[4,16,1024]{2,1,0:T(8,128)(2,1)S(1)} %get-tuple-element.22.refs_0_.own, bf16[64,5120]{1,0:T(8,128)(2,1)} %refs_1_.1, bf16[64,4096]{1,0:T(8,128)(2,1)} %refs_2_.1), custom_call_target="tpu_custom_call" | custom-call | tf_op jit(solution)/shard_map/pack/pallas_call | solution.py:378
  6.7 9.8 %all-to-all-start = ((bf16[16,144,256]{2,1,0:T(8,128)(2,1)}), bf16[16,144,256]{2,1,0:T(8,128)(2,1)S(1)}, u32[]{:S(2)}, u32[]{:S(2)}) async-start(bf16[16,144,256]{2,1,0:T(8,128)(2,1)} %get-tuple-element.25), calls=%async_computation | async-start | bytes 2359296 | tf_op jit(solution)/shard_map/all_to_all | solution.py:334
  16.5 3.0 %collective-permute-start.3 = (bf16[2,16,1024]{2,1,0:T(8,128)(2,1)S(1)}, bf16[2,16,1024]{2,1,0:T(8,128)(2,1)S(1)}, u32[]{:S(2)}, u32[]{:S(2)}) collective-permute-start(bf16[2,16,1024]{2,1,0:T(8,128)(2,1)S(1)} %pad_maximum_fusion.2), channel_id=1, source_target_pairs={{0,32},{16,48},{32,0},{48,16},{64,96},{80,112},{96,64},{112,80},{1... | collective-permute-start | bytes 196616 | tf_op jit(solution)/shard_map/ppermute | solution.py:362
  19.5 0.8 collective-permute-start.2
  20.4 0.8 collective-permute-start.1
  21.1 0.6 collective-permute-done.3.far
  21.7 1.7 %collective-permute-done.2.high = bf16[2,16,1024]{2,1,0:T(8,128)(2,1)S(1)} collective-permute-done((bf16[2,16,1024]{2,1,0:T(8,128)(2,1)S(1)}, bf16[2,16,1024]{2,1,0:T(8,128)(2,1)S(1)}, u32[]{:S(2)}, u32[]{:S(2)}) %collective-permute-start.2) | collective-permute-done | bytes 65568 | tf_op jit(solution)/shard_map/ppermute | solution.py:362
  23.4 1.6 %collective-permute-done.1.low = bf16[2,16,1024]{2,1,0:T(8,128)(2,1)S(1)} collective-permute-done((bf16[2,16,1024]{2,1,0:T(8,128)(2,1)S(1)}, bf16[2,16,1024]{2,1,0:T(8,128)(2,1)S(1)}, u32[]{:S(2)}, u32[]{:S(2)}) %collective-permute-start.1) | collective-permute-done | bytes 65568 | tf_op jit(solution)/shard_map/ppermute | solution.py:362
  25.1 10.0 %all-to-all-done.packed_ref = bf16[16,144,256]{2,1,0:T(8,128)(2,1)S(1)} async-done(((bf16[16,144,256]{2,1,0:T(8,128)(2,1)}), bf16[16,144,256]{2,1,0:T(8,128)(2,1)S(1)}, u32[]{:S(2)}, u32[]{:S(2)}) %all-to-all-start) | async-done | bytes 1179680 | tf_op jit(solution)/shard_map/all_to_all | solution.py:334
  35.1 1.1 terms.1
  36.2 0.3 collective-permute-start.4
  36.5 1.3 %collective-permute-start.10 = (bf16[1024,256]{1,0:T(8,128)(2,1)}, bf16[1024,256]{1,0:T(8,128)(2,1)}, u32[]{:S(2)}, u32[]{:S(2)}) collective-permute-start(bf16[1024,256]{1,0:T(8,128)(2,1)} %get-tuple-element.27.refs_0_), channel_id=1, source_target_pairs={{0,16},{16,32},{32,48},{48,0},{64,80},{80,96},{96,112},{112,64},{1... | collective-permute-start | bytes 1572872 | tf_op jit(solution)/shard_map/ppermute | solution.py:362
  37.8 1.4 %collective-permute-start.11 = (bf16[1024,256]{1,0:T(8,128)(2,1)}, bf16[1024,256]{1,0:T(8,128)(2,1)}, u32[]{:S(2)}, u32[]{:S(2)}) collective-permute-start(bf16[1024,256]{1,0:T(8,128)(2,1)} %get-tuple-element.27.refs_0_), channel_id=1, source_target_pairs={{0,48},{16,0},{32,16},{48,32},{64,112},{80,64},{96,80},{112,96},{1... | collective-permute-start | bytes 1572872 | tf_op jit(solution)/shard_map/ppermute | solution.py:362
  39.3 3.8 %all-to-all-start.1 = ((bf16[8,16,320]{2,1,0:T(8,128)(2,1)}), bf16[8,16,320]{2,1,0:T(8,128)(2,1)S(1)}, u32[]{:S(2)}, u32[]{:S(2)}) async-start(bf16[8,16,320]{2,1,0:T(8,128)(2,1)} %get-tuple-element.26), calls=%async_computation.1 | async-start | bytes 196608 | tf_op jit(solution)/shard_map/all_to_all | solution.py:334
  43.4 1.5 %collective-permute-start.7 = (bf16[320,1024]{1,0:T(8,128)(2,1)S(1)}, bf16[320,1024]{1,0:T(8,128)(2,1)S(1)}, u32[]{:S(2)}, u32[]{:S(2)}) collective-permute-start(bf16[320,1024]{1,0:T(8,128)(2,1)S(1)} %turn.1.refs_0_), channel_id=1, source_target_pairs={{0,16},{16,32},{32,48},{48,0},{64,80},{80,96},{96,112},{112,64},{1... | collective-permute-start | bytes 1966088 | tf_op jit(solution)/shard_map/ppermute | solution.py:362
  44.9 1.3 %collective-permute-start.8 = (bf16[320,1024]{1,0:T(8,128)(2,1)S(1)}, bf16[320,1024]{1,0:T(8,128)(2,1)S(1)}, u32[]{:S(2)}, u32[]{:S(2)}) collective-permute-start(bf16[320,1024]{1,0:T(8,128)(2,1)S(1)} %turn.1.refs_0_), channel_id=1, source_target_pairs={{0,48},{16,0},{32,16},{48,32},{64,112},{80,64},{96,80},{112,96},{1... | collective-permute-start | bytes 1966088 | tf_op jit(solution)/shard_map/ppermute | solution.py:362
  46.2 2.8 %collective-permute-done.4.refs_0_ = bf16[1024,256]{1,0:T(8,128)(2,1)S(1)} collective-permute-done((bf16[1024,256]{1,0:T(8,128)(2,1)}, bf16[1024,256]{1,0:T(8,128)(2,1)S(1)}, u32[]{:S(2)}, u32[]{:S(2)}) %collective-permute-start.4) | collective-permute-done | bytes 524320 | tf_op jit(solution)/shard_map/ppermute | solution.py:362
  49.4 2.6 %all-to-all-done.1.terms_ref = bf16[8,16,320]{2,1,0:T(8,128)(2,1)S(1)} async-done(((bf16[8,16,320]{2,1,0:T(8,128)(2,1)}), bf16[8,16,320]{2,1,0:T(8,128)(2,1)S(1)}, u32[]{:S(2)}, u32[]{:S(2)}) %all-to-all-start.1) | async-done | bytes 81952 | tf_op jit(solution)/shard_map/all_to_all | solution.py:334
  52.0 0.7 sum.1
  52.7 0.5 collective-permute-start.5
  53.2 2.1 %collective-permute-start.6 = (bf16[1024,256]{1,0:T(8,128)(2,1)}, bf16[1024,256]{1,0:T(8,128)(2,1)}, u32[]{:S(2)}, u32[]{:S(2)}) collective-permute-start(bf16[1024,256]{1,0:T(8,128)(2,1)} %get-tuple-element.29.refs_1_), channel_id=1, source_target_pairs={{0,48},{16,0},{32,16},{48,32},{64,112},{80,64},{96,80},{112,96},{1... | collective-permute-start | bytes 1572872 | tf_op jit(solution)/shard_map/ppermute | solution.py:362
  55.4 8.0 %all-to-all-start.2 = ((bf16[16,16,320]{2,1,0:T(8,128)(2,1)}), bf16[16,16,320]{2,1,0:T(8,128)(2,1)S(1)}, u32[]{:S(2)}, u32[]{:S(2)}) async-start(bf16[16,16,320]{2,1,0:T(8,128)(2,1)} %get-tuple-element.28), calls=%async_computation.2 | async-start | bytes 393216 | tf_op jit(solution)/shard_map/all_to_all | solution.py:334
  63.6 1.0 copy-done.1
  64.7 2.0 %place.6.refs_2_ = bf16[8192,256]{1,0:T(8,128)(2,1)} custom-call(bf16[1024,256]{1,0:T(8,128)(2,1)} %get-tuple-element.27.refs_0_, bf16[1024,256]{1,0:T(8,128)(2,1)S(1)} %copy-done.1), custom_call_target="tpu_custom_call" | custom-call | tf_op jit(solution)/shard_map/place/pallas_call | solution.py:170
  66.7 2.2 %place.7.refs_6_ = bf16[8192,256]{1,0:T(8,128)(2,1)} custom-call(bf16[1024,256]{1,0:T(8,128)(2,1)} %collective-permute-done.10.refs_0_, bf16[1024,256]{1,0:T(8,128)(2,1)} %collective-permute-done.11.refs_1_, bf16[8192,256]{1,0:T(8,128)(2,1)} %place.6.refs_2_), custom_call_target="tpu_custom_call", output_to_operand_aliasing={{}: (2, {})} | custom-call | tf_op jit(solution)/shard_map/place/pallas_call | solution.py:170
  68.9 2.8 %all-to-all-done.2.refs_3_ = bf16[16,16,320]{2,1,0:T(8,128)(2,1)S(1)} async-done(((bf16[16,16,320]{2,1,0:T(8,128)(2,1)}), bf16[16,16,320]{2,1,0:T(8,128)(2,1)S(1)}, u32[]{:S(2)}, u32[]{:S(2)}) %all-to-all-start.2) | async-done | bytes 163872 | tf_op jit(solution)/shard_map/all_to_all | solution.py:334
  71.6 4.6 %attend.1.refs_0_ = bf16[16,48,128]{2,1,0:T(8,128)(2,1)} custom-call(s32[8]{0:T(128)S(1)} %copy-done.2, f32[16,128]{1,0:T(8,128)S(1)} %get-tuple-element.50.refs_1_, f32[16,128]{1,0:T(8,128)S(1)} %get-tuple-element.51.refs_2_, bf16[16,16,320]{2,1,0:T(8,128)(2,1)S(1)} %all-to-all-done.2.refs_3_, bf16[8,256,512]{2,1,0:T(8,128)(2,1)} %refs_4_.1, ...), custom_call_target="tpu_custom_call" | custom-call | tf_op jit(solution)/shard_map/attend/pallas_call | solution.py:453
  76.3 0.4 collective-permute-done.5.refs_1_
  76.7 1.2 collective-permute-start.16
  77.8 1.0 collective-permute-start.12
  78.8 1.7 %collective-permute-start.13 = (bf16[1024,256]{1,0:T(8,128)(2,1)}, bf16[1024,256]{1,0:T(8,128)(2,1)}, u32[]{:S(2)}, u32[]{:S(2)}) collective-permute-start(bf16[1024,256]{1,0:T(8,128)(2,1)} %get-tuple-element.31.refs_1_), channel_id=1, source_target_pairs={{0,48},{16,0},{32,16},{48,32},{64,112},{80,64},{96,80},{112,96},{1... | collective-permute-start | bytes 1572872 | tf_op jit(solution)/shard_map/ppermute | solution.py:362
  80.5 6.3 %all-to-all-start.3 = ((bf16[16,48,128]{2,1,0:T(8,128)(2,1)}), bf16[16,48,128]{2,1,0:T(8,128)(2,1)S(1)}, u32[]{:S(2)}, u32[]{:S(2)}) async-start(bf16[16,48,128]{2,1,0:T(8,128)(2,1)} %get-tuple-element.30), calls=%async_computation.3 | async-start | bytes 393216 | tf_op jit(solution)/shard_map/all_to_all | solution.py:334
  86.9 0.3 collective-permute-start.15
  87.2 3.7 %collective-permute-done.16.refs_2_ = bf16[320,1024]{1,0:T(8,128)(2,1)} collective-permute-done((bf16[320,1024]{1,0:T(8,128)(2,1)S(1)}, bf16[320,1024]{1,0:T(8,128)(2,1)}, u32[]{:S(2)}, u32[]{:S(2)}) %collective-permute-start.16) | collective-permute-done | bytes 655392 | tf_op jit(solution)/shard_map/ppermute | solution.py:362
  90.9 2.2 %collective-permute-start.17 = (bf16[320,1024]{1,0:T(8,128)(2,1)}, bf16[320,1024]{1,0:T(8,128)(2,1)}, u32[]{:S(2)}, u32[]{:S(2)}) collective-permute-start(bf16[320,1024]{1,0:T(8,128)(2,1)} %collective-permute-done.16.refs_2_), channel_id=1, source_target_pairs={{0,48},{16,0},{32,16},{48,32},{64,112},{80,64},{96,80},{112,96},{1... | collective-permute-start | bytes 1966088 | tf_op jit(solution)/shard_map/ppermute | solution.py:362
  93.1 2.0 %place.8.refs_3_ = bf16[8192,256]{1,0:T(8,128)(2,1)} custom-call(bf16[1024,256]{1,0:T(8,128)(2,1)S(1)} %get-tuple-element.32.refs_0_, bf16[1024,256]{1,0:T(8,128)(2,1)} %get-tuple-element.31.refs_1_, bf16[8192,256]{1,0:T(8,128)(2,1)} %get-tuple-element.33.refs_2_), custom_call_target="tpu_custom_call", output_to_operand_aliasing={{}: (2, {})} | custom-call | tf_op jit(solution)/shard_map/place/pallas_call | solution.py:170
  95.1 3.4 %all-to-all-done.3.refs_0_ = bf16[16,48,128]{2,1,0:T(8,128)(2,1)S(1)} async-done(((bf16[16,48,128]{2,1,0:T(8,128)(2,1)}), bf16[16,48,128]{2,1,0:T(8,128)(2,1)S(1)}, u32[]{:S(2)}, u32[]{:S(2)}) %all-to-all-start.3) | async-done | bytes 196640 | tf_op jit(solution)/shard_map/all_to_all | solution.py:334
  98.6 2.4 %place_and_merge.1 = (bf16[8192,256]{1,0:T(8,128)(2,1)}, bf16[16,256]{1,0:T(8,128)(2,1)S(1)}) custom-call(bf16[16,48,128]{2,1,0:T(8,128)(2,1)S(1)} %all-to-all-done.3.refs_0_, bf16[1024,256]{1,0:T(8,128)(2,1)} %collective-permute-done.12.refs_1_, bf16[1024,256]{1,0:T(8,128)(2,1)} %collective-permute-done.13.refs_2_, ...), custom_call_target="tpu_custom_call", output_to_operand_aliasing={{0}: (3, {})} | custom-call | tf_op jit(solution)/shard_map/place_and_merge/pallas_call | solution.py:484
  101.0 3.4 %convolution_convert_fusion = bf16[16,8192]{1,0:T(8,128)(2,1)S(1)} fusion(bf16[16,256]{1,0:T(8,128)(2,1)S(1)} %get-tuple-element.34, bf16[8192,256]{1,0:T(8,128)(2,1)} %get-tuple-element.21), kind=kOutput, calls=%fused_computation | convolution fusion | flops 67239936 | bytes 4464640 | tf_op jit(solution)/shard_map/dot_general | solution.py:515
  104.4 0.7 copy.29
  105.1 6.5 %all-to-all-start.4 = ((bf16[16,16,512]{2,1,0:T(8,128)(2,1)}), bf16[16,16,512]{2,1,0:T(8,128)(2,1)S(1)}, u32[]{:S(2)}, u32[]{:S(2)}) async-start(bf16[16,16,512]{2,1,0:T(8,128)(2,1)} %bitcast.10), calls=%async_computation.4 | async-start | bytes 524288 | tf_op jit(solution)/shard_map/all_to_all | solution.py:334
  111.7 1.1 place.9.refs_3_
  112.7 2.4 %place.10.refs_3_ = bf16[320,8192]{1,0:T(8,128)(2,1)} custom-call(bf16[320,1024]{1,0:T(8,128)(2,1)S(1)} %get-tuple-element.36.refs_0_, bf16[320,1024]{1,0:T(8,128)(2,1)S(1)} %get-tuple-element.37.refs_1_, bf16[320,1024]{1,0:T(8,128)(2,1)} %collective-permute-done.16.refs_2_, bf16[320,8192]{1,0:T(8,128)(2,1)} %place.9.refs_3_), custom_call_target="tpu_custom_call", output_to_operand_aliasing={{}: (3, {})} | custom-call | tf_op jit(solution)/shard_map/place/pallas_call | solution.py:170
  115.2 2.8 %place.11 = (bf16[320,8192]{1,0:T(8,128)(2,1)}, f32[8,128]{1,0:T(8,128)S(1)}) custom-call(bf16[320,1024]{1,0:T(8,128)(2,1)} %collective-permute-done.14.refs_0_, bf16[320,1024]{1,0:T(8,128)(2,1)} %collective-permute-done.15.refs_1_, bf16[320,1024]{1,0:T(8,128)(2,1)} %collective-permute-done.17.refs_2_, ...), custom_call_target="tpu_custom_call", output_to_operand_aliasing={{0}: (3, {})} | custom-call | tf_op jit(solution)/shard_map/place/pallas_call | solution.py:170
  118.0 2.4 %all-to-all-done.4.terms_ref = bf16[16,16,512]{2,1,0:T(8,128)(2,1)S(1)} async-done(((bf16[16,16,512]{2,1,0:T(8,128)(2,1)}), bf16[16,16,512]{2,1,0:T(8,128)(2,1)S(1)}, u32[]{:S(2)}, u32[]{:S(2)}) %all-to-all-start.4) | async-done | bytes 262176 | tf_op jit(solution)/shard_map/all_to_all | solution.py:334
  120.3 0.6 total.1
  (35 shorter events, 1.2 us)
Async XLA Ops:
  1.8 4.8 %collective-permute-start = (bf16[4,16,1024]{2,1,0:T(8,128)(2,1)S(1)}, bf16[4,16,1024]{2,1,0:T(8,128)(2,1)S(1)}, u32[]{:S(2)}, u32[]{:S(2)}) collective-permute-start(bf16[4,16,1024]{2,1,0:T(8,128)(2,1)S(1)} %get-tuple-element.23), channel_id=1, source_target_pairs={{0,64},{16,80},{32,96},{48,112},{64,0},{80,16},{96,32},{112,48},{1... | collective-permute-start | bytes 393224 | tf_op jit(solution)/shard_map/ppermute | solution.py:362
  4.0 39.1 %copy-start.3 = (bf16[320]{0:T(512)(128)(2,1)S(1)}, bf16[320]{0:T(512)(128)(2,1)}, u32[]{:S(2)}) copy-start(bf16[320]{0:T(512)(128)(2,1)} %param.10) | copy-start | bytes 1924
  6.5 48.8 %copy-start.2 = (s32[8]{0:T(128)S(1)}, s32[8]{0:T(128)}, u32[]{:S(2)}) copy-start(s32[8]{0:T(128)} %refs_0_.1) | copy-start | bytes 100
  6.7 28.4 %all-to-all-start = ((bf16[16,144,256]{2,1,0:T(8,128)(2,1)}), bf16[16,144,256]{2,1,0:T(8,128)(2,1)S(1)}, u32[]{:S(2)}, u32[]{:S(2)}) async-start(bf16[16,144,256]{2,1,0:T(8,128)(2,1)} %get-tuple-element.25), calls=%async_computation | async-start | bytes 2359296 | tf_op jit(solution)/shard_map/all_to_all | solution.py:334
  16.5 5.2 %collective-permute-start.3 = (bf16[2,16,1024]{2,1,0:T(8,128)(2,1)S(1)}, bf16[2,16,1024]{2,1,0:T(8,128)(2,1)S(1)}, u32[]{:S(2)}, u32[]{:S(2)}) collective-permute-start(bf16[2,16,1024]{2,1,0:T(8,128)(2,1)S(1)} %pad_maximum_fusion.2), channel_id=1, source_target_pairs={{0,32},{16,48},{32,0},{48,16},{64,96},{80,112},{96,64},{112,80},{1... | collective-permute-start | bytes 196616 | tf_op jit(solution)/shard_map/ppermute | solution.py:362
  19.5 3.9 %collective-permute-start.2 = (bf16[2,16,1024]{2,1,0:T(8,128)(2,1)S(1)}, bf16[2,16,1024]{2,1,0:T(8,128)(2,1)S(1)}, u32[]{:S(2)}, u32[]{:S(2)}) collective-permute-start(bf16[2,16,1024]{2,1,0:T(8,128)(2,1)S(1)} %pad_maximum_fusion.1), channel_id=1, source_target_pairs={{0,48},{16,0},{32,16},{48,32},{64,112},{80,64},{96,80},{112,96},{1... | collective-permute-start | bytes 196616 | tf_op jit(solution)/shard_map/ppermute | solution.py:362
  20.4 4.7 %collective-permute-start.1 = (bf16[2,16,1024]{2,1,0:T(8,128)(2,1)S(1)}, bf16[2,16,1024]{2,1,0:T(8,128)(2,1)S(1)}, u32[]{:S(2)}, u32[]{:S(2)}) collective-permute-start(bf16[2,16,1024]{2,1,0:T(8,128)(2,1)S(1)} %pad_maximum_fusion), channel_id=1, source_target_pairs={{0,16},{16,32},{32,48},{48,0},{64,80},{80,96},{96,112},{112,64},{1... | collective-permute-start | bytes 196616 | tf_op jit(solution)/shard_map/ppermute | solution.py:362
  36.2 12.8 %collective-permute-start.4 = (bf16[1024,256]{1,0:T(8,128)(2,1)}, bf16[1024,256]{1,0:T(8,128)(2,1)S(1)}, u32[]{:S(2)}, u32[]{:S(2)}) collective-permute-start(bf16[1024,256]{1,0:T(8,128)(2,1)} %get-tuple-element.27.refs_0_), channel_id=1, source_target_pairs={{0,64},{16,80},{32,96},{48,112},{64,0},{80,16},{96,32},{112,48},{1... | collective-permute-start | bytes 1572872 | tf_op jit(solution)/shard_map/ppermute | solution.py:362
  36.5 16.1 %collective-permute-start.10 = (bf16[1024,256]{1,0:T(8,128)(2,1)}, bf16[1024,256]{1,0:T(8,128)(2,1)}, u32[]{:S(2)}, u32[]{:S(2)}) collective-permute-start(bf16[1024,256]{1,0:T(8,128)(2,1)} %get-tuple-element.27.refs_0_), channel_id=1, source_target_pairs={{0,16},{16,32},{32,48},{48,0},{64,80},{80,96},{96,112},{112,64},{1... | collective-permute-start | bytes 1572872 | tf_op jit(solution)/shard_map/ppermute | solution.py:362
  37.8 15.4 %collective-permute-start.11 = (bf16[1024,256]{1,0:T(8,128)(2,1)}, bf16[1024,256]{1,0:T(8,128)(2,1)}, u32[]{:S(2)}, u32[]{:S(2)}) collective-permute-start(bf16[1024,256]{1,0:T(8,128)(2,1)} %get-tuple-element.27.refs_0_), channel_id=1, source_target_pairs={{0,48},{16,0},{32,16},{48,32},{64,112},{80,64},{96,80},{112,96},{1... | collective-permute-start | bytes 1572872 | tf_op jit(solution)/shard_map/ppermute | solution.py:362
  39.3 12.7 %all-to-all-start.1 = ((bf16[8,16,320]{2,1,0:T(8,128)(2,1)}), bf16[8,16,320]{2,1,0:T(8,128)(2,1)S(1)}, u32[]{:S(2)}, u32[]{:S(2)}) async-start(bf16[8,16,320]{2,1,0:T(8,128)(2,1)} %get-tuple-element.26), calls=%async_computation.1 | async-start | bytes 196608 | tf_op jit(solution)/shard_map/all_to_all | solution.py:334
  43.4 32.9 %collective-permute-start.7 = (bf16[320,1024]{1,0:T(8,128)(2,1)S(1)}, bf16[320,1024]{1,0:T(8,128)(2,1)S(1)}, u32[]{:S(2)}, u32[]{:S(2)}) collective-permute-start(bf16[320,1024]{1,0:T(8,128)(2,1)S(1)} %turn.1.refs_0_), channel_id=1, source_target_pairs={{0,16},{16,32},{32,48},{48,0},{64,80},{80,96},{96,112},{112,64},{1... | collective-permute-start | bytes 1966088 | tf_op jit(solution)/shard_map/ppermute | solution.py:362
  44.9 31.3 %collective-permute-start.8 = (bf16[320,1024]{1,0:T(8,128)(2,1)S(1)}, bf16[320,1024]{1,0:T(8,128)(2,1)S(1)}, u32[]{:S(2)}, u32[]{:S(2)}) collective-permute-start(bf16[320,1024]{1,0:T(8,128)(2,1)S(1)} %turn.1.refs_0_), channel_id=1, source_target_pairs={{0,48},{16,0},{32,16},{48,32},{64,112},{80,64},{96,80},{112,96},{1... | collective-permute-start | bytes 1966088 | tf_op jit(solution)/shard_map/ppermute | solution.py:362
  49.0 2.9 %copy-start = (bf16[1024,256]{1,0:T(8,128)(2,1)}, bf16[1024,256]{1,0:T(8,128)(2,1)S(1)}, u32[]{:S(2)}) copy-start(bf16[1024,256]{1,0:T(8,128)(2,1)S(1)} %collective-permute-done.4.refs_0_) | copy-start | bytes 1572868
  49.0 27.2 %collective-permute-start.9 = (bf16[320,1024]{1,0:T(8,128)(2,1)S(1)}, bf16[320,1024]{1,0:T(8,128)(2,1)S(1)}, u32[]{:S(2)}, u32[]{:S(2)}) collective-permute-start(bf16[320,1024]{1,0:T(8,128)(2,1)S(1)} %turn.1.refs_0_), channel_id=1, source_target_pairs={{0,64},{16,80},{32,96},{48,112},{64,0},{80,16},{96,32},{112,48},{1... | collective-permute-start | bytes 1966088 | tf_op jit(solution)/shard_map/ppermute | solution.py:362
  52.7 24.0 %collective-permute-start.5 = (bf16[1024,256]{1,0:T(8,128)(2,1)}, bf16[1024,256]{1,0:T(8,128)(2,1)S(1)}, u32[]{:S(2)}, u32[]{:S(2)}) collective-permute-start(bf16[1024,256]{1,0:T(8,128)(2,1)} %get-tuple-element.29.refs_1_), channel_id=1, source_target_pairs={{0,16},{16,32},{32,48},{48,0},{64,80},{80,96},{96,112},{112,64},{1... | collective-permute-start | bytes 1572872 | tf_op jit(solution)/shard_map/ppermute | solution.py:362
  53.2 23.5 %collective-permute-start.6 = (bf16[1024,256]{1,0:T(8,128)(2,1)}, bf16[1024,256]{1,0:T(8,128)(2,1)}, u32[]{:S(2)}, u32[]{:S(2)}) collective-permute-start(bf16[1024,256]{1,0:T(8,128)(2,1)} %get-tuple-element.29.refs_1_), channel_id=1, source_target_pairs={{0,48},{16,0},{32,16},{48,32},{64,112},{80,64},{96,80},{112,96},{1... | collective-permute-start | bytes 1572872 | tf_op jit(solution)/shard_map/ppermute | solution.py:362
  55.4 16.2 %all-to-all-start.2 = ((bf16[16,16,320]{2,1,0:T(8,128)(2,1)}), bf16[16,16,320]{2,1,0:T(8,128)(2,1)S(1)}, u32[]{:S(2)}, u32[]{:S(2)}) async-start(bf16[16,16,320]{2,1,0:T(8,128)(2,1)} %get-tuple-element.28), calls=%async_computation.2 | async-start | bytes 393216 | tf_op jit(solution)/shard_map/all_to_all | solution.py:334
  63.6 1.0 copy-start.1
  76.7 14.2 %collective-permute-start.16 = (bf16[320,1024]{1,0:T(8,128)(2,1)S(1)}, bf16[320,1024]{1,0:T(8,128)(2,1)}, u32[]{:S(2)}, u32[]{:S(2)}) collective-permute-start(bf16[320,1024]{1,0:T(8,128)(2,1)S(1)} %get-tuple-element.37.refs_1_), channel_id=1, source_target_pairs={{0,64},{16,80},{32,96},{48,112},{64,0},{80,16},{96,32},{112,48},{1... | collective-permute-start | bytes 1966088 | tf_op jit(solution)/shard_map/ppermute | solution.py:362
  77.8 17.3 %collective-permute-start.12 = (bf16[1024,256]{1,0:T(8,128)(2,1)}, bf16[1024,256]{1,0:T(8,128)(2,1)}, u32[]{:S(2)}, u32[]{:S(2)}) collective-permute-start(bf16[1024,256]{1,0:T(8,128)(2,1)} %collective-permute-done.10.refs_0_), channel_id=1, source_target_pairs={{0,16},{16,32},{32,48},{48,0},{64,80},{80,96},{96,112},{112,64},{1... | collective-permute-start | bytes 1572872 | tf_op jit(solution)/shard_map/ppermute | solution.py:362
  78.8 19.7 %collective-permute-start.13 = (bf16[1024,256]{1,0:T(8,128)(2,1)}, bf16[1024,256]{1,0:T(8,128)(2,1)}, u32[]{:S(2)}, u32[]{:S(2)}) collective-permute-start(bf16[1024,256]{1,0:T(8,128)(2,1)} %get-tuple-element.31.refs_1_), channel_id=1, source_target_pairs={{0,48},{16,0},{32,16},{48,32},{64,112},{80,64},{96,80},{112,96},{1... | collective-permute-start | bytes 1572872 | tf_op jit(solution)/shard_map/ppermute | solution.py:362
  80.5 18.1 %all-to-all-start.3 = ((bf16[16,48,128]{2,1,0:T(8,128)(2,1)}), bf16[16,48,128]{2,1,0:T(8,128)(2,1)S(1)}, u32[]{:S(2)}, u32[]{:S(2)}) async-start(bf16[16,48,128]{2,1,0:T(8,128)(2,1)} %get-tuple-element.30), calls=%async_computation.3 | async-start | bytes 393216 | tf_op jit(solution)/shard_map/all_to_all | solution.py:334
  86.8 28.3 %collective-permute-start.14 = (bf16[320,1024]{1,0:T(8,128)(2,1)S(1)}, bf16[320,1024]{1,0:T(8,128)(2,1)}, u32[]{:S(2)}, u32[]{:S(2)}) collective-permute-start(bf16[320,1024]{1,0:T(8,128)(2,1)S(1)} %get-tuple-element.36.refs_0_), channel_id=1, source_target_pairs={{0,16},{16,32},{32,48},{48,0},{64,80},{80,96},{96,112},{112,64},{1... | collective-permute-start | bytes 1966088 | tf_op jit(solution)/shard_map/ppermute | solution.py:362
  86.9 28.3 %collective-permute-start.15 = (bf16[320,1024]{1,0:T(8,128)(2,1)S(1)}, bf16[320,1024]{1,0:T(8,128)(2,1)}, u32[]{:S(2)}, u32[]{:S(2)}) collective-permute-start(bf16[320,1024]{1,0:T(8,128)(2,1)S(1)} %get-tuple-element.36.refs_0_), channel_id=1, source_target_pairs={{0,64},{16,80},{32,96},{48,112},{64,0},{80,16},{96,32},{112,48},{1... | collective-permute-start | bytes 1966088 | tf_op jit(solution)/shard_map/ppermute | solution.py:362
  90.9 24.3 %collective-permute-start.17 = (bf16[320,1024]{1,0:T(8,128)(2,1)}, bf16[320,1024]{1,0:T(8,128)(2,1)}, u32[]{:S(2)}, u32[]{:S(2)}) collective-permute-start(bf16[320,1024]{1,0:T(8,128)(2,1)} %collective-permute-done.16.refs_2_), channel_id=1, source_target_pairs={{0,48},{16,0},{32,16},{48,32},{64,112},{80,64},{96,80},{112,96},{1... | collective-permute-start | bytes 1966088 | tf_op jit(solution)/shard_map/ppermute | solution.py:362
  105.1 15.2 %all-to-all-start.4 = ((bf16[16,16,512]{2,1,0:T(8,128)(2,1)}), bf16[16,16,512]{2,1,0:T(8,128)(2,1)S(1)}, u32[]{:S(2)}, u32[]{:S(2)}) async-start(bf16[16,16,512]{2,1,0:T(8,128)(2,1)} %bitcast.10), calls=%async_computation.4 | async-start | bytes 524288 | tf_op jit(solution)/shard_map/all_to_all | solution.py:334
